TPU v7x, 512 devices: a whole 4x4x16 slice. The times are simulated.
512 devices in a mesh: layer: 16 (over z), row: 8 (over x, core), col: 4 (over y).
Axes of the slice: x: 4, y: 4, z: 16, core: 2. Of those that a mesh axis runs over, the one named last changes fastest.
Arguments:
- graph: float32 [16384, 4096], P('layer', ('row', 'col')), as said below
- pattern: int32 [128, 32], P('layer', ('row', 'col')), may hold values 0 or 1
Outputs:
- expanded: float32 [4096, 4096], P(('row', 'layer'), 'col')
Inputs may be any that keep to these rules, and one draw needn't show every extreme that they name: `graph`: every edge weight is nonnegative.
All inputs are finite; a program needn't handle non-finite values. No bound on the sum of `pattern` on one device may be relied on, other than what follows from the above.
Results may differ from a plain program's by a relative error of at most 0.00005.
Values sent between devices are 32-bit elements; how exact they have to be, the bound alone decides.
No kernel may reach another device: no remote copies, remote signals or barrier semaphores. Data moves between devices by JAX's collectives and lax.ppermute only.
A program may use at most 64 MiB of HBM per device.

v0:
```python
import jax
import jax.numpy as jnp
from jax import lax
from jax.sharding import PartitionSpec as P


def inner_product(left, right):
    return lax.dot_general(
        left,
        right,
        (((0,), (0,)), ((), ())),
        precision=lax.Precision.HIGHEST,
        preferred_element_type=jnp.float32,
    )


def on_device(graph, pattern):
    inner_rows = graph.shape[0]
    width = graph.shape[1]
    occupied = pattern.astype(jnp.float32)
    masked = (graph.reshape(inner_rows // width, width, width) * occupied[:, :, None]).reshape(
        inner_rows, width
    )
    left = lax.all_gather(masked, "col", axis=1, tiled=True)
    right = lax.all_gather(masked, "row", axis=1, tiled=True)
    return lax.psum_scatter(inner_product(left, right), "layer", scatter_dimension=0, tiled=True)


def solution(mesh):
    placed = (P("layer", ("row", "col")), P("layer", ("row", "col")))
    return jax.shard_map(
        on_device, mesh=mesh, in_specs=placed, out_specs=P(("row", "layer"), "col"), check_vma=False
    )
```

profile of v0, /device:TPU:6, one launch (start us, length us, event | category | flops | bytes accessed | tf_op | source)
XLA Modules:
  0.0 194.4 jit_solution(9703430387936405335)
XLA Ops:
  6.5 0.0 all-gather.3.cloned.1.call-start
  6.5 0.7 convert_bitcast_fusion
  7.2 0.1 broadcast_bitcast_fusion
  7.3 2.1 %broadcast_multiply_fusion = f32[1024,128]{1,0:T(8,128)} fusion(f32[1024,128]{1,0:T(8,128)} %param.2, f32[1024]{0:T(1024)S(1)} %broadcast_bitcast_fusion), kind=kLoop, calls=%fused_computation | loop fusion | flops 131072 | bytes 1052672 | tf_op jit(solution)/shard_map/mul | solution.py:21
  9.3 0.0 all-gather.3.cloned.1.call-update
  9.4 0.0 all-gather.5.cloned.1.call-start
  9.4 0.7 all-gather.5.cloned.1.call-update
  10.1 0.0 reduce-scatter.2.cloned.1.call-start
  10.2 46.0 %all-gather.3.cloned.1.call-done = f32[1024,512]{1,0:T(8,128)} async-done(((f32[1024,128]{1,0:T(8,128)}), f32[1024,512]{1,0:T(8,128)}) %all-gather.3.cloned.1.call-update) | async-done | bytes 2097168 | tf_op jit(solution)/shard_map/all_gather | solution.py:24
  56.1 46.3 %all-gather.5.cloned.1.call-done = f32[1024,1024]{1,0:T(8,128)} async-done(((f32[1024,128]{1,0:T(8,128)}), f32[1024,1024]{1,0:T(8,128)}) %all-gather.5.cloned.1.call-update) | async-done | bytes 4194320 | tf_op jit(solution)/shard_map/all_gather | solution.py:25
  102.4 10.2 %fusion = f32[512,1024]{1,0:T(8,128)} fusion(f32[1024,512]{1,0:T(8,128)} %all-gather.3.cloned.1.call-done, f32[1024,1024]{1,0:T(8,128)} %all-gather.5.cloned.1.call-done), kind=kOutput, calls=%fused_computation.3 | convolution fusion | flops 6442450944 | bytes 8388608 | tf_op jit(solution)/shard_map/dot_general | solution.py:8
  112.6 0.0 reduce-scatter.2.cloned.1.call-update
  112.6 75.2 %reduce-scatter.2.cloned.1.call-done = f32[32,1024]{1,0:T(8,128)} async-done(((f32[512,1024]{1,0:T(8,128)}), f32[32,1024]{1,0:T(8,128)}) %reduce-scatter.2.cloned.1.call-update) | async-done | bytes 131088 | tf_op jit(solution)/shard_map/reduce_scatter | solution.py:26
Async XLA Ops:
  6.5 49.6 %all-gather.3.cloned.1.call-start = ((), (), s32[]{:S(2)}) async-start(), calls=%async_computation.1 | async-start | bytes 2621440 | tf_op jit(solution)/shard_map/all_gather | solution.py:24
  9.4 93.0 %all-gather.5.cloned.1.call-start = ((), (), s32[]{:S(2)}) async-start(), calls=%async_computation.2 | async-start | bytes 4718592 | tf_op jit(solution)/shard_map/all_gather | solution.py:25
  10.1 177.7 %reduce-scatter.2.cloned.1.call-start = ((), (), s32[]{:S(2)}) async-start(), calls=%async_computation.3 | async-start | bytes 2228224 | tf_op jit(solution)/shard_map/reduce_scatter | solution.py:26
Sparse Core Ops, SparseCore 0:
  9.5 46.5 all-gather.2
  58.2 44.1 all-gather.4
  112.8 75.0 reduce-scatter.1
where the time goes:
time: 195 us; the launch traced here: 194 us
  waiting for transfers between devices  168 us (86%)
  between operations  13.1 us (7%)
  matrix products  10.2 us (5%)
  other arithmetic  2.72 us (1%)
    reduce_scatter x1, waiting for transfers between devices, on_device(): lax.psum_scatter(inner_product(left, right), 'layer', scatter_dimension=0...  75.2 us
    all_gather x1, waiting for transfers between devices, on_device(): right = lax.all_gather(masked, 'row', axis=1, tiled=True)  46.3 us
    all_gather x1, waiting for transfers between devices, on_device(): left = lax.all_gather(masked, 'col', axis=1, tiled=True)  46 us
    dot_general x1, matrix products, inner_product(): lax.dot_general(left, right, (((0,), (0,)), ((), ())), precision=lax.Prec...  10.2 us
  transfers between devices with their start and end apart: 3, of which 3 were waited for; matrix products, arithmetic and copies ran while one was open for 0% of the time, Pallas kernels for 0%

commit v1 on v0

v1 whole, which is shorter than its diff:
```python
import functools

import jax
import jax.numpy as jnp
from jax import lax
from jax.experimental import pallas as pl
from jax.experimental.pallas import tpu as pltpu
from jax.sharding import PartitionSpec as P

TILE = 128
N_LAYER = 16
N_X = 4
N_COL = 4
SUB = 32
VMEM = pl.BlockSpec(memory_space=pltpu.VMEM)
SMEM = pl.BlockSpec(memory_space=pltpu.SMEM)
LIMIT = 40 * 1024 * 1024


def call(kernel, outs, operands, specs=None, scratch=(), flops=0, nbytes=1 << 20):
    return pl.pallas_call(
        kernel,
        out_shape=tuple(jax.ShapeDtypeStruct(s, jnp.float32) for s in outs),
        in_specs=specs or [VMEM] * len(operands),
        out_specs=tuple(VMEM for _ in outs),
        scratch_shapes=list(scratch),
        compiler_params=pltpu.CompilerParams(vmem_limit_bytes=LIMIT),
        cost_estimate=pl.CostEstimate(flops=flops, bytes_accessed=nbytes, transcendentals=0),
    )(*operands)


def mask_kernel(graph, pattern, masked, turned):
    for k in range(graph.shape[0] // TILE):
        rows = pl.ds(k * TILE, TILE)
        block = graph[rows, :] * pattern[k].astype(jnp.float32)
        masked[rows, :] = block
        turned[:, rows] = block.T


def split(value):
    high = value.astype(jnp.bfloat16)
    low = (value - high.astype(jnp.float32)).astype(jnp.bfloat16)
    return high, low


def product_kernel(*refs):
    lefts, rights, others = refs[:4], refs[4:8], refs[8:12]
    own, up, down, far_a, far_b = refs[12:17]
    left_high, left_low, total = refs[17:]
    z, row, y = lax.axis_index("layer"), lax.axis_index("row"), lax.axis_index("col")
    for t in range(4):
        rows = pl.ds(t * TILE, TILE)
        left_high[rows, :], left_low[rows, :] = split(lefts[t][...])

    for t in range(4):
        right = jnp.concatenate([rights[t][...], others[t][...]], axis=1)
        high, low = split(right)
        dot = functools.partial(jnp.dot, preferred_element_type=jnp.float32)
        block = dot(left_high[...], high) + (dot(left_high[...], low) + dot(left_low[...], high))
        q = lax.rem(row + 2 * t, 2 * N_X)
        partner = q + 1 - 2 * lax.rem(q, 2)
        total[:, pl.ds(pl.multiple_of(q * TILE, TILE), TILE)] = block[:, :TILE]
        total[:, pl.ds(pl.multiple_of(partner * TILE, TILE), TILE)] = block[:, TILE:]

    for c in range(N_COL):
        t = lax.rem(c - y + N_COL, N_COL)

        def strip(shift):
            return pl.ds(pl.multiple_of(t * TILE + lax.rem(z + shift, 4) * SUB, SUB), SUB)

        rows = pl.ds(c * SUB, SUB)
        half = total.shape[1] // 2
        own[rows, :] = total[strip(0), :]
        up[rows, :] = total[strip(1), :]
        down[rows, :] = total[strip(3), :]
        far_a[rows, :] = total[strip(2), :half]
        far_b[rows, :] = total[strip(2), half:]


def near_sum_kernel(own, up, down, far_a, far_b, *outs):
    home = lax.axis_index("layer") // 4
    half = own.shape[1] // 2
    for shift in range(4):
        c = lax.rem(home + shift, 4)
        rows = pl.ds(pl.multiple_of(c * SUB, SUB), SUB)
        near = own[rows, :] + (up[rows, :] + down[rows, :])
        outs[shift][:, :half] = near[:, :half] + far_a[rows, :]
        outs[shift][:, half:] = near[:, half:] + far_b[rows, :]


def last_sum_kernel(a, b, c, d, out):
    out[...] = (a[...] + b[...]) + (c[...] + d[...])


def layers_up(value, shift):
    return lax.ppermute(value, "layer", [(i, (i + shift) % N_LAYER) for i in range(N_LAYER)])


def from_col(value, t):
    return lax.ppermute(value, "col", [((i + t) % N_COL, i) for i in range(N_COL)])


def from_chip(value, t):
    return lax.ppermute(
        value, "row", [(2 * ((x + t) % N_X) + k, 2 * x + k) for x in range(N_X) for k in range(2)]
    )


def swap(value):
    return lax.ppermute(value, "row", [(i, i ^ 1) for i in range(2 * N_X)])


def on_device(graph, pattern):
    inner = graph.shape[0]
    masked, turned = call(
        mask_kernel, [(inner, TILE), (TILE, inner)], (graph, pattern.reshape(-1)), [VMEM, SMEM]
    )
    lefts, rights, others = {0: turned}, {0: masked}, {}
    for t in (1, 3, 2):
        lefts[t] = from_col(turned, t)
        rights[t] = from_chip(masked, t)
    for t in (0, 1, 3, 2):
        others[t] = swap(rights[t])
    operands = [d[t] for d in (lefts, rights, others) for t in range(4)]
    rows, width = 4 * SUB, 8 * TILE
    sends = call(
        product_kernel,
        [(rows, width)] * 3 + [(rows, width // 2)] * 2,
        operands,
        scratch=[
            pltpu.VMEM((4 * TILE, inner), jnp.bfloat16),
            pltpu.VMEM((4 * TILE, inner), jnp.bfloat16),
            pltpu.VMEM((4 * TILE, width), jnp.float32),
        ],
        flops=6 * 512 * 1024 * 1024,
        nbytes=8 << 20,
    )
    own, up, down, far_a, far_b = sends
    chunks = call(
        near_sum_kernel,
        [(SUB, width)] * 4,
        (own, layers_up(up, 1), layers_up(down, -1), layers_up(far_a, -2), layers_up(far_b, 2)),
    )
    return call(
        last_sum_kernel,
        [(SUB, width)],
        (chunks[0], layers_up(chunks[1], 4), layers_up(chunks[3], -4), layers_up(chunks[2], 8)),
    )[0]


def solution(mesh):
    placed = (P("layer", ("row", "col")), P("layer", ("row", "col")))
    return jax.shard_map(
        on_device, mesh=mesh, in_specs=placed, out_specs=P(("row", "layer"), "col"), check_vma=False
    )
```

time: 195 us -> 121 us (0.62)
  the two profiles are of different devices: /device:TPU:6 before, /device:TPU:34 now
where the time goes in v1:
time: 121 us
  starting transfers between devices  67.8 us (56%)
  waiting for transfers between devices  45.5 us (38%)
  Pallas kernels  5.3 us (4%)
  local copies, waits for them, and re-layouts  1.7 us (1%)
    ppermute x7, starting transfers between devices, layers_up(): lax.ppermute(value, 'layer', [(i, (i + shift) % N_LAYER) for i in range(N...  37.6 us
    ppermute x7, waiting for transfers between devices, layers_up(): lax.ppermute(value, 'layer', [(i, (i + shift) % N_LAYER) for i in range(N...  32.8 us
    ppermute x3, starting transfers between devices, from_col(): lax.ppermute(value, 'col', [((i + t) % N_COL, i) for i in range(N_COL)])  11.6 us
    ppermute x3, starting transfers between devices, from_chip(): lax.ppermute(value, 'row', [(2 * ((x + t) % N_X) + k, 2 * x + k) for x in...  10.5 us
    ppermute x4, starting transfers between devices, swap(): return lax.ppermute(value, 'row', [(i, i ^ 1) for i in range(2 * N_X)])  8.15 us
    ppermute x3, waiting for transfers between devices, from_col(): lax.ppermute(value, 'col', [((i + t) % N_COL, i) for i in range(N_COL)])  7.16 us
    pallas_call x4, Pallas kernels, call(): pl.pallas_call(kernel, out_shape=tuple((jax.ShapeDtypeStruct(s, jnp.float...  5.3 us
    ppermute x3, waiting for transfers between devices, from_chip(): lax.ppermute(value, 'row', [(2 * ((x + t) % N_X) + k, 2 * x + k) for x in...  3.65 us
  transfers between devices with their start and end apart: 17, of which 6 were waited for; matrix products, arithmetic and copies ran while one was open for 0% of the time, Pallas kernels for 0%

profile of v1, /device:TPU:34, one launch (start us, length us, event | category | flops | bytes accessed | tf_op | source)
XLA Modules:
  0.0 120.5 jit_solution(14141868092662849297)
XLA Ops:
  2.5 3.5 %collective-permute-start.2 = (f32[128,1024]{1,0:T(8,128)S(1)}, f32[128,1024]{1,0:T(8,128)S(1)}, u32[]{:S(2)}, u32[]{:S(2)}) collective-permute-start(f32[128,1024]{1,0:T(8,128)S(1)} %get-tuple-element.16.refs_0_), channel_id=1, source_target_pairs={{3,0},{0,1},{1,2},{2,3},{7,4},{4,5},{5,6},{6,7},{11,8},{8,9},{9,10... | collective-permute-start | bytes 1572872 | tf_op jit(solution)/shard_map/ppermute | solution.py:100
  5.9 4.8 %collective-permute-start.1 = (f32[128,1024]{1,0:T(8,128)S(1)}, f32[128,1024]{1,0:T(8,128)S(1)}, u32[]{:S(2)}, u32[]{:S(2)}) collective-permute-start(f32[128,1024]{1,0:T(8,128)S(1)} %get-tuple-element.16.refs_0_), channel_id=1, source_target_pairs={{2,0},{3,1},{0,2},{1,3},{6,4},{7,5},{4,6},{5,7},{10,8},{11,9},{8,1... | collective-permute-start | bytes 1572872 | tf_op jit(solution)/shard_map/ppermute | solution.py:100
  10.8 3.4 %collective-permute-start.5 = (f32[1024,128]{1,0:T(8,128)S(1)}, f32[1024,128]{1,0:T(8,128)S(1)}, u32[]{:S(2)}, u32[]{:S(2)}) collective-permute-start(f32[1024,128]{1,0:T(8,128)S(1)} %get-tuple-element.17.refs_4_), channel_id=1, source_target_pairs={{24,0},{28,4},{0,8},{4,12},{8,16},{12,20},{16,24},{20,28},{25,1},{... | collective-permute-start | bytes 1572872 | tf_op jit(solution)/shard_map/ppermute | solution.py:104
  14.2 3.0 %collective-permute-start.4 = (f32[1024,128]{1,0:T(8,128)S(1)}, f32[1024,128]{1,0:T(8,128)S(1)}, u32[]{:S(2)}, u32[]{:S(2)}) collective-permute-start(f32[1024,128]{1,0:T(8,128)S(1)} %get-tuple-element.17.refs_4_), channel_id=1, source_target_pairs={{16,0},{20,4},{24,8},{28,12},{0,16},{4,20},{8,24},{12,28},{17,1},{... | collective-permute-start | bytes 1572872 | tf_op jit(solution)/shard_map/ppermute | solution.py:104
  17.2 4.1 %collective-permute-start.3 = (f32[1024,128]{1,0:T(8,128)S(1)}, f32[1024,128]{1,0:T(8,128)S(1)}, u32[]{:S(2)}, u32[]{:S(2)}) collective-permute-start(f32[1024,128]{1,0:T(8,128)S(1)} %get-tuple-element.17.refs_4_), channel_id=1, source_target_pairs={{8,0},{12,4},{16,8},{20,12},{24,16},{28,20},{0,24},{4,28},{9,1},{1... | collective-permute-start | bytes 1572872 | tf_op jit(solution)/shard_map/ppermute | solution.py:104
  21.3 3.3 %collective-permute-start = (f32[128,1024]{1,0:T(8,128)S(1)}, f32[128,1024]{1,0:T(8,128)S(1)}, u32[]{:S(2)}, u32[]{:S(2)}) collective-permute-start(f32[128,1024]{1,0:T(8,128)S(1)} %get-tuple-element.16.refs_0_), channel_id=1, source_target_pairs={{1,0},{2,1},{3,2},{0,3},{5,4},{6,5},{7,6},{4,7},{9,8},{10,9},{11,1... | collective-permute-start | bytes 1572872 | tf_op jit(solution)/shard_map/ppermute | solution.py:100
  24.5 7.2 %collective-permute-done.1.refs_2_ = f32[128,1024]{1,0:T(8,128)S(1)} collective-permute-done((f32[128,1024]{1,0:T(8,128)S(1)}, f32[128,1024]{1,0:T(8,128)S(1)}, u32[]{:S(2)}, u32[]{:S(2)}) %collective-permute-start.1) | collective-permute-done | bytes 524320 | tf_op jit(solution)/shard_map/ppermute | solution.py:100
  31.7 1.9 %collective-permute-start.6 = (f32[1024,128]{1,0:T(8,128)S(1)}, f32[1024,128]{1,0:T(8,128)S(1)}, u32[]{:S(2)}, u32[]{:S(2)}) collective-permute-start(f32[1024,128]{1,0:T(8,128)S(1)} %get-tuple-element.17.refs_4_), channel_id=1, source_target_pairs={{0,4},{4,0},{8,12},{12,8},{16,20},{20,16},{24,28},{28,24},{1,5},{5... | collective-permute-start | bytes 1572872 | tf_op jit(solution)/shard_map/ppermute | solution.py:110
  33.6 2.4 %collective-permute-start.9 = (f32[1024,128]{1,0:T(8,128)S(1)}, f32[1024,128]{1,0:T(8,128)S(1)}, u32[]{:S(2)}, u32[]{:S(2)}) collective-permute-start(f32[1024,128]{1,0:T(8,128)S(1)} %collective-permute-done.5.refs_7_), channel_id=1, source_target_pairs={{0,4},{4,0},{8,12},{12,8},{16,20},{20,16},{24,28},{28,24},{1,5},{5... | collective-permute-start | bytes 1572872 | tf_op jit(solution)/shard_map/ppermute | solution.py:110
  36.0 1.9 %collective-permute-start.8 = (f32[1024,128]{1,0:T(8,128)S(1)}, f32[1024,128]{1,0:T(8,128)S(1)}, u32[]{:S(2)}, u32[]{:S(2)}) collective-permute-start(f32[1024,128]{1,0:T(8,128)S(1)} %collective-permute-done.4.refs_6_), channel_id=1, source_target_pairs={{0,4},{4,0},{8,12},{12,8},{16,20},{20,16},{24,28},{28,24},{1,5},{5... | collective-permute-start | bytes 1572872 | tf_op jit(solution)/shard_map/ppermute | solution.py:110
  38.0 3.6 %collective-permute-done.3.refs_5_ = f32[1024,128]{1,0:T(8,128)S(1)} collective-permute-done((f32[1024,128]{1,0:T(8,128)S(1)}, f32[1024,128]{1,0:T(8,128)S(1)}, u32[]{:S(2)}, u32[]{:S(2)}) %collective-permute-start.3) | collective-permute-done | bytes 524320 | tf_op jit(solution)/shard_map/ppermute | solution.py:104
  41.6 1.9 %collective-permute-start.7 = (f32[1024,128]{1,0:T(8,128)S(1)}, f32[1024,128]{1,0:T(8,128)S(1)}, u32[]{:S(2)}, u32[]{:S(2)}) collective-permute-start(f32[1024,128]{1,0:T(8,128)S(1)} %collective-permute-done.3.refs_5_), channel_id=1, source_target_pairs={{0,4},{4,0},{8,12},{12,8},{16,20},{20,16},{24,28},{28,24},{1,5},{5... | collective-permute-start | bytes 1572872 | tf_op jit(solution)/shard_map/ppermute | solution.py:110
  43.6 1.8 %collective-permute-done.7.refs_9_ = f32[1024,128]{1,0:T(8,128)S(1)} collective-permute-done((f32[1024,128]{1,0:T(8,128)S(1)}, f32[1024,128]{1,0:T(8,128)S(1)}, u32[]{:S(2)}, u32[]{:S(2)}) %collective-permute-start.7) | collective-permute-done | bytes 524320 | tf_op jit(solution)/shard_map/ppermute | solution.py:110
  45.4 3.8 %shard_map.29 = (f32[128,1024]{1,0:T(8,128)S(1)}, f32[128,1024]{1,0:T(8,128)S(1)}, f32[128,1024]{1,0:T(8,128)S(1)}, f32[128,512]{1,0:T(8,128)S(1)}, f32[128,512]{1,0:T(8,128)S(1)}) custom-call(f32[128,1024]{1,0:T(8,128)S(1)} %get-tuple-element.16.refs_0_, f32[128,1024]{1,0:T(8,128)S(1)} %collective-permute-done.refs_1_, ...), custom_call_target="tpu_custom_call" | custom-call | flops 3221225472 | bytes 8388608 | tf_op jit(solution)/shard_map/pallas_call | solution.py:21
  49.2 3.8 %collective-permute-start.10 = (f32[128,1024]{1,0:T(8,128)S(1)}, f32[128,1024]{1,0:T(8,128)S(1)}, u32[]{:S(2)}, u32[]{:S(2)}) collective-permute-start(f32[128,1024]{1,0:T(8,128)S(1)} %get-tuple-element.19), channel_id=1, source_target_pairs={{0,32},{32,64},{64,96},{96,128},{128,160},{160,192},{192,224},{224... | collective-permute-start | bytes 1572872 | tf_op jit(solution)/shard_map/ppermute | solution.py:96
  53.0 2.0 %collective-permute-start.11 = (f32[128,1024]{1,0:T(8,128)S(1)}, f32[128,1024]{1,0:T(8,128)S(1)}, u32[]{:S(2)}, u32[]{:S(2)}) collective-permute-start(f32[128,1024]{1,0:T(8,128)S(1)} %get-tuple-element.20), channel_id=1, source_target_pairs={{0,480},{32,0},{64,32},{96,64},{128,96},{160,128},{192,160},{224,1... | collective-permute-start | bytes 1572872 | tf_op jit(solution)/shard_map/ppermute | solution.py:96
  55.1 11.0 %collective-permute-start.12 = (f32[128,512]{1,0:T(8,128)S(1)}, f32[128,512]{1,0:T(8,128)S(1)}, u32[]{:S(2)}, u32[]{:S(2)}) collective-permute-start(f32[128,512]{1,0:T(8,128)S(1)} %get-tuple-element.21), channel_id=1, source_target_pairs={{0,448},{32,480},{64,0},{96,32},{128,64},{160,96},{192,128},{224,1... | collective-permute-start | bytes 786440 | tf_op jit(solution)/shard_map/ppermute | solution.py:96
  66.0 1.9 %collective-permute-start.13 = (f32[128,512]{1,0:T(8,128)S(1)}, f32[128,512]{1,0:T(8,128)S(1)}, u32[]{:S(2)}, u32[]{:S(2)}) collective-permute-start(f32[128,512]{1,0:T(8,128)S(1)} %get-tuple-element.22), channel_id=1, source_target_pairs={{0,64},{32,96},{64,128},{96,160},{128,192},{160,224},{192,256},{22... | collective-permute-start | bytes 786440 | tf_op jit(solution)/shard_map/ppermute | solution.py:96
  68.0 12.0 %collective-permute-done.12.far_a = f32[128,512]{1,0:T(8,128)S(1)} collective-permute-done((f32[128,512]{1,0:T(8,128)S(1)}, f32[128,512]{1,0:T(8,128)S(1)}, u32[]{:S(2)}, u32[]{:S(2)}) %collective-permute-start.12) | collective-permute-done | bytes 262176 | tf_op jit(solution)/shard_map/ppermute | solution.py:96
  80.0 3.6 %collective-permute-done.13.far_b = f32[128,512]{1,0:T(8,128)S(1)} collective-permute-done((f32[128,512]{1,0:T(8,128)S(1)}, f32[128,512]{1,0:T(8,128)S(1)}, u32[]{:S(2)}, u32[]{:S(2)}) %collective-permute-start.13) | collective-permute-done | bytes 262176 | tf_op jit(solution)/shard_map/ppermute | solution.py:96
  83.7 3.3 %collective-permute-start.14 = (f32[32,1024]{1,0:T(8,128)S(1)}, f32[32,1024]{1,0:T(8,128)S(1)}, u32[]{:S(2)}, u32[]{:S(2)}) collective-permute-start(f32[32,1024]{1,0:T(8,128)S(1)} %get-tuple-element.24), channel_id=1, source_target_pairs={{0,128},{32,160},{64,192},{96,224},{128,256},{160,288},{192,320},{... | collective-permute-start | bytes 393224 | tf_op jit(solution)/shard_map/ppermute | solution.py:96
  87.0 6.5 %collective-permute-start.15 = (f32[32,1024]{1,0:T(8,128)S(1)}, f32[32,1024]{1,0:T(8,128)S(1)}, u32[]{:S(2)}, u32[]{:S(2)}) collective-permute-start(f32[32,1024]{1,0:T(8,128)S(1)} %get-tuple-element.25), channel_id=1, source_target_pairs={{0,384},{32,416},{64,448},{96,480},{128,0},{160,32},{192,64},{224,... | collective-permute-start | bytes 393224 | tf_op jit(solution)/shard_map/ppermute | solution.py:96
  93.5 9.2 %collective-permute-start.16 = (f32[32,1024]{1,0:T(8,128)S(1)}, f32[32,1024]{1,0:T(8,128)S(1)}, u32[]{:S(2)}, u32[]{:S(2)}) collective-permute-start(f32[32,1024]{1,0:T(8,128)S(1)} %get-tuple-element.26), channel_id=1, source_target_pairs={{0,256},{32,288},{64,320},{96,352},{128,384},{160,416},{192,448},{... | collective-permute-start | bytes 393224 | tf_op jit(solution)/shard_map/ppermute | solution.py:96
  102.7 17.2 %collective-permute-done.16.d = f32[32,1024]{1,0:T(8,128)S(1)} collective-permute-done((f32[32,1024]{1,0:T(8,128)S(1)}, f32[32,1024]{1,0:T(8,128)S(1)}, u32[]{:S(2)}, u32[]{:S(2)}) %collective-permute-start.16) | collective-permute-done | bytes 131104 | tf_op jit(solution)/shard_map/ppermute | solution.py:96
  (18 shorter events, 3.2 us)
Async XLA Ops:
  0.0 0.7 copy-start.1
  0.7 1.0 copy-start
  2.5 18.8 %collective-permute-start.2 = (f32[128,1024]{1,0:T(8,128)S(1)}, f32[128,1024]{1,0:T(8,128)S(1)}, u32[]{:S(2)}, u32[]{:S(2)}) collective-permute-start(f32[128,1024]{1,0:T(8,128)S(1)} %get-tuple-element.16.refs_0_), channel_id=1, source_target_pairs={{3,0},{0,1},{1,2},{2,3},{7,4},{4,5},{5,6},{6,7},{11,8},{8,9},{9,10... | collective-permute-start | bytes 1572872 | tf_op jit(solution)/shard_map/ppermute | solution.py:100
  5.9 25.8 %collective-permute-start.1 = (f32[128,1024]{1,0:T(8,128)S(1)}, f32[128,1024]{1,0:T(8,128)S(1)}, u32[]{:S(2)}, u32[]{:S(2)}) collective-permute-start(f32[128,1024]{1,0:T(8,128)S(1)} %get-tuple-element.16.refs_0_), channel_id=1, source_target_pairs={{2,0},{3,1},{0,2},{1,3},{6,4},{7,5},{4,6},{5,7},{10,8},{11,9},{8,1... | collective-permute-start | bytes 1572872 | tf_op jit(solution)/shard_map/ppermute | solution.py:100
  10.8 22.9 %collective-permute-start.5 = (f32[1024,128]{1,0:T(8,128)S(1)}, f32[1024,128]{1,0:T(8,128)S(1)}, u32[]{:S(2)}, u32[]{:S(2)}) collective-permute-start(f32[1024,128]{1,0:T(8,128)S(1)} %get-tuple-element.17.refs_4_), channel_id=1, source_target_pairs={{24,0},{28,4},{0,8},{4,12},{8,16},{12,20},{16,24},{20,28},{25,1},{... | collective-permute-start | bytes 1572872 | tf_op jit(solution)/shard_map/ppermute | solution.py:104
  14.2 21.9 %collective-permute-start.4 = (f32[1024,128]{1,0:T(8,128)S(1)}, f32[1024,128]{1,0:T(8,128)S(1)}, u32[]{:S(2)}, u32[]{:S(2)}) collective-permute-start(f32[1024,128]{1,0:T(8,128)S(1)} %get-tuple-element.17.refs_4_), channel_id=1, source_target_pairs={{16,0},{20,4},{24,8},{28,12},{0,16},{4,20},{8,24},{12,28},{17,1},{... | collective-permute-start | bytes 1572872 | tf_op jit(solution)/shard_map/ppermute | solution.py:104
  17.2 24.4 %collective-permute-start.3 = (f32[1024,128]{1,0:T(8,128)S(1)}, f32[1024,128]{1,0:T(8,128)S(1)}, u32[]{:S(2)}, u32[]{:S(2)}) collective-permute-start(f32[1024,128]{1,0:T(8,128)S(1)} %get-tuple-element.17.refs_4_), channel_id=1, source_target_pairs={{8,0},{12,4},{16,8},{20,12},{24,16},{28,20},{0,24},{4,28},{9,1},{1... | collective-permute-start | bytes 1572872 | tf_op jit(solution)/shard_map/ppermute | solution.py:104
  21.3 22.3 %collective-permute-start = (f32[128,1024]{1,0:T(8,128)S(1)}, f32[128,1024]{1,0:T(8,128)S(1)}, u32[]{:S(2)}, u32[]{:S(2)}) collective-permute-start(f32[128,1024]{1,0:T(8,128)S(1)} %get-tuple-element.16.refs_0_), channel_id=1, source_target_pairs={{1,0},{2,1},{3,2},{0,3},{5,4},{6,5},{7,6},{4,7},{9,8},{10,9},{11,1... | collective-permute-start | bytes 1572872 | tf_op jit(solution)/shard_map/ppermute | solution.py:100
  31.7 11.9 %collective-permute-start.6 = (f32[1024,128]{1,0:T(8,128)S(1)}, f32[1024,128]{1,0:T(8,128)S(1)}, u32[]{:S(2)}, u32[]{:S(2)}) collective-permute-start(f32[1024,128]{1,0:T(8,128)S(1)} %get-tuple-element.17.refs_4_), channel_id=1, source_target_pairs={{0,4},{4,0},{8,12},{12,8},{16,20},{20,16},{24,28},{28,24},{1,5},{5... | collective-permute-start | bytes 1572872 | tf_op jit(solution)/shard_map/ppermute | solution.py:110
  33.6 9.9 %collective-permute-start.9 = (f32[1024,128]{1,0:T(8,128)S(1)}, f32[1024,128]{1,0:T(8,128)S(1)}, u32[]{:S(2)}, u32[]{:S(2)}) collective-permute-start(f32[1024,128]{1,0:T(8,128)S(1)} %collective-permute-done.5.refs_7_), channel_id=1, source_target_pairs={{0,4},{4,0},{8,12},{12,8},{16,20},{20,16},{24,28},{28,24},{1,5},{5... | collective-permute-start | bytes 1572872 | tf_op jit(solution)/shard_map/ppermute | solution.py:110
  36.0 7.5 %collective-permute-start.8 = (f32[1024,128]{1,0:T(8,128)S(1)}, f32[1024,128]{1,0:T(8,128)S(1)}, u32[]{:S(2)}, u32[]{:S(2)}) collective-permute-start(f32[1024,128]{1,0:T(8,128)S(1)} %collective-permute-done.4.refs_6_), channel_id=1, source_target_pairs={{0,4},{4,0},{8,12},{12,8},{16,20},{20,16},{24,28},{28,24},{1,5},{5... | collective-permute-start | bytes 1572872 | tf_op jit(solution)/shard_map/ppermute | solution.py:110
  41.6 3.8 %collective-permute-start.7 = (f32[1024,128]{1,0:T(8,128)S(1)}, f32[1024,128]{1,0:T(8,128)S(1)}, u32[]{:S(2)}, u32[]{:S(2)}) collective-permute-start(f32[1024,128]{1,0:T(8,128)S(1)} %collective-permute-done.3.refs_5_), channel_id=1, source_target_pairs={{0,4},{4,0},{8,12},{12,8},{16,20},{20,16},{24,28},{28,24},{1,5},{5... | collective-permute-start | bytes 1572872 | tf_op jit(solution)/shard_map/ppermute | solution.py:110
  49.2 34.4 %collective-permute-start.10 = (f32[128,1024]{1,0:T(8,128)S(1)}, f32[128,1024]{1,0:T(8,128)S(1)}, u32[]{:S(2)}, u32[]{:S(2)}) collective-permute-start(f32[128,1024]{1,0:T(8,128)S(1)} %get-tuple-element.19), channel_id=1, source_target_pairs={{0,32},{32,64},{64,96},{96,128},{128,160},{160,192},{192,224},{224... | collective-permute-start | bytes 1572872 | tf_op jit(solution)/shard_map/ppermute | solution.py:96
  53.0 30.6 %collective-permute-start.11 = (f32[128,1024]{1,0:T(8,128)S(1)}, f32[128,1024]{1,0:T(8,128)S(1)}, u32[]{:S(2)}, u32[]{:S(2)}) collective-permute-start(f32[128,1024]{1,0:T(8,128)S(1)} %get-tuple-element.20), channel_id=1, source_target_pairs={{0,480},{32,0},{64,32},{96,64},{128,96},{160,128},{192,160},{224,1... | collective-permute-start | bytes 1572872 | tf_op jit(solution)/shard_map/ppermute | solution.py:96
  55.1 24.9 %collective-permute-start.12 = (f32[128,512]{1,0:T(8,128)S(1)}, f32[128,512]{1,0:T(8,128)S(1)}, u32[]{:S(2)}, u32[]{:S(2)}) collective-permute-start(f32[128,512]{1,0:T(8,128)S(1)} %get-tuple-element.21), channel_id=1, source_target_pairs={{0,448},{32,480},{64,0},{96,32},{128,64},{160,96},{192,128},{224,1... | collective-permute-start | bytes 786440 | tf_op jit(solution)/shard_map/ppermute | solution.py:96
  66.0 17.6 %collective-permute-start.13 = (f32[128,512]{1,0:T(8,128)S(1)}, f32[128,512]{1,0:T(8,128)S(1)}, u32[]{:S(2)}, u32[]{:S(2)}) collective-permute-start(f32[128,512]{1,0:T(8,128)S(1)} %get-tuple-element.22), channel_id=1, source_target_pairs={{0,64},{32,96},{64,128},{96,160},{128,192},{160,224},{192,256},{22... | collective-permute-start | bytes 786440 | tf_op jit(solution)/shard_map/ppermute | solution.py:96
  83.7 18.9 %collective-permute-start.14 = (f32[32,1024]{1,0:T(8,128)S(1)}, f32[32,1024]{1,0:T(8,128)S(1)}, u32[]{:S(2)}, u32[]{:S(2)}) collective-permute-start(f32[32,1024]{1,0:T(8,128)S(1)} %get-tuple-element.24), channel_id=1, source_target_pairs={{0,128},{32,160},{64,192},{96,224},{128,256},{160,288},{192,320},{... | collective-permute-start | bytes 393224 | tf_op jit(solution)/shard_map/ppermute | solution.py:96
  87.0 15.7 %collective-permute-start.15 = (f32[32,1024]{1,0:T(8,128)S(1)}, f32[32,1024]{1,0:T(8,128)S(1)}, u32[]{:S(2)}, u32[]{:S(2)}) collective-permute-start(f32[32,1024]{1,0:T(8,128)S(1)} %get-tuple-element.25), channel_id=1, source_target_pairs={{0,384},{32,416},{64,448},{96,480},{128,0},{160,32},{192,64},{224,... | collective-permute-start | bytes 393224 | tf_op jit(solution)/shard_map/ppermute | solution.py:96
  93.5 26.4 %collective-permute-start.16 = (f32[32,1024]{1,0:T(8,128)S(1)}, f32[32,1024]{1,0:T(8,128)S(1)}, u32[]{:S(2)}, u32[]{:S(2)}) collective-permute-start(f32[32,1024]{1,0:T(8,128)S(1)} %get-tuple-element.26), channel_id=1, source_target_pairs={{0,256},{32,288},{64,320},{96,352},{128,384},{160,416},{192,448},{... | collective-permute-start | bytes 393224 | tf_op jit(solution)/shard_map/ppermute | solution.py:96

commit v2 on v0

v2 whole, which is shorter than its diff:
```python
import functools

import jax
import jax.numpy as jnp
from jax import lax
from jax.experimental import pallas as pl
from jax.experimental.pallas import tpu as pltpu
from jax.sharding import PartitionSpec as P

TILE = 128
N_LAYER = 16
N_X = 4
N_ROW = 8
N_COL = 4
SUB = 32
ORDER = (0, 1, 3, 2)
VMEM = pl.BlockSpec(memory_space=pltpu.VMEM)
SMEM = pl.BlockSpec(memory_space=pltpu.SMEM)
LIMIT = 40 * 1024 * 1024
F32, BF16 = jnp.float32, jnp.bfloat16


def call(kernel, outs, operands, specs=None, scratch=(), flops=0, nbytes=1 << 20):
    outs = [o if isinstance(o[0], tuple) else (o, F32) for o in outs]
    return pl.pallas_call(
        kernel,
        out_shape=tuple(jax.ShapeDtypeStruct(s, d) for s, d in outs),
        in_specs=specs or [VMEM] * len(operands),
        out_specs=tuple(VMEM for _ in outs),
        scratch_shapes=list(scratch),
        compiler_params=pltpu.CompilerParams(vmem_limit_bytes=LIMIT),
        cost_estimate=pl.CostEstimate(flops=flops, bytes_accessed=nbytes, transcendentals=0),
    )(*operands)


def mask_kernel(graph, pattern, masked):
    for k in range(graph.shape[0] // TILE):
        rows = pl.ds(k * TILE, TILE)
        masked[rows, :] = graph[rows, :] * pattern[k].astype(F32)


def core():
    return lax.rem(lax.axis_index("row"), 2)


def pair_kernel(own, other, pair):
    inner = own.shape[0]
    k = core()
    pair[pl.ds(pl.multiple_of(k * inner, inner), inner), :] = own[...]
    pair[pl.ds(pl.multiple_of((1 - k) * inner, inner), inner), :] = other[...]


def split(value):
    high = value.astype(BF16)
    low = (value - high.astype(F32)).astype(BF16)
    return high, low


dot = functools.partial(jnp.dot, preferred_element_type=F32)


def product(left_high, left_low, right_high, right_low):
    return dot(left_high, right_high) + (dot(left_high, right_low) + dot(left_low, right_high))


def place(pair, swapped, along_y, along_x):
    k = core()

    @pl.when(k == 0)
    def _():
        along_y(pair)
        along_x(swapped)

    @pl.when(k == 1)
    def _():
        along_y(swapped)
        along_x(pair)


def take_left(index, left_high, left_low):
    def write(pair):
        inner = pair.shape[0] // 2
        block = pair[pl.ds(pl.multiple_of(core() * inner, inner), inner), :]
        rows = pl.ds(index * TILE, TILE)
        high, low = split(block.T)
        left_high[rows, :] = high
        left_low[rows, :] = low

    return write


def take_right(index, right_high, right_low):
    def write(pair):
        inner = pair.shape[0] // 2
        for k in range(2):
            columns = pl.ds((2 * index + k) * TILE, TILE)
            high, low = split(pair[pl.ds(k * inner, inner), :])
            right_high[:, columns] = high
            right_low[:, columns] = low

    return write


def first_product_kernel(p0, p1, s1, p3, s3, left_high, left_low, right_high, right_low, total):
    take_left(0, left_high, left_low)(p0)
    take_right(0, right_high, right_low)(p0)
    for index, pair, swapped in ((1, p1, s1), (2, p3, s3)):
        place(pair, swapped, take_left(index, left_high, left_low), take_right(index, right_high, right_low))
    for index in range(3):
        columns = pl.ds(index * 2 * TILE, 2 * TILE)
        total[:, columns] = product(left_high[...], left_low[...], right_high[:, columns], right_low[:, columns])


def turn():
    return 1 - 2 * core()


def strip(index):
    return pl.ds(pl.multiple_of(index * SUB, SUB), SUB)


def second_product_kernel(p2, s2, left_high, left_low, right_high, right_low, part, *refs):
    sends, keeps = refs[0:2], refs[2:4]
    last_high, last_low, far_high, far_low, total = refs[4:]
    z, y = lax.axis_index("layer"), lax.axis_index("col")
    place(p2, s2, take_left(0, last_high, last_low), take_right(0, far_high, far_low))
    known = part.shape[0]
    total[:known, : part.shape[1]] = part[...]
    total[known:, : part.shape[1]] = product(last_high[...], last_low[...], right_high[...], right_low[...])
    columns = pl.ds(part.shape[1], 2 * TILE)
    total[:known, columns] = product(left_high[...], left_low[...], far_high[...], far_low[...])
    total[known:, columns] = product(last_high[...], last_low[...], far_high[...], far_low[...])

    def rows_of(layer):
        t = lax.rem(layer // 4 - y + N_COL, N_COL)
        index = jnp.where(t < 2, t, 5 - t)
        return strip(index * 4 + lax.rem(layer, 4))

    for j in range(N_LAYER // 2):
        keep = rows_of(lax.rem(z + 2 * j, N_LAYER))
        send = rows_of(lax.rem(z + turn() + 2 * j + N_LAYER, N_LAYER))
        rows = pl.ds(j * SUB, SUB)
        for half in range(2):
            columns = pl.ds(half * 4 * TILE, 4 * TILE)
            keeps[half][rows, :] = total[keep, columns]
            sends[half][rows, :] = total[send, columns]


def stage_kernel(held, came, send, keep):
    count = held.shape[0] // SUB
    for i in range(count // 2):
        rows = pl.ds(i * SUB, SUB)
        near = pl.ds(2 * i * SUB, SUB)
        far = strip(lax.rem(turn() + 2 * i + count, count))
        keep[rows, :] = held[near, :] + came[near, :]
        send[rows, :] = held[far, :] + came[far, :]


def last_kernel(held_a, came_a, held_b, came_b, out):
    x = lax.axis_index("row") // 2
    for index, t in enumerate(ORDER):
        held, came = ((held_a, came_a), (held_b, came_b))[index // 2]
        source = pl.ds((index % 2) * 2 * TILE, 2 * TILE)
        target = pl.ds(pl.multiple_of(lax.rem(x + t, N_X) * 2 * TILE, 2 * TILE), 2 * TILE)
        out[:, target] = held[:, source] + came[:, source]


def swap(value):
    return lax.ppermute(value, "row", [(i, i ^ 1) for i in range(N_ROW)])


def fetch(value, t):
    pairs = []
    for x in range(N_X):
        for y in range(N_COL):
            pairs.append(((2 * x) * N_COL + (y + t) % N_COL, (2 * x) * N_COL + y))
            pairs.append(((2 * ((x + t) % N_X) + 1) * N_COL + y, (2 * x + 1) * N_COL + y))
    return lax.ppermute(value, ("row", "col"), pairs)


def pass_on(value, distance):
    pairs = []
    for z in range(N_LAYER):
        for row in range(N_ROW):
            to = (z + (distance if row % 2 == 0 else -distance)) % N_LAYER
            pairs.append((z * N_ROW + row, to * N_ROW + row))
    return lax.ppermute(value, ("layer", "row"), pairs)


def on_device(graph, pattern):
    inner = graph.shape[0]
    (masked,) = call(mask_kernel, [(inner, TILE)], (graph, pattern.reshape(-1)), [VMEM, SMEM])
    (pair,) = call(pair_kernel, [(2 * inner, TILE)], (masked, swap(masked)))
    came = {t: fetch(pair, t) for t in (1, 3, 2)}
    swapped = {t: swap(came[t]) for t in (1, 3, 2)}
    known, wide = 3 * TILE, 6 * TILE
    parts = call(
        first_product_kernel,
        [((known, inner), BF16)] * 2 + [((inner, wide), BF16)] * 2 + [(known, wide)],
        (pair, came[1], swapped[1], came[3], swapped[3]),
        flops=6 * known * wide * inner,
        nbytes=8 << 20,
    )
    split_scratch = [pltpu.VMEM((TILE, inner), BF16)] * 2 + [pltpu.VMEM((inner, 2 * TILE), BF16)] * 2
    made = call(
        second_product_kernel,
        [(8 * SUB, 4 * TILE)] * 4,
        (came[2], swapped[2], *parts),
        scratch=split_scratch + [pltpu.VMEM((4 * TILE, 8 * TILE), F32)],
        flops=6 * 7 * TILE * 2 * TILE * inner,
        nbytes=8 << 20,
    )
    sends, keeps = list(made[:2]), list(made[2:])
    arrived = [pass_on(sends[half], 1) for half in range(2)]
    for stage in (1, 2, 3):
        count = 8 >> stage
        for half in range(2):
            sends[half], keeps[half] = call(
                stage_kernel, [(count * SUB, 4 * TILE)] * 2, (keeps[half], arrived[half])
            )
            arrived[half] = pass_on(sends[half], 1 << stage)
    return call(last_kernel, [(SUB, 8 * TILE)], (keeps[0], arrived[0], keeps[1], arrived[1]))[0]


def solution(mesh):
    placed = (P("layer", ("row", "col")), P("layer", ("row", "col")))
    return jax.shard_map(
        on_device, mesh=mesh, in_specs=placed, out_specs=P(("row", "layer"), "col"), check_vma=False
    )
```

time: 195 us -> 121 us (0.62)
  waiting for transfers between devices: 168 us -> 57.7 us
  starting transfers between devices: 0.08 us -> 54.1 us
  between operations: 13.1 us -> 0.22 us
  matrix products: 10.2 us -> 0 us
  Pallas kernels: 0 us -> 7.24 us
  other arithmetic: 2.72 us -> 0 us
    all_gather x2 -> x0, waiting for transfers between devices: 92.2 us -> none  [the longest x1 46.3 us: on_device(): right = lax.all_gather(masked, 'row', axis=1, tiled=True)]
    reduce_scatter x1 -> x0, waiting for transfers between devices: 75.2 us -> none  [on_device(): lax.psum_scatter(inner_product(left, right), 'layer', scatter_dimension=0...]
    ppermute x0 -> x15, waiting for transfers between devices: none -> 57.7 us  [the longest x8 34.4 us: pass_on(): return lax.ppermute(value, ('layer', 'row'), pairs)]
    ppermute x0 -> x15, starting transfers between devices: none -> 54.1 us  [the longest x8 35 us: pass_on(): return lax.ppermute(value, ('layer', 'row'), pairs)]
    dot_general x1 -> x0, matrix products: 10.2 us -> none  [inner_product(): lax.dot_general(left, right, (((0,), (0,)), ((), ())), precision=lax.Prec...]
    pallas_call x0 -> x11, Pallas kernels: none -> 7.24 us  [call(): pl.pallas_call(kernel, out_shape=tuple((jax.ShapeDtypeStruct(s, d) for s,...]
    mul x2 -> x0, other arithmetic: 2.72 us -> none  [on_device(): graph.reshape(inner_rows // width, width, width) * occupied[:, :, None]]
  transfers between devices with their start and end apart: 3 -> 15, of which waited for: 3 -> 11; matrix products, arithmetic and copies ran while one was open for 0% -> 0% of each run, Pallas kernels for 0% -> 3%
where the time goes in v2:
time: 121 us
  waiting for transfers between devices  57.7 us (48%)
  starting transfers between devices  54.1 us (45%)
  Pallas kernels  7.24 us (6%)
  local copies, waits for them, and re-layouts  1.7 us (1%)
    ppermute x8, starting transfers between devices, pass_on(): return lax.ppermute(value, ('layer', 'row'), pairs)  35 us
    ppermute x8, waiting for transfers between devices, pass_on(): return lax.ppermute(value, ('layer', 'row'), pairs)  34.4 us
    ppermute x3, waiting for transfers between devices, fetch(): return lax.ppermute(value, ('row', 'col'), pairs)  21.2 us
    ppermute x3, starting transfers between devices, fetch(): return lax.ppermute(value, ('row', 'col'), pairs)  10.9 us
    ppermute x4, starting transfers between devices, swap(): return lax.ppermute(value, 'row', [(i, i ^ 1) for i in range(N_ROW)])  8.14 us
    pallas_call x11, Pallas kernels, call(): pl.pallas_call(kernel, out_shape=tuple((jax.ShapeDtypeStruct(s, d) for s,...  7.24 us
  transfers between devices with their start and end apart: 15, of which 11 were waited for; matrix products, arithmetic and copies ran while one was open for 0% of the time, Pallas kernels for 3%

profile of v2, /device:TPU:6, one launch (start us, length us, event | category | flops | bytes accessed | tf_op | source)
XLA Modules:
  0.0 120.9 jit_solution(14619507116910882283)
XLA Ops:
  2.3 1.9 %collective-permute-start = (f32[1024,128]{1,0:T(8,128)S(1)}, f32[1024,128]{1,0:T(8,128)S(1)}, u32[]{:S(2)}, u32[]{:S(2)}) collective-permute-start(f32[1024,128]{1,0:T(8,128)S(1)} %shard_map.28.own), channel_id=1, source_target_pairs={{0,4},{4,0},{8,12},{12,8},{16,20},{20,16},{24,28},{28,24},{1,5},{5... | collective-permute-start | bytes 1572872 | tf_op jit(solution)/shard_map/ppermute | solution.py:169
  6.2 4.9 %collective-permute-start.3 = (f32[2048,128]{1,0:T(8,128)S(1)}, f32[2048,128]{1,0:T(8,128)S(1)}, u32[]{:S(2)}, u32[]{:S(2)}) collective-permute-start(f32[2048,128]{1,0:T(8,128)S(1)} %shard_map.29.p0), channel_id=1, source_target_pairs={{1,0},{12,4},{2,1},{13,5},{3,2},{14,6},{0,3},{15,7},{9,8},{20,12},... | collective-permute-start | bytes 3145736 | tf_op jit(solution)/shard_map/ppermute | solution.py:178
  11.1 1.9 %collective-permute-start.5 = (f32[2048,128]{1,0:T(8,128)S(1)}, f32[2048,128]{1,0:T(8,128)S(1)}, u32[]{:S(2)}, u32[]{:S(2)}) collective-permute-start(f32[2048,128]{1,0:T(8,128)S(1)} %shard_map.29.p0), channel_id=1, source_target_pairs={{3,0},{28,4},{0,1},{29,5},{1,2},{30,6},{2,3},{31,7},{11,8},{4,12},... | collective-permute-start | bytes 3145736 | tf_op jit(solution)/shard_map/ppermute | solution.py:178
  13.0 4.1 %collective-permute-start.1 = (f32[2048,128]{1,0:T(8,128)S(1)}, f32[2048,128]{1,0:T(8,128)S(1)}, u32[]{:S(2)}, u32[]{:S(2)}) collective-permute-start(f32[2048,128]{1,0:T(8,128)S(1)} %shard_map.29.p0), channel_id=1, source_target_pairs={{2,0},{20,4},{3,1},{21,5},{0,2},{22,6},{1,3},{23,7},{10,8},{28,12}... | collective-permute-start | bytes 3145736 | tf_op jit(solution)/shard_map/ppermute | solution.py:178
  17.1 17.5 %collective-permute-done.3.p1 = f32[2048,128]{1,0:T(8,128)S(1)} collective-permute-done((f32[2048,128]{1,0:T(8,128)S(1)}, f32[2048,128]{1,0:T(8,128)S(1)}, u32[]{:S(2)}, u32[]{:S(2)}) %collective-permute-start.3) | collective-permute-done | bytes 1048608 | tf_op jit(solution)/shard_map/ppermute | solution.py:178
  36.6 3.7 %collective-permute-done.5.p3 = f32[2048,128]{1,0:T(8,128)S(1)} collective-permute-done((f32[2048,128]{1,0:T(8,128)S(1)}, f32[2048,128]{1,0:T(8,128)S(1)}, u32[]{:S(2)}, u32[]{:S(2)}) %collective-permute-start.5) | collective-permute-done | bytes 1048608 | tf_op jit(solution)/shard_map/ppermute | solution.py:178
  40.2 1.9 %collective-permute-start.6 = (f32[2048,128]{1,0:T(8,128)S(1)}, f32[2048,128]{1,0:T(8,128)S(1)}, u32[]{:S(2)}, u32[]{:S(2)}) collective-permute-start(f32[2048,128]{1,0:T(8,128)S(1)} %collective-permute-done.5.p3), channel_id=1, source_target_pairs={{0,4},{4,0},{8,12},{12,8},{16,20},{20,16},{24,28},{28,24},{1,5},{5... | collective-permute-start | bytes 3145736 | tf_op jit(solution)/shard_map/ppermute | solution.py:169
  42.2 2.4 %collective-permute-start.2 = (f32[2048,128]{1,0:T(8,128)S(1)}, f32[2048,128]{1,0:T(8,128)S(1)}, u32[]{:S(2)}, u32[]{:S(2)}) collective-permute-start(f32[2048,128]{1,0:T(8,128)S(1)} %collective-permute-done.1.p2), channel_id=1, source_target_pairs={{0,4},{4,0},{8,12},{12,8},{16,20},{20,16},{24,28},{28,24},{1,5},{5... | collective-permute-start | bytes 3145736 | tf_op jit(solution)/shard_map/ppermute | solution.py:169
  44.8 3.4 %shard_map.30 = (bf16[384,1024]{1,0:T(8,128)(2,1)S(1)}, bf16[384,1024]{1,0:T(8,128)(2,1)S(1)}, bf16[1024,768]{1,0:T(8,128)(2,1)S(1)}, bf16[1024,768]{1,0:T(8,128)(2,1)S(1)}, f32[384,768]{1,0:T(8,128)S(1)}) custom-call(f32[2048,128]{1,0:T(8,128)S(1)} %shard_map.29.p0, f32[2048,128]{1,0:T(8,128)S(1)} %collective-permute-done.3.p1, ...), custom_call_target="tpu_custom_call" | custom-call | flops 1811939328 | bytes 8388608 | tf_op jit(solution)/shard_map/pallas_call | solution.py:25
  48.2 2.3 %shard_map.31 = (f32[256,512]{1,0:T(8,128)S(1)}, f32[256,512]{1,0:T(8,128)S(1)}, f32[256,512]{1,0:T(8,128)S(1)}, f32[256,512]{1,0:T(8,128)S(1)}) custom-call(f32[2048,128]{1,0:T(8,128)S(1)} %collective-permute-done.1.p2, f32[2048,128]{1,0:T(8,128)S(1)} %collective-permute-done.2.s2, bf16[384,1024]{1,0:T(8,128)(2,1)S(1)} %get-tuple-element.26.left_high, ...), custom_call_target="tpu_custom_call" | custom-call | flops 1409286144 | bytes 8388608 | tf_op jit(solution)/shard_map/pallas_call | solution.py:25
  50.5 3.8 %collective-permute-start.11 = (f32[256,512]{1,0:T(8,128)S(1)}, f32[256,512]{1,0:T(8,128)S(1)}, u32[]{:S(2)}, u32[]{:S(2)}) collective-permute-start(f32[256,512]{1,0:T(8,128)S(1)} %get-tuple-element.40), channel_id=1, source_target_pairs={{0,32},{4,484},{8,40},{12,492},{16,48},{20,500},{24,56},{28,508},{... | collective-permute-start | bytes 1572872 | tf_op jit(solution)/shard_map/ppermute | solution.py:187
  54.3 3.8 %collective-permute-start.7 = (f32[256,512]{1,0:T(8,128)S(1)}, f32[256,512]{1,0:T(8,128)S(1)}, u32[]{:S(2)}, u32[]{:S(2)}) collective-permute-start(f32[256,512]{1,0:T(8,128)S(1)} %get-tuple-element.32), channel_id=1, source_target_pairs={{0,32},{4,484},{8,40},{12,492},{16,48},{20,500},{24,56},{28,508},{... | collective-permute-start | bytes 1572872 | tf_op jit(solution)/shard_map/ppermute | solution.py:187
  58.2 10.9 %collective-permute-done.11.came = f32[256,512]{1,0:T(8,128)S(1)} collective-permute-done((f32[256,512]{1,0:T(8,128)S(1)}, f32[256,512]{1,0:T(8,128)S(1)}, u32[]{:S(2)}, u32[]{:S(2)}) %collective-permute-start.11) | collective-permute-done | bytes 524320 | tf_op jit(solution)/shard_map/ppermute | solution.py:187
  69.1 1.9 %collective-permute-start.12 = (f32[128,512]{1,0:T(8,128)S(1)}, f32[128,512]{1,0:T(8,128)S(1)}, u32[]{:S(2)}, u32[]{:S(2)}) collective-permute-start(f32[128,512]{1,0:T(8,128)S(1)} %get-tuple-element.42), channel_id=1, source_target_pairs={{0,64},{4,452},{8,72},{12,460},{16,80},{20,468},{24,88},{28,476},{... | collective-permute-start | bytes 786440 | tf_op jit(solution)/shard_map/ppermute | solution.py:187
  71.0 3.6 %collective-permute-done.7.came = f32[256,512]{1,0:T(8,128)S(1)} collective-permute-done((f32[256,512]{1,0:T(8,128)S(1)}, f32[256,512]{1,0:T(8,128)S(1)}, u32[]{:S(2)}, u32[]{:S(2)}) %collective-permute-start.7) | collective-permute-done | bytes 524320 | tf_op jit(solution)/shard_map/ppermute | solution.py:187
  74.7 1.9 %collective-permute-start.8 = (f32[128,512]{1,0:T(8,128)S(1)}, f32[128,512]{1,0:T(8,128)S(1)}, u32[]{:S(2)}, u32[]{:S(2)}) collective-permute-start(f32[128,512]{1,0:T(8,128)S(1)} %get-tuple-element.34), channel_id=1, source_target_pairs={{0,64},{4,452},{8,72},{12,460},{16,80},{20,468},{24,88},{28,476},{... | collective-permute-start | bytes 786440 | tf_op jit(solution)/shard_map/ppermute | solution.py:187
  76.7 5.2 %collective-permute-done.12.came = f32[128,512]{1,0:T(8,128)S(1)} collective-permute-done((f32[128,512]{1,0:T(8,128)S(1)}, f32[128,512]{1,0:T(8,128)S(1)}, u32[]{:S(2)}, u32[]{:S(2)}) %collective-permute-start.12) | collective-permute-done | bytes 262176 | tf_op jit(solution)/shard_map/ppermute | solution.py:187
  81.9 1.9 %collective-permute-start.13 = (f32[64,512]{1,0:T(8,128)S(1)}, f32[64,512]{1,0:T(8,128)S(1)}, u32[]{:S(2)}, u32[]{:S(2)}) collective-permute-start(f32[64,512]{1,0:T(8,128)S(1)} %get-tuple-element.44), channel_id=1, source_target_pairs={{0,128},{4,388},{8,136},{12,396},{16,144},{20,404},{24,152},{28,41... | collective-permute-start | bytes 393224 | tf_op jit(solution)/shard_map/ppermute | solution.py:187
  83.9 3.6 %collective-permute-done.8.came = f32[128,512]{1,0:T(8,128)S(1)} collective-permute-done((f32[128,512]{1,0:T(8,128)S(1)}, f32[128,512]{1,0:T(8,128)S(1)}, u32[]{:S(2)}, u32[]{:S(2)}) %collective-permute-start.8) | collective-permute-done | bytes 262176 | tf_op jit(solution)/shard_map/ppermute | solution.py:187
  87.5 7.0 %collective-permute-start.9 = (f32[64,512]{1,0:T(8,128)S(1)}, f32[64,512]{1,0:T(8,128)S(1)}, u32[]{:S(2)}, u32[]{:S(2)}) collective-permute-start(f32[64,512]{1,0:T(8,128)S(1)} %get-tuple-element.36), channel_id=1, source_target_pairs={{0,128},{4,388},{8,136},{12,396},{16,144},{20,404},{24,152},{28,41... | collective-permute-start | bytes 393224 | tf_op jit(solution)/shard_map/ppermute | solution.py:187
  94.5 3.2 %collective-permute-done.13.came = f32[64,512]{1,0:T(8,128)S(1)} collective-permute-done((f32[64,512]{1,0:T(8,128)S(1)}, f32[64,512]{1,0:T(8,128)S(1)}, u32[]{:S(2)}, u32[]{:S(2)}) %collective-permute-start.13) | collective-permute-done | bytes 131104 | tf_op jit(solution)/shard_map/ppermute | solution.py:187
  97.7 7.5 %collective-permute-start.14 = (f32[32,512]{1,0:T(8,128)S(1)}, f32[32,512]{1,0:T(8,128)S(1)}, u32[]{:S(2)}, u32[]{:S(2)}) collective-permute-start(f32[32,512]{1,0:T(8,128)S(1)} %get-tuple-element.46), channel_id=1, source_target_pairs={{0,256},{4,260},{8,264},{12,268},{16,272},{20,276},{24,280},{28,28... | collective-permute-start | bytes 196616 | tf_op jit(solution)/shard_map/ppermute | solution.py:187
  105.2 7.1 %collective-permute-start.10 = (f32[32,512]{1,0:T(8,128)S(1)}, f32[32,512]{1,0:T(8,128)S(1)}, u32[]{:S(2)}, u32[]{:S(2)}) collective-permute-start(f32[32,512]{1,0:T(8,128)S(1)} %get-tuple-element.38), channel_id=1, source_target_pairs={{0,256},{4,260},{8,264},{12,268},{16,272},{20,276},{24,280},{28,28... | collective-permute-start | bytes 196616 | tf_op jit(solution)/shard_map/ppermute | solution.py:187
  112.6 7.6 %collective-permute-done.10.came_a = f32[32,512]{1,0:T(8,128)S(1)} collective-permute-done((f32[32,512]{1,0:T(8,128)S(1)}, f32[32,512]{1,0:T(8,128)S(1)}, u32[]{:S(2)}, u32[]{:S(2)}) %collective-permute-start.10) | collective-permute-done | bytes 65568 | tf_op jit(solution)/shard_map/ppermute | solution.py:187
  (21 shorter events, 7.5 us)
Async XLA Ops:
  0.0 1.0 copy-start
  1.0 0.7 copy-start.1
  2.3 3.8 %collective-permute-start = (f32[1024,128]{1,0:T(8,128)S(1)}, f32[1024,128]{1,0:T(8,128)S(1)}, u32[]{:S(2)}, u32[]{:S(2)}) collective-permute-start(f32[1024,128]{1,0:T(8,128)S(1)} %shard_map.28.own), channel_id=1, source_target_pairs={{0,4},{4,0},{8,12},{12,8},{16,20},{20,16},{24,28},{28,24},{1,5},{5... | collective-permute-start | bytes 1572872 | tf_op jit(solution)/shard_map/ppermute | solution.py:169
  6.2 28.5 %collective-permute-start.3 = (f32[2048,128]{1,0:T(8,128)S(1)}, f32[2048,128]{1,0:T(8,128)S(1)}, u32[]{:S(2)}, u32[]{:S(2)}) collective-permute-start(f32[2048,128]{1,0:T(8,128)S(1)} %shard_map.29.p0), channel_id=1, source_target_pairs={{1,0},{12,4},{2,1},{13,5},{3,2},{14,6},{0,3},{15,7},{9,8},{20,12},... | collective-permute-start | bytes 3145736 | tf_op jit(solution)/shard_map/ppermute | solution.py:178
  11.1 29.1 %collective-permute-start.5 = (f32[2048,128]{1,0:T(8,128)S(1)}, f32[2048,128]{1,0:T(8,128)S(1)}, u32[]{:S(2)}, u32[]{:S(2)}) collective-permute-start(f32[2048,128]{1,0:T(8,128)S(1)} %shard_map.29.p0), channel_id=1, source_target_pairs={{3,0},{28,4},{0,1},{29,5},{1,2},{30,6},{2,3},{31,7},{11,8},{4,12},... | collective-permute-start | bytes 3145736 | tf_op jit(solution)/shard_map/ppermute | solution.py:178
  13.0 29.1 %collective-permute-start.1 = (f32[2048,128]{1,0:T(8,128)S(1)}, f32[2048,128]{1,0:T(8,128)S(1)}, u32[]{:S(2)}, u32[]{:S(2)}) collective-permute-start(f32[2048,128]{1,0:T(8,128)S(1)} %shard_map.29.p0), channel_id=1, source_target_pairs={{2,0},{20,4},{3,1},{21,5},{0,2},{22,6},{1,3},{23,7},{10,8},{28,12}... | collective-permute-start | bytes 3145736 | tf_op jit(solution)/shard_map/ppermute | solution.py:178
  34.6 10.0 %collective-permute-start.4 = (f32[2048,128]{1,0:T(8,128)S(1)}, f32[2048,128]{1,0:T(8,128)S(1)}, u32[]{:S(2)}, u32[]{:S(2)}) collective-permute-start(f32[2048,128]{1,0:T(8,128)S(1)} %collective-permute-done.3.p1), channel_id=1, source_target_pairs={{0,4},{4,0},{8,12},{12,8},{16,20},{20,16},{24,28},{28,24},{1,5},{5... | collective-permute-start | bytes 3145736 | tf_op jit(solution)/shard_map/ppermute | solution.py:169
  40.2 4.5 %collective-permute-start.6 = (f32[2048,128]{1,0:T(8,128)S(1)}, f32[2048,128]{1,0:T(8,128)S(1)}, u32[]{:S(2)}, u32[]{:S(2)}) collective-permute-start(f32[2048,128]{1,0:T(8,128)S(1)} %collective-permute-done.5.p3), channel_id=1, source_target_pairs={{0,4},{4,0},{8,12},{12,8},{16,20},{20,16},{24,28},{28,24},{1,5},{5... | collective-permute-start | bytes 3145736 | tf_op jit(solution)/shard_map/ppermute | solution.py:169
  42.2 6.0 %collective-permute-start.2 = (f32[2048,128]{1,0:T(8,128)S(1)}, f32[2048,128]{1,0:T(8,128)S(1)}, u32[]{:S(2)}, u32[]{:S(2)}) collective-permute-start(f32[2048,128]{1,0:T(8,128)S(1)} %collective-permute-done.1.p2), channel_id=1, source_target_pairs={{0,4},{4,0},{8,12},{12,8},{16,20},{20,16},{24,28},{28,24},{1,5},{5... | collective-permute-start | bytes 3145736 | tf_op jit(solution)/shard_map/ppermute | solution.py:169
  50.5 18.6 %collective-permute-start.11 = (f32[256,512]{1,0:T(8,128)S(1)}, f32[256,512]{1,0:T(8,128)S(1)}, u32[]{:S(2)}, u32[]{:S(2)}) collective-permute-start(f32[256,512]{1,0:T(8,128)S(1)} %get-tuple-element.40), channel_id=1, source_target_pairs={{0,32},{4,484},{8,40},{12,492},{16,48},{20,500},{24,56},{28,508},{... | collective-permute-start | bytes 1572872 | tf_op jit(solution)/shard_map/ppermute | solution.py:187
  54.3 20.3 %collective-permute-start.7 = (f32[256,512]{1,0:T(8,128)S(1)}, f32[256,512]{1,0:T(8,128)S(1)}, u32[]{:S(2)}, u32[]{:S(2)}) collective-permute-start(f32[256,512]{1,0:T(8,128)S(1)} %get-tuple-element.32), channel_id=1, source_target_pairs={{0,32},{4,484},{8,40},{12,492},{16,48},{20,500},{24,56},{28,508},{... | collective-permute-start | bytes 1572872 | tf_op jit(solution)/shard_map/ppermute | solution.py:187
  69.1 12.8 %collective-permute-start.12 = (f32[128,512]{1,0:T(8,128)S(1)}, f32[128,512]{1,0:T(8,128)S(1)}, u32[]{:S(2)}, u32[]{:S(2)}) collective-permute-start(f32[128,512]{1,0:T(8,128)S(1)} %get-tuple-element.42), channel_id=1, source_target_pairs={{0,64},{4,452},{8,72},{12,460},{16,80},{20,468},{24,88},{28,476},{... | collective-permute-start | bytes 786440 | tf_op jit(solution)/shard_map/ppermute | solution.py:187
  74.7 12.7 %collective-permute-start.8 = (f32[128,512]{1,0:T(8,128)S(1)}, f32[128,512]{1,0:T(8,128)S(1)}, u32[]{:S(2)}, u32[]{:S(2)}) collective-permute-start(f32[128,512]{1,0:T(8,128)S(1)} %get-tuple-element.34), channel_id=1, source_target_pairs={{0,64},{4,452},{8,72},{12,460},{16,80},{20,468},{24,88},{28,476},{... | collective-permute-start | bytes 786440 | tf_op jit(solution)/shard_map/ppermute | solution.py:187
  81.9 15.7 %collective-permute-start.13 = (f32[64,512]{1,0:T(8,128)S(1)}, f32[64,512]{1,0:T(8,128)S(1)}, u32[]{:S(2)}, u32[]{:S(2)}) collective-permute-start(f32[64,512]{1,0:T(8,128)S(1)} %get-tuple-element.44), channel_id=1, source_target_pairs={{0,128},{4,388},{8,136},{12,396},{16,144},{20,404},{24,152},{28,41... | collective-permute-start | bytes 393224 | tf_op jit(solution)/shard_map/ppermute | solution.py:187
  87.5 17.7 %collective-permute-start.9 = (f32[64,512]{1,0:T(8,128)S(1)}, f32[64,512]{1,0:T(8,128)S(1)}, u32[]{:S(2)}, u32[]{:S(2)}) collective-permute-start(f32[64,512]{1,0:T(8,128)S(1)} %get-tuple-element.36), channel_id=1, source_target_pairs={{0,128},{4,388},{8,136},{12,396},{16,144},{20,404},{24,152},{28,41... | collective-permute-start | bytes 393224 | tf_op jit(solution)/shard_map/ppermute | solution.py:187
  97.7 14.9 %collective-permute-start.14 = (f32[32,512]{1,0:T(8,128)S(1)}, f32[32,512]{1,0:T(8,128)S(1)}, u32[]{:S(2)}, u32[]{:S(2)}) collective-permute-start(f32[32,512]{1,0:T(8,128)S(1)} %get-tuple-element.46), channel_id=1, source_target_pairs={{0,256},{4,260},{8,264},{12,268},{16,272},{20,276},{24,280},{28,28... | collective-permute-start | bytes 196616 | tf_op jit(solution)/shard_map/ppermute | solution.py:187
  105.2 15.0 %collective-permute-start.10 = (f32[32,512]{1,0:T(8,128)S(1)}, f32[32,512]{1,0:T(8,128)S(1)}, u32[]{:S(2)}, u32[]{:S(2)}) collective-permute-start(f32[32,512]{1,0:T(8,128)S(1)} %get-tuple-element.38), channel_id=1, source_target_pairs={{0,256},{4,260},{8,264},{12,268},{16,272},{20,276},{24,280},{28,28... | collective-permute-start | bytes 196616 | tf_op jit(solution)/shard_map/ppermute | solution.py:187

commit v3 on v2

--- a/solution.py
+++ b/solution.py
@@ -50,6 +50,12 @@
     pair[pl.ds(pl.multiple_of((1 - k) * inner, inner), inner), :] = other[...]
 
 
+def join_kernel(first, second, pair):
+    inner = first.shape[0]
+    pair[:inner, :] = first[...]
+    pair[inner:, :] = second[...]
+
+
 def split(value):
     high = value.astype(BF16)
     low = (value - high.astype(F32)).astype(BF16)
@@ -120,9 +126,9 @@
 
 
 def second_product_kernel(p2, s2, left_high, left_low, right_high, right_low, part, *refs):
-    sends, keeps = refs[0:2], refs[2:4]
-    last_high, last_low, far_high, far_low, total = refs[4:]
-    z, y = lax.axis_index("layer"), lax.axis_index("col")
+    outs = refs[:8]
+    last_high, last_low, far_high, far_low, total = refs[8:]
+    z = lax.axis_index("layer")
     place(p2, s2, take_left(0, last_high, last_low), take_right(0, far_high, far_low))
     known = part.shape[0]
     total[:known, : part.shape[1]] = part[...]
@@ -130,30 +136,24 @@
     columns = pl.ds(part.shape[1], 2 * TILE)
     total[:known, columns] = product(left_high[...], left_low[...], far_high[...], far_low[...])
     total[known:, columns] = product(last_high[...], last_low[...], far_high[...], far_low[...])
-
-    def rows_of(layer):
-        t = lax.rem(layer // 4 - y + N_COL, N_COL)
-        index = jnp.where(t < 2, t, 5 - t)
-        return strip(index * 4 + lax.rem(layer, 4))
-
-    for j in range(N_LAYER // 2):
-        keep = rows_of(lax.rem(z + 2 * j, N_LAYER))
-        send = rows_of(lax.rem(z + turn() + 2 * j + N_LAYER, N_LAYER))
-        rows = pl.ds(j * SUB, SUB)
+    for steps in range(4):
+        s = lax.rem(z + turn() * steps + 4, 4)
         for half in range(2):
-            columns = pl.ds(half * 4 * TILE, 4 * TILE)
-            keeps[half][rows, :] = total[keep, columns]
-            sends[half][rows, :] = total[send, columns]
-
-
-def stage_kernel(held, came, send, keep):
-    count = held.shape[0] // SUB
-    for i in range(count // 2):
-        rows = pl.ds(i * SUB, SUB)
-        near = pl.ds(2 * i * SUB, SUB)
-        far = strip(lax.rem(turn() + 2 * i + count, count))
-        keep[rows, :] = held[near, :] + came[near, :]
-        send[rows, :] = held[far, :] + came[far, :]
+            for t in range(4):
+                columns = pl.ds(half * 4 * TILE, 4 * TILE)
+                outs[4 * half + steps][pl.ds(t * SUB, SUB), :] = total[strip(t * 4 + s), columns]
+
+
+def add_kernel(held, came, out):
+    out[...] = held[...] + came[...]
+
+
+def near_end_kernel(held, came, *outs):
+    group, y = lax.axis_index("layer") // 4, lax.axis_index("col")
+    for steps in range(4):
+        t = lax.rem(group + turn() * steps - y + 8, 4)
+        rows = strip(jnp.where(t < 2, t, 5 - t))
+        outs[steps][...] = held[rows, :] + came[rows, :]
 
 
 def last_kernel(held_a, came_a, held_b, came_b, out):
@@ -191,8 +191,9 @@
     inner = graph.shape[0]
     (masked,) = call(mask_kernel, [(inner, TILE)], (graph, pattern.reshape(-1)), [VMEM, SMEM])
     (pair,) = call(pair_kernel, [(2 * inner, TILE)], (masked, swap(masked)))
-    came = {t: fetch(pair, t) for t in (1, 3, 2)}
-    swapped = {t: swap(came[t]) for t in (1, 3, 2)}
+    came = {t: fetch(pair, t) for t in (1, 3)}
+    far = (fetch(came[1][:inner], 1), fetch(came[3][inner:], 3))
+    swapped = {t: swap(came[t]) for t in (1, 3)}
     known, wide = 3 * TILE, 6 * TILE
     parts = call(
         first_product_kernel,
@@ -201,25 +202,33 @@
         flops=6 * known * wide * inner,
         nbytes=8 << 20,
     )
+    far, parts = lax.optimization_barrier((far, parts))
+    (last,) = call(join_kernel, [(2 * inner, TILE)], far)
     split_scratch = [pltpu.VMEM((TILE, inner), BF16)] * 2 + [pltpu.VMEM((inner, 2 * TILE), BF16)] * 2
     made = call(
         second_product_kernel,
-        [(8 * SUB, 4 * TILE)] * 4,
-        (came[2], swapped[2], *parts),
+        [(4 * SUB, 4 * TILE)] * 8,
+        (last, swap(last), *parts),
         scratch=split_scratch + [pltpu.VMEM((4 * TILE, 8 * TILE), F32)],
         flops=6 * 7 * TILE * 2 * TILE * inner,
         nbytes=8 << 20,
     )
-    sends, keeps = list(made[:2]), list(made[2:])
-    arrived = [pass_on(sends[half], 1) for half in range(2)]
-    for stage in (1, 2, 3):
-        count = 8 >> stage
+    held = [made[:4], made[4:]]
+    moving = [held[half][3] for half in range(2)]
+    for steps in (2, 1):
         for half in range(2):
-            sends[half], keeps[half] = call(
-                stage_kernel, [(count * SUB, 4 * TILE)] * 2, (keeps[half], arrived[half])
-            )
-            arrived[half] = pass_on(sends[half], 1 << stage)
-    return call(last_kernel, [(SUB, 8 * TILE)], (keeps[0], arrived[0], keeps[1], arrived[1]))[0]
+            operands = (held[half][steps], pass_on(moving[half], 1))
+            (moving[half],) = call(add_kernel, [(4 * SUB, 4 * TILE)], operands)
+    for half in range(2):
+        operands = (held[half][0], pass_on(moving[half], 1))
+        held[half] = call(near_end_kernel, [(SUB, 4 * TILE)] * 4, operands)
+        moving[half] = held[half][3]
+    for steps in (2, 1):
+        for half in range(2):
+            operands = (held[half][steps], pass_on(moving[half], 4))
+            (moving[half],) = call(add_kernel, [(SUB, 4 * TILE)], operands)
+    ends = [operand for half in range(2) for operand in (held[half][0], pass_on(moving[half], 4))]
+    return call(last_kernel, [(SUB, 8 * TILE)], ends)[0]
 
 
 def solution(mesh):

time: 121 us -> 127 us (1.050)
  starting transfers between devices: 54.1 us -> 71.1 us
  waiting for transfers between devices: 57.7 us -> 46 us
    ppermute x8 -> x12, starting transfers between devices: 35 us -> 47.9 us  [pass_on(): return lax.ppermute(value, ('layer', 'row'), pairs)]
    ppermute x8 -> x12, waiting for transfers between devices: 34.4 us -> 24.8 us  [pass_on(): return lax.ppermute(value, ('layer', 'row'), pairs)]
    ppermute x3 -> x4, waiting for transfers between devices: 21.2 us -> 16.7 us  [fetch(): return lax.ppermute(value, ('row', 'col'), pairs)]
    ppermute x4, waiting for transfers between devices: 2.07 us -> 4.51 us  [swap(): return lax.ppermute(value, 'row', [(i, i ^ 1) for i in range(N_ROW)])]
    ppermute x4, starting transfers between devices: 8.14 us -> 10.5 us  [swap(): return lax.ppermute(value, 'row', [(i, i ^ 1) for i in range(N_ROW)])]
    ppermute x3 -> x4, starting transfers between devices: 10.9 us -> 12.7 us  [fetch(): return lax.ppermute(value, ('row', 'col'), pairs)]
    pallas_call x11 -> x16, Pallas kernels: 7.24 us -> 7.41 us  [call(): pl.pallas_call(kernel, out_shape=tuple((jax.ShapeDtypeStruct(s, d) for s,...]
  transfers between devices with their start and end apart: 15 -> 20, of which waited for: 11 -> 14; matrix products, arithmetic and copies ran while one was open for 0% -> 0% of each run, Pallas kernels for 3% -> 3%
where the time goes in v3:
time: 127 us
  starting transfers between devices  71.1 us (56%)
  waiting for transfers between devices  46 us (36%)
  Pallas kernels  7.41 us (6%)
  local copies, waits for them, and re-layouts  1.77 us (1%)
    ppermute x12, starting transfers between devices, pass_on(): return lax.ppermute(value, ('layer', 'row'), pairs)  47.9 us
    ppermute x12, waiting for transfers between devices, pass_on(): return lax.ppermute(value, ('layer', 'row'), pairs)  24.8 us
    ppermute x4, waiting for transfers between devices, fetch(): return lax.ppermute(value, ('row', 'col'), pairs)  16.7 us
    ppermute x4, starting transfers between devices, fetch(): return lax.ppermute(value, ('row', 'col'), pairs)  12.7 us
    ppermute x4, starting transfers between devices, swap(): return lax.ppermute(value, 'row', [(i, i ^ 1) for i in range(N_ROW)])  10.5 us
    pallas_call x16, Pallas kernels, call(): pl.pallas_call(kernel, out_shape=tuple((jax.ShapeDtypeStruct(s, d) for s,...  7.41 us
    ppermute x4, waiting for transfers between devices, swap(): return lax.ppermute(value, 'row', [(i, i ^ 1) for i in range(N_ROW)])  4.51 us
  transfers between devices with their start and end apart: 20, of which 14 were waited for; matrix products, arithmetic and copies ran while one was open for 0% of the time, Pallas kernels for 3%

profile of v3, /device:TPU:6, one launch (start us, length us, event | category | flops | bytes accessed | tf_op | source)
XLA Modules:
  0.0 126.6 jit_solution(3322237210677283011)
XLA Ops:
  2.3 1.9 %collective-permute-start = (f32[1024,128]{1,0:T(8,128)S(1)}, f32[1024,128]{1,0:T(8,128)S(1)}, u32[]{:S(2)}, u32[]{:S(2)}) collective-permute-start(f32[1024,128]{1,0:T(8,128)S(1)} %shard_map.28.own), channel_id=1, source_target_pairs={{0,4},{4,0},{8,12},{12,8},{16,20},{20,16},{24,28},{28,24},{1,5},{5... | collective-permute-start | bytes 1572872 | tf_op jit(solution)/shard_map/ppermute | solution.py:169
  6.2 4.9 %collective-permute-start.1 = (f32[2048,128]{1,0:T(8,128)S(1)}, f32[2048,128]{1,0:T(8,128)S(1)}, u32[]{:S(2)}, u32[]{:S(2)}) collective-permute-start(f32[2048,128]{1,0:T(8,128)S(1)} %shard_map.29.p0), channel_id=1, source_target_pairs={{1,0},{12,4},{2,1},{13,5},{3,2},{14,6},{0,3},{15,7},{9,8},{20,12},... | collective-permute-start | bytes 3145736 | tf_op jit(solution)/shard_map/ppermute | solution.py:178
  11.1 1.9 %collective-permute-start.3 = (f32[2048,128]{1,0:T(8,128)S(1)}, f32[2048,128]{1,0:T(8,128)S(1)}, u32[]{:S(2)}, u32[]{:S(2)}) collective-permute-start(f32[2048,128]{1,0:T(8,128)S(1)} %shard_map.29.p0), channel_id=1, source_target_pairs={{3,0},{28,4},{0,1},{29,5},{1,2},{30,6},{2,3},{31,7},{11,8},{4,12},... | collective-permute-start | bytes 3145736 | tf_op jit(solution)/shard_map/ppermute | solution.py:178
  13.0 10.4 %collective-permute-done.1.p1 = f32[2048,128]{1,0:T(8,128)S(1)} collective-permute-done((f32[2048,128]{1,0:T(8,128)S(1)}, f32[2048,128]{1,0:T(8,128)S(1)}, u32[]{:S(2)}, u32[]{:S(2)}) %collective-permute-start.1) | collective-permute-done | bytes 1048608 | tf_op jit(solution)/shard_map/ppermute | solution.py:178
  23.4 4.8 %collective-permute-start.5 = (f32[2048,128]{1,0:T(8,128)S(1)}, f32[2048,128]{1,0:T(8,128)S(1)}, u32[]{:S(2)}, u32[]{:S(2)}) collective-permute-start(f32[2048,128]{1,0:T(8,128)S(1)} %collective-permute-done.1.p1), channel_id=1, source_target_pairs={{0,4},{4,0},{8,12},{12,8},{16,20},{20,16},{24,28},{28,24},{1,5},{5... | collective-permute-start | bytes 3145736 | tf_op jit(solution)/shard_map/ppermute | solution.py:169
  31.0 2.4 %collective-permute-start.2 = (f32[1024,128]{1,0:T(8,128)S(1)}, f32[1024,128]{1,0:T(8,128)S(1)}, u32[]{:S(2)}, u32[]{:S(2)}) collective-permute-start(f32[1024,128]{1,0:T(8,128)S(1)} %slice.8), channel_id=1, source_target_pairs={{1,0},{12,4},{2,1},{13,5},{3,2},{14,6},{0,3},{15,7},{9,8},{20,12},... | collective-permute-start | bytes 1572872 | tf_op jit(solution)/shard_map/ppermute | solution.py:178
  33.4 3.4 %collective-permute-start.4 = (f32[1024,128]{1,0:T(8,128)S(1)}, f32[1024,128]{1,0:T(8,128)S(1)}, u32[]{:S(2)}, u32[]{:S(2)}) collective-permute-start(f32[1024,128]{1,0:T(8,128)S(1)} %slice.9), channel_id=1, source_target_pairs={{3,0},{28,4},{0,1},{29,5},{1,2},{30,6},{2,3},{31,7},{11,8},{4,12},... | collective-permute-start | bytes 1572872 | tf_op jit(solution)/shard_map/ppermute | solution.py:178
  36.9 3.4 %shard_map.30 = (bf16[384,1024]{1,0:T(8,128)(2,1)S(1)}, bf16[384,1024]{1,0:T(8,128)(2,1)S(1)}, bf16[1024,768]{1,0:T(8,128)(2,1)S(1)}, bf16[1024,768]{1,0:T(8,128)(2,1)S(1)}, f32[384,768]{1,0:T(8,128)S(1)}) custom-call(f32[2048,128]{1,0:T(8,128)S(1)} %shard_map.29.p0, f32[2048,128]{1,0:T(8,128)S(1)} %collective-permute-done.1.p1, ...), custom_call_target="tpu_custom_call" | custom-call | flops 1811939328 | bytes 8388608 | tf_op jit(solution)/shard_map/pallas_call | solution.py:25
  42.0 3.7 %collective-permute-done.4.second = f32[1024,128]{1,0:T(8,128)S(1)} collective-permute-done((f32[1024,128]{1,0:T(8,128)S(1)}, f32[1024,128]{1,0:T(8,128)S(1)}, u32[]{:S(2)}, u32[]{:S(2)}) %collective-permute-start.4) | collective-permute-done | bytes 524320 | tf_op jit(solution)/shard_map/ppermute | solution.py:178
  47.7 2.6 %collective-permute-done.7.s2 = f32[2048,128]{1,0:T(8,128)S(1)} collective-permute-done((f32[2048,128]{1,0:T(8,128)S(1)}, f32[2048,128]{1,0:T(8,128)S(1)}, u32[]{:S(2)}, u32[]{:S(2)}) %collective-permute-start.7) | collective-permute-done | bytes 1048608 | tf_op jit(solution)/shard_map/ppermute | solution.py:169
  50.4 2.4 %shard_map.32 = (f32[128,512]{1,0:T(8,128)S(1)}, f32[128,512]{1,0:T(8,128)S(1)}, f32[128,512]{1,0:T(8,128)S(1)}, f32[128,512]{1,0:T(8,128)S(1)}, f32[128,512]{1,...) custom-call(f32[2048,128]{1,0:T(8,128)S(1)} %shard_map.31.p2, ...), custom_call_target="tpu_custom_call" | custom-call | flops 1409286144 | bytes 8388608 | tf_op jit(solution)/shard_map/pallas_call | solution.py:25
  52.8 3.8 %collective-permute-start.14 = (f32[128,512]{1,0:T(8,128)S(1)}, f32[128,512]{1,0:T(8,128)S(1)}, u32[]{:S(2)}, u32[]{:S(2)}) collective-permute-start(f32[128,512]{1,0:T(8,128)S(1)} %get-tuple-element.56), channel_id=1, source_target_pairs={{0,32},{4,484},{8,40},{12,492},{16,48},{20,500},{24,56},{28,508},{... | collective-permute-start | bytes 786440 | tf_op jit(solution)/shard_map/ppermute | solution.py:187
  56.6 3.8 %collective-permute-start.8 = (f32[128,512]{1,0:T(8,128)S(1)}, f32[128,512]{1,0:T(8,128)S(1)}, u32[]{:S(2)}, u32[]{:S(2)}) collective-permute-start(f32[128,512]{1,0:T(8,128)S(1)} %get-tuple-element.48), channel_id=1, source_target_pairs={{0,32},{4,484},{8,40},{12,492},{16,48},{20,500},{24,56},{28,508},{... | collective-permute-start | bytes 786440 | tf_op jit(solution)/shard_map/ppermute | solution.py:187
  60.4 8.1 %collective-permute-done.14.came = f32[128,512]{1,0:T(8,128)S(1)} collective-permute-done((f32[128,512]{1,0:T(8,128)S(1)}, f32[128,512]{1,0:T(8,128)S(1)}, u32[]{:S(2)}, u32[]{:S(2)}) %collective-permute-start.14) | collective-permute-done | bytes 262176 | tf_op jit(solution)/shard_map/ppermute | solution.py:187
  73.3 4.7 %collective-permute-done.15.came = f32[128,512]{1,0:T(8,128)S(1)} collective-permute-done((f32[128,512]{1,0:T(8,128)S(1)}, f32[128,512]{1,0:T(8,128)S(1)}, u32[]{:S(2)}, u32[]{:S(2)}) %collective-permute-start.15) | collective-permute-done | bytes 262176 | tf_op jit(solution)/shard_map/ppermute | solution.py:187
  80.9 1.9 %collective-permute-start.10 = (f32[128,512]{1,0:T(8,128)S(1)}, f32[128,512]{1,0:T(8,128)S(1)}, u32[]{:S(2)}, u32[]{:S(2)}) collective-permute-start(f32[128,512]{1,0:T(8,128)S(1)} %shard_map.34), channel_id=1, source_target_pairs={{0,32},{4,484},{8,40},{12,492},{16,48},{20,500},{24,56},{28,508},{... | collective-permute-start | bytes 786440 | tf_op jit(solution)/shard_map/ppermute | solution.py:187
  82.8 4.7 %collective-permute-done.16.came = f32[128,512]{1,0:T(8,128)S(1)} collective-permute-done((f32[128,512]{1,0:T(8,128)S(1)}, f32[128,512]{1,0:T(8,128)S(1)}, u32[]{:S(2)}, u32[]{:S(2)}) %collective-permute-start.16) | collective-permute-done | bytes 262176 | tf_op jit(solution)/shard_map/ppermute | solution.py:187
  87.6 2.8 %collective-permute-start.17 = (f32[32,512]{1,0:T(8,128)S(1)}, f32[32,512]{1,0:T(8,128)S(1)}, u32[]{:S(2)}, u32[]{:S(2)}) collective-permute-start(f32[32,512]{1,0:T(8,128)S(1)} %get-tuple-element.60), channel_id=1, source_target_pairs={{0,128},{4,388},{8,136},{12,396},{16,144},{20,404},{24,152},{28,41... | collective-permute-start | bytes 196616 | tf_op jit(solution)/shard_map/ppermute | solution.py:187
  90.5 9.1 %collective-permute-start.11 = (f32[32,512]{1,0:T(8,128)S(1)}, f32[32,512]{1,0:T(8,128)S(1)}, u32[]{:S(2)}, u32[]{:S(2)}) collective-permute-start(f32[32,512]{1,0:T(8,128)S(1)} %get-tuple-element.52), channel_id=1, source_target_pairs={{0,128},{4,388},{8,136},{12,396},{16,144},{20,404},{24,152},{28,41... | collective-permute-start | bytes 196616 | tf_op jit(solution)/shard_map/ppermute | solution.py:187
  99.6 4.3 %collective-permute-start.18 = (f32[32,512]{1,0:T(8,128)S(1)}, f32[32,512]{1,0:T(8,128)S(1)}, u32[]{:S(2)}, u32[]{:S(2)}) collective-permute-start(f32[32,512]{1,0:T(8,128)S(1)} %shard_map.41), channel_id=1, source_target_pairs={{0,128},{4,388},{8,136},{12,396},{16,144},{20,404},{24,152},{28,41... | collective-permute-start | bytes 196616 | tf_op jit(solution)/shard_map/ppermute | solution.py:187
  103.9 6.6 %collective-permute-start.12 = (f32[32,512]{1,0:T(8,128)S(1)}, f32[32,512]{1,0:T(8,128)S(1)}, u32[]{:S(2)}, u32[]{:S(2)}) collective-permute-start(f32[32,512]{1,0:T(8,128)S(1)} %shard_map.36), channel_id=1, source_target_pairs={{0,128},{4,388},{8,136},{12,396},{16,144},{20,404},{24,152},{28,41... | collective-permute-start | bytes 196616 | tf_op jit(solution)/shard_map/ppermute | solution.py:187
  110.5 4.2 %collective-permute-start.19 = (f32[32,512]{1,0:T(8,128)S(1)}, f32[32,512]{1,0:T(8,128)S(1)}, u32[]{:S(2)}, u32[]{:S(2)}) collective-permute-start(f32[32,512]{1,0:T(8,128)S(1)} %shard_map.42), channel_id=1, source_target_pairs={{0,128},{4,388},{8,136},{12,396},{16,144},{20,404},{24,152},{28,41... | collective-permute-start | bytes 196616 | tf_op jit(solution)/shard_map/ppermute | solution.py:187
  115.5 5.6 %collective-permute-start.13 = (f32[32,512]{1,0:T(8,128)S(1)}, f32[32,512]{1,0:T(8,128)S(1)}, u32[]{:S(2)}, u32[]{:S(2)}) collective-permute-start(f32[32,512]{1,0:T(8,128)S(1)} %shard_map.37), channel_id=1, source_target_pairs={{0,128},{4,388},{8,136},{12,396},{16,144},{20,404},{24,152},{28,41... | collective-permute-start | bytes 196616 | tf_op jit(solution)/shard_map/ppermute | solution.py:187
  121.5 4.4 %collective-permute-done.13.came_a = f32[32,512]{1,0:T(8,128)S(1)} collective-permute-done((f32[32,512]{1,0:T(8,128)S(1)}, f32[32,512]{1,0:T(8,128)S(1)}, u32[]{:S(2)}, u32[]{:S(2)}) %collective-permute-start.13) | collective-permute-done | bytes 65568 | tf_op jit(solution)/shard_map/ppermute | solution.py:187
  (38 shorter events, 20.3 us)
Async XLA Ops:
  0.0 1.0 copy-start
  1.0 0.7 copy-start.1
  2.3 3.8 %collective-permute-start = (f32[1024,128]{1,0:T(8,128)S(1)}, f32[1024,128]{1,0:T(8,128)S(1)}, u32[]{:S(2)}, u32[]{:S(2)}) collective-permute-start(f32[1024,128]{1,0:T(8,128)S(1)} %shard_map.28.own), channel_id=1, source_target_pairs={{0,4},{4,0},{8,12},{12,8},{16,20},{20,16},{24,28},{28,24},{1,5},{5... | collective-permute-start | bytes 1572872 | tf_op jit(solution)/shard_map/ppermute | solution.py:169
  6.2 17.2 %collective-permute-start.1 = (f32[2048,128]{1,0:T(8,128)S(1)}, f32[2048,128]{1,0:T(8,128)S(1)}, u32[]{:S(2)}, u32[]{:S(2)}) collective-permute-start(f32[2048,128]{1,0:T(8,128)S(1)} %shard_map.29.p0), channel_id=1, source_target_pairs={{1,0},{12,4},{2,1},{13,5},{3,2},{14,6},{0,3},{15,7},{9,8},{20,12},... | collective-permute-start | bytes 3145736 | tf_op jit(solution)/shard_map/ppermute | solution.py:178
  11.1 17.9 %collective-permute-start.3 = (f32[2048,128]{1,0:T(8,128)S(1)}, f32[2048,128]{1,0:T(8,128)S(1)}, u32[]{:S(2)}, u32[]{:S(2)}) collective-permute-start(f32[2048,128]{1,0:T(8,128)S(1)} %shard_map.29.p0), channel_id=1, source_target_pairs={{3,0},{28,4},{0,1},{29,5},{1,2},{30,6},{2,3},{31,7},{11,8},{4,12},... | collective-permute-start | bytes 3145736 | tf_op jit(solution)/shard_map/ppermute | solution.py:178
  23.4 13.5 %collective-permute-start.5 = (f32[2048,128]{1,0:T(8,128)S(1)}, f32[2048,128]{1,0:T(8,128)S(1)}, u32[]{:S(2)}, u32[]{:S(2)}) collective-permute-start(f32[2048,128]{1,0:T(8,128)S(1)} %collective-permute-done.1.p1), channel_id=1, source_target_pairs={{0,4},{4,0},{8,12},{12,8},{16,20},{20,16},{24,28},{28,24},{1,5},{5... | collective-permute-start | bytes 3145736 | tf_op jit(solution)/shard_map/ppermute | solution.py:169
  29.0 7.9 %collective-permute-start.6 = (f32[2048,128]{1,0:T(8,128)S(1)}, f32[2048,128]{1,0:T(8,128)S(1)}, u32[]{:S(2)}, u32[]{:S(2)}) collective-permute-start(f32[2048,128]{1,0:T(8,128)S(1)} %collective-permute-done.3.p3), channel_id=1, source_target_pairs={{0,4},{4,0},{8,12},{12,8},{16,20},{20,16},{24,28},{28,24},{1,5},{5... | collective-permute-start | bytes 3145736 | tf_op jit(solution)/shard_map/ppermute | solution.py:169
  31.0 11.1 %collective-permute-start.2 = (f32[1024,128]{1,0:T(8,128)S(1)}, f32[1024,128]{1,0:T(8,128)S(1)}, u32[]{:S(2)}, u32[]{:S(2)}) collective-permute-start(f32[1024,128]{1,0:T(8,128)S(1)} %slice.8), channel_id=1, source_target_pairs={{1,0},{12,4},{2,1},{13,5},{3,2},{14,6},{0,3},{15,7},{9,8},{20,12},... | collective-permute-start | bytes 1572872 | tf_op jit(solution)/shard_map/ppermute | solution.py:178
  33.4 12.3 %collective-permute-start.4 = (f32[1024,128]{1,0:T(8,128)S(1)}, f32[1024,128]{1,0:T(8,128)S(1)}, u32[]{:S(2)}, u32[]{:S(2)}) collective-permute-start(f32[1024,128]{1,0:T(8,128)S(1)} %slice.9), channel_id=1, source_target_pairs={{3,0},{28,4},{0,1},{29,5},{1,2},{30,6},{2,3},{31,7},{11,8},{4,12},... | collective-permute-start | bytes 1572872 | tf_op jit(solution)/shard_map/ppermute | solution.py:178
  45.8 4.6 %collective-permute-start.7 = (f32[2048,128]{1,0:T(8,128)S(1)}, f32[2048,128]{1,0:T(8,128)S(1)}, u32[]{:S(2)}, u32[]{:S(2)}) collective-permute-start(f32[2048,128]{1,0:T(8,128)S(1)} %shard_map.31.p2), channel_id=1, source_target_pairs={{0,4},{4,0},{8,12},{12,8},{16,20},{20,16},{24,28},{28,24},{1,5},{5... | collective-permute-start | bytes 3145736 | tf_op jit(solution)/shard_map/ppermute | solution.py:169
  52.8 15.8 %collective-permute-start.14 = (f32[128,512]{1,0:T(8,128)S(1)}, f32[128,512]{1,0:T(8,128)S(1)}, u32[]{:S(2)}, u32[]{:S(2)}) collective-permute-start(f32[128,512]{1,0:T(8,128)S(1)} %get-tuple-element.56), channel_id=1, source_target_pairs={{0,32},{4,484},{8,40},{12,492},{16,48},{20,500},{24,56},{28,508},{... | collective-permute-start | bytes 786440 | tf_op jit(solution)/shard_map/ppermute | solution.py:187
  56.6 14.7 %collective-permute-start.8 = (f32[128,512]{1,0:T(8,128)S(1)}, f32[128,512]{1,0:T(8,128)S(1)}, u32[]{:S(2)}, u32[]{:S(2)}) collective-permute-start(f32[128,512]{1,0:T(8,128)S(1)} %get-tuple-element.48), channel_id=1, source_target_pairs={{0,32},{4,484},{8,40},{12,492},{16,48},{20,500},{24,56},{28,508},{... | collective-permute-start | bytes 786440 | tf_op jit(solution)/shard_map/ppermute | solution.py:187
  68.6 9.5 %collective-permute-start.15 = (f32[128,512]{1,0:T(8,128)S(1)}, f32[128,512]{1,0:T(8,128)S(1)}, u32[]{:S(2)}, u32[]{:S(2)}) collective-permute-start(f32[128,512]{1,0:T(8,128)S(1)} %shard_map.38), channel_id=1, source_target_pairs={{0,32},{4,484},{8,40},{12,492},{16,48},{20,500},{24,56},{28,508},{... | collective-permute-start | bytes 786440 | tf_op jit(solution)/shard_map/ppermute | solution.py:187
  71.4 9.5 %collective-permute-start.9 = (f32[128,512]{1,0:T(8,128)S(1)}, f32[128,512]{1,0:T(8,128)S(1)}, u32[]{:S(2)}, u32[]{:S(2)}) collective-permute-start(f32[128,512]{1,0:T(8,128)S(1)} %shard_map.33), channel_id=1, source_target_pairs={{0,32},{4,484},{8,40},{12,492},{16,48},{20,500},{24,56},{28,508},{... | collective-permute-start | bytes 786440 | tf_op jit(solution)/shard_map/ppermute | solution.py:187
  78.1 9.5 %collective-permute-start.16 = (f32[128,512]{1,0:T(8,128)S(1)}, f32[128,512]{1,0:T(8,128)S(1)}, u32[]{:S(2)}, u32[]{:S(2)}) collective-permute-start(f32[128,512]{1,0:T(8,128)S(1)} %shard_map.39), channel_id=1, source_target_pairs={{0,32},{4,484},{8,40},{12,492},{16,48},{20,500},{24,56},{28,508},{... | collective-permute-start | bytes 786440 | tf_op jit(solution)/shard_map/ppermute | solution.py:187
  80.9 9.5 %collective-permute-start.10 = (f32[128,512]{1,0:T(8,128)S(1)}, f32[128,512]{1,0:T(8,128)S(1)}, u32[]{:S(2)}, u32[]{:S(2)}) collective-permute-start(f32[128,512]{1,0:T(8,128)S(1)} %shard_map.34), channel_id=1, source_target_pairs={{0,32},{4,484},{8,40},{12,492},{16,48},{20,500},{24,56},{28,508},{... | collective-permute-start | bytes 786440 | tf_op jit(solution)/shard_map/ppermute | solution.py:187
  87.6 12.0 %collective-permute-start.17 = (f32[32,512]{1,0:T(8,128)S(1)}, f32[32,512]{1,0:T(8,128)S(1)}, u32[]{:S(2)}, u32[]{:S(2)}) collective-permute-start(f32[32,512]{1,0:T(8,128)S(1)} %get-tuple-element.60), channel_id=1, source_target_pairs={{0,128},{4,388},{8,136},{12,396},{16,144},{20,404},{24,152},{28,41... | collective-permute-start | bytes 196616 | tf_op jit(solution)/shard_map/ppermute | solution.py:187
  90.5 13.4 %collective-permute-start.11 = (f32[32,512]{1,0:T(8,128)S(1)}, f32[32,512]{1,0:T(8,128)S(1)}, u32[]{:S(2)}, u32[]{:S(2)}) collective-permute-start(f32[32,512]{1,0:T(8,128)S(1)} %get-tuple-element.52), channel_id=1, source_target_pairs={{0,128},{4,388},{8,136},{12,396},{16,144},{20,404},{24,152},{28,41... | collective-permute-start | bytes 196616 | tf_op jit(solution)/shard_map/ppermute | solution.py:187
  99.6 10.9 %collective-permute-start.18 = (f32[32,512]{1,0:T(8,128)S(1)}, f32[32,512]{1,0:T(8,128)S(1)}, u32[]{:S(2)}, u32[]{:S(2)}) collective-permute-start(f32[32,512]{1,0:T(8,128)S(1)} %shard_map.41), channel_id=1, source_target_pairs={{0,128},{4,388},{8,136},{12,396},{16,144},{20,404},{24,152},{28,41... | collective-permute-start | bytes 196616 | tf_op jit(solution)/shard_map/ppermute | solution.py:187
  103.9 11.5 %collective-permute-start.12 = (f32[32,512]{1,0:T(8,128)S(1)}, f32[32,512]{1,0:T(8,128)S(1)}, u32[]{:S(2)}, u32[]{:S(2)}) collective-permute-start(f32[32,512]{1,0:T(8,128)S(1)} %shard_map.36), channel_id=1, source_target_pairs={{0,128},{4,388},{8,136},{12,396},{16,144},{20,404},{24,152},{28,41... | collective-permute-start | bytes 196616 | tf_op jit(solution)/shard_map/ppermute | solution.py:187
  110.5 11.0 %collective-permute-start.19 = (f32[32,512]{1,0:T(8,128)S(1)}, f32[32,512]{1,0:T(8,128)S(1)}, u32[]{:S(2)}, u32[]{:S(2)}) collective-permute-start(f32[32,512]{1,0:T(8,128)S(1)} %shard_map.42), channel_id=1, source_target_pairs={{0,128},{4,388},{8,136},{12,396},{16,144},{20,404},{24,152},{28,41... | collective-permute-start | bytes 196616 | tf_op jit(solution)/shard_map/ppermute | solution.py:187
  115.5 10.4 %collective-permute-start.13 = (f32[32,512]{1,0:T(8,128)S(1)}, f32[32,512]{1,0:T(8,128)S(1)}, u32[]{:S(2)}, u32[]{:S(2)}) collective-permute-start(f32[32,512]{1,0:T(8,128)S(1)} %shard_map.37), channel_id=1, source_target_pairs={{0,128},{4,388},{8,136},{12,396},{16,144},{20,404},{24,152},{28,41... | collective-permute-start | bytes 196616 | tf_op jit(solution)/shard_map/ppermute | solution.py:187

commit v4 on v2

--- a/solution.py
+++ b/solution.py
@@ -50,6 +50,12 @@
     pair[pl.ds(pl.multiple_of((1 - k) * inner, inner), inner), :] = other[...]
 
 
+def join_kernel(first, second, pair):
+    inner = first.shape[0]
+    pair[:inner, :] = first[...]
+    pair[inner:, :] = second[...]
+
+
 def split(value):
     high = value.astype(BF16)
     low = (value - high.astype(F32)).astype(BF16)
@@ -156,13 +162,22 @@
         send[rows, :] = held[far, :] + came[far, :]
 
 
-def last_kernel(held_a, came_a, held_b, came_b, out):
+def group_kernel(held_a, came_a, held_b, came_b, out):
+    group = lax.axis_index("layer") // 4
+    half = held_a.shape[1]
+    for i in range(4):
+        source, target = pl.ds(i * SUB, SUB), strip(lax.rem(group + i, 4))
+        out[target, :half] = held_a[source, :] + came_a[source, :]
+        out[target, half:] = held_b[source, :] + came_b[source, :]
+
+
+def last_kernel(came, out):
     x = lax.axis_index("row") // 2
     for index, t in enumerate(ORDER):
-        held, came = ((held_a, came_a), (held_b, came_b))[index // 2]
-        source = pl.ds((index % 2) * 2 * TILE, 2 * TILE)
+        source = pl.ds(index * 2 * TILE, 2 * TILE)
         target = pl.ds(pl.multiple_of(lax.rem(x + t, N_X) * 2 * TILE, 2 * TILE), 2 * TILE)
-        out[:, target] = held[:, source] + came[:, source]
+        a, b, c, d = (came[pl.ds(i * SUB, SUB), source] for i in range(4))
+        out[:, target] = (a + b) + (c + d)
 
 
 def swap(value):
@@ -191,8 +206,9 @@
     inner = graph.shape[0]
     (masked,) = call(mask_kernel, [(inner, TILE)], (graph, pattern.reshape(-1)), [VMEM, SMEM])
     (pair,) = call(pair_kernel, [(2 * inner, TILE)], (masked, swap(masked)))
-    came = {t: fetch(pair, t) for t in (1, 3, 2)}
-    swapped = {t: swap(came[t]) for t in (1, 3, 2)}
+    came = {t: fetch(pair, t) for t in (1, 3)}
+    far = (fetch(came[1][:inner], 1), fetch(came[3][inner:], 3))
+    swapped = {t: swap(came[t]) for t in (1, 3)}
     known, wide = 3 * TILE, 6 * TILE
     parts = call(
         first_product_kernel,
@@ -201,25 +217,29 @@
         flops=6 * known * wide * inner,
         nbytes=8 << 20,
     )
+    (last,) = call(join_kernel, [(2 * inner, TILE)], far)
     split_scratch = [pltpu.VMEM((TILE, inner), BF16)] * 2 + [pltpu.VMEM((inner, 2 * TILE), BF16)] * 2
     made = call(
         second_product_kernel,
         [(8 * SUB, 4 * TILE)] * 4,
-        (came[2], swapped[2], *parts),
+        (last, swap(last), *parts),
         scratch=split_scratch + [pltpu.VMEM((4 * TILE, 8 * TILE), F32)],
         flops=6 * 7 * TILE * 2 * TILE * inner,
         nbytes=8 << 20,
     )
     sends, keeps = list(made[:2]), list(made[2:])
     arrived = [pass_on(sends[half], 1) for half in range(2)]
-    for stage in (1, 2, 3):
-        count = 8 >> stage
-        for half in range(2):
-            sends[half], keeps[half] = call(
-                stage_kernel, [(count * SUB, 4 * TILE)] * 2, (keeps[half], arrived[half])
-            )
-            arrived[half] = pass_on(sends[half], 1 << stage)
-    return call(last_kernel, [(SUB, 8 * TILE)], (keeps[0], arrived[0], keeps[1], arrived[1]))[0]
+    for half in range(2):
+        sends[half], keeps[half] = call(
+            stage_kernel, [(4 * SUB, 4 * TILE)] * 2, (keeps[half], arrived[half])
+        )
+        arrived[half] = pass_on(sends[half], 2)
+    (chunks,) = call(
+        group_kernel, [(4 * SUB, 8 * TILE)], (keeps[0], arrived[0], keeps[1], arrived[1])
+    )
+    groups = [[4 * g + s for g in range(4)] for s in range(4)]
+    came = lax.all_to_all(chunks, "layer", 0, 0, tiled=True, axis_index_groups=groups)
+    return call(last_kernel, [(SUB, 8 * TILE)], (came,))[0]
 
 
 def solution(mesh):

time: 121 us -> 125 us (1.033)
  the two profiles are of different devices: /device:TPU:6 before, /device:TPU:32 now
where the time goes in v4:
time: 125 us
  starting transfers between devices  41.1 us (33%)
  blocking collectives  39.9 us (32%)
  waiting for transfers between devices  34.2 us (27%)
  Pallas kernels  7.27 us (6%)
  local copies, waits for them, and re-layouts  1.77 us (1%)
    all_to_all x1, blocking collectives, on_device(): lax.all_to_all(chunks, 'layer', 0, 0, tiled=True, axis_index_groups=groups)  39.9 us
    ppermute x4, starting transfers between devices, pass_on(): return lax.ppermute(value, ('layer', 'row'), pairs)  18.6 us
    ppermute x4, waiting for transfers between devices, fetch(): return lax.ppermute(value, ('row', 'col'), pairs)  16.4 us
    ppermute x4, waiting for transfers between devices, pass_on(): return lax.ppermute(value, ('layer', 'row'), pairs)  16 us
    ppermute x4, starting transfers between devices, fetch(): return lax.ppermute(value, ('row', 'col'), pairs)  14.4 us
    ppermute x4, starting transfers between devices, swap(): return lax.ppermute(value, 'row', [(i, i ^ 1) for i in range(N_ROW)])  8.17 us
    pallas_call x9, Pallas kernels, call(): pl.pallas_call(kernel, out_shape=tuple((jax.ShapeDtypeStruct(s, d) for s,...  7.27 us
  transfers between devices with their start and end apart: 12, of which 8 were waited for; matrix products, arithmetic and copies ran while one was open for 0% of the time, Pallas kernels for 3%

profile of v4, /device:TPU:32, one launch (start us, length us, event | category | flops | bytes accessed | tf_op | source)
XLA Modules:
  0.0 124.5 jit_solution(11136192098606771510)
XLA Ops:
  0.0 1.0 copy-done
  1.0 0.7 copy-done.1
  2.3 1.9 %collective-permute-start = (f32[1024,128]{1,0:T(8,128)S(1)}, f32[1024,128]{1,0:T(8,128)S(1)}, u32[]{:S(2)}, u32[]{:S(2)}) collective-permute-start(f32[1024,128]{1,0:T(8,128)S(1)} %shard_map.28.own), channel_id=1, source_target_pairs={{0,4},{4,0},{8,12},{12,8},{16,20},{20,16},{24,28},{28,24},{1,5},{5... | collective-permute-start | bytes 1572872 | tf_op jit(solution)/shard_map/ppermute | solution.py:184
  4.2 1.9 %collective-permute-done.other = f32[1024,128]{1,0:T(8,128)S(1)} collective-permute-done((f32[1024,128]{1,0:T(8,128)S(1)}, f32[1024,128]{1,0:T(8,128)S(1)}, u32[]{:S(2)}, u32[]{:S(2)}) %collective-permute-start) | collective-permute-done | bytes 524320 | tf_op jit(solution)/shard_map/ppermute | solution.py:184
  6.2 4.9 %collective-permute-start.1 = (f32[2048,128]{1,0:T(8,128)S(1)}, f32[2048,128]{1,0:T(8,128)S(1)}, u32[]{:S(2)}, u32[]{:S(2)}) collective-permute-start(f32[2048,128]{1,0:T(8,128)S(1)} %shard_map.29.p0), channel_id=1, source_target_pairs={{1,0},{12,4},{2,1},{13,5},{3,2},{14,6},{0,3},{15,7},{9,8},{20,12},... | collective-permute-start | bytes 3145736 | tf_op jit(solution)/shard_map/ppermute | solution.py:193
  11.1 1.9 %collective-permute-start.3 = (f32[2048,128]{1,0:T(8,128)S(1)}, f32[2048,128]{1,0:T(8,128)S(1)}, u32[]{:S(2)}, u32[]{:S(2)}) collective-permute-start(f32[2048,128]{1,0:T(8,128)S(1)} %shard_map.29.p0), channel_id=1, source_target_pairs={{3,0},{28,4},{0,1},{29,5},{1,2},{30,6},{2,3},{31,7},{11,8},{4,12},... | collective-permute-start | bytes 3145736 | tf_op jit(solution)/shard_map/ppermute | solution.py:193
  13.0 10.4 %collective-permute-done.1.p1 = f32[2048,128]{1,0:T(8,128)S(1)} collective-permute-done((f32[2048,128]{1,0:T(8,128)S(1)}, f32[2048,128]{1,0:T(8,128)S(1)}, u32[]{:S(2)}, u32[]{:S(2)}) %collective-permute-start.1) | collective-permute-done | bytes 1048608 | tf_op jit(solution)/shard_map/ppermute | solution.py:193
  23.4 5.6 %collective-permute-start.2 = (f32[1024,128]{1,0:T(8,128)S(1)}, f32[1024,128]{1,0:T(8,128)S(1)}, u32[]{:S(2)}, u32[]{:S(2)}) collective-permute-start(f32[1024,128]{1,0:T(8,128)S(1)} %slice.8), channel_id=1, source_target_pairs={{1,0},{12,4},{2,1},{13,5},{3,2},{14,6},{0,3},{15,7},{9,8},{20,12},... | collective-permute-start | bytes 1572872 | tf_op jit(solution)/shard_map/ppermute | solution.py:193
  29.1 1.9 %collective-permute-start.4 = (f32[1024,128]{1,0:T(8,128)S(1)}, f32[1024,128]{1,0:T(8,128)S(1)}, u32[]{:S(2)}, u32[]{:S(2)}) collective-permute-start(f32[1024,128]{1,0:T(8,128)S(1)} %slice.9), channel_id=1, source_target_pairs={{3,0},{28,4},{0,1},{29,5},{1,2},{30,6},{2,3},{31,7},{11,8},{4,12},... | collective-permute-start | bytes 1572872 | tf_op jit(solution)/shard_map/ppermute | solution.py:193
  31.0 1.9 %collective-permute-start.6 = (f32[2048,128]{1,0:T(8,128)S(1)}, f32[2048,128]{1,0:T(8,128)S(1)}, u32[]{:S(2)}, u32[]{:S(2)}) collective-permute-start(f32[2048,128]{1,0:T(8,128)S(1)} %collective-permute-done.1.p1), channel_id=1, source_target_pairs={{0,4},{4,0},{8,12},{12,8},{16,20},{20,16},{24,28},{28,24},{1,5},{5... | collective-permute-start | bytes 3145736 | tf_op jit(solution)/shard_map/ppermute | solution.py:184
  33.0 2.4 %collective-permute-start.7 = (f32[2048,128]{1,0:T(8,128)S(1)}, f32[2048,128]{1,0:T(8,128)S(1)}, u32[]{:S(2)}, u32[]{:S(2)}) collective-permute-start(f32[2048,128]{1,0:T(8,128)S(1)} %collective-permute-done.3.p3), channel_id=1, source_target_pairs={{0,4},{4,0},{8,12},{12,8},{16,20},{20,16},{24,28},{28,24},{1,5},{5... | collective-permute-start | bytes 3145736 | tf_op jit(solution)/shard_map/ppermute | solution.py:184
  35.7 5.7 %collective-permute-done.4.second = f32[1024,128]{1,0:T(8,128)S(1)} collective-permute-done((f32[1024,128]{1,0:T(8,128)S(1)}, f32[1024,128]{1,0:T(8,128)S(1)}, u32[]{:S(2)}, u32[]{:S(2)}) %collective-permute-start.4) | collective-permute-done | bytes 524320 | tf_op jit(solution)/shard_map/ppermute | solution.py:193
  41.5 1.9 %collective-permute-start.5 = (f32[2048,128]{1,0:T(8,128)S(1)}, f32[2048,128]{1,0:T(8,128)S(1)}, u32[]{:S(2)}, u32[]{:S(2)}) collective-permute-start(f32[2048,128]{1,0:T(8,128)S(1)} %shard_map.30.p2), channel_id=1, source_target_pairs={{0,4},{4,0},{8,12},{12,8},{16,20},{20,16},{24,28},{28,24},{1,5},{5... | collective-permute-start | bytes 3145736 | tf_op jit(solution)/shard_map/ppermute | solution.py:184
  43.4 3.4 %shard_map.31 = (bf16[384,1024]{1,0:T(8,128)(2,1)S(1)}, bf16[384,1024]{1,0:T(8,128)(2,1)S(1)}, bf16[1024,768]{1,0:T(8,128)(2,1)S(1)}, bf16[1024,768]{1,0:T(8,128)(2,1)S(1)}, f32[384,768]{1,0:T(8,128)S(1)}) custom-call(f32[2048,128]{1,0:T(8,128)S(1)} %shard_map.29.p0, f32[2048,128]{1,0:T(8,128)S(1)} %collective-permute-done.1.p1, ...), custom_call_target="tpu_custom_call" | custom-call | flops 1811939328 | bytes 8388608 | tf_op jit(solution)/shard_map/pallas_call | solution.py:25
  46.8 2.3 %shard_map.32 = (f32[256,512]{1,0:T(8,128)S(1)}, f32[256,512]{1,0:T(8,128)S(1)}, f32[256,512]{1,0:T(8,128)S(1)}, f32[256,512]{1,0:T(8,128)S(1)}) custom-call(f32[2048,128]{1,0:T(8,128)S(1)} %shard_map.30.p2, f32[2048,128]{1,0:T(8,128)S(1)} %collective-permute-done.5.s2, bf16[384,1024]{1,0:T(8,128)(2,1)S(1)} %get-tuple-element.18.left_high, ...), custom_call_target="tpu_custom_call" | custom-call | flops 1409286144 | bytes 8388608 | tf_op jit(solution)/shard_map/pallas_call | solution.py:25
  49.1 3.8 %collective-permute-start.10 = (f32[256,512]{1,0:T(8,128)S(1)}, f32[256,512]{1,0:T(8,128)S(1)}, u32[]{:S(2)}, u32[]{:S(2)}) collective-permute-start(f32[256,512]{1,0:T(8,128)S(1)} %get-tuple-element.28), channel_id=1, source_target_pairs={{0,32},{4,484},{8,40},{12,492},{16,48},{20,500},{24,56},{28,508},{... | collective-permute-start | bytes 1572872 | tf_op jit(solution)/shard_map/ppermute | solution.py:202
  53.0 3.8 %collective-permute-start.8 = (f32[256,512]{1,0:T(8,128)S(1)}, f32[256,512]{1,0:T(8,128)S(1)}, u32[]{:S(2)}, u32[]{:S(2)}) collective-permute-start(f32[256,512]{1,0:T(8,128)S(1)} %get-tuple-element.24), channel_id=1, source_target_pairs={{0,32},{4,484},{8,40},{12,492},{16,48},{20,500},{24,56},{28,508},{... | collective-permute-start | bytes 1572872 | tf_op jit(solution)/shard_map/ppermute | solution.py:202
  56.8 3.9 %collective-permute-done.10.came = f32[256,512]{1,0:T(8,128)S(1)} collective-permute-done((f32[256,512]{1,0:T(8,128)S(1)}, f32[256,512]{1,0:T(8,128)S(1)}, u32[]{:S(2)}, u32[]{:S(2)}) %collective-permute-start.10) | collective-permute-done | bytes 524320 | tf_op jit(solution)/shard_map/ppermute | solution.py:202
  60.7 5.4 %collective-permute-start.11 = (f32[128,512]{1,0:T(8,128)S(1)}, f32[128,512]{1,0:T(8,128)S(1)}, u32[]{:S(2)}, u32[]{:S(2)}) collective-permute-start(f32[128,512]{1,0:T(8,128)S(1)} %get-tuple-element.30), channel_id=1, source_target_pairs={{0,64},{4,452},{8,72},{12,460},{16,80},{20,468},{24,88},{28,476},{... | collective-permute-start | bytes 786440 | tf_op jit(solution)/shard_map/ppermute | solution.py:202
  66.3 5.6 %collective-permute-start.9 = (f32[128,512]{1,0:T(8,128)S(1)}, f32[128,512]{1,0:T(8,128)S(1)}, u32[]{:S(2)}, u32[]{:S(2)}) collective-permute-start(f32[128,512]{1,0:T(8,128)S(1)} %get-tuple-element.26), channel_id=1, source_target_pairs={{0,64},{4,452},{8,72},{12,460},{16,80},{20,468},{24,88},{28,476},{... | collective-permute-start | bytes 786440 | tf_op jit(solution)/shard_map/ppermute | solution.py:202
  71.9 5.8 %collective-permute-done.11.came_b = f32[128,512]{1,0:T(8,128)S(1)} collective-permute-done((f32[128,512]{1,0:T(8,128)S(1)}, f32[128,512]{1,0:T(8,128)S(1)}, u32[]{:S(2)}, u32[]{:S(2)}) %collective-permute-start.11) | collective-permute-done | bytes 262176 | tf_op jit(solution)/shard_map/ppermute | solution.py:202
  77.7 6.1 %collective-permute-done.9.came_a = f32[128,512]{1,0:T(8,128)S(1)} collective-permute-done((f32[128,512]{1,0:T(8,128)S(1)}, f32[128,512]{1,0:T(8,128)S(1)}, u32[]{:S(2)}, u32[]{:S(2)}) %collective-permute-start.9) | collective-permute-done | bytes 262176 | tf_op jit(solution)/shard_map/ppermute | solution.py:202
  83.9 39.9 %all_to_all.11 = f32[4,32,1024]{2,1,0:T(8,128)S(1)} all-to-all(f32[4,32,1024]{2,1,0:T(8,128)S(1)} %bitcast.3), channel_id=1, replica_groups={{0,128,256,384},{32,160,288,416},{64,192,320,448},{96,224,352,480},{1,1..., dimensions={0} | all-to-all | bytes 1048576 | tf_op jit(solution)/shard_map/all_to_all | solution.py:241
  123.8 0.7 shard_map.36
  (16 shorter events, 1.5 us)
Async XLA Ops:
  0.0 1.0 copy-start
  1.0 0.7 copy-start.1
  2.3 3.8 %collective-permute-start = (f32[1024,128]{1,0:T(8,128)S(1)}, f32[1024,128]{1,0:T(8,128)S(1)}, u32[]{:S(2)}, u32[]{:S(2)}) collective-permute-start(f32[1024,128]{1,0:T(8,128)S(1)} %shard_map.28.own), channel_id=1, source_target_pairs={{0,4},{4,0},{8,12},{12,8},{16,20},{20,16},{24,28},{28,24},{1,5},{5... | collective-permute-start | bytes 1572872 | tf_op jit(solution)/shard_map/ppermute | solution.py:184
  6.2 17.2 %collective-permute-start.1 = (f32[2048,128]{1,0:T(8,128)S(1)}, f32[2048,128]{1,0:T(8,128)S(1)}, u32[]{:S(2)}, u32[]{:S(2)}) collective-permute-start(f32[2048,128]{1,0:T(8,128)S(1)} %shard_map.29.p0), channel_id=1, source_target_pairs={{1,0},{12,4},{2,1},{13,5},{3,2},{14,6},{0,3},{15,7},{9,8},{20,12},... | collective-permute-start | bytes 3145736 | tf_op jit(solution)/shard_map/ppermute | solution.py:193
  11.1 17.9 %collective-permute-start.3 = (f32[2048,128]{1,0:T(8,128)S(1)}, f32[2048,128]{1,0:T(8,128)S(1)}, u32[]{:S(2)}, u32[]{:S(2)}) collective-permute-start(f32[2048,128]{1,0:T(8,128)S(1)} %shard_map.29.p0), channel_id=1, source_target_pairs={{3,0},{28,4},{0,1},{29,5},{1,2},{30,6},{2,3},{31,7},{11,8},{4,12},... | collective-permute-start | bytes 3145736 | tf_op jit(solution)/shard_map/ppermute | solution.py:193
  23.4 12.3 %collective-permute-start.2 = (f32[1024,128]{1,0:T(8,128)S(1)}, f32[1024,128]{1,0:T(8,128)S(1)}, u32[]{:S(2)}, u32[]{:S(2)}) collective-permute-start(f32[1024,128]{1,0:T(8,128)S(1)} %slice.8), channel_id=1, source_target_pairs={{1,0},{12,4},{2,1},{13,5},{3,2},{14,6},{0,3},{15,7},{9,8},{20,12},... | collective-permute-start | bytes 1572872 | tf_op jit(solution)/shard_map/ppermute | solution.py:193
  29.1 12.3 %collective-permute-start.4 = (f32[1024,128]{1,0:T(8,128)S(1)}, f32[1024,128]{1,0:T(8,128)S(1)}, u32[]{:S(2)}, u32[]{:S(2)}) collective-permute-start(f32[1024,128]{1,0:T(8,128)S(1)} %slice.9), channel_id=1, source_target_pairs={{3,0},{28,4},{0,1},{29,5},{1,2},{30,6},{2,3},{31,7},{11,8},{4,12},... | collective-permute-start | bytes 1572872 | tf_op jit(solution)/shard_map/ppermute | solution.py:193
  31.0 12.4 %collective-permute-start.6 = (f32[2048,128]{1,0:T(8,128)S(1)}, f32[2048,128]{1,0:T(8,128)S(1)}, u32[]{:S(2)}, u32[]{:S(2)}) collective-permute-start(f32[2048,128]{1,0:T(8,128)S(1)} %collective-permute-done.1.p1), channel_id=1, source_target_pairs={{0,4},{4,0},{8,12},{12,8},{16,20},{20,16},{24,28},{28,24},{1,5},{5... | collective-permute-start | bytes 3145736 | tf_op jit(solution)/shard_map/ppermute | solution.py:184
  33.0 10.4 %collective-permute-start.7 = (f32[2048,128]{1,0:T(8,128)S(1)}, f32[2048,128]{1,0:T(8,128)S(1)}, u32[]{:S(2)}, u32[]{:S(2)}) collective-permute-start(f32[2048,128]{1,0:T(8,128)S(1)} %collective-permute-done.3.p3), channel_id=1, source_target_pairs={{0,4},{4,0},{8,12},{12,8},{16,20},{20,16},{24,28},{28,24},{1,5},{5... | collective-permute-start | bytes 3145736 | tf_op jit(solution)/shard_map/ppermute | solution.py:184
  41.5 5.3 %collective-permute-start.5 = (f32[2048,128]{1,0:T(8,128)S(1)}, f32[2048,128]{1,0:T(8,128)S(1)}, u32[]{:S(2)}, u32[]{:S(2)}) collective-permute-start(f32[2048,128]{1,0:T(8,128)S(1)} %shard_map.30.p2), channel_id=1, source_target_pairs={{0,4},{4,0},{8,12},{12,8},{16,20},{20,16},{24,28},{28,24},{1,5},{5... | collective-permute-start | bytes 3145736 | tf_op jit(solution)/shard_map/ppermute | solution.py:184
  49.1 11.5 %collective-permute-start.10 = (f32[256,512]{1,0:T(8,128)S(1)}, f32[256,512]{1,0:T(8,128)S(1)}, u32[]{:S(2)}, u32[]{:S(2)}) collective-permute-start(f32[256,512]{1,0:T(8,128)S(1)} %get-tuple-element.28), channel_id=1, source_target_pairs={{0,32},{4,484},{8,40},{12,492},{16,48},{20,500},{24,56},{28,508},{... | collective-permute-start | bytes 1572872 | tf_op jit(solution)/shard_map/ppermute | solution.py:202
  53.0 13.3 %collective-permute-start.8 = (f32[256,512]{1,0:T(8,128)S(1)}, f32[256,512]{1,0:T(8,128)S(1)}, u32[]{:S(2)}, u32[]{:S(2)}) collective-permute-start(f32[256,512]{1,0:T(8,128)S(1)} %get-tuple-element.24), channel_id=1, source_target_pairs={{0,32},{4,484},{8,40},{12,492},{16,48},{20,500},{24,56},{28,508},{... | collective-permute-start | bytes 1572872 | tf_op jit(solution)/shard_map/ppermute | solution.py:202
  60.7 17.0 %collective-permute-start.11 = (f32[128,512]{1,0:T(8,128)S(1)}, f32[128,512]{1,0:T(8,128)S(1)}, u32[]{:S(2)}, u32[]{:S(2)}) collective-permute-start(f32[128,512]{1,0:T(8,128)S(1)} %get-tuple-element.30), channel_id=1, source_target_pairs={{0,64},{4,452},{8,72},{12,460},{16,80},{20,468},{24,88},{28,476},{... | collective-permute-start | bytes 786440 | tf_op jit(solution)/shard_map/ppermute | solution.py:202
  66.3 17.5 %collective-permute-start.9 = (f32[128,512]{1,0:T(8,128)S(1)}, f32[128,512]{1,0:T(8,128)S(1)}, u32[]{:S(2)}, u32[]{:S(2)}) collective-permute-start(f32[128,512]{1,0:T(8,128)S(1)} %get-tuple-element.26), channel_id=1, source_target_pairs={{0,64},{4,452},{8,72},{12,460},{16,80},{20,468},{24,88},{28,476},{... | collective-permute-start | bytes 786440 | tf_op jit(solution)/shard_map/ppermute | solution.py:202

commit v5 on v2

--- a/solution.py
+++ b/solution.py
@@ -43,11 +43,10 @@
     return lax.rem(lax.axis_index("row"), 2)
 
 
-def pair_kernel(own, other, pair):
-    inner = own.shape[0]
-    k = core()
-    pair[pl.ds(pl.multiple_of(k * inner, inner), inner), :] = own[...]
-    pair[pl.ds(pl.multiple_of((1 - k) * inner, inner), inner), :] = other[...]
+def join_kernel(first, second, pair):
+    inner = first.shape[0]
+    pair[:inner, :] = first[...]
+    pair[inner:, :] = second[...]
 
 
 def split(value):
@@ -63,49 +62,48 @@
     return dot(left_high, right_high) + (dot(left_high, right_low) + dot(left_low, right_high))
 
 
-def place(pair, swapped, along_y, along_x):
-    k = core()
-
-    @pl.when(k == 0)
+def take_left(index, block, left_high, left_low):
+    rows = pl.ds(index * TILE, TILE)
+    high, low = split(block[...].T)
+    left_high[rows, :] = high
+    left_low[rows, :] = low
+
+
+def take_right(index, parity, block, right_high, right_low):
+    start = 2 * index * TILE + parity * TILE
+    columns = pl.ds(start if isinstance(start, int) else pl.multiple_of(start, TILE), TILE)
+    high, low = split(block[...])
+    right_high[:, columns] = high
+    right_low[:, columns] = low
+
+
+def place(index, first, second, first_swapped, second_swapped, left, right):
+    @pl.when(core() == 0)
     def _():
-        along_y(pair)
-        along_x(swapped)
-
-    @pl.when(k == 1)
+        take_left(index, first, *left)
+        take_right(index, 0, second_swapped, *right)
+        take_right(index, 1, first_swapped, *right)
+
+    @pl.when(core() == 1)
     def _():
-        along_y(swapped)
-        along_x(pair)
-
-
-def take_left(index, left_high, left_low):
-    def write(pair):
-        inner = pair.shape[0] // 2
-        block = pair[pl.ds(pl.multiple_of(core() * inner, inner), inner), :]
-        rows = pl.ds(index * TILE, TILE)
-        high, low = split(block.T)
-        left_high[rows, :] = high
-        left_low[rows, :] = low
-
-    return write
-
-
-def take_right(index, right_high, right_low):
-    def write(pair):
-        inner = pair.shape[0] // 2
-        for k in range(2):
-            columns = pl.ds((2 * index + k) * TILE, TILE)
-            high, low = split(pair[pl.ds(k * inner, inner), :])
-            right_high[:, columns] = high
-            right_low[:, columns] = low
-
-    return write
-
-
-def first_product_kernel(p0, p1, s1, p3, s3, left_high, left_low, right_high, right_low, total):
-    take_left(0, left_high, left_low)(p0)
-    take_right(0, right_high, right_low)(p0)
-    for index, pair, swapped in ((1, p1, s1), (2, p3, s3)):
-        place(pair, swapped, take_left(index, left_high, left_low), take_right(index, right_high, right_low))
+        take_left(index, second_swapped, *left)
+        take_right(index, 0, second, *right)
+        take_right(index, 1, first, *right)
+
+
+def halves(pair):
+    inner = pair.shape[0] // 2
+    return pair.at[pl.ds(0, inner), :], pair.at[pl.ds(inner, inner), :]
+
+
+def first_product_kernel(own, other, o1, s1, o3, s3, oo, ss, left_high, left_low, right_high, right_low, total):
+    left, right = (left_high, left_low), (right_high, right_low)
+    take_left(0, own, *left)
+    take_right(0, core(), own, *right)
+    take_right(0, 1 - core(), other, *right)
+    (o1_swapped, o3_swapped), (s1_swapped, s3_swapped) = halves(oo), halves(ss)
+    place(1, o1, s1, o1_swapped, s1_swapped, left, right)
+    place(2, o3, s3, o3_swapped, s3_swapped, left, right)
     for index in range(3):
         columns = pl.ds(index * 2 * TILE, 2 * TILE)
         total[:, columns] = product(left_high[...], left_low[...], right_high[:, columns], right_low[:, columns])
@@ -119,11 +117,11 @@
     return pl.ds(pl.multiple_of(index * SUB, SUB), SUB)
 
 
-def second_product_kernel(p2, s2, left_high, left_low, right_high, right_low, part, *refs):
+def second_product_kernel(o2, s2, both, left_high, left_low, right_high, right_low, part, *refs):
     sends, keeps = refs[0:2], refs[2:4]
     last_high, last_low, far_high, far_low, total = refs[4:]
     z, y = lax.axis_index("layer"), lax.axis_index("col")
-    place(p2, s2, take_left(0, last_high, last_low), take_right(0, far_high, far_low))
+    place(0, o2, s2, *halves(both), (last_high, last_low), (far_high, far_low))
     known = part.shape[0]
     total[:known, : part.shape[1]] = part[...]
     total[known:, : part.shape[1]] = product(last_high[...], last_low[...], right_high[...], right_low[...])
@@ -190,14 +188,19 @@
 def on_device(graph, pattern):
     inner = graph.shape[0]
     (masked,) = call(mask_kernel, [(inner, TILE)], (graph, pattern.reshape(-1)), [VMEM, SMEM])
-    (pair,) = call(pair_kernel, [(2 * inner, TILE)], (masked, swap(masked)))
-    came = {t: fetch(pair, t) for t in (1, 3, 2)}
-    swapped = {t: swap(came[t]) for t in (1, 3, 2)}
+    other = swap(masked)
+    o1, o3 = fetch(masked, 1), fetch(masked, 3)
+    s3, s1 = fetch(other, 3), fetch(other, 1)
+    o2, s2 = fetch(o1, 1), fetch(s3, 3)
+
+    def swap_two(first, second):
+        return swap(call(join_kernel, [(2 * inner, TILE)], (first, second))[0])
+
     known, wide = 3 * TILE, 6 * TILE
     parts = call(
         first_product_kernel,
         [((known, inner), BF16)] * 2 + [((inner, wide), BF16)] * 2 + [(known, wide)],
-        (pair, came[1], swapped[1], came[3], swapped[3]),
+        (masked, other, o1, s1, o3, s3, swap_two(o1, o3), swap_two(s1, s3)),
         flops=6 * known * wide * inner,
         nbytes=8 << 20,
     )
@@ -205,7 +208,7 @@
     made = call(
         second_product_kernel,
         [(8 * SUB, 4 * TILE)] * 4,
-        (came[2], swapped[2], *parts),
+        (o2, s2, swap_two(o2, s2), *parts),
         scratch=split_scratch + [pltpu.VMEM((4 * TILE, 8 * TILE), F32)],
         flops=6 * 7 * TILE * 2 * TILE * inner,
         nbytes=8 << 20,

time: 121 us -> 113 us (0.934)
  waiting for transfers between devices: 57.7 us -> 40.3 us
  starting transfers between devices: 54.1 us -> 62.9 us
    ppermute x3 -> x6, waiting for transfers between devices: 21.2 us -> 5.85 us  [fetch(): return lax.ppermute(value, ('row', 'col'), pairs)]
    ppermute x3 -> x6, starting transfers between devices: 10.9 us -> 19.7 us  [fetch(): return lax.ppermute(value, ('row', 'col'), pairs)]
    ppermute x4, waiting for transfers between devices: 2.07 us -> 0.01 us  [swap(): return lax.ppermute(value, 'row', [(i, i ^ 1) for i in range(N_ROW)])]
    pallas_call x11 -> x13, Pallas kernels: 7.24 us -> 7.4 us  [call(): pl.pallas_call(kernel, out_shape=tuple((jax.ShapeDtypeStruct(s, d) for s,...]
  transfers between devices with their start and end apart: 15 -> 18, of which waited for: 11 -> 9; matrix products, arithmetic and copies ran while one was open for 0% -> 0% of each run, Pallas kernels for 3% -> 3%
where the time goes in v5:
time: 113 us
  starting transfers between devices  62.9 us (56%)
  waiting for transfers between devices  40.3 us (36%)
  Pallas kernels  7.4 us (7%)
  local copies, waits for them, and re-layouts  1.7 us (2%)
    ppermute x8, starting transfers between devices, pass_on(): return lax.ppermute(value, ('layer', 'row'), pairs)  34.9 us
    ppermute x8, waiting for transfers between devices, pass_on(): return lax.ppermute(value, ('layer', 'row'), pairs)  34.4 us
    ppermute x6, starting transfers between devices, fetch(): return lax.ppermute(value, ('row', 'col'), pairs)  19.7 us
    ppermute x4, starting transfers between devices, swap(): return lax.ppermute(value, 'row', [(i, i ^ 1) for i in range(N_ROW)])  8.27 us
    pallas_call x13, Pallas kernels, call(): pl.pallas_call(kernel, out_shape=tuple((jax.ShapeDtypeStruct(s, d) for s,...  7.4 us
    ppermute x6, waiting for transfers between devices, fetch(): return lax.ppermute(value, ('row', 'col'), pairs)  5.85 us
  transfers between devices with their start and end apart: 18, of which 9 were waited for; matrix products, arithmetic and copies ran while one was open for 0% of the time, Pallas kernels for 3%

profile of v5, /device:TPU:6, one launch (start us, length us, event | category | flops | bytes accessed | tf_op | source)
XLA Modules:
  0.0 112.5 jit_solution(9580455034450803736)
XLA Ops:
  2.3 1.9 %collective-permute-start.2 = (f32[1024,128]{1,0:T(8,128)S(1)}, f32[1024,128]{1,0:T(8,128)S(1)}, u32[]{:S(2)}, u32[]{:S(2)}) collective-permute-start(f32[1024,128]{1,0:T(8,128)S(1)} %shard_map.28.own), channel_id=1, source_target_pairs={{0,4},{4,0},{8,12},{12,8},{16,20},{20,16},{24,28},{28,24},{1,5},{5... | collective-permute-start | bytes 1572872 | tf_op jit(solution)/shard_map/ppermute | solution.py:167
  4.2 4.9 %collective-permute-start = (f32[1024,128]{1,0:T(8,128)S(1)}, f32[1024,128]{1,0:T(8,128)S(1)}, u32[]{:S(2)}, u32[]{:S(2)}) collective-permute-start(f32[1024,128]{1,0:T(8,128)S(1)} %shard_map.28.own), channel_id=1, source_target_pairs={{1,0},{12,4},{2,1},{13,5},{3,2},{14,6},{0,3},{15,7},{9,8},{20,12},... | collective-permute-start | bytes 1572872 | tf_op jit(solution)/shard_map/ppermute | solution.py:176
  9.2 1.9 %collective-permute-start.3 = (f32[1024,128]{1,0:T(8,128)S(1)}, f32[1024,128]{1,0:T(8,128)S(1)}, u32[]{:S(2)}, u32[]{:S(2)}) collective-permute-start(f32[1024,128]{1,0:T(8,128)S(1)} %collective-permute-done.2.other), channel_id=1, source_target_pairs={{3,0},{28,4},{0,1},{29,5},{1,2},{30,6},{2,3},{31,7},{11,8},{4,12},... | collective-permute-start | bytes 1572872 | tf_op jit(solution)/shard_map/ppermute | solution.py:176
  11.1 2.5 %collective-permute-start.7 = (f32[1024,128]{1,0:T(8,128)S(1)}, f32[1024,128]{1,0:T(8,128)S(1)}, u32[]{:S(2)}, u32[]{:S(2)}) collective-permute-start(f32[1024,128]{1,0:T(8,128)S(1)} %shard_map.28.own), channel_id=1, source_target_pairs={{3,0},{28,4},{0,1},{29,5},{1,2},{30,6},{2,3},{31,7},{11,8},{4,12},... | collective-permute-start | bytes 1572872 | tf_op jit(solution)/shard_map/ppermute | solution.py:176
  13.6 4.6 %collective-permute-start.6 = (f32[1024,128]{1,0:T(8,128)S(1)}, f32[1024,128]{1,0:T(8,128)S(1)}, u32[]{:S(2)}, u32[]{:S(2)}) collective-permute-start(f32[1024,128]{1,0:T(8,128)S(1)} %collective-permute-done.2.other), channel_id=1, source_target_pairs={{1,0},{12,4},{2,1},{13,5},{3,2},{14,6},{0,3},{15,7},{9,8},{20,12},... | collective-permute-start | bytes 1572872 | tf_op jit(solution)/shard_map/ppermute | solution.py:176
  18.2 3.9 %collective-permute-start.1 = (f32[1024,128]{1,0:T(8,128)S(1)}, f32[1024,128]{1,0:T(8,128)S(1)}, u32[]{:S(2)}, u32[]{:S(2)}) collective-permute-start(f32[1024,128]{1,0:T(8,128)S(1)} %collective-permute-done.first.o1), channel_id=1, source_target_pairs={{1,0},{12,4},{2,1},{13,5},{3,2},{14,6},{0,3},{15,7},{9,8},{20,12},... | collective-permute-start | bytes 1572872 | tf_op jit(solution)/shard_map/ppermute | solution.py:176
  24.0 3.0 %collective-permute-done.7.second.o3 = f32[1024,128]{1,0:T(8,128)S(1)} collective-permute-done((f32[1024,128]{1,0:T(8,128)S(1)}, f32[1024,128]{1,0:T(8,128)S(1)}, u32[]{:S(2)}, u32[]{:S(2)}) %collective-permute-start.7) | collective-permute-done | bytes 524320 | tf_op jit(solution)/shard_map/ppermute | solution.py:176
  29.1 2.4 %collective-permute-start.9 = (f32[2048,128]{1,0:T(8,128)S(1)}, f32[2048,128]{1,0:T(8,128)S(1)}, u32[]{:S(2)}, u32[]{:S(2)}) collective-permute-start(f32[2048,128]{1,0:T(8,128)S(1)} %shard_map.31), channel_id=1, source_target_pairs={{0,4},{4,0},{8,12},{12,8},{16,20},{20,16},{24,28},{28,24},{1,5},{5... | collective-permute-start | bytes 3145736 | tf_op jit(solution)/shard_map/ppermute | solution.py:167
  31.6 2.8 %collective-permute-done.4.second.s2 = f32[1024,128]{1,0:T(8,128)S(1)} collective-permute-done((f32[1024,128]{1,0:T(8,128)S(1)}, f32[1024,128]{1,0:T(8,128)S(1)}, u32[]{:S(2)}, u32[]{:S(2)}) %collective-permute-start.4) | collective-permute-done | bytes 524320 | tf_op jit(solution)/shard_map/ppermute | solution.py:176
  34.5 2.0 %collective-permute-start.5 = (f32[2048,128]{1,0:T(8,128)S(1)}, f32[2048,128]{1,0:T(8,128)S(1)}, u32[]{:S(2)}, u32[]{:S(2)}) collective-permute-start(f32[2048,128]{1,0:T(8,128)S(1)} %shard_map.29), channel_id=1, source_target_pairs={{0,4},{4,0},{8,12},{12,8},{16,20},{20,16},{24,28},{28,24},{1,5},{5... | collective-permute-start | bytes 3145736 | tf_op jit(solution)/shard_map/ppermute | solution.py:167
  36.5 3.4 %shard_map.32 = (bf16[384,1024]{1,0:T(8,128)(2,1)S(1)}, bf16[384,1024]{1,0:T(8,128)(2,1)S(1)}, bf16[1024,768]{1,0:T(8,128)(2,1)S(1)}, bf16[1024,768]{1,0:T(8,128)(2,1)S(1)}, f32[384,768]{1,0:T(8,128)S(1)}) custom-call(f32[1024,128]{1,0:T(8,128)S(1)} %shard_map.28.own, f32[1024,128]{1,0:T(8,128)S(1)} %collective-permute-done.2.other, ...), custom_call_target="tpu_custom_call" | custom-call | flops 1811939328 | bytes 8388608 | tf_op jit(solution)/shard_map/pallas_call | solution.py:25
  39.9 2.3 %shard_map.33 = (f32[256,512]{1,0:T(8,128)S(1)}, f32[256,512]{1,0:T(8,128)S(1)}, f32[256,512]{1,0:T(8,128)S(1)}, f32[256,512]{1,0:T(8,128)S(1)}) custom-call(f32[1024,128]{1,0:T(8,128)S(1)} %collective-permute-done.1.first.o2, f32[1024,128]{1,0:T(8,128)S(1)} %collective-permute-done.4.second.s2, f32[2048,128]{1,0:T(8,128)S(1)} %collective-permute-done.5.both, ...), custom_call_target="tpu_custom_call" | custom-call | flops 1409286144 | bytes 8388608 | tf_op jit(solution)/shard_map/pallas_call | solution.py:25
  42.3 3.7 %collective-permute-start.14 = (f32[256,512]{1,0:T(8,128)S(1)}, f32[256,512]{1,0:T(8,128)S(1)}, u32[]{:S(2)}, u32[]{:S(2)}) collective-permute-start(f32[256,512]{1,0:T(8,128)S(1)} %get-tuple-element.40), channel_id=1, source_target_pairs={{0,32},{4,484},{8,40},{12,492},{16,48},{20,500},{24,56},{28,508},{... | collective-permute-start | bytes 1572872 | tf_op jit(solution)/shard_map/ppermute | solution.py:185
  46.0 3.8 %collective-permute-start.10 = (f32[256,512]{1,0:T(8,128)S(1)}, f32[256,512]{1,0:T(8,128)S(1)}, u32[]{:S(2)}, u32[]{:S(2)}) collective-permute-start(f32[256,512]{1,0:T(8,128)S(1)} %get-tuple-element.32), channel_id=1, source_target_pairs={{0,32},{4,484},{8,40},{12,492},{16,48},{20,500},{24,56},{28,508},{... | collective-permute-start | bytes 1572872 | tf_op jit(solution)/shard_map/ppermute | solution.py:185
  49.8 10.9 %collective-permute-done.14.came = f32[256,512]{1,0:T(8,128)S(1)} collective-permute-done((f32[256,512]{1,0:T(8,128)S(1)}, f32[256,512]{1,0:T(8,128)S(1)}, u32[]{:S(2)}, u32[]{:S(2)}) %collective-permute-start.14) | collective-permute-done | bytes 524320 | tf_op jit(solution)/shard_map/ppermute | solution.py:185
  62.7 3.6 %collective-permute-done.10.came = f32[256,512]{1,0:T(8,128)S(1)} collective-permute-done((f32[256,512]{1,0:T(8,128)S(1)}, f32[256,512]{1,0:T(8,128)S(1)}, u32[]{:S(2)}, u32[]{:S(2)}) %collective-permute-start.10) | collective-permute-done | bytes 524320 | tf_op jit(solution)/shard_map/ppermute | solution.py:185
  68.3 5.2 %collective-permute-done.15.came = f32[128,512]{1,0:T(8,128)S(1)} collective-permute-done((f32[128,512]{1,0:T(8,128)S(1)}, f32[128,512]{1,0:T(8,128)S(1)}, u32[]{:S(2)}, u32[]{:S(2)}) %collective-permute-start.15) | collective-permute-done | bytes 262176 | tf_op jit(solution)/shard_map/ppermute | solution.py:185
  73.6 1.9 %collective-permute-start.16 = (f32[64,512]{1,0:T(8,128)S(1)}, f32[64,512]{1,0:T(8,128)S(1)}, u32[]{:S(2)}, u32[]{:S(2)}) collective-permute-start(f32[64,512]{1,0:T(8,128)S(1)} %get-tuple-element.44), channel_id=1, source_target_pairs={{0,128},{4,388},{8,136},{12,396},{16,144},{20,404},{24,152},{28,41... | collective-permute-start | bytes 393224 | tf_op jit(solution)/shard_map/ppermute | solution.py:185
  75.5 3.6 %collective-permute-done.11.came = f32[128,512]{1,0:T(8,128)S(1)} collective-permute-done((f32[128,512]{1,0:T(8,128)S(1)}, f32[128,512]{1,0:T(8,128)S(1)}, u32[]{:S(2)}, u32[]{:S(2)}) %collective-permute-start.11) | collective-permute-done | bytes 262176 | tf_op jit(solution)/shard_map/ppermute | solution.py:185
  79.1 7.0 %collective-permute-start.12 = (f32[64,512]{1,0:T(8,128)S(1)}, f32[64,512]{1,0:T(8,128)S(1)}, u32[]{:S(2)}, u32[]{:S(2)}) collective-permute-start(f32[64,512]{1,0:T(8,128)S(1)} %get-tuple-element.36), channel_id=1, source_target_pairs={{0,128},{4,388},{8,136},{12,396},{16,144},{20,404},{24,152},{28,41... | collective-permute-start | bytes 393224 | tf_op jit(solution)/shard_map/ppermute | solution.py:185
  86.1 3.2 %collective-permute-done.16.came = f32[64,512]{1,0:T(8,128)S(1)} collective-permute-done((f32[64,512]{1,0:T(8,128)S(1)}, f32[64,512]{1,0:T(8,128)S(1)}, u32[]{:S(2)}, u32[]{:S(2)}) %collective-permute-start.16) | collective-permute-done | bytes 131104 | tf_op jit(solution)/shard_map/ppermute | solution.py:185
  89.4 7.5 %collective-permute-start.17 = (f32[32,512]{1,0:T(8,128)S(1)}, f32[32,512]{1,0:T(8,128)S(1)}, u32[]{:S(2)}, u32[]{:S(2)}) collective-permute-start(f32[32,512]{1,0:T(8,128)S(1)} %get-tuple-element.46), channel_id=1, source_target_pairs={{0,256},{4,260},{8,264},{12,268},{16,272},{20,276},{24,280},{28,28... | collective-permute-start | bytes 196616 | tf_op jit(solution)/shard_map/ppermute | solution.py:185
  96.9 7.1 %collective-permute-start.13 = (f32[32,512]{1,0:T(8,128)S(1)}, f32[32,512]{1,0:T(8,128)S(1)}, u32[]{:S(2)}, u32[]{:S(2)}) collective-permute-start(f32[32,512]{1,0:T(8,128)S(1)} %get-tuple-element.38), channel_id=1, source_target_pairs={{0,256},{4,260},{8,264},{12,268},{16,272},{20,276},{24,280},{28,28... | collective-permute-start | bytes 196616 | tf_op jit(solution)/shard_map/ppermute | solution.py:185
  104.2 7.6 %collective-permute-done.13.came_a = f32[32,512]{1,0:T(8,128)S(1)} collective-permute-done((f32[32,512]{1,0:T(8,128)S(1)}, f32[32,512]{1,0:T(8,128)S(1)}, u32[]{:S(2)}, u32[]{:S(2)}) %collective-permute-start.13) | collective-permute-done | bytes 65568 | tf_op jit(solution)/shard_map/ppermute | solution.py:185
  (29 shorter events, 11.3 us)
Async XLA Ops:
  0.0 1.0 copy-start
  1.0 0.7 copy-start.1
  2.3 6.9 %collective-permute-start.2 = (f32[1024,128]{1,0:T(8,128)S(1)}, f32[1024,128]{1,0:T(8,128)S(1)}, u32[]{:S(2)}, u32[]{:S(2)}) collective-permute-start(f32[1024,128]{1,0:T(8,128)S(1)} %shard_map.28.own), channel_id=1, source_target_pairs={{0,4},{4,0},{8,12},{12,8},{16,20},{20,16},{24,28},{28,24},{1,5},{5... | collective-permute-start | bytes 1572872 | tf_op jit(solution)/shard_map/ppermute | solution.py:167
  4.2 13.9 %collective-permute-start = (f32[1024,128]{1,0:T(8,128)S(1)}, f32[1024,128]{1,0:T(8,128)S(1)}, u32[]{:S(2)}, u32[]{:S(2)}) collective-permute-start(f32[1024,128]{1,0:T(8,128)S(1)} %shard_map.28.own), channel_id=1, source_target_pairs={{1,0},{12,4},{2,1},{13,5},{3,2},{14,6},{0,3},{15,7},{9,8},{20,12},... | collective-permute-start | bytes 1572872 | tf_op jit(solution)/shard_map/ppermute | solution.py:176
  9.2 12.9 %collective-permute-start.3 = (f32[1024,128]{1,0:T(8,128)S(1)}, f32[1024,128]{1,0:T(8,128)S(1)}, u32[]{:S(2)}, u32[]{:S(2)}) collective-permute-start(f32[1024,128]{1,0:T(8,128)S(1)} %collective-permute-done.2.other), channel_id=1, source_target_pairs={{3,0},{28,4},{0,1},{29,5},{1,2},{30,6},{2,3},{31,7},{11,8},{4,12},... | collective-permute-start | bytes 1572872 | tf_op jit(solution)/shard_map/ppermute | solution.py:176
  11.1 16.0 %collective-permute-start.7 = (f32[1024,128]{1,0:T(8,128)S(1)}, f32[1024,128]{1,0:T(8,128)S(1)}, u32[]{:S(2)}, u32[]{:S(2)}) collective-permute-start(f32[1024,128]{1,0:T(8,128)S(1)} %shard_map.28.own), channel_id=1, source_target_pairs={{3,0},{28,4},{0,1},{29,5},{1,2},{30,6},{2,3},{31,7},{11,8},{4,12},... | collective-permute-start | bytes 1572872 | tf_op jit(solution)/shard_map/ppermute | solution.py:176
  13.6 15.5 %collective-permute-start.6 = (f32[1024,128]{1,0:T(8,128)S(1)}, f32[1024,128]{1,0:T(8,128)S(1)}, u32[]{:S(2)}, u32[]{:S(2)}) collective-permute-start(f32[1024,128]{1,0:T(8,128)S(1)} %collective-permute-done.2.other), channel_id=1, source_target_pairs={{1,0},{12,4},{2,1},{13,5},{3,2},{14,6},{0,3},{15,7},{9,8},{20,12},... | collective-permute-start | bytes 1572872 | tf_op jit(solution)/shard_map/ppermute | solution.py:176
  18.2 13.4 %collective-permute-start.1 = (f32[1024,128]{1,0:T(8,128)S(1)}, f32[1024,128]{1,0:T(8,128)S(1)}, u32[]{:S(2)}, u32[]{:S(2)}) collective-permute-start(f32[1024,128]{1,0:T(8,128)S(1)} %collective-permute-done.first.o1), channel_id=1, source_target_pairs={{1,0},{12,4},{2,1},{13,5},{3,2},{14,6},{0,3},{15,7},{9,8},{20,12},... | collective-permute-start | bytes 1572872 | tf_op jit(solution)/shard_map/ppermute | solution.py:176
  22.1 12.3 %collective-permute-start.4 = (f32[1024,128]{1,0:T(8,128)S(1)}, f32[1024,128]{1,0:T(8,128)S(1)}, u32[]{:S(2)}, u32[]{:S(2)}) collective-permute-start(f32[1024,128]{1,0:T(8,128)S(1)} %collective-permute-done.3.second.s3), channel_id=1, source_target_pairs={{3,0},{28,4},{0,1},{29,5},{1,2},{30,6},{2,3},{31,7},{11,8},{4,12},... | collective-permute-start | bytes 1572872 | tf_op jit(solution)/shard_map/ppermute | solution.py:176
  27.1 9.4 %collective-permute-start.8 = (f32[2048,128]{1,0:T(8,128)S(1)}, f32[2048,128]{1,0:T(8,128)S(1)}, u32[]{:S(2)}, u32[]{:S(2)}) collective-permute-start(f32[2048,128]{1,0:T(8,128)S(1)} %shard_map.30), channel_id=1, source_target_pairs={{0,4},{4,0},{8,12},{12,8},{16,20},{20,16},{24,28},{28,24},{1,5},{5... | collective-permute-start | bytes 3145736 | tf_op jit(solution)/shard_map/ppermute | solution.py:167
  29.1 7.4 %collective-permute-start.9 = (f32[2048,128]{1,0:T(8,128)S(1)}, f32[2048,128]{1,0:T(8,128)S(1)}, u32[]{:S(2)}, u32[]{:S(2)}) collective-permute-start(f32[2048,128]{1,0:T(8,128)S(1)} %shard_map.31), channel_id=1, source_target_pairs={{0,4},{4,0},{8,12},{12,8},{16,20},{20,16},{24,28},{28,24},{1,5},{5... | collective-permute-start | bytes 3145736 | tf_op jit(solution)/shard_map/ppermute | solution.py:167
  34.5 5.5 %collective-permute-start.5 = (f32[2048,128]{1,0:T(8,128)S(1)}, f32[2048,128]{1,0:T(8,128)S(1)}, u32[]{:S(2)}, u32[]{:S(2)}) collective-permute-start(f32[2048,128]{1,0:T(8,128)S(1)} %shard_map.29), channel_id=1, source_target_pairs={{0,4},{4,0},{8,12},{12,8},{16,20},{20,16},{24,28},{28,24},{1,5},{5... | collective-permute-start | bytes 3145736 | tf_op jit(solution)/shard_map/ppermute | solution.py:167
  42.3 18.5 %collective-permute-start.14 = (f32[256,512]{1,0:T(8,128)S(1)}, f32[256,512]{1,0:T(8,128)S(1)}, u32[]{:S(2)}, u32[]{:S(2)}) collective-permute-start(f32[256,512]{1,0:T(8,128)S(1)} %get-tuple-element.40), channel_id=1, source_target_pairs={{0,32},{4,484},{8,40},{12,492},{16,48},{20,500},{24,56},{28,508},{... | collective-permute-start | bytes 1572872 | tf_op jit(solution)/shard_map/ppermute | solution.py:185
  46.0 20.3 %collective-permute-start.10 = (f32[256,512]{1,0:T(8,128)S(1)}, f32[256,512]{1,0:T(8,128)S(1)}, u32[]{:S(2)}, u32[]{:S(2)}) collective-permute-start(f32[256,512]{1,0:T(8,128)S(1)} %get-tuple-element.32), channel_id=1, source_target_pairs={{0,32},{4,484},{8,40},{12,492},{16,48},{20,500},{24,56},{28,508},{... | collective-permute-start | bytes 1572872 | tf_op jit(solution)/shard_map/ppermute | solution.py:185
  60.8 12.8 %collective-permute-start.15 = (f32[128,512]{1,0:T(8,128)S(1)}, f32[128,512]{1,0:T(8,128)S(1)}, u32[]{:S(2)}, u32[]{:S(2)}) collective-permute-start(f32[128,512]{1,0:T(8,128)S(1)} %get-tuple-element.42), channel_id=1, source_target_pairs={{0,64},{4,452},{8,72},{12,460},{16,80},{20,468},{24,88},{28,476},{... | collective-permute-start | bytes 786440 | tf_op jit(solution)/shard_map/ppermute | solution.py:185
  66.4 12.7 %collective-permute-start.11 = (f32[128,512]{1,0:T(8,128)S(1)}, f32[128,512]{1,0:T(8,128)S(1)}, u32[]{:S(2)}, u32[]{:S(2)}) collective-permute-start(f32[128,512]{1,0:T(8,128)S(1)} %get-tuple-element.34), channel_id=1, source_target_pairs={{0,64},{4,452},{8,72},{12,460},{16,80},{20,468},{24,88},{28,476},{... | collective-permute-start | bytes 786440 | tf_op jit(solution)/shard_map/ppermute | solution.py:185
  73.6 15.7 %collective-permute-start.16 = (f32[64,512]{1,0:T(8,128)S(1)}, f32[64,512]{1,0:T(8,128)S(1)}, u32[]{:S(2)}, u32[]{:S(2)}) collective-permute-start(f32[64,512]{1,0:T(8,128)S(1)} %get-tuple-element.44), channel_id=1, source_target_pairs={{0,128},{4,388},{8,136},{12,396},{16,144},{20,404},{24,152},{28,41... | collective-permute-start | bytes 393224 | tf_op jit(solution)/shard_map/ppermute | solution.py:185
  79.1 17.7 %collective-permute-start.12 = (f32[64,512]{1,0:T(8,128)S(1)}, f32[64,512]{1,0:T(8,128)S(1)}, u32[]{:S(2)}, u32[]{:S(2)}) collective-permute-start(f32[64,512]{1,0:T(8,128)S(1)} %get-tuple-element.36), channel_id=1, source_target_pairs={{0,128},{4,388},{8,136},{12,396},{16,144},{20,404},{24,152},{28,41... | collective-permute-start | bytes 393224 | tf_op jit(solution)/shard_map/ppermute | solution.py:185
  89.4 14.9 %collective-permute-start.17 = (f32[32,512]{1,0:T(8,128)S(1)}, f32[32,512]{1,0:T(8,128)S(1)}, u32[]{:S(2)}, u32[]{:S(2)}) collective-permute-start(f32[32,512]{1,0:T(8,128)S(1)} %get-tuple-element.46), channel_id=1, source_target_pairs={{0,256},{4,260},{8,264},{12,268},{16,272},{20,276},{24,280},{28,28... | collective-permute-start | bytes 196616 | tf_op jit(solution)/shard_map/ppermute | solution.py:185
  96.9 14.9 %collective-permute-start.13 = (f32[32,512]{1,0:T(8,128)S(1)}, f32[32,512]{1,0:T(8,128)S(1)}, u32[]{:S(2)}, u32[]{:S(2)}) collective-permute-start(f32[32,512]{1,0:T(8,128)S(1)} %get-tuple-element.38), channel_id=1, source_target_pairs={{0,256},{4,260},{8,264},{12,268},{16,272},{20,276},{24,280},{28,28... | collective-permute-start | bytes 196616 | tf_op jit(solution)/shard_map/ppermute | solution.py:185

commit v6 on v5

--- a/solution.py
+++ b/solution.py
@@ -154,13 +154,31 @@
         send[rows, :] = held[far, :] + came[far, :]
 
 
-def last_kernel(held_a, came_a, held_b, came_b, out):
+def group_kernel(held, came, own, up, far, down):
+    for i, out in enumerate((own, up, far, down)):
+        rows = pl.ds(i * SUB, SUB)
+        out[...] = held[rows, :] + came[rows, :]
+
+
+def up_kernel(first, second, came, out):
+    half = first.shape[1]
+    out[:, :half] = first[...] + came[...]
+    out[:, half:] = second[...]
+
+
+def down_kernel(first, second, came, out):
+    half = first.shape[1]
+    out[:, :half] = first[...]
+    out[:, half:] = second[...] + came[...]
+
+
+def last_kernel(first, second, from_below, from_above, out):
     x = lax.axis_index("row") // 2
     for index, t in enumerate(ORDER):
-        held, came = ((held_a, came_a), (held_b, came_b))[index // 2]
-        source = pl.ds((index % 2) * 2 * TILE, 2 * TILE)
+        source = pl.ds(index * 2 * TILE, 2 * TILE)
+        own = (first, second)[index // 2][:, pl.ds((index % 2) * 2 * TILE, 2 * TILE)]
         target = pl.ds(pl.multiple_of(lax.rem(x + t, N_X) * 2 * TILE, 2 * TILE), 2 * TILE)
-        out[:, target] = held[:, source] + came[:, source]
+        out[:, target] = own + (from_below[:, source] + from_above[:, source])
 
 
 def swap(value):
@@ -183,6 +201,10 @@
             to = (z + (distance if row % 2 == 0 else -distance)) % N_LAYER
             pairs.append((z * N_ROW + row, to * N_ROW + row))
     return lax.ppermute(value, ("layer", "row"), pairs)
+
+
+def shift_layers(value, distance):
+    return lax.ppermute(value, "layer", [(z, (z + distance) % N_LAYER) for z in range(N_LAYER)])
 
 
 def on_device(graph, pattern):
@@ -215,14 +237,19 @@
     )
     sends, keeps = list(made[:2]), list(made[2:])
     arrived = [pass_on(sends[half], 1) for half in range(2)]
-    for stage in (1, 2, 3):
-        count = 8 >> stage
-        for half in range(2):
-            sends[half], keeps[half] = call(
-                stage_kernel, [(count * SUB, 4 * TILE)] * 2, (keeps[half], arrived[half])
-            )
-            arrived[half] = pass_on(sends[half], 1 << stage)
-    return call(last_kernel, [(SUB, 8 * TILE)], (keeps[0], arrived[0], keeps[1], arrived[1]))[0]
+    for half in range(2):
+        sends[half], keeps[half] = call(
+            stage_kernel, [(4 * SUB, 4 * TILE)] * 2, (keeps[half], arrived[half])
+        )
+        arrived[half] = pass_on(sends[half], 2)
+    first, second = (
+        call(group_kernel, [(SUB, 4 * TILE)] * 4, (keeps[half], arrived[half])) for half in range(2)
+    )
+    chunk = [(SUB, 8 * TILE)]
+    (up,) = call(up_kernel, chunk, (first[1], second[1], shift_layers(first[2], 4)))
+    (down,) = call(down_kernel, chunk, (first[3], second[3], shift_layers(second[2], -4)))
+    ends = (first[0], second[0], shift_layers(up, 4), shift_layers(down, -4))
+    return call(last_kernel, chunk, ends)[0]
 
 
 def solution(mesh):

time: 113 us -> 111 us (0.982)
  starting transfers between devices: 62.9 us -> 56.1 us
  waiting for transfers between devices: 40.3 us -> 44.6 us
    ppermute x8 -> x4, starting transfers between devices: 34.9 us -> 11.4 us  [pass_on(): return lax.ppermute(value, ('layer', 'row'), pairs)]
    ppermute x0 -> x4, waiting for transfers between devices: none -> 19 us  [shift_layers(): lax.ppermute(value, 'layer', [(z, (z + distance) % N_LAYER) for z in rang...]
    ppermute x0 -> x4, starting transfers between devices: none -> 16.7 us  [shift_layers(): lax.ppermute(value, 'layer', [(z, (z + distance) % N_LAYER) for z in rang...]
    ppermute x8 -> x4, waiting for transfers between devices: 34.4 us -> 19.8 us  [pass_on(): return lax.ppermute(value, ('layer', 'row'), pairs)]
where the time goes in v6:
time: 111 us; the launch traced here: 110 us
  starting transfers between devices  56.1 us (51%)
  waiting for transfers between devices  44.6 us (40%)
  Pallas kernels  7.38 us (7%)
  local copies, waits for them, and re-layouts  1.7 us (2%)
    ppermute x4, waiting for transfers between devices, pass_on(): return lax.ppermute(value, ('layer', 'row'), pairs)  19.8 us
    ppermute x6, starting transfers between devices, fetch(): return lax.ppermute(value, ('row', 'col'), pairs)  19.7 us
    ppermute x4, waiting for transfers between devices, shift_layers(): lax.ppermute(value, 'layer', [(z, (z + distance) % N_LAYER) for z in rang...  19 us
    ppermute x4, starting transfers between devices, shift_layers(): lax.ppermute(value, 'layer', [(z, (z + distance) % N_LAYER) for z in rang...  16.7 us
    ppermute x4, starting transfers between devices, pass_on(): return lax.ppermute(value, ('layer', 'row'), pairs)  11.4 us
    ppermute x4, starting transfers between devices, swap(): return lax.ppermute(value, 'row', [(i, i ^ 1) for i in range(N_ROW)])  8.27 us
    pallas_call x13, Pallas kernels, call(): pl.pallas_call(kernel, out_shape=tuple((jax.ShapeDtypeStruct(s, d) for s,...  7.38 us
    ppermute x6, waiting for transfers between devices, fetch(): return lax.ppermute(value, ('row', 'col'), pairs)  5.85 us
  transfers between devices with their start and end apart: 18, of which 9 were waited for; matrix products, arithmetic and copies ran while one was open for 0% of the time, Pallas kernels for 3%

profile of v6, /device:TPU:6, one launch (start us, length us, event | category | flops | bytes accessed | tf_op | source)
XLA Modules:
  0.0 110.1 jit_solution(9633403312258897770)
XLA Ops:
  2.3 1.9 %collective-permute-start.2 = (f32[1024,128]{1,0:T(8,128)S(1)}, f32[1024,128]{1,0:T(8,128)S(1)}, u32[]{:S(2)}, u32[]{:S(2)}) collective-permute-start(f32[1024,128]{1,0:T(8,128)S(1)} %shard_map.28.own), channel_id=1, source_target_pairs={{0,4},{4,0},{8,12},{12,8},{16,20},{20,16},{24,28},{28,24},{1,5},{5... | collective-permute-start | bytes 1572872 | tf_op jit(solution)/shard_map/ppermute | solution.py:185
  4.2 4.9 %collective-permute-start = (f32[1024,128]{1,0:T(8,128)S(1)}, f32[1024,128]{1,0:T(8,128)S(1)}, u32[]{:S(2)}, u32[]{:S(2)}) collective-permute-start(f32[1024,128]{1,0:T(8,128)S(1)} %shard_map.28.own), channel_id=1, source_target_pairs={{1,0},{12,4},{2,1},{13,5},{3,2},{14,6},{0,3},{15,7},{9,8},{20,12},... | collective-permute-start | bytes 1572872 | tf_op jit(solution)/shard_map/ppermute | solution.py:194
  9.2 1.9 %collective-permute-start.3 = (f32[1024,128]{1,0:T(8,128)S(1)}, f32[1024,128]{1,0:T(8,128)S(1)}, u32[]{:S(2)}, u32[]{:S(2)}) collective-permute-start(f32[1024,128]{1,0:T(8,128)S(1)} %collective-permute-done.2.other), channel_id=1, source_target_pairs={{3,0},{28,4},{0,1},{29,5},{1,2},{30,6},{2,3},{31,7},{11,8},{4,12},... | collective-permute-start | bytes 1572872 | tf_op jit(solution)/shard_map/ppermute | solution.py:194
  11.1 2.5 %collective-permute-start.7 = (f32[1024,128]{1,0:T(8,128)S(1)}, f32[1024,128]{1,0:T(8,128)S(1)}, u32[]{:S(2)}, u32[]{:S(2)}) collective-permute-start(f32[1024,128]{1,0:T(8,128)S(1)} %shard_map.28.own), channel_id=1, source_target_pairs={{3,0},{28,4},{0,1},{29,5},{1,2},{30,6},{2,3},{31,7},{11,8},{4,12},... | collective-permute-start | bytes 1572872 | tf_op jit(solution)/shard_map/ppermute | solution.py:194
  13.6 4.6 %collective-permute-start.6 = (f32[1024,128]{1,0:T(8,128)S(1)}, f32[1024,128]{1,0:T(8,128)S(1)}, u32[]{:S(2)}, u32[]{:S(2)}) collective-permute-start(f32[1024,128]{1,0:T(8,128)S(1)} %collective-permute-done.2.other), channel_id=1, source_target_pairs={{1,0},{12,4},{2,1},{13,5},{3,2},{14,6},{0,3},{15,7},{9,8},{20,12},... | collective-permute-start | bytes 1572872 | tf_op jit(solution)/shard_map/ppermute | solution.py:194
  18.2 3.9 %collective-permute-start.1 = (f32[1024,128]{1,0:T(8,128)S(1)}, f32[1024,128]{1,0:T(8,128)S(1)}, u32[]{:S(2)}, u32[]{:S(2)}) collective-permute-start(f32[1024,128]{1,0:T(8,128)S(1)} %collective-permute-done.first.o1), channel_id=1, source_target_pairs={{1,0},{12,4},{2,1},{13,5},{3,2},{14,6},{0,3},{15,7},{9,8},{20,12},... | collective-permute-start | bytes 1572872 | tf_op jit(solution)/shard_map/ppermute | solution.py:194
  24.0 3.0 %collective-permute-done.7.second.o3 = f32[1024,128]{1,0:T(8,128)S(1)} collective-permute-done((f32[1024,128]{1,0:T(8,128)S(1)}, f32[1024,128]{1,0:T(8,128)S(1)}, u32[]{:S(2)}, u32[]{:S(2)}) %collective-permute-start.7) | collective-permute-done | bytes 524320 | tf_op jit(solution)/shard_map/ppermute | solution.py:194
  29.1 2.4 %collective-permute-start.9 = (f32[2048,128]{1,0:T(8,128)S(1)}, f32[2048,128]{1,0:T(8,128)S(1)}, u32[]{:S(2)}, u32[]{:S(2)}) collective-permute-start(f32[2048,128]{1,0:T(8,128)S(1)} %shard_map.31), channel_id=1, source_target_pairs={{0,4},{4,0},{8,12},{12,8},{16,20},{20,16},{24,28},{28,24},{1,5},{5... | collective-permute-start | bytes 3145736 | tf_op jit(solution)/shard_map/ppermute | solution.py:185
  31.6 2.8 %collective-permute-done.4.second.s2 = f32[1024,128]{1,0:T(8,128)S(1)} collective-permute-done((f32[1024,128]{1,0:T(8,128)S(1)}, f32[1024,128]{1,0:T(8,128)S(1)}, u32[]{:S(2)}, u32[]{:S(2)}) %collective-permute-start.4) | collective-permute-done | bytes 524320 | tf_op jit(solution)/shard_map/ppermute | solution.py:194
  34.5 2.0 %collective-permute-start.5 = (f32[2048,128]{1,0:T(8,128)S(1)}, f32[2048,128]{1,0:T(8,128)S(1)}, u32[]{:S(2)}, u32[]{:S(2)}) collective-permute-start(f32[2048,128]{1,0:T(8,128)S(1)} %shard_map.29), channel_id=1, source_target_pairs={{0,4},{4,0},{8,12},{12,8},{16,20},{20,16},{24,28},{28,24},{1,5},{5... | collective-permute-start | bytes 3145736 | tf_op jit(solution)/shard_map/ppermute | solution.py:185
  36.5 3.4 %shard_map.32 = (bf16[384,1024]{1,0:T(8,128)(2,1)S(1)}, bf16[384,1024]{1,0:T(8,128)(2,1)S(1)}, bf16[1024,768]{1,0:T(8,128)(2,1)S(1)}, bf16[1024,768]{1,0:T(8,128)(2,1)S(1)}, f32[384,768]{1,0:T(8,128)S(1)}) custom-call(f32[1024,128]{1,0:T(8,128)S(1)} %shard_map.28.own, f32[1024,128]{1,0:T(8,128)S(1)} %collective-permute-done.2.other, ...), custom_call_target="tpu_custom_call" | custom-call | flops 1811939328 | bytes 8388608 | tf_op jit(solution)/shard_map/pallas_call | solution.py:25
  39.9 2.3 %shard_map.33 = (f32[256,512]{1,0:T(8,128)S(1)}, f32[256,512]{1,0:T(8,128)S(1)}, f32[256,512]{1,0:T(8,128)S(1)}, f32[256,512]{1,0:T(8,128)S(1)}) custom-call(f32[1024,128]{1,0:T(8,128)S(1)} %collective-permute-done.1.first.o2, f32[1024,128]{1,0:T(8,128)S(1)} %collective-permute-done.4.second.s2, f32[2048,128]{1,0:T(8,128)S(1)} %collective-permute-done.5.both, ...), custom_call_target="tpu_custom_call" | custom-call | flops 1409286144 | bytes 8388608 | tf_op jit(solution)/shard_map/pallas_call | solution.py:25
  42.3 3.7 %collective-permute-start.12 = (f32[256,512]{1,0:T(8,128)S(1)}, f32[256,512]{1,0:T(8,128)S(1)}, u32[]{:S(2)}, u32[]{:S(2)}) collective-permute-start(f32[256,512]{1,0:T(8,128)S(1)} %get-tuple-element.37), channel_id=1, source_target_pairs={{0,32},{4,484},{8,40},{12,492},{16,48},{20,500},{24,56},{28,508},{... | collective-permute-start | bytes 1572872 | tf_op jit(solution)/shard_map/ppermute | solution.py:203
  46.0 3.8 %collective-permute-start.10 = (f32[256,512]{1,0:T(8,128)S(1)}, f32[256,512]{1,0:T(8,128)S(1)}, u32[]{:S(2)}, u32[]{:S(2)}) collective-permute-start(f32[256,512]{1,0:T(8,128)S(1)} %get-tuple-element.32), channel_id=1, source_target_pairs={{0,32},{4,484},{8,40},{12,492},{16,48},{20,500},{24,56},{28,508},{... | collective-permute-start | bytes 1572872 | tf_op jit(solution)/shard_map/ppermute | solution.py:203
  49.8 10.9 %collective-permute-done.12.came = f32[256,512]{1,0:T(8,128)S(1)} collective-permute-done((f32[256,512]{1,0:T(8,128)S(1)}, f32[256,512]{1,0:T(8,128)S(1)}, u32[]{:S(2)}, u32[]{:S(2)}) %collective-permute-start.12) | collective-permute-done | bytes 524320 | tf_op jit(solution)/shard_map/ppermute | solution.py:203
  62.7 3.6 %collective-permute-done.10.came = f32[256,512]{1,0:T(8,128)S(1)} collective-permute-done((f32[256,512]{1,0:T(8,128)S(1)}, f32[256,512]{1,0:T(8,128)S(1)}, u32[]{:S(2)}, u32[]{:S(2)}) %collective-permute-start.10) | collective-permute-done | bytes 524320 | tf_op jit(solution)/shard_map/ppermute | solution.py:203
  68.3 5.2 %collective-permute-done.13.came = f32[128,512]{1,0:T(8,128)S(1)} collective-permute-done((f32[128,512]{1,0:T(8,128)S(1)}, f32[128,512]{1,0:T(8,128)S(1)}, u32[]{:S(2)}, u32[]{:S(2)}) %collective-permute-start.13) | collective-permute-done | bytes 262176 | tf_op jit(solution)/shard_map/ppermute | solution.py:203
  73.6 6.9 %collective-permute-start.16 = (f32[32,512]{1,0:T(8,128)S(1)}, f32[32,512]{1,0:T(8,128)S(1)}, u32[]{:S(2)}, u32[]{:S(2)}) collective-permute-start(f32[32,512]{1,0:T(8,128)S(1)} %get-tuple-element.46), channel_id=1, source_target_pairs={{0,384},{32,416},{64,448},{96,480},{128,0},{160,32},{192,64},{224,... | collective-permute-start | bytes 196616 | tf_op jit(solution)/shard_map/ppermute | solution.py:207
  80.6 2.8 %collective-permute-start.14 = (f32[32,512]{1,0:T(8,128)S(1)}, f32[32,512]{1,0:T(8,128)S(1)}, u32[]{:S(2)}, u32[]{:S(2)}) collective-permute-start(f32[32,512]{1,0:T(8,128)S(1)} %get-tuple-element.43), channel_id=1, source_target_pairs={{0,128},{32,160},{64,192},{96,224},{128,256},{160,288},{192,320},{... | collective-permute-start | bytes 196616 | tf_op jit(solution)/shard_map/ppermute | solution.py:207
  83.4 2.1 %collective-permute-done.16.came = f32[32,512]{1,0:T(8,128)S(1)} collective-permute-done((f32[32,512]{1,0:T(8,128)S(1)}, f32[32,512]{1,0:T(8,128)S(1)}, u32[]{:S(2)}, u32[]{:S(2)}) %collective-permute-start.16) | collective-permute-done | bytes 65568 | tf_op jit(solution)/shard_map/ppermute | solution.py:207
  85.6 5.1 %collective-permute-start.17 = (f32[32,1024]{1,0:T(8,128)S(1)}, f32[32,1024]{1,0:T(8,128)S(1)}, u32[]{:S(2)}, u32[]{:S(2)}) collective-permute-start(f32[32,1024]{1,0:T(8,128)S(1)} %shard_map.39), channel_id=1, source_target_pairs={{0,384},{32,416},{64,448},{96,480},{128,0},{160,32},{192,64},{224,... | collective-permute-start | bytes 393224 | tf_op jit(solution)/shard_map/ppermute | solution.py:207
  90.6 2.9 %collective-permute-done.14.came = f32[32,512]{1,0:T(8,128)S(1)} collective-permute-done((f32[32,512]{1,0:T(8,128)S(1)}, f32[32,512]{1,0:T(8,128)S(1)}, u32[]{:S(2)}, u32[]{:S(2)}) %collective-permute-start.14) | collective-permute-done | bytes 65568 | tf_op jit(solution)/shard_map/ppermute | solution.py:207
  95.5 4.0 %collective-permute-done.17.from_above = f32[32,1024]{1,0:T(8,128)S(1)} collective-permute-done((f32[32,1024]{1,0:T(8,128)S(1)}, f32[32,1024]{1,0:T(8,128)S(1)}, u32[]{:S(2)}, u32[]{:S(2)}) %collective-permute-start.17) | collective-permute-done | bytes 131104 | tf_op jit(solution)/shard_map/ppermute | solution.py:207
  99.5 10.0 %collective-permute-done.15.from_below = f32[32,1024]{1,0:T(8,128)S(1)} collective-permute-done((f32[32,1024]{1,0:T(8,128)S(1)}, f32[32,1024]{1,0:T(8,128)S(1)}, u32[]{:S(2)}, u32[]{:S(2)}) %collective-permute-start.15) | collective-permute-done | bytes 131104 | tf_op jit(solution)/shard_map/ppermute | solution.py:207
  (29 shorter events, 13.0 us)
Async XLA Ops:
  0.0 1.0 copy-start
  1.0 0.7 copy-start.1
  2.3 6.9 %collective-permute-start.2 = (f32[1024,128]{1,0:T(8,128)S(1)}, f32[1024,128]{1,0:T(8,128)S(1)}, u32[]{:S(2)}, u32[]{:S(2)}) collective-permute-start(f32[1024,128]{1,0:T(8,128)S(1)} %shard_map.28.own), channel_id=1, source_target_pairs={{0,4},{4,0},{8,12},{12,8},{16,20},{20,16},{24,28},{28,24},{1,5},{5... | collective-permute-start | bytes 1572872 | tf_op jit(solution)/shard_map/ppermute | solution.py:185
  4.2 13.9 %collective-permute-start = (f32[1024,128]{1,0:T(8,128)S(1)}, f32[1024,128]{1,0:T(8,128)S(1)}, u32[]{:S(2)}, u32[]{:S(2)}) collective-permute-start(f32[1024,128]{1,0:T(8,128)S(1)} %shard_map.28.own), channel_id=1, source_target_pairs={{1,0},{12,4},{2,1},{13,5},{3,2},{14,6},{0,3},{15,7},{9,8},{20,12},... | collective-permute-start | bytes 1572872 | tf_op jit(solution)/shard_map/ppermute | solution.py:194
  9.2 12.9 %collective-permute-start.3 = (f32[1024,128]{1,0:T(8,128)S(1)}, f32[1024,128]{1,0:T(8,128)S(1)}, u32[]{:S(2)}, u32[]{:S(2)}) collective-permute-start(f32[1024,128]{1,0:T(8,128)S(1)} %collective-permute-done.2.other), channel_id=1, source_target_pairs={{3,0},{28,4},{0,1},{29,5},{1,2},{30,6},{2,3},{31,7},{11,8},{4,12},... | collective-permute-start | bytes 1572872 | tf_op jit(solution)/shard_map/ppermute | solution.py:194
  11.1 16.0 %collective-permute-start.7 = (f32[1024,128]{1,0:T(8,128)S(1)}, f32[1024,128]{1,0:T(8,128)S(1)}, u32[]{:S(2)}, u32[]{:S(2)}) collective-permute-start(f32[1024,128]{1,0:T(8,128)S(1)} %shard_map.28.own), channel_id=1, source_target_pairs={{3,0},{28,4},{0,1},{29,5},{1,2},{30,6},{2,3},{31,7},{11,8},{4,12},... | collective-permute-start | bytes 1572872 | tf_op jit(solution)/shard_map/ppermute | solution.py:194
  13.6 15.5 %collective-permute-start.6 = (f32[1024,128]{1,0:T(8,128)S(1)}, f32[1024,128]{1,0:T(8,128)S(1)}, u32[]{:S(2)}, u32[]{:S(2)}) collective-permute-start(f32[1024,128]{1,0:T(8,128)S(1)} %collective-permute-done.2.other), channel_id=1, source_target_pairs={{1,0},{12,4},{2,1},{13,5},{3,2},{14,6},{0,3},{15,7},{9,8},{20,12},... | collective-permute-start | bytes 1572872 | tf_op jit(solution)/shard_map/ppermute | solution.py:194
  18.2 13.4 %collective-permute-start.1 = (f32[1024,128]{1,0:T(8,128)S(1)}, f32[1024,128]{1,0:T(8,128)S(1)}, u32[]{:S(2)}, u32[]{:S(2)}) collective-permute-start(f32[1024,128]{1,0:T(8,128)S(1)} %collective-permute-done.first.o1), channel_id=1, source_target_pairs={{1,0},{12,4},{2,1},{13,5},{3,2},{14,6},{0,3},{15,7},{9,8},{20,12},... | collective-permute-start | bytes 1572872 | tf_op jit(solution)/shard_map/ppermute | solution.py:194
  22.1 12.3 %collective-permute-start.4 = (f32[1024,128]{1,0:T(8,128)S(1)}, f32[1024,128]{1,0:T(8,128)S(1)}, u32[]{:S(2)}, u32[]{:S(2)}) collective-permute-start(f32[1024,128]{1,0:T(8,128)S(1)} %collective-permute-done.3.second.s3), channel_id=1, source_target_pairs={{3,0},{28,4},{0,1},{29,5},{1,2},{30,6},{2,3},{31,7},{11,8},{4,12},... | collective-permute-start | bytes 1572872 | tf_op jit(solution)/shard_map/ppermute | solution.py:194
  27.1 9.4 %collective-permute-start.8 = (f32[2048,128]{1,0:T(8,128)S(1)}, f32[2048,128]{1,0:T(8,128)S(1)}, u32[]{:S(2)}, u32[]{:S(2)}) collective-permute-start(f32[2048,128]{1,0:T(8,128)S(1)} %shard_map.30), channel_id=1, source_target_pairs={{0,4},{4,0},{8,12},{12,8},{16,20},{20,16},{24,28},{28,24},{1,5},{5... | collective-permute-start | bytes 3145736 | tf_op jit(solution)/shard_map/ppermute | solution.py:185
  29.1 7.4 %collective-permute-start.9 = (f32[2048,128]{1,0:T(8,128)S(1)}, f32[2048,128]{1,0:T(8,128)S(1)}, u32[]{:S(2)}, u32[]{:S(2)}) collective-permute-start(f32[2048,128]{1,0:T(8,128)S(1)} %shard_map.31), channel_id=1, source_target_pairs={{0,4},{4,0},{8,12},{12,8},{16,20},{20,16},{24,28},{28,24},{1,5},{5... | collective-permute-start | bytes 3145736 | tf_op jit(solution)/shard_map/ppermute | solution.py:185
  34.5 5.5 %collective-permute-start.5 = (f32[2048,128]{1,0:T(8,128)S(1)}, f32[2048,128]{1,0:T(8,128)S(1)}, u32[]{:S(2)}, u32[]{:S(2)}) collective-permute-start(f32[2048,128]{1,0:T(8,128)S(1)} %shard_map.29), channel_id=1, source_target_pairs={{0,4},{4,0},{8,12},{12,8},{16,20},{20,16},{24,28},{28,24},{1,5},{5... | collective-permute-start | bytes 3145736 | tf_op jit(solution)/shard_map/ppermute | solution.py:185
  42.3 18.5 %collective-permute-start.12 = (f32[256,512]{1,0:T(8,128)S(1)}, f32[256,512]{1,0:T(8,128)S(1)}, u32[]{:S(2)}, u32[]{:S(2)}) collective-permute-start(f32[256,512]{1,0:T(8,128)S(1)} %get-tuple-element.37), channel_id=1, source_target_pairs={{0,32},{4,484},{8,40},{12,492},{16,48},{20,500},{24,56},{28,508},{... | collective-permute-start | bytes 1572872 | tf_op jit(solution)/shard_map/ppermute | solution.py:203
  46.0 20.3 %collective-permute-start.10 = (f32[256,512]{1,0:T(8,128)S(1)}, f32[256,512]{1,0:T(8,128)S(1)}, u32[]{:S(2)}, u32[]{:S(2)}) collective-permute-start(f32[256,512]{1,0:T(8,128)S(1)} %get-tuple-element.32), channel_id=1, source_target_pairs={{0,32},{4,484},{8,40},{12,492},{16,48},{20,500},{24,56},{28,508},{... | collective-permute-start | bytes 1572872 | tf_op jit(solution)/shard_map/ppermute | solution.py:203
  60.8 12.8 %collective-permute-start.13 = (f32[128,512]{1,0:T(8,128)S(1)}, f32[128,512]{1,0:T(8,128)S(1)}, u32[]{:S(2)}, u32[]{:S(2)}) collective-permute-start(f32[128,512]{1,0:T(8,128)S(1)} %get-tuple-element.39), channel_id=1, source_target_pairs={{0,64},{4,452},{8,72},{12,460},{16,80},{20,468},{24,88},{28,476},{... | collective-permute-start | bytes 786440 | tf_op jit(solution)/shard_map/ppermute | solution.py:203
  66.4 14.1 %collective-permute-start.11 = (f32[128,512]{1,0:T(8,128)S(1)}, f32[128,512]{1,0:T(8,128)S(1)}, u32[]{:S(2)}, u32[]{:S(2)}) collective-permute-start(f32[128,512]{1,0:T(8,128)S(1)} %get-tuple-element.34), channel_id=1, source_target_pairs={{0,64},{4,452},{8,72},{12,460},{16,80},{20,468},{24,88},{28,476},{... | collective-permute-start | bytes 786440 | tf_op jit(solution)/shard_map/ppermute | solution.py:203
  73.6 12.0 %collective-permute-start.16 = (f32[32,512]{1,0:T(8,128)S(1)}, f32[32,512]{1,0:T(8,128)S(1)}, u32[]{:S(2)}, u32[]{:S(2)}) collective-permute-start(f32[32,512]{1,0:T(8,128)S(1)} %get-tuple-element.46), channel_id=1, source_target_pairs={{0,384},{32,416},{64,448},{96,480},{128,0},{160,32},{192,64},{224,... | collective-permute-start | bytes 196616 | tf_op jit(solution)/shard_map/ppermute | solution.py:207
  80.6 12.9 %collective-permute-start.14 = (f32[32,512]{1,0:T(8,128)S(1)}, f32[32,512]{1,0:T(8,128)S(1)}, u32[]{:S(2)}, u32[]{:S(2)}) collective-permute-start(f32[32,512]{1,0:T(8,128)S(1)} %get-tuple-element.43), channel_id=1, source_target_pairs={{0,128},{32,160},{64,192},{96,224},{128,256},{160,288},{192,320},{... | collective-permute-start | bytes 196616 | tf_op jit(solution)/shard_map/ppermute | solution.py:207
  85.6 13.9 %collective-permute-start.17 = (f32[32,1024]{1,0:T(8,128)S(1)}, f32[32,1024]{1,0:T(8,128)S(1)}, u32[]{:S(2)}, u32[]{:S(2)}) collective-permute-start(f32[32,1024]{1,0:T(8,128)S(1)} %shard_map.39), channel_id=1, source_target_pairs={{0,384},{32,416},{64,448},{96,480},{128,0},{160,32},{192,64},{224,... | collective-permute-start | bytes 393224 | tf_op jit(solution)/shard_map/ppermute | solution.py:207
  93.5 15.9 %collective-permute-start.15 = (f32[32,1024]{1,0:T(8,128)S(1)}, f32[32,1024]{1,0:T(8,128)S(1)}, u32[]{:S(2)}, u32[]{:S(2)}) collective-permute-start(f32[32,1024]{1,0:T(8,128)S(1)} %shard_map.38), channel_id=1, source_target_pairs={{0,128},{32,160},{64,192},{96,224},{128,256},{160,288},{192,320},{... | collective-permute-start | bytes 393224 | tf_op jit(solution)/shard_map/ppermute | solution.py:207

commit v7 on v6

--- a/solution.py
+++ b/solution.py
@@ -160,25 +160,18 @@
         out[...] = held[rows, :] + came[rows, :]
 
 
-def up_kernel(first, second, came, out):
-    half = first.shape[1]
-    out[:, :half] = first[...] + came[...]
-    out[:, half:] = second[...]
-
-
-def down_kernel(first, second, came, out):
-    half = first.shape[1]
-    out[:, :half] = first[...]
-    out[:, half:] = second[...] + came[...]
-
-
-def last_kernel(first, second, from_below, from_above, out):
+def add_kernel(held, came, out):
+    out[...] = held[...] + came[...]
+
+
+def last_kernel(*refs):
+    halves_of, out = (refs[0:3], refs[3:6]), refs[6]
     x = lax.axis_index("row") // 2
     for index, t in enumerate(ORDER):
-        source = pl.ds(index * 2 * TILE, 2 * TILE)
-        own = (first, second)[index // 2][:, pl.ds((index % 2) * 2 * TILE, 2 * TILE)]
+        source = pl.ds((index % 2) * 2 * TILE, 2 * TILE)
         target = pl.ds(pl.multiple_of(lax.rem(x + t, N_X) * 2 * TILE, 2 * TILE), 2 * TILE)
-        out[:, target] = own + (from_below[:, source] + from_above[:, source])
+        own, below, above = halves_of[index // 2]
+        out[:, target] = own[:, source] + (below[:, source] + above[:, source])
 
 
 def swap(value):
@@ -245,11 +238,13 @@
     first, second = (
         call(group_kernel, [(SUB, 4 * TILE)] * 4, (keeps[half], arrived[half])) for half in range(2)
     )
-    chunk = [(SUB, 8 * TILE)]
-    (up,) = call(up_kernel, chunk, (first[1], second[1], shift_layers(first[2], 4)))
-    (down,) = call(down_kernel, chunk, (first[3], second[3], shift_layers(second[2], -4)))
-    ends = (first[0], second[0], shift_layers(up, 4), shift_layers(down, -4))
-    return call(last_kernel, chunk, ends)[0]
+    piece = [(SUB, 4 * TILE)]
+    relayed_up, relayed_down = shift_layers(first[2], 4), shift_layers(second[2], -4)
+    first_above, second_below = shift_layers(first[3], -4), shift_layers(second[1], 4)
+    first_below = shift_layers(call(add_kernel, piece, (first[1], relayed_up))[0], 4)
+    second_above = shift_layers(call(add_kernel, piece, (second[3], relayed_down))[0], -4)
+    ends = (first[0], first_below, first_above, second[0], second_below, second_above)
+    return call(last_kernel, [(SUB, 8 * TILE)], ends)[0]
 
 
 def solution(mesh):

time: 111 us -> 113 us (1.018)
  starting transfers between devices: 56.1 us -> 68.7 us
  waiting for transfers between devices: 44.6 us -> 34.3 us
    ppermute x4 -> x6, starting transfers between devices: 16.7 us -> 29.2 us  [shift_layers(): lax.ppermute(value, 'layer', [(z, (z + distance) % N_LAYER) for z in rang...]
    ppermute x4 -> x6, waiting for transfers between devices: 19 us -> 8.72 us  [shift_layers(): lax.ppermute(value, 'layer', [(z, (z + distance) % N_LAYER) for z in rang...]
  transfers between devices with their start and end apart: 18 -> 20, of which waited for: 9 -> 8; matrix products, arithmetic and copies ran while one was open for 0% -> 0% of each run, Pallas kernels for 3% -> 3%
where the time goes in v7:
time: 113 us; the launch traced here: 112 us
  starting transfers between devices  68.7 us (61%)
  waiting for transfers between devices  34.3 us (30%)
  Pallas kernels  7.37 us (7%)
  local copies, waits for them, and re-layouts  1.7 us (2%)
    ppermute x6, starting transfers between devices, shift_layers(): lax.ppermute(value, 'layer', [(z, (z + distance) % N_LAYER) for z in rang...  29.2 us
    ppermute x4, waiting for transfers between devices, pass_on(): return lax.ppermute(value, ('layer', 'row'), pairs)  19.8 us
    ppermute x6, starting transfers between devices, fetch(): return lax.ppermute(value, ('row', 'col'), pairs)  19.7 us
    ppermute x4, starting transfers between devices, pass_on(): return lax.ppermute(value, ('layer', 'row'), pairs)  11.4 us
    ppermute x6, waiting for transfers between devices, shift_layers(): lax.ppermute(value, 'layer', [(z, (z + distance) % N_LAYER) for z in rang...  8.72 us
    ppermute x4, starting transfers between devices, swap(): return lax.ppermute(value, 'row', [(i, i ^ 1) for i in range(N_ROW)])  8.27 us
    pallas_call x13, Pallas kernels, call(): pl.pallas_call(kernel, out_shape=tuple((jax.ShapeDtypeStruct(s, d) for s,...  7.37 us
    ppermute x6, waiting for transfers between devices, fetch(): return lax.ppermute(value, ('row', 'col'), pairs)  5.85 us
  transfers between devices with their start and end apart: 20, of which 8 were waited for; matrix products, arithmetic and copies ran while one was open for 0% of the time, Pallas kernels for 3%

profile of v7, /device:TPU:6, one launch (start us, length us, event | category | flops | bytes accessed | tf_op | source)
XLA Modules:
  0.0 112.4 jit_solution(4321003651017464965)
XLA Ops:
  4.2 4.9 %collective-permute-start = (f32[1024,128]{1,0:T(8,128)S(1)}, f32[1024,128]{1,0:T(8,128)S(1)}, u32[]{:S(2)}, u32[]{:S(2)}) collective-permute-start(f32[1024,128]{1,0:T(8,128)S(1)} %shard_map.28.own), channel_id=1, source_target_pairs={{1,0},{12,4},{2,1},{13,5},{3,2},{14,6},{0,3},{15,7},{9,8},{20,12},... | collective-permute-start | bytes 1572872 | tf_op jit(solution)/shard_map/ppermute | solution.py:187
  11.1 2.5 %collective-permute-start.7 = (f32[1024,128]{1,0:T(8,128)S(1)}, f32[1024,128]{1,0:T(8,128)S(1)}, u32[]{:S(2)}, u32[]{:S(2)}) collective-permute-start(f32[1024,128]{1,0:T(8,128)S(1)} %shard_map.28.own), channel_id=1, source_target_pairs={{3,0},{28,4},{0,1},{29,5},{1,2},{30,6},{2,3},{31,7},{11,8},{4,12},... | collective-permute-start | bytes 1572872 | tf_op jit(solution)/shard_map/ppermute | solution.py:187
  13.6 4.6 %collective-permute-start.6 = (f32[1024,128]{1,0:T(8,128)S(1)}, f32[1024,128]{1,0:T(8,128)S(1)}, u32[]{:S(2)}, u32[]{:S(2)}) collective-permute-start(f32[1024,128]{1,0:T(8,128)S(1)} %collective-permute-done.2.other), channel_id=1, source_target_pairs={{1,0},{12,4},{2,1},{13,5},{3,2},{14,6},{0,3},{15,7},{9,8},{20,12},... | collective-permute-start | bytes 1572872 | tf_op jit(solution)/shard_map/ppermute | solution.py:187
  18.2 3.9 %collective-permute-start.1 = (f32[1024,128]{1,0:T(8,128)S(1)}, f32[1024,128]{1,0:T(8,128)S(1)}, u32[]{:S(2)}, u32[]{:S(2)}) collective-permute-start(f32[1024,128]{1,0:T(8,128)S(1)} %collective-permute-done.first.o1), channel_id=1, source_target_pairs={{1,0},{12,4},{2,1},{13,5},{3,2},{14,6},{0,3},{15,7},{9,8},{20,12},... | collective-permute-start | bytes 1572872 | tf_op jit(solution)/shard_map/ppermute | solution.py:187
  24.0 3.0 %collective-permute-done.7.second.o3 = f32[1024,128]{1,0:T(8,128)S(1)} collective-permute-done((f32[1024,128]{1,0:T(8,128)S(1)}, f32[1024,128]{1,0:T(8,128)S(1)}, u32[]{:S(2)}, u32[]{:S(2)}) %collective-permute-start.7) | collective-permute-done | bytes 524320 | tf_op jit(solution)/shard_map/ppermute | solution.py:187
  29.1 2.4 %collective-permute-start.9 = (f32[2048,128]{1,0:T(8,128)S(1)}, f32[2048,128]{1,0:T(8,128)S(1)}, u32[]{:S(2)}, u32[]{:S(2)}) collective-permute-start(f32[2048,128]{1,0:T(8,128)S(1)} %shard_map.31), channel_id=1, source_target_pairs={{0,4},{4,0},{8,12},{12,8},{16,20},{20,16},{24,28},{28,24},{1,5},{5... | collective-permute-start | bytes 3145736 | tf_op jit(solution)/shard_map/ppermute | solution.py:178
  31.6 2.8 %collective-permute-done.4.second.s2 = f32[1024,128]{1,0:T(8,128)S(1)} collective-permute-done((f32[1024,128]{1,0:T(8,128)S(1)}, f32[1024,128]{1,0:T(8,128)S(1)}, u32[]{:S(2)}, u32[]{:S(2)}) %collective-permute-start.4) | collective-permute-done | bytes 524320 | tf_op jit(solution)/shard_map/ppermute | solution.py:187
  34.5 2.0 %collective-permute-start.5 = (f32[2048,128]{1,0:T(8,128)S(1)}, f32[2048,128]{1,0:T(8,128)S(1)}, u32[]{:S(2)}, u32[]{:S(2)}) collective-permute-start(f32[2048,128]{1,0:T(8,128)S(1)} %shard_map.29), channel_id=1, source_target_pairs={{0,4},{4,0},{8,12},{12,8},{16,20},{20,16},{24,28},{28,24},{1,5},{5... | collective-permute-start | bytes 3145736 | tf_op jit(solution)/shard_map/ppermute | solution.py:178
  36.5 3.4 %shard_map.32 = (bf16[384,1024]{1,0:T(8,128)(2,1)S(1)}, bf16[384,1024]{1,0:T(8,128)(2,1)S(1)}, bf16[1024,768]{1,0:T(8,128)(2,1)S(1)}, bf16[1024,768]{1,0:T(8,128)(2,1)S(1)}, f32[384,768]{1,0:T(8,128)S(1)}) custom-call(f32[1024,128]{1,0:T(8,128)S(1)} %shard_map.28.own, f32[1024,128]{1,0:T(8,128)S(1)} %collective-permute-done.2.other, ...), custom_call_target="tpu_custom_call" | custom-call | flops 1811939328 | bytes 8388608 | tf_op jit(solution)/shard_map/pallas_call | solution.py:25
  39.9 2.3 %shard_map.33 = (f32[256,512]{1,0:T(8,128)S(1)}, f32[256,512]{1,0:T(8,128)S(1)}, f32[256,512]{1,0:T(8,128)S(1)}, f32[256,512]{1,0:T(8,128)S(1)}) custom-call(f32[1024,128]{1,0:T(8,128)S(1)} %collective-permute-done.1.first.o2, f32[1024,128]{1,0:T(8,128)S(1)} %collective-permute-done.4.second.s2, f32[2048,128]{1,0:T(8,128)S(1)} %collective-permute-done.5.both, ...), custom_call_target="tpu_custom_call" | custom-call | flops 1409286144 | bytes 8388608 | tf_op jit(solution)/shard_map/pallas_call | solution.py:25
  42.3 3.7 %collective-permute-start.15 = (f32[256,512]{1,0:T(8,128)S(1)}, f32[256,512]{1,0:T(8,128)S(1)}, u32[]{:S(2)}, u32[]{:S(2)}) collective-permute-start(f32[256,512]{1,0:T(8,128)S(1)} %get-tuple-element.40), channel_id=1, source_target_pairs={{0,32},{4,484},{8,40},{12,492},{16,48},{20,500},{24,56},{28,508},{... | collective-permute-start | bytes 1572872 | tf_op jit(solution)/shard_map/ppermute | solution.py:196
  46.0 3.8 %collective-permute-start.10 = (f32[256,512]{1,0:T(8,128)S(1)}, f32[256,512]{1,0:T(8,128)S(1)}, u32[]{:S(2)}, u32[]{:S(2)}) collective-permute-start(f32[256,512]{1,0:T(8,128)S(1)} %get-tuple-element.32), channel_id=1, source_target_pairs={{0,32},{4,484},{8,40},{12,492},{16,48},{20,500},{24,56},{28,508},{... | collective-permute-start | bytes 1572872 | tf_op jit(solution)/shard_map/ppermute | solution.py:196
  49.8 10.9 %collective-permute-done.15.came = f32[256,512]{1,0:T(8,128)S(1)} collective-permute-done((f32[256,512]{1,0:T(8,128)S(1)}, f32[256,512]{1,0:T(8,128)S(1)}, u32[]{:S(2)}, u32[]{:S(2)}) %collective-permute-start.15) | collective-permute-done | bytes 524320 | tf_op jit(solution)/shard_map/ppermute | solution.py:196
  62.7 3.6 %collective-permute-done.10.came = f32[256,512]{1,0:T(8,128)S(1)} collective-permute-done((f32[256,512]{1,0:T(8,128)S(1)}, f32[256,512]{1,0:T(8,128)S(1)}, u32[]{:S(2)}, u32[]{:S(2)}) %collective-permute-start.10) | collective-permute-done | bytes 524320 | tf_op jit(solution)/shard_map/ppermute | solution.py:196
  68.3 5.2 %collective-permute-done.16.came = f32[128,512]{1,0:T(8,128)S(1)} collective-permute-done((f32[128,512]{1,0:T(8,128)S(1)}, f32[128,512]{1,0:T(8,128)S(1)}, u32[]{:S(2)}, u32[]{:S(2)}) %collective-permute-start.16) | collective-permute-done | bytes 262176 | tf_op jit(solution)/shard_map/ppermute | solution.py:196
  73.6 6.9 %collective-permute-start.18 = (f32[32,512]{1,0:T(8,128)S(1)}, f32[32,512]{1,0:T(8,128)S(1)}, u32[]{:S(2)}, u32[]{:S(2)}) collective-permute-start(f32[32,512]{1,0:T(8,128)S(1)} %get-tuple-element.46), channel_id=1, source_target_pairs={{0,384},{32,416},{64,448},{96,480},{128,0},{160,32},{192,64},{224,... | collective-permute-start | bytes 196616 | tf_op jit(solution)/shard_map/ppermute | solution.py:200
  80.6 2.8 %collective-permute-start.12 = (f32[32,512]{1,0:T(8,128)S(1)}, f32[32,512]{1,0:T(8,128)S(1)}, u32[]{:S(2)}, u32[]{:S(2)}) collective-permute-start(f32[32,512]{1,0:T(8,128)S(1)} %get-tuple-element.37), channel_id=1, source_target_pairs={{0,128},{32,160},{64,192},{96,224},{128,256},{160,288},{192,320},{... | collective-permute-start | bytes 196616 | tf_op jit(solution)/shard_map/ppermute | solution.py:200
  83.4 6.9 %collective-permute-start.17 = (f32[32,512]{1,0:T(8,128)S(1)}, f32[32,512]{1,0:T(8,128)S(1)}, u32[]{:S(2)}, u32[]{:S(2)}) collective-permute-start(f32[32,512]{1,0:T(8,128)S(1)} %get-tuple-element.44), channel_id=1, source_target_pairs={{0,128},{32,160},{64,192},{96,224},{128,256},{160,288},{192,320},{... | collective-permute-start | bytes 196616 | tf_op jit(solution)/shard_map/ppermute | solution.py:200
  90.3 2.9 %collective-permute-start.14 = (f32[32,512]{1,0:T(8,128)S(1)}, f32[32,512]{1,0:T(8,128)S(1)}, u32[]{:S(2)}, u32[]{:S(2)}) collective-permute-start(f32[32,512]{1,0:T(8,128)S(1)} %get-tuple-element.38), channel_id=1, source_target_pairs={{0,384},{32,416},{64,448},{96,480},{128,0},{160,32},{192,64},{224,... | collective-permute-start | bytes 196616 | tf_op jit(solution)/shard_map/ppermute | solution.py:200
  93.2 6.9 %collective-permute-start.19 = (f32[32,512]{1,0:T(8,128)S(1)}, f32[32,512]{1,0:T(8,128)S(1)}, u32[]{:S(2)}, u32[]{:S(2)}) collective-permute-start(f32[32,512]{1,0:T(8,128)S(1)} %shard_map.39), channel_id=1, source_target_pairs={{0,384},{32,416},{64,448},{96,480},{128,0},{160,32},{192,64},{224,... | collective-permute-start | bytes 196616 | tf_op jit(solution)/shard_map/ppermute | solution.py:200
  100.2 2.8 %collective-permute-start.13 = (f32[32,512]{1,0:T(8,128)S(1)}, f32[32,512]{1,0:T(8,128)S(1)}, u32[]{:S(2)}, u32[]{:S(2)}) collective-permute-start(f32[32,512]{1,0:T(8,128)S(1)} %shard_map.36), channel_id=1, source_target_pairs={{0,128},{32,160},{64,192},{96,224},{128,256},{160,288},{192,320},{... | collective-permute-start | bytes 196616 | tf_op jit(solution)/shard_map/ppermute | solution.py:200
  103.0 2.4 %collective-permute-done.14.refs_2_ = f32[32,512]{1,0:T(8,128)S(1)} collective-permute-done((f32[32,512]{1,0:T(8,128)S(1)}, f32[32,512]{1,0:T(8,128)S(1)}, u32[]{:S(2)}, u32[]{:S(2)}) %collective-permute-start.14) | collective-permute-done | bytes 65568 | tf_op jit(solution)/shard_map/ppermute | solution.py:200
  105.4 2.5 %collective-permute-done.19.refs_5_ = f32[32,512]{1,0:T(8,128)S(1)} collective-permute-done((f32[32,512]{1,0:T(8,128)S(1)}, f32[32,512]{1,0:T(8,128)S(1)}, u32[]{:S(2)}, u32[]{:S(2)}) %collective-permute-start.19) | collective-permute-done | bytes 65568 | tf_op jit(solution)/shard_map/ppermute | solution.py:200
  107.9 3.8 %collective-permute-done.13.refs_1_ = f32[32,512]{1,0:T(8,128)S(1)} collective-permute-done((f32[32,512]{1,0:T(8,128)S(1)}, f32[32,512]{1,0:T(8,128)S(1)}, u32[]{:S(2)}, u32[]{:S(2)}) %collective-permute-start.13) | collective-permute-done | bytes 65568 | tf_op jit(solution)/shard_map/ppermute | solution.py:200
  (33 shorter events, 14.9 us)
Async XLA Ops:
  0.0 1.0 copy-start
  1.0 0.7 copy-start.1
  2.3 6.9 %collective-permute-start.2 = (f32[1024,128]{1,0:T(8,128)S(1)}, f32[1024,128]{1,0:T(8,128)S(1)}, u32[]{:S(2)}, u32[]{:S(2)}) collective-permute-start(f32[1024,128]{1,0:T(8,128)S(1)} %shard_map.28.own), channel_id=1, source_target_pairs={{0,4},{4,0},{8,12},{12,8},{16,20},{20,16},{24,28},{28,24},{1,5},{5... | collective-permute-start | bytes 1572872 | tf_op jit(solution)/shard_map/ppermute | solution.py:178
  4.2 13.9 %collective-permute-start = (f32[1024,128]{1,0:T(8,128)S(1)}, f32[1024,128]{1,0:T(8,128)S(1)}, u32[]{:S(2)}, u32[]{:S(2)}) collective-permute-start(f32[1024,128]{1,0:T(8,128)S(1)} %shard_map.28.own), channel_id=1, source_target_pairs={{1,0},{12,4},{2,1},{13,5},{3,2},{14,6},{0,3},{15,7},{9,8},{20,12},... | collective-permute-start | bytes 1572872 | tf_op jit(solution)/shard_map/ppermute | solution.py:187
  9.2 12.9 %collective-permute-start.3 = (f32[1024,128]{1,0:T(8,128)S(1)}, f32[1024,128]{1,0:T(8,128)S(1)}, u32[]{:S(2)}, u32[]{:S(2)}) collective-permute-start(f32[1024,128]{1,0:T(8,128)S(1)} %collective-permute-done.2.other), channel_id=1, source_target_pairs={{3,0},{28,4},{0,1},{29,5},{1,2},{30,6},{2,3},{31,7},{11,8},{4,12},... | collective-permute-start | bytes 1572872 | tf_op jit(solution)/shard_map/ppermute | solution.py:187
  11.1 16.0 %collective-permute-start.7 = (f32[1024,128]{1,0:T(8,128)S(1)}, f32[1024,128]{1,0:T(8,128)S(1)}, u32[]{:S(2)}, u32[]{:S(2)}) collective-permute-start(f32[1024,128]{1,0:T(8,128)S(1)} %shard_map.28.own), channel_id=1, source_target_pairs={{3,0},{28,4},{0,1},{29,5},{1,2},{30,6},{2,3},{31,7},{11,8},{4,12},... | collective-permute-start | bytes 1572872 | tf_op jit(solution)/shard_map/ppermute | solution.py:187
  13.6 15.5 %collective-permute-start.6 = (f32[1024,128]{1,0:T(8,128)S(1)}, f32[1024,128]{1,0:T(8,128)S(1)}, u32[]{:S(2)}, u32[]{:S(2)}) collective-permute-start(f32[1024,128]{1,0:T(8,128)S(1)} %collective-permute-done.2.other), channel_id=1, source_target_pairs={{1,0},{12,4},{2,1},{13,5},{3,2},{14,6},{0,3},{15,7},{9,8},{20,12},... | collective-permute-start | bytes 1572872 | tf_op jit(solution)/shard_map/ppermute | solution.py:187
  18.2 13.4 %collective-permute-start.1 = (f32[1024,128]{1,0:T(8,128)S(1)}, f32[1024,128]{1,0:T(8,128)S(1)}, u32[]{:S(2)}, u32[]{:S(2)}) collective-permute-start(f32[1024,128]{1,0:T(8,128)S(1)} %collective-permute-done.first.o1), channel_id=1, source_target_pairs={{1,0},{12,4},{2,1},{13,5},{3,2},{14,6},{0,3},{15,7},{9,8},{20,12},... | collective-permute-start | bytes 1572872 | tf_op jit(solution)/shard_map/ppermute | solution.py:187
  22.1 12.3 %collective-permute-start.4 = (f32[1024,128]{1,0:T(8,128)S(1)}, f32[1024,128]{1,0:T(8,128)S(1)}, u32[]{:S(2)}, u32[]{:S(2)}) collective-permute-start(f32[1024,128]{1,0:T(8,128)S(1)} %collective-permute-done.3.second.s3), channel_id=1, source_target_pairs={{3,0},{28,4},{0,1},{29,5},{1,2},{30,6},{2,3},{31,7},{11,8},{4,12},... | collective-permute-start | bytes 1572872 | tf_op jit(solution)/shard_map/ppermute | solution.py:187
  27.1 9.4 %collective-permute-start.8 = (f32[2048,128]{1,0:T(8,128)S(1)}, f32[2048,128]{1,0:T(8,128)S(1)}, u32[]{:S(2)}, u32[]{:S(2)}) collective-permute-start(f32[2048,128]{1,0:T(8,128)S(1)} %shard_map.30), channel_id=1, source_target_pairs={{0,4},{4,0},{8,12},{12,8},{16,20},{20,16},{24,28},{28,24},{1,5},{5... | collective-permute-start | bytes 3145736 | tf_op jit(solution)/shard_map/ppermute | solution.py:178
  29.1 7.4 %collective-permute-start.9 = (f32[2048,128]{1,0:T(8,128)S(1)}, f32[2048,128]{1,0:T(8,128)S(1)}, u32[]{:S(2)}, u32[]{:S(2)}) collective-permute-start(f32[2048,128]{1,0:T(8,128)S(1)} %shard_map.31), channel_id=1, source_target_pairs={{0,4},{4,0},{8,12},{12,8},{16,20},{20,16},{24,28},{28,24},{1,5},{5... | collective-permute-start | bytes 3145736 | tf_op jit(solution)/shard_map/ppermute | solution.py:178
  34.5 5.5 %collective-permute-start.5 = (f32[2048,128]{1,0:T(8,128)S(1)}, f32[2048,128]{1,0:T(8,128)S(1)}, u32[]{:S(2)}, u32[]{:S(2)}) collective-permute-start(f32[2048,128]{1,0:T(8,128)S(1)} %shard_map.29), channel_id=1, source_target_pairs={{0,4},{4,0},{8,12},{12,8},{16,20},{20,16},{24,28},{28,24},{1,5},{5... | collective-permute-start | bytes 3145736 | tf_op jit(solution)/shard_map/ppermute | solution.py:178
  42.3 18.5 %collective-permute-start.15 = (f32[256,512]{1,0:T(8,128)S(1)}, f32[256,512]{1,0:T(8,128)S(1)}, u32[]{:S(2)}, u32[]{:S(2)}) collective-permute-start(f32[256,512]{1,0:T(8,128)S(1)} %get-tuple-element.40), channel_id=1, source_target_pairs={{0,32},{4,484},{8,40},{12,492},{16,48},{20,500},{24,56},{28,508},{... | collective-permute-start | bytes 1572872 | tf_op jit(solution)/shard_map/ppermute | solution.py:196
  46.0 20.3 %collective-permute-start.10 = (f32[256,512]{1,0:T(8,128)S(1)}, f32[256,512]{1,0:T(8,128)S(1)}, u32[]{:S(2)}, u32[]{:S(2)}) collective-permute-start(f32[256,512]{1,0:T(8,128)S(1)} %get-tuple-element.32), channel_id=1, source_target_pairs={{0,32},{4,484},{8,40},{12,492},{16,48},{20,500},{24,56},{28,508},{... | collective-permute-start | bytes 1572872 | tf_op jit(solution)/shard_map/ppermute | solution.py:196
  60.8 12.8 %collective-permute-start.16 = (f32[128,512]{1,0:T(8,128)S(1)}, f32[128,512]{1,0:T(8,128)S(1)}, u32[]{:S(2)}, u32[]{:S(2)}) collective-permute-start(f32[128,512]{1,0:T(8,128)S(1)} %get-tuple-element.42), channel_id=1, source_target_pairs={{0,64},{4,452},{8,72},{12,460},{16,80},{20,468},{24,88},{28,476},{... | collective-permute-start | bytes 786440 | tf_op jit(solution)/shard_map/ppermute | solution.py:196
  66.4 14.1 %collective-permute-start.11 = (f32[128,512]{1,0:T(8,128)S(1)}, f32[128,512]{1,0:T(8,128)S(1)}, u32[]{:S(2)}, u32[]{:S(2)}) collective-permute-start(f32[128,512]{1,0:T(8,128)S(1)} %get-tuple-element.34), channel_id=1, source_target_pairs={{0,64},{4,452},{8,72},{12,460},{16,80},{20,468},{24,88},{28,476},{... | collective-permute-start | bytes 786440 | tf_op jit(solution)/shard_map/ppermute | solution.py:196
  73.6 19.6 %collective-permute-start.18 = (f32[32,512]{1,0:T(8,128)S(1)}, f32[32,512]{1,0:T(8,128)S(1)}, u32[]{:S(2)}, u32[]{:S(2)}) collective-permute-start(f32[32,512]{1,0:T(8,128)S(1)} %get-tuple-element.46), channel_id=1, source_target_pairs={{0,384},{32,416},{64,448},{96,480},{128,0},{160,32},{192,64},{224,... | collective-permute-start | bytes 196616 | tf_op jit(solution)/shard_map/ppermute | solution.py:200
  80.6 19.6 %collective-permute-start.12 = (f32[32,512]{1,0:T(8,128)S(1)}, f32[32,512]{1,0:T(8,128)S(1)}, u32[]{:S(2)}, u32[]{:S(2)}) collective-permute-start(f32[32,512]{1,0:T(8,128)S(1)} %get-tuple-element.37), channel_id=1, source_target_pairs={{0,128},{32,160},{64,192},{96,224},{128,256},{160,288},{192,320},{... | collective-permute-start | bytes 196616 | tf_op jit(solution)/shard_map/ppermute | solution.py:200
  83.4 19.6 %collective-permute-start.17 = (f32[32,512]{1,0:T(8,128)S(1)}, f32[32,512]{1,0:T(8,128)S(1)}, u32[]{:S(2)}, u32[]{:S(2)}) collective-permute-start(f32[32,512]{1,0:T(8,128)S(1)} %get-tuple-element.44), channel_id=1, source_target_pairs={{0,128},{32,160},{64,192},{96,224},{128,256},{160,288},{192,320},{... | collective-permute-start | bytes 196616 | tf_op jit(solution)/shard_map/ppermute | solution.py:200
  90.3 15.1 %collective-permute-start.14 = (f32[32,512]{1,0:T(8,128)S(1)}, f32[32,512]{1,0:T(8,128)S(1)}, u32[]{:S(2)}, u32[]{:S(2)}) collective-permute-start(f32[32,512]{1,0:T(8,128)S(1)} %get-tuple-element.38), channel_id=1, source_target_pairs={{0,384},{32,416},{64,448},{96,480},{128,0},{160,32},{192,64},{224,... | collective-permute-start | bytes 196616 | tf_op jit(solution)/shard_map/ppermute | solution.py:200
  93.2 14.7 %collective-permute-start.19 = (f32[32,512]{1,0:T(8,128)S(1)}, f32[32,512]{1,0:T(8,128)S(1)}, u32[]{:S(2)}, u32[]{:S(2)}) collective-permute-start(f32[32,512]{1,0:T(8,128)S(1)} %shard_map.39), channel_id=1, source_target_pairs={{0,384},{32,416},{64,448},{96,480},{128,0},{160,32},{192,64},{224,... | collective-permute-start | bytes 196616 | tf_op jit(solution)/shard_map/ppermute | solution.py:200
  100.2 11.6 %collective-permute-start.13 = (f32[32,512]{1,0:T(8,128)S(1)}, f32[32,512]{1,0:T(8,128)S(1)}, u32[]{:S(2)}, u32[]{:S(2)}) collective-permute-start(f32[32,512]{1,0:T(8,128)S(1)} %shard_map.36), channel_id=1, source_target_pairs={{0,128},{32,160},{64,192},{96,224},{128,256},{160,288},{192,320},{... | collective-permute-start | bytes 196616 | tf_op jit(solution)/shard_map/ppermute | solution.py:200

commit v8 on v6

--- a/solution.py
+++ b/solution.py
@@ -20,7 +20,12 @@
 F32, BF16 = jnp.float32, jnp.bfloat16
 
 
-def call(kernel, outs, operands, specs=None, scratch=(), flops=0, nbytes=1 << 20):
+def call(kernel, outs, operands, specs=None, scratch=(), flops=0, nbytes=1 << 20, after=None):
+    if after is not None:
+        inner_kernel, count = kernel, len(operands)
+        kernel = lambda *refs: inner_kernel(*refs[:count], *refs[count + 1 :])
+        specs = [VMEM] * count + [pl.BlockSpec(memory_space=pl.ANY)]
+        operands = (*operands, after)
     outs = [o if isinstance(o[0], tuple) else (o, F32) for o in outs]
     return pl.pallas_call(
         kernel,
@@ -117,17 +122,8 @@
     return pl.ds(pl.multiple_of(index * SUB, SUB), SUB)
 
 
-def second_product_kernel(o2, s2, both, left_high, left_low, right_high, right_low, part, *refs):
-    sends, keeps = refs[0:2], refs[2:4]
-    last_high, last_low, far_high, far_low, total = refs[4:]
+def scatter(total, send, keep):
     z, y = lax.axis_index("layer"), lax.axis_index("col")
-    place(0, o2, s2, *halves(both), (last_high, last_low), (far_high, far_low))
-    known = part.shape[0]
-    total[:known, : part.shape[1]] = part[...]
-    total[known:, : part.shape[1]] = product(last_high[...], last_low[...], right_high[...], right_low[...])
-    columns = pl.ds(part.shape[1], 2 * TILE)
-    total[:known, columns] = product(left_high[...], left_low[...], far_high[...], far_low[...])
-    total[known:, columns] = product(last_high[...], last_low[...], far_high[...], far_low[...])
 
     def rows_of(layer):
         t = lax.rem(layer // 4 - y + N_COL, N_COL)
@@ -135,13 +131,49 @@
         return strip(index * 4 + lax.rem(layer, 4))
 
     for j in range(N_LAYER // 2):
-        keep = rows_of(lax.rem(z + 2 * j, N_LAYER))
-        send = rows_of(lax.rem(z + turn() + 2 * j + N_LAYER, N_LAYER))
         rows = pl.ds(j * SUB, SUB)
-        for half in range(2):
-            columns = pl.ds(half * 4 * TILE, 4 * TILE)
-            keeps[half][rows, :] = total[keep, columns]
-            sends[half][rows, :] = total[send, columns]
+        keep[rows, :] = total[rows_of(lax.rem(z + 2 * j, N_LAYER)), :]
+        send[rows, :] = total[rows_of(lax.rem(z + turn() + 2 * j + N_LAYER, N_LAYER)), :]
+
+
+def second_product_kernel(o2, s2, both, right_high, right_low, part, send, keep, last_high, last_low, total):
+    swapped = both.at[pl.ds(s2.shape[0], s2.shape[0]), :]
+
+    @pl.when(core() == 0)
+    def _():
+        take_left(0, o2, last_high, last_low)
+
+    @pl.when(core() == 1)
+    def _():
+        take_left(0, swapped, last_high, last_low)
+
+    known, columns = part.shape[0], pl.ds(0, total.shape[1])
+    total[:known, :] = part[:, columns]
+    total[known:, :] = product(last_high[...], last_low[...], right_high[:, columns], right_low[:, columns])
+    scatter(total, send, keep)
+
+
+def third_product_kernel(o2, s2, both, last_high, last_low, left_high, left_low, right_high, right_low, part, *refs):
+    send, keep, far_high, far_low, total = refs
+    o2_swapped, s2_swapped = halves(both)
+
+    @pl.when(core() == 0)
+    def _():
+        take_right(0, 0, s2_swapped, far_high, far_low)
+        take_right(0, 1, o2_swapped, far_high, far_low)
+
+    @pl.when(core() == 1)
+    def _():
+        take_right(0, 0, s2, far_high, far_low)
+        take_right(0, 1, o2, far_high, far_low)
+
+    known, wide = part.shape[0], 2 * TILE
+    columns = pl.ds(part.shape[1] - wide, wide)
+    total[:known, :wide] = part[:, columns]
+    total[known:, :wide] = product(last_high[...], last_low[...], right_high[:, columns], right_low[:, columns])
+    total[:known, wide:] = product(left_high[...], left_low[...], far_high[...], far_low[...])
+    total[known:, wide:] = product(last_high[...], last_low[...], far_high[...], far_low[...])
+    scatter(total, send, keep)
 
 
 def stage_kernel(held, came, send, keep):
@@ -172,13 +204,18 @@
     out[:, half:] = second[...] + came[...]
 
 
-def last_kernel(first, second, from_below, from_above, out):
+def below_kernel(first, second, from_below, out):
+    half = first.shape[1]
+    out[:, :half] = first[...] + from_below[:, :half]
+    out[:, half:] = second[...] + from_below[:, half:]
+
+
+def last_kernel(held, from_above, out):
     x = lax.axis_index("row") // 2
     for index, t in enumerate(ORDER):
         source = pl.ds(index * 2 * TILE, 2 * TILE)
-        own = (first, second)[index // 2][:, pl.ds((index % 2) * 2 * TILE, 2 * TILE)]
         target = pl.ds(pl.multiple_of(lax.rem(x + t, N_X) * 2 * TILE, 2 * TILE), 2 * TILE)
-        out[:, target] = own + (from_below[:, source] + from_above[:, source])
+        out[:, target] = held[:, source] + from_above[:, source]
 
 
 def swap(value):
@@ -226,30 +263,42 @@
         flops=6 * known * wide * inner,
         nbytes=8 << 20,
     )
-    split_scratch = [pltpu.VMEM((TILE, inner), BF16)] * 2 + [pltpu.VMEM((inner, 2 * TILE), BF16)] * 2
-    made = call(
+    left_high, left_low, right_high, right_low, part = parts
+    second = (o2, s2, swap_two(o2, s2))
+    out = (8 * SUB, 4 * TILE)
+    total = pltpu.VMEM((4 * TILE, 4 * TILE), F32)
+    send_a, keep_a, *last = call(
         second_product_kernel,
-        [(8 * SUB, 4 * TILE)] * 4,
-        (o2, s2, swap_two(o2, s2), *parts),
-        scratch=split_scratch + [pltpu.VMEM((4 * TILE, 8 * TILE), F32)],
-        flops=6 * 7 * TILE * 2 * TILE * inner,
-        nbytes=8 << 20,
+        [out, out, ((TILE, inner), BF16), ((TILE, inner), BF16)],
+        (*second, right_high, right_low, part),
+        scratch=[total],
+        flops=6 * TILE * 4 * TILE * inner,
+        nbytes=4 << 20,
     )
-    sends, keeps = list(made[:2]), list(made[2:])
+    send_b, keep_b = call(
+        third_product_kernel,
+        [out, out],
+        (*second, *last, left_high, left_low, right_high, right_low, part),
+        scratch=[pltpu.VMEM((inner, 2 * TILE), BF16)] * 2 + [total],
+        flops=6 * 5 * TILE * 2 * TILE * inner,
+        nbytes=4 << 20,
+    )
+    sends, keeps = [send_a, send_b], [keep_a, keep_b]
     arrived = [pass_on(sends[half], 1) for half in range(2)]
+    done = None
     for half in range(2):
         sends[half], keeps[half] = call(
-            stage_kernel, [(4 * SUB, 4 * TILE)] * 2, (keeps[half], arrived[half])
+            stage_kernel, [(4 * SUB, 4 * TILE)] * 2, (keeps[half], arrived[half]), after=done
         )
+        done = keeps[half]
         arrived[half] = pass_on(sends[half], 2)
-    first, second = (
-        call(group_kernel, [(SUB, 4 * TILE)] * 4, (keeps[half], arrived[half])) for half in range(2)
-    )
+    first = call(group_kernel, [(SUB, 4 * TILE)] * 4, (keeps[0], arrived[0]))
+    second = call(group_kernel, [(SUB, 4 * TILE)] * 4, (keeps[1], arrived[1]), after=first[0])
     chunk = [(SUB, 8 * TILE)]
     (up,) = call(up_kernel, chunk, (first[1], second[1], shift_layers(first[2], 4)))
-    (down,) = call(down_kernel, chunk, (first[3], second[3], shift_layers(second[2], -4)))
-    ends = (first[0], second[0], shift_layers(up, 4), shift_layers(down, -4))
-    return call(last_kernel, chunk, ends)[0]
+    (down,) = call(down_kernel, chunk, (first[3], second[3], shift_layers(second[2], -4)), after=up)
+    (held,) = call(below_kernel, chunk, (first[0], second[0], shift_layers(up, 4)))
+    return call(last_kernel, chunk, (held, shift_layers(down, -4)))[0]
 
 
 def solution(mesh):

time: 111 us -> 106 us (0.955)
  the two profiles are of different devices: /device:TPU:6 before, /device:TPU:24 now
where the time goes in v8:
time: 106 us
  starting transfers between devices  55.1 us (52%)
  waiting for transfers between devices  41.1 us (39%)
  Pallas kernels  7.6 us (7%)
  local copies, waits for them, and re-layouts  1.7 us (2%)
    ppermute x4, waiting for transfers between devices, pass_on(): return lax.ppermute(value, ('layer', 'row'), pairs)  25.3 us
    ppermute x6, starting transfers between devices, fetch(): return lax.ppermute(value, ('row', 'col'), pairs)  22.3 us
    ppermute x4, starting transfers between devices, shift_layers(): lax.ppermute(value, 'layer', [(z, (z + distance) % N_LAYER) for z in rang...  17 us
    ppermute x4, waiting for transfers between devices, shift_layers(): lax.ppermute(value, 'layer', [(z, (z + distance) % N_LAYER) for z in rang...  10.8 us
    ppermute x4, starting transfers between devices, pass_on(): return lax.ppermute(value, ('layer', 'row'), pairs)  8.06 us
    ppermute x4, starting transfers between devices, swap(): return lax.ppermute(value, 'row', [(i, i ^ 1) for i in range(N_ROW)])  7.68 us
    pallas_call x15, Pallas kernels, call(): pl.pallas_call(kernel, out_shape=tuple((jax.ShapeDtypeStruct(s, d) for s,...  7.6 us
    ppermute x6, waiting for transfers between devices, fetch(): return lax.ppermute(value, ('row', 'col'), pairs)  4.88 us
  transfers between devices with their start and end apart: 18, of which 9 were waited for; matrix products, arithmetic and copies ran while one was open for 0% of the time, Pallas kernels for 5%

profile of v8, /device:TPU:24, one launch (start us, length us, event | category | flops | bytes accessed | tf_op | source)
XLA Modules:
  0.0 105.7 jit_solution(3665345089665068114)
XLA Ops:
  2.3 1.9 %collective-permute-start.2 = (f32[1024,128]{1,0:T(8,128)S(1)}, f32[1024,128]{1,0:T(8,128)S(1)}, u32[]{:S(2)}, u32[]{:S(2)}) collective-permute-start(f32[1024,128]{1,0:T(8,128)S(1)} %shard_map.28.own), channel_id=1, source_target_pairs={{0,4},{4,0},{8,12},{12,8},{16,20},{20,16},{24,28},{28,24},{1,5},{5... | collective-permute-start | bytes 1572872 | tf_op jit(solution)/shard_map/ppermute | solution.py:222
  4.2 2.7 %collective-permute-start = (f32[1024,128]{1,0:T(8,128)S(1)}, f32[1024,128]{1,0:T(8,128)S(1)}, u32[]{:S(2)}, u32[]{:S(2)}) collective-permute-start(f32[1024,128]{1,0:T(8,128)S(1)} %shard_map.28.own), channel_id=1, source_target_pairs={{1,0},{12,4},{2,1},{13,5},{3,2},{14,6},{0,3},{15,7},{9,8},{20,12},... | collective-permute-start | bytes 1572872 | tf_op jit(solution)/shard_map/ppermute | solution.py:231
  6.9 6.8 %collective-permute-start.3 = (f32[1024,128]{1,0:T(8,128)S(1)}, f32[1024,128]{1,0:T(8,128)S(1)}, u32[]{:S(2)}, u32[]{:S(2)}) collective-permute-start(f32[1024,128]{1,0:T(8,128)S(1)} %collective-permute-done.2.other), channel_id=1, source_target_pairs={{3,0},{28,4},{0,1},{29,5},{1,2},{30,6},{2,3},{31,7},{11,8},{4,12},... | collective-permute-start | bytes 1572872 | tf_op jit(solution)/shard_map/ppermute | solution.py:231
  13.7 3.9 %collective-permute-start.7 = (f32[1024,128]{1,0:T(8,128)S(1)}, f32[1024,128]{1,0:T(8,128)S(1)}, u32[]{:S(2)}, u32[]{:S(2)}) collective-permute-start(f32[1024,128]{1,0:T(8,128)S(1)} %shard_map.28.own), channel_id=1, source_target_pairs={{3,0},{28,4},{0,1},{29,5},{1,2},{30,6},{2,3},{31,7},{11,8},{4,12},... | collective-permute-start | bytes 1572872 | tf_op jit(solution)/shard_map/ppermute | solution.py:231
  17.6 1.9 %collective-permute-start.6 = (f32[1024,128]{1,0:T(8,128)S(1)}, f32[1024,128]{1,0:T(8,128)S(1)}, u32[]{:S(2)}, u32[]{:S(2)}) collective-permute-start(f32[1024,128]{1,0:T(8,128)S(1)} %collective-permute-done.2.other), channel_id=1, source_target_pairs={{1,0},{12,4},{2,1},{13,5},{3,2},{14,6},{0,3},{15,7},{9,8},{20,12},... | collective-permute-start | bytes 1572872 | tf_op jit(solution)/shard_map/ppermute | solution.py:231
  19.5 1.9 %collective-permute-start.1 = (f32[1024,128]{1,0:T(8,128)S(1)}, f32[1024,128]{1,0:T(8,128)S(1)}, u32[]{:S(2)}, u32[]{:S(2)}) collective-permute-start(f32[1024,128]{1,0:T(8,128)S(1)} %collective-permute-done.first.o1), channel_id=1, source_target_pairs={{1,0},{12,4},{2,1},{13,5},{3,2},{14,6},{0,3},{15,7},{9,8},{20,12},... | collective-permute-start | bytes 1572872 | tf_op jit(solution)/shard_map/ppermute | solution.py:231
  21.5 5.1 %collective-permute-start.4 = (f32[1024,128]{1,0:T(8,128)S(1)}, f32[1024,128]{1,0:T(8,128)S(1)}, u32[]{:S(2)}, u32[]{:S(2)}) collective-permute-start(f32[1024,128]{1,0:T(8,128)S(1)} %collective-permute-done.3.second.s3), channel_id=1, source_target_pairs={{3,0},{28,4},{0,1},{29,5},{1,2},{30,6},{2,3},{31,7},{11,8},{4,12},... | collective-permute-start | bytes 1572872 | tf_op jit(solution)/shard_map/ppermute | solution.py:231
  26.7 1.9 %collective-permute-start.8 = (f32[2048,128]{1,0:T(8,128)S(1)}, f32[2048,128]{1,0:T(8,128)S(1)}, u32[]{:S(2)}, u32[]{:S(2)}) collective-permute-start(f32[2048,128]{1,0:T(8,128)S(1)} %shard_map.30), channel_id=1, source_target_pairs={{0,4},{4,0},{8,12},{12,8},{16,20},{20,16},{24,28},{28,24},{1,5},{5... | collective-permute-start | bytes 3145736 | tf_op jit(solution)/shard_map/ppermute | solution.py:222
  30.0 1.9 %collective-permute-start.9 = (f32[2048,128]{1,0:T(8,128)S(1)}, f32[2048,128]{1,0:T(8,128)S(1)}, u32[]{:S(2)}, u32[]{:S(2)}) collective-permute-start(f32[2048,128]{1,0:T(8,128)S(1)} %shard_map.31), channel_id=1, source_target_pairs={{0,4},{4,0},{8,12},{12,8},{16,20},{20,16},{24,28},{28,24},{1,5},{5... | collective-permute-start | bytes 3145736 | tf_op jit(solution)/shard_map/ppermute | solution.py:222
  31.9 3.6 %collective-permute-done.1.first.o2 = f32[1024,128]{1,0:T(8,128)S(1)} collective-permute-done((f32[1024,128]{1,0:T(8,128)S(1)}, f32[1024,128]{1,0:T(8,128)S(1)}, u32[]{:S(2)}, u32[]{:S(2)}) %collective-permute-start.1) | collective-permute-done | bytes 524320 | tf_op jit(solution)/shard_map/ppermute | solution.py:231
  35.6 1.9 %collective-permute-start.5 = (f32[2048,128]{1,0:T(8,128)S(1)}, f32[2048,128]{1,0:T(8,128)S(1)}, u32[]{:S(2)}, u32[]{:S(2)}) collective-permute-start(f32[2048,128]{1,0:T(8,128)S(1)} %shard_map.29), channel_id=1, source_target_pairs={{0,4},{4,0},{8,12},{12,8},{16,20},{20,16},{24,28},{28,24},{1,5},{5... | collective-permute-start | bytes 3145736 | tf_op jit(solution)/shard_map/ppermute | solution.py:222
  37.5 3.4 %shard_map.32 = (bf16[384,1024]{1,0:T(8,128)(2,1)S(1)}, bf16[384,1024]{1,0:T(8,128)(2,1)S(1)}, bf16[1024,768]{1,0:T(8,128)(2,1)S(1)}, bf16[1024,768]{1,0:T(8,128)(2,1)S(1)}, f32[384,768]{1,0:T(8,128)S(1)}) custom-call(f32[1024,128]{1,0:T(8,128)S(1)} %shard_map.28.own, f32[1024,128]{1,0:T(8,128)S(1)} %collective-permute-done.2.other, ...), custom_call_target="tpu_custom_call" | custom-call | flops 1811939328 | bytes 8388608 | tf_op jit(solution)/shard_map/pallas_call | solution.py:30
  41.9 1.9 %collective-permute-start.10 = (f32[256,512]{1,0:T(8,128)S(1)}, f32[256,512]{1,0:T(8,128)S(1)}, u32[]{:S(2)}, u32[]{:S(2)}) collective-permute-start(f32[256,512]{1,0:T(8,128)S(1)} %get-tuple-element.32), channel_id=1, source_target_pairs={{0,32},{4,484},{8,40},{12,492},{16,48},{20,500},{24,56},{28,508},{... | collective-permute-start | bytes 1572872 | tf_op jit(solution)/shard_map/ppermute | solution.py:240
  45.4 2.3 %collective-permute-start.12 = (f32[256,512]{1,0:T(8,128)S(1)}, f32[256,512]{1,0:T(8,128)S(1)}, u32[]{:S(2)}, u32[]{:S(2)}) collective-permute-start(f32[256,512]{1,0:T(8,128)S(1)} %get-tuple-element.41), channel_id=1, source_target_pairs={{0,32},{4,484},{8,40},{12,492},{16,48},{20,500},{24,56},{28,508},{... | collective-permute-start | bytes 1572872 | tf_op jit(solution)/shard_map/ppermute | solution.py:240
  47.7 9.3 %collective-permute-done.10.came = f32[256,512]{1,0:T(8,128)S(1)} collective-permute-done((f32[256,512]{1,0:T(8,128)S(1)}, f32[256,512]{1,0:T(8,128)S(1)}, u32[]{:S(2)}, u32[]{:S(2)}) %collective-permute-start.10) | collective-permute-done | bytes 524320 | tf_op jit(solution)/shard_map/ppermute | solution.py:240
  59.0 3.6 %collective-permute-done.12.refs_1_ = f32[256,512]{1,0:T(8,128)S(1)} collective-permute-done((f32[256,512]{1,0:T(8,128)S(1)}, f32[256,512]{1,0:T(8,128)S(1)}, u32[]{:S(2)}, u32[]{:S(2)}) %collective-permute-start.12) | collective-permute-done | bytes 524320 | tf_op jit(solution)/shard_map/ppermute | solution.py:240
  62.7 1.9 %collective-permute-start.13 = (f32[128,512]{1,0:T(8,128)S(1)}, f32[128,512]{1,0:T(8,128)S(1)}, u32[]{:S(2)}, u32[]{:S(2)}) collective-permute-start(f32[128,512]{1,0:T(8,128)S(1)} %get-tuple-element.43), channel_id=1, source_target_pairs={{0,64},{4,452},{8,72},{12,460},{16,80},{20,468},{24,88},{28,476},{... | collective-permute-start | bytes 786440 | tf_op jit(solution)/shard_map/ppermute | solution.py:240
  64.6 5.2 %collective-permute-done.11.came = f32[128,512]{1,0:T(8,128)S(1)} collective-permute-done((f32[128,512]{1,0:T(8,128)S(1)}, f32[128,512]{1,0:T(8,128)S(1)}, u32[]{:S(2)}, u32[]{:S(2)}) %collective-permute-start.11) | collective-permute-done | bytes 262176 | tf_op jit(solution)/shard_map/ppermute | solution.py:240
  71.8 7.2 %collective-permute-done.13.refs_1_ = f32[128,512]{1,0:T(8,128)S(1)} collective-permute-done((f32[128,512]{1,0:T(8,128)S(1)}, f32[128,512]{1,0:T(8,128)S(1)}, u32[]{:S(2)}, u32[]{:S(2)}) %collective-permute-start.13) | collective-permute-done | bytes 262176 | tf_op jit(solution)/shard_map/ppermute | solution.py:240
  79.0 5.3 %collective-permute-start.16 = (f32[32,512]{1,0:T(8,128)S(1)}, f32[32,512]{1,0:T(8,128)S(1)}, u32[]{:S(2)}, u32[]{:S(2)}) collective-permute-start(f32[32,512]{1,0:T(8,128)S(1)} %get-tuple-element.50), channel_id=1, source_target_pairs={{0,384},{32,416},{64,448},{96,480},{128,0},{160,32},{192,64},{224,... | collective-permute-start | bytes 196616 | tf_op jit(solution)/shard_map/ppermute | solution.py:244
  84.4 4.4 %collective-permute-start.15 = (f32[32,1024]{1,0:T(8,128)S(1)}, f32[32,1024]{1,0:T(8,128)S(1)}, u32[]{:S(2)}, u32[]{:S(2)}) collective-permute-start(f32[32,1024]{1,0:T(8,128)S(1)} %shard_map.39.refs_3_), channel_id=1, source_target_pairs={{0,128},{32,160},{64,192},{96,224},{128,256},{160,288},{192,320},{... | collective-permute-start | bytes 393224 | tf_op jit(solution)/shard_map/ppermute | solution.py:244
  89.1 5.3 %collective-permute-start.17 = (f32[32,1024]{1,0:T(8,128)S(1)}, f32[32,1024]{1,0:T(8,128)S(1)}, u32[]{:S(2)}, u32[]{:S(2)}) collective-permute-start(f32[32,1024]{1,0:T(8,128)S(1)} %shard_map.41), channel_id=1, source_target_pairs={{0,384},{32,416},{64,448},{96,480},{128,0},{160,32},{192,64},{224,... | collective-permute-start | bytes 393224 | tf_op jit(solution)/shard_map/ppermute | solution.py:244
  94.4 6.0 %collective-permute-done.15.from_below = f32[32,1024]{1,0:T(8,128)S(1)} collective-permute-done((f32[32,1024]{1,0:T(8,128)S(1)}, f32[32,1024]{1,0:T(8,128)S(1)}, u32[]{:S(2)}, u32[]{:S(2)}) %collective-permute-start.15) | collective-permute-done | bytes 131104 | tf_op jit(solution)/shard_map/ppermute | solution.py:244
  100.5 4.6 %collective-permute-done.17.from_above = f32[32,1024]{1,0:T(8,128)S(1)} collective-permute-done((f32[32,1024]{1,0:T(8,128)S(1)}, f32[32,1024]{1,0:T(8,128)S(1)}, u32[]{:S(2)}, u32[]{:S(2)}) %collective-permute-start.17) | collective-permute-done | bytes 131104 | tf_op jit(solution)/shard_map/ppermute | solution.py:244
  (31 shorter events, 11.3 us)
Async XLA Ops:
  0.0 1.0 copy-start
  1.0 0.7 copy-start.1
  2.3 4.6 %collective-permute-start.2 = (f32[1024,128]{1,0:T(8,128)S(1)}, f32[1024,128]{1,0:T(8,128)S(1)}, u32[]{:S(2)}, u32[]{:S(2)}) collective-permute-start(f32[1024,128]{1,0:T(8,128)S(1)} %shard_map.28.own), channel_id=1, source_target_pairs={{0,4},{4,0},{8,12},{12,8},{16,20},{20,16},{24,28},{28,24},{1,5},{5... | collective-permute-start | bytes 1572872 | tf_op jit(solution)/shard_map/ppermute | solution.py:222
  4.2 15.3 %collective-permute-start = (f32[1024,128]{1,0:T(8,128)S(1)}, f32[1024,128]{1,0:T(8,128)S(1)}, u32[]{:S(2)}, u32[]{:S(2)}) collective-permute-start(f32[1024,128]{1,0:T(8,128)S(1)} %shard_map.28.own), channel_id=1, source_target_pairs={{1,0},{12,4},{2,1},{13,5},{3,2},{14,6},{0,3},{15,7},{9,8},{20,12},... | collective-permute-start | bytes 1572872 | tf_op jit(solution)/shard_map/ppermute | solution.py:231
  6.9 14.6 %collective-permute-start.3 = (f32[1024,128]{1,0:T(8,128)S(1)}, f32[1024,128]{1,0:T(8,128)S(1)}, u32[]{:S(2)}, u32[]{:S(2)}) collective-permute-start(f32[1024,128]{1,0:T(8,128)S(1)} %collective-permute-done.2.other), channel_id=1, source_target_pairs={{3,0},{28,4},{0,1},{29,5},{1,2},{30,6},{2,3},{31,7},{11,8},{4,12},... | collective-permute-start | bytes 1572872 | tf_op jit(solution)/shard_map/ppermute | solution.py:231
  13.7 13.0 %collective-permute-start.7 = (f32[1024,128]{1,0:T(8,128)S(1)}, f32[1024,128]{1,0:T(8,128)S(1)}, u32[]{:S(2)}, u32[]{:S(2)}) collective-permute-start(f32[1024,128]{1,0:T(8,128)S(1)} %shard_map.28.own), channel_id=1, source_target_pairs={{3,0},{28,4},{0,1},{29,5},{1,2},{30,6},{2,3},{31,7},{11,8},{4,12},... | collective-permute-start | bytes 1572872 | tf_op jit(solution)/shard_map/ppermute | solution.py:231
  17.6 12.3 %collective-permute-start.6 = (f32[1024,128]{1,0:T(8,128)S(1)}, f32[1024,128]{1,0:T(8,128)S(1)}, u32[]{:S(2)}, u32[]{:S(2)}) collective-permute-start(f32[1024,128]{1,0:T(8,128)S(1)} %collective-permute-done.2.other), channel_id=1, source_target_pairs={{1,0},{12,4},{2,1},{13,5},{3,2},{14,6},{0,3},{15,7},{9,8},{20,12},... | collective-permute-start | bytes 1572872 | tf_op jit(solution)/shard_map/ppermute | solution.py:231
  19.5 16.0 %collective-permute-start.1 = (f32[1024,128]{1,0:T(8,128)S(1)}, f32[1024,128]{1,0:T(8,128)S(1)}, u32[]{:S(2)}, u32[]{:S(2)}) collective-permute-start(f32[1024,128]{1,0:T(8,128)S(1)} %collective-permute-done.first.o1), channel_id=1, source_target_pairs={{1,0},{12,4},{2,1},{13,5},{3,2},{14,6},{0,3},{15,7},{9,8},{20,12},... | collective-permute-start | bytes 1572872 | tf_op jit(solution)/shard_map/ppermute | solution.py:231
  21.5 14.0 %collective-permute-start.4 = (f32[1024,128]{1,0:T(8,128)S(1)}, f32[1024,128]{1,0:T(8,128)S(1)}, u32[]{:S(2)}, u32[]{:S(2)}) collective-permute-start(f32[1024,128]{1,0:T(8,128)S(1)} %collective-permute-done.3.second.s3), channel_id=1, source_target_pairs={{3,0},{28,4},{0,1},{29,5},{1,2},{30,6},{2,3},{31,7},{11,8},{4,12},... | collective-permute-start | bytes 1572872 | tf_op jit(solution)/shard_map/ppermute | solution.py:231
  26.7 10.8 %collective-permute-start.8 = (f32[2048,128]{1,0:T(8,128)S(1)}, f32[2048,128]{1,0:T(8,128)S(1)}, u32[]{:S(2)}, u32[]{:S(2)}) collective-permute-start(f32[2048,128]{1,0:T(8,128)S(1)} %shard_map.30), channel_id=1, source_target_pairs={{0,4},{4,0},{8,12},{12,8},{16,20},{20,16},{24,28},{28,24},{1,5},{5... | collective-permute-start | bytes 3145736 | tf_op jit(solution)/shard_map/ppermute | solution.py:222
  30.0 7.6 %collective-permute-start.9 = (f32[2048,128]{1,0:T(8,128)S(1)}, f32[2048,128]{1,0:T(8,128)S(1)}, u32[]{:S(2)}, u32[]{:S(2)}) collective-permute-start(f32[2048,128]{1,0:T(8,128)S(1)} %shard_map.31), channel_id=1, source_target_pairs={{0,4},{4,0},{8,12},{12,8},{16,20},{20,16},{24,28},{28,24},{1,5},{5... | collective-permute-start | bytes 3145736 | tf_op jit(solution)/shard_map/ppermute | solution.py:222
  35.6 5.4 %collective-permute-start.5 = (f32[2048,128]{1,0:T(8,128)S(1)}, f32[2048,128]{1,0:T(8,128)S(1)}, u32[]{:S(2)}, u32[]{:S(2)}) collective-permute-start(f32[2048,128]{1,0:T(8,128)S(1)} %shard_map.29), channel_id=1, source_target_pairs={{0,4},{4,0},{8,12},{12,8},{16,20},{20,16},{24,28},{28,24},{1,5},{5... | collective-permute-start | bytes 3145736 | tf_op jit(solution)/shard_map/ppermute | solution.py:222
  41.9 15.1 %collective-permute-start.10 = (f32[256,512]{1,0:T(8,128)S(1)}, f32[256,512]{1,0:T(8,128)S(1)}, u32[]{:S(2)}, u32[]{:S(2)}) collective-permute-start(f32[256,512]{1,0:T(8,128)S(1)} %get-tuple-element.32), channel_id=1, source_target_pairs={{0,32},{4,484},{8,40},{12,492},{16,48},{20,500},{24,56},{28,508},{... | collective-permute-start | bytes 1572872 | tf_op jit(solution)/shard_map/ppermute | solution.py:240
  45.4 17.2 %collective-permute-start.12 = (f32[256,512]{1,0:T(8,128)S(1)}, f32[256,512]{1,0:T(8,128)S(1)}, u32[]{:S(2)}, u32[]{:S(2)}) collective-permute-start(f32[256,512]{1,0:T(8,128)S(1)} %get-tuple-element.41), channel_id=1, source_target_pairs={{0,32},{4,484},{8,40},{12,492},{16,48},{20,500},{24,56},{28,508},{... | collective-permute-start | bytes 1572872 | tf_op jit(solution)/shard_map/ppermute | solution.py:240
  57.1 12.8 %collective-permute-start.11 = (f32[128,512]{1,0:T(8,128)S(1)}, f32[128,512]{1,0:T(8,128)S(1)}, u32[]{:S(2)}, u32[]{:S(2)}) collective-permute-start(f32[128,512]{1,0:T(8,128)S(1)} %get-tuple-element.34), channel_id=1, source_target_pairs={{0,64},{4,452},{8,72},{12,460},{16,80},{20,468},{24,88},{28,476},{... | collective-permute-start | bytes 786440 | tf_op jit(solution)/shard_map/ppermute | solution.py:240
  62.7 16.3 %collective-permute-start.13 = (f32[128,512]{1,0:T(8,128)S(1)}, f32[128,512]{1,0:T(8,128)S(1)}, u32[]{:S(2)}, u32[]{:S(2)}) collective-permute-start(f32[128,512]{1,0:T(8,128)S(1)} %get-tuple-element.43), channel_id=1, source_target_pairs={{0,64},{4,452},{8,72},{12,460},{16,80},{20,468},{24,88},{28,476},{... | collective-permute-start | bytes 786440 | tf_op jit(solution)/shard_map/ppermute | solution.py:240
  69.9 14.4 %collective-permute-start.14 = (f32[32,512]{1,0:T(8,128)S(1)}, f32[32,512]{1,0:T(8,128)S(1)}, u32[]{:S(2)}, u32[]{:S(2)}) collective-permute-start(f32[32,512]{1,0:T(8,128)S(1)} %get-tuple-element.47), channel_id=1, source_target_pairs={{0,128},{32,160},{64,192},{96,224},{128,256},{160,288},{192,320},{... | collective-permute-start | bytes 196616 | tf_op jit(solution)/shard_map/ppermute | solution.py:244
  79.0 10.1 %collective-permute-start.16 = (f32[32,512]{1,0:T(8,128)S(1)}, f32[32,512]{1,0:T(8,128)S(1)}, u32[]{:S(2)}, u32[]{:S(2)}) collective-permute-start(f32[32,512]{1,0:T(8,128)S(1)} %get-tuple-element.50), channel_id=1, source_target_pairs={{0,384},{32,416},{64,448},{96,480},{128,0},{160,32},{192,64},{224,... | collective-permute-start | bytes 196616 | tf_op jit(solution)/shard_map/ppermute | solution.py:244
  84.4 16.1 %collective-permute-start.15 = (f32[32,1024]{1,0:T(8,128)S(1)}, f32[32,1024]{1,0:T(8,128)S(1)}, u32[]{:S(2)}, u32[]{:S(2)}) collective-permute-start(f32[32,1024]{1,0:T(8,128)S(1)} %shard_map.39.refs_3_), channel_id=1, source_target_pairs={{0,128},{32,160},{64,192},{96,224},{128,256},{160,288},{192,320},{... | collective-permute-start | bytes 393224 | tf_op jit(solution)/shard_map/ppermute | solution.py:244
  89.1 15.9 %collective-permute-start.17 = (f32[32,1024]{1,0:T(8,128)S(1)}, f32[32,1024]{1,0:T(8,128)S(1)}, u32[]{:S(2)}, u32[]{:S(2)}) collective-permute-start(f32[32,1024]{1,0:T(8,128)S(1)} %shard_map.41), channel_id=1, source_target_pairs={{0,384},{32,416},{64,448},{96,480},{128,0},{160,32},{192,64},{224,... | collective-permute-start | bytes 393224 | tf_op jit(solution)/shard_map/ppermute | solution.py:244

commit v9 on v8

--- a/solution.py
+++ b/solution.py
@@ -122,21 +122,16 @@
     return pl.ds(pl.multiple_of(index * SUB, SUB), SUB)
 
 
-def scatter(total, send, keep):
-    z, y = lax.axis_index("layer"), lax.axis_index("col")
-
-    def rows_of(layer):
-        t = lax.rem(layer // 4 - y + N_COL, N_COL)
-        index = jnp.where(t < 2, t, 5 - t)
-        return strip(index * 4 + lax.rem(layer, 4))
-
-    for j in range(N_LAYER // 2):
-        rows = pl.ds(j * SUB, SUB)
-        keep[rows, :] = total[rows_of(lax.rem(z + 2 * j, N_LAYER)), :]
-        send[rows, :] = total[rows_of(lax.rem(z + turn() + 2 * j + N_LAYER, N_LAYER)), :]
-
-
-def second_product_kernel(o2, s2, both, right_high, right_low, part, send, keep, last_high, last_low, total):
+def scatter(total, outs):
+    z = lax.axis_index("layer")
+    for shift, out in zip((0, 1, 3, 2), outs):
+        s = lax.rem(z + shift, 4)
+        for index in range(4):
+            out[pl.ds(index * SUB, SUB), :] = total[strip(index * 4 + s), :]
+
+
+def second_product_kernel(o2, s2, both, right_high, right_low, part, *refs):
+    outs, (last_high, last_low, total) = refs[:4], refs[4:]
     swapped = both.at[pl.ds(s2.shape[0], s2.shape[0]), :]
 
     @pl.when(core() == 0)
@@ -150,11 +145,11 @@
     known, columns = part.shape[0], pl.ds(0, total.shape[1])
     total[:known, :] = part[:, columns]
     total[known:, :] = product(last_high[...], last_low[...], right_high[:, columns], right_low[:, columns])
-    scatter(total, send, keep)
+    scatter(total, outs)
 
 
 def third_product_kernel(o2, s2, both, last_high, last_low, left_high, left_low, right_high, right_low, part, *refs):
-    send, keep, far_high, far_low, total = refs
+    outs, (far_high, far_low, total) = refs[:4], refs[4:]
     o2_swapped, s2_swapped = halves(both)
 
     @pl.when(core() == 0)
@@ -173,23 +168,15 @@
     total[known:, :wide] = product(last_high[...], last_low[...], right_high[:, columns], right_low[:, columns])
     total[:known, wide:] = product(left_high[...], left_low[...], far_high[...], far_low[...])
     total[known:, wide:] = product(last_high[...], last_low[...], far_high[...], far_low[...])
-    scatter(total, send, keep)
-
-
-def stage_kernel(held, came, send, keep):
-    count = held.shape[0] // SUB
-    for i in range(count // 2):
-        rows = pl.ds(i * SUB, SUB)
-        near = pl.ds(2 * i * SUB, SUB)
-        far = strip(lax.rem(turn() + 2 * i + count, count))
-        keep[rows, :] = held[near, :] + came[near, :]
-        send[rows, :] = held[far, :] + came[far, :]
-
-
-def group_kernel(held, came, own, up, far, down):
+    scatter(total, outs)
+
+
+def group_kernel(mine, below, above, two, own, up, far, down):
+    group, y = lax.axis_index("layer") // 4, lax.axis_index("col")
     for i, out in enumerate((own, up, far, down)):
-        rows = pl.ds(i * SUB, SUB)
-        out[...] = held[rows, :] + came[rows, :]
+        t = lax.rem(group + i - y + 4, 4)
+        rows = strip(jnp.where(t < 2, t, 5 - t))
+        out[...] = (mine[rows, :] + two[rows, :]) + (below[rows, :] + above[rows, :])
 
 
 def up_kernel(first, second, came, out):
@@ -198,10 +185,8 @@
     out[:, half:] = second[...]
 
 
-def down_kernel(first, second, came, out):
-    half = first.shape[1]
-    out[:, :half] = first[...]
-    out[:, half:] = second[...] + came[...]
+def add_kernel(held, came, out):
+    out[...] = held[...] + came[...]
 
 
 def below_kernel(first, second, from_below, out):
@@ -210,12 +195,15 @@
     out[:, half:] = second[...] + from_below[:, half:]
 
 
-def last_kernel(held, from_above, out):
-    x = lax.axis_index("row") // 2
+def last_kernel(held, above, out):
+    x, half = lax.axis_index("row") // 2, held.shape[1] // 2
     for index, t in enumerate(ORDER):
         source = pl.ds(index * 2 * TILE, 2 * TILE)
         target = pl.ds(pl.multiple_of(lax.rem(x + t, N_X) * 2 * TILE, 2 * TILE), 2 * TILE)
-        out[:, target] = held[:, source] + from_above[:, source]
+        value = held[:, source]
+        if index >= 2:
+            value = value + above[:, pl.ds(index * 2 * TILE - half, 2 * TILE)]
+        out[:, target] = value
 
 
 def swap(value):
@@ -265,40 +253,36 @@
     )
     left_high, left_low, right_high, right_low, part = parts
     second = (o2, s2, swap_two(o2, s2))
-    out = (8 * SUB, 4 * TILE)
+    outs = [(4 * SUB, 4 * TILE)] * 4
     total = pltpu.VMEM((4 * TILE, 4 * TILE), F32)
-    send_a, keep_a, *last = call(
+    *cut_a, last_high, last_low = call(
         second_product_kernel,
-        [out, out, ((TILE, inner), BF16), ((TILE, inner), BF16)],
+        outs + [((TILE, inner), BF16)] * 2,
         (*second, right_high, right_low, part),
         scratch=[total],
         flops=6 * TILE * 4 * TILE * inner,
         nbytes=4 << 20,
     )
-    send_b, keep_b = call(
+    cut_b = call(
         third_product_kernel,
-        [out, out],
-        (*second, *last, left_high, left_low, right_high, right_low, part),
+        outs,
+        (*second, last_high, last_low, left_high, left_low, right_high, right_low, part),
         scratch=[pltpu.VMEM((inner, 2 * TILE), BF16)] * 2 + [total],
         flops=6 * 5 * TILE * 2 * TILE * inner,
         nbytes=4 << 20,
     )
-    sends, keeps = [send_a, send_b], [keep_a, keep_b]
-    arrived = [pass_on(sends[half], 1) for half in range(2)]
-    done = None
-    for half in range(2):
-        sends[half], keeps[half] = call(
-            stage_kernel, [(4 * SUB, 4 * TILE)] * 2, (keeps[half], arrived[half]), after=done
-        )
-        done = keeps[half]
-        arrived[half] = pass_on(sends[half], 2)
-    first = call(group_kernel, [(SUB, 4 * TILE)] * 4, (keeps[0], arrived[0]))
-    second = call(group_kernel, [(SUB, 4 * TILE)] * 4, (keeps[1], arrived[1]), after=first[0])
-    chunk = [(SUB, 8 * TILE)]
-    (up,) = call(up_kernel, chunk, (first[1], second[1], shift_layers(first[2], 4)))
-    (down,) = call(down_kernel, chunk, (first[3], second[3], shift_layers(second[2], -4)), after=up)
-    (held,) = call(below_kernel, chunk, (first[0], second[0], shift_layers(up, 4)))
-    return call(last_kernel, chunk, (held, shift_layers(down, -4)))[0]
+
+    def neighbours(cut):
+        return cut[0], shift_layers(cut[1], 1), shift_layers(cut[2], -1), pass_on(cut[3], 2)
+
+    piece, chunk = (SUB, 4 * TILE), (SUB, 8 * TILE)
+    own_a, up_a, far_a, down_a = call(group_kernel, [piece] * 4, neighbours(cut_a))
+    own_b, up_b, far_b, down_b = call(group_kernel, [piece] * 4, neighbours(cut_b), after=own_a)
+    (up,) = call(up_kernel, [chunk], (up_a, up_b, shift_layers(far_a, 4)), flops=1 << 30)
+    (own_a,) = call(add_kernel, [piece], (own_a, shift_layers(down_a, -4)))
+    (down,) = call(add_kernel, [piece], (down_b, shift_layers(far_b, -4)), flops=1 << 30, after=own_a)
+    (held,) = call(below_kernel, [chunk], (own_a, own_b, shift_layers(up, 4)))
+    return call(last_kernel, [chunk], (held, shift_layers(down, -4)))[0]
 
 
 def solution(mesh):

time: 106 us -> 111 us (1.047)
  the two profiles are of different devices: /device:TPU:24 before, /device:TPU:6 now
where the time goes in v9:
time: 111 us
  starting transfers between devices  82.1 us (74%)
  waiting for transfers between devices  19.1 us (17%)
  Pallas kernels  7.42 us (7%)
  local copies, waits for them, and re-layouts  1.7 us (2%)
    ppermute x9, starting transfers between devices, shift_layers(): lax.ppermute(value, 'layer', [(z, (z + distance) % N_LAYER) for z in rang...  50 us
    ppermute x6, starting transfers between devices, fetch(): return lax.ppermute(value, ('row', 'col'), pairs)  19.7 us
    ppermute x4, starting transfers between devices, swap(): return lax.ppermute(value, 'row', [(i, i ^ 1) for i in range(N_ROW)])  8.27 us
    ppermute x2, waiting for transfers between devices, pass_on(): return lax.ppermute(value, ('layer', 'row'), pairs)  7.8 us
    pallas_call x14, Pallas kernels, call(): pl.pallas_call(kernel, out_shape=tuple((jax.ShapeDtypeStruct(s, d) for s,...  7.42 us
    ppermute x6, waiting for transfers between devices, fetch(): return lax.ppermute(value, ('row', 'col'), pairs)  5.85 us
    ppermute x9, waiting for transfers between devices, shift_layers(): lax.ppermute(value, 'layer', [(z, (z + distance) % N_LAYER) for z in rang...  5.46 us
    ppermute x2, starting transfers between devices, pass_on(): return lax.ppermute(value, ('layer', 'row'), pairs)  4.08 us
  transfers between devices with their start and end apart: 21, of which 7 were waited for; matrix products, arithmetic and copies ran while one was open for 0% of the time, Pallas kernels for 5%

profile of v9, /device:TPU:6, one launch (start us, length us, event | category | flops | bytes accessed | tf_op | source)
XLA Modules:
  0.0 110.7 jit_solution(15122327100937355759)
XLA Ops:
  2.3 1.9 %collective-permute-start.2 = (f32[1024,128]{1,0:T(8,128)S(1)}, f32[1024,128]{1,0:T(8,128)S(1)}, u32[]{:S(2)}, u32[]{:S(2)}) collective-permute-start(f32[1024,128]{1,0:T(8,128)S(1)} %shard_map.28.own), channel_id=1, source_target_pairs={{0,4},{4,0},{8,12},{12,8},{16,20},{20,16},{24,28},{28,24},{1,5},{5... | collective-permute-start | bytes 1572872 | tf_op jit(solution)/shard_map/ppermute | solution.py:210
  4.2 4.9 %collective-permute-start = (f32[1024,128]{1,0:T(8,128)S(1)}, f32[1024,128]{1,0:T(8,128)S(1)}, u32[]{:S(2)}, u32[]{:S(2)}) collective-permute-start(f32[1024,128]{1,0:T(8,128)S(1)} %shard_map.28.own), channel_id=1, source_target_pairs={{1,0},{12,4},{2,1},{13,5},{3,2},{14,6},{0,3},{15,7},{9,8},{20,12},... | collective-permute-start | bytes 1572872 | tf_op jit(solution)/shard_map/ppermute | solution.py:219
  9.2 1.9 %collective-permute-start.3 = (f32[1024,128]{1,0:T(8,128)S(1)}, f32[1024,128]{1,0:T(8,128)S(1)}, u32[]{:S(2)}, u32[]{:S(2)}) collective-permute-start(f32[1024,128]{1,0:T(8,128)S(1)} %collective-permute-done.2.other), channel_id=1, source_target_pairs={{3,0},{28,4},{0,1},{29,5},{1,2},{30,6},{2,3},{31,7},{11,8},{4,12},... | collective-permute-start | bytes 1572872 | tf_op jit(solution)/shard_map/ppermute | solution.py:219
  11.1 2.5 %collective-permute-start.7 = (f32[1024,128]{1,0:T(8,128)S(1)}, f32[1024,128]{1,0:T(8,128)S(1)}, u32[]{:S(2)}, u32[]{:S(2)}) collective-permute-start(f32[1024,128]{1,0:T(8,128)S(1)} %shard_map.28.own), channel_id=1, source_target_pairs={{3,0},{28,4},{0,1},{29,5},{1,2},{30,6},{2,3},{31,7},{11,8},{4,12},... | collective-permute-start | bytes 1572872 | tf_op jit(solution)/shard_map/ppermute | solution.py:219
  13.6 4.6 %collective-permute-start.6 = (f32[1024,128]{1,0:T(8,128)S(1)}, f32[1024,128]{1,0:T(8,128)S(1)}, u32[]{:S(2)}, u32[]{:S(2)}) collective-permute-start(f32[1024,128]{1,0:T(8,128)S(1)} %collective-permute-done.2.other), channel_id=1, source_target_pairs={{1,0},{12,4},{2,1},{13,5},{3,2},{14,6},{0,3},{15,7},{9,8},{20,12},... | collective-permute-start | bytes 1572872 | tf_op jit(solution)/shard_map/ppermute | solution.py:219
  18.2 3.9 %collective-permute-start.1 = (f32[1024,128]{1,0:T(8,128)S(1)}, f32[1024,128]{1,0:T(8,128)S(1)}, u32[]{:S(2)}, u32[]{:S(2)}) collective-permute-start(f32[1024,128]{1,0:T(8,128)S(1)} %collective-permute-done.first.o1), channel_id=1, source_target_pairs={{1,0},{12,4},{2,1},{13,5},{3,2},{14,6},{0,3},{15,7},{9,8},{20,12},... | collective-permute-start | bytes 1572872 | tf_op jit(solution)/shard_map/ppermute | solution.py:219
  24.0 3.0 %collective-permute-done.7.second.o3 = f32[1024,128]{1,0:T(8,128)S(1)} collective-permute-done((f32[1024,128]{1,0:T(8,128)S(1)}, f32[1024,128]{1,0:T(8,128)S(1)}, u32[]{:S(2)}, u32[]{:S(2)}) %collective-permute-start.7) | collective-permute-done | bytes 524320 | tf_op jit(solution)/shard_map/ppermute | solution.py:219
  29.1 2.4 %collective-permute-start.9 = (f32[2048,128]{1,0:T(8,128)S(1)}, f32[2048,128]{1,0:T(8,128)S(1)}, u32[]{:S(2)}, u32[]{:S(2)}) collective-permute-start(f32[2048,128]{1,0:T(8,128)S(1)} %shard_map.31), channel_id=1, source_target_pairs={{0,4},{4,0},{8,12},{12,8},{16,20},{20,16},{24,28},{28,24},{1,5},{5... | collective-permute-start | bytes 3145736 | tf_op jit(solution)/shard_map/ppermute | solution.py:210
  31.6 2.8 %collective-permute-done.4.second.s2 = f32[1024,128]{1,0:T(8,128)S(1)} collective-permute-done((f32[1024,128]{1,0:T(8,128)S(1)}, f32[1024,128]{1,0:T(8,128)S(1)}, u32[]{:S(2)}, u32[]{:S(2)}) %collective-permute-start.4) | collective-permute-done | bytes 524320 | tf_op jit(solution)/shard_map/ppermute | solution.py:219
  34.5 2.0 %collective-permute-start.5 = (f32[2048,128]{1,0:T(8,128)S(1)}, f32[2048,128]{1,0:T(8,128)S(1)}, u32[]{:S(2)}, u32[]{:S(2)}) collective-permute-start(f32[2048,128]{1,0:T(8,128)S(1)} %shard_map.29), channel_id=1, source_target_pairs={{0,4},{4,0},{8,12},{12,8},{16,20},{20,16},{24,28},{28,24},{1,5},{5... | collective-permute-start | bytes 3145736 | tf_op jit(solution)/shard_map/ppermute | solution.py:210
  36.5 3.4 %shard_map.32 = (bf16[384,1024]{1,0:T(8,128)(2,1)S(1)}, bf16[384,1024]{1,0:T(8,128)(2,1)S(1)}, bf16[1024,768]{1,0:T(8,128)(2,1)S(1)}, bf16[1024,768]{1,0:T(8,128)(2,1)S(1)}, f32[384,768]{1,0:T(8,128)S(1)}) custom-call(f32[1024,128]{1,0:T(8,128)S(1)} %shard_map.28.own, f32[1024,128]{1,0:T(8,128)S(1)} %collective-permute-done.2.other, ...), custom_call_target="tpu_custom_call" | custom-call | flops 1811939328 | bytes 8388608 | tf_op jit(solution)/shard_map/pallas_call | solution.py:30
  40.8 3.7 %collective-permute-start.10 = (f32[128,512]{1,0:T(8,128)S(1)}, f32[128,512]{1,0:T(8,128)S(1)}, u32[]{:S(2)}, u32[]{:S(2)}) collective-permute-start(f32[128,512]{1,0:T(8,128)S(1)} %get-tuple-element.32), channel_id=1, source_target_pairs={{0,32},{32,64},{64,96},{96,128},{128,160},{160,192},{192,224},{224... | collective-permute-start | bytes 786440 | tf_op jit(solution)/shard_map/ppermute | solution.py:232
  44.5 9.5 %collective-permute-start.11 = (f32[128,512]{1,0:T(8,128)S(1)}, f32[128,512]{1,0:T(8,128)S(1)}, u32[]{:S(2)}, u32[]{:S(2)}) collective-permute-start(f32[128,512]{1,0:T(8,128)S(1)} %get-tuple-element.33), channel_id=1, source_target_pairs={{0,480},{32,0},{64,32},{96,64},{128,96},{160,128},{192,160},{224,1... | collective-permute-start | bytes 786440 | tf_op jit(solution)/shard_map/ppermute | solution.py:232
  54.1 1.9 %collective-permute-start.12 = (f32[128,512]{1,0:T(8,128)S(1)}, f32[128,512]{1,0:T(8,128)S(1)}, u32[]{:S(2)}, u32[]{:S(2)}) collective-permute-start(f32[128,512]{1,0:T(8,128)S(1)} %get-tuple-element.34), channel_id=1, source_target_pairs={{0,64},{4,452},{8,72},{12,460},{16,80},{20,468},{24,88},{28,476},{... | collective-permute-start | bytes 786440 | tf_op jit(solution)/shard_map/ppermute | solution.py:228
  57.5 1.9 %collective-permute-start.14 = (f32[128,512]{1,0:T(8,128)S(1)}, f32[128,512]{1,0:T(8,128)S(1)}, u32[]{:S(2)}, u32[]{:S(2)}) collective-permute-start(f32[128,512]{1,0:T(8,128)S(1)} %get-tuple-element.42), channel_id=1, source_target_pairs={{0,32},{32,64},{64,96},{96,128},{128,160},{160,192},{192,224},{224... | collective-permute-start | bytes 786440 | tf_op jit(solution)/shard_map/ppermute | solution.py:232
  59.4 5.1 %collective-permute-start.15 = (f32[128,512]{1,0:T(8,128)S(1)}, f32[128,512]{1,0:T(8,128)S(1)}, u32[]{:S(2)}, u32[]{:S(2)}) collective-permute-start(f32[128,512]{1,0:T(8,128)S(1)} %get-tuple-element.43), channel_id=1, source_target_pairs={{0,480},{32,0},{64,32},{96,64},{128,96},{160,128},{192,160},{224,1... | collective-permute-start | bytes 786440 | tf_op jit(solution)/shard_map/ppermute | solution.py:232
  64.6 2.2 %collective-permute-start.16 = (f32[128,512]{1,0:T(8,128)S(1)}, f32[128,512]{1,0:T(8,128)S(1)}, u32[]{:S(2)}, u32[]{:S(2)}) collective-permute-start(f32[128,512]{1,0:T(8,128)S(1)} %get-tuple-element.44), channel_id=1, source_target_pairs={{0,64},{4,452},{8,72},{12,460},{16,80},{20,468},{24,88},{28,476},{... | collective-permute-start | bytes 786440 | tf_op jit(solution)/shard_map/ppermute | solution.py:228
  68.0 8.0 %collective-permute-start.17 = (f32[32,512]{1,0:T(8,128)S(1)}, f32[32,512]{1,0:T(8,128)S(1)}, u32[]{:S(2)}, u32[]{:S(2)}) collective-permute-start(f32[32,512]{1,0:T(8,128)S(1)} %get-tuple-element.48), channel_id=1, source_target_pairs={{0,128},{32,160},{64,192},{96,224},{128,256},{160,288},{192,320},{... | collective-permute-start | bytes 196616 | tf_op jit(solution)/shard_map/ppermute | solution.py:232
  76.0 6.7 %collective-permute-done.16.refs_3_ = f32[128,512]{1,0:T(8,128)S(1)} collective-permute-done((f32[128,512]{1,0:T(8,128)S(1)}, f32[128,512]{1,0:T(8,128)S(1)}, u32[]{:S(2)}, u32[]{:S(2)}) %collective-permute-start.16) | collective-permute-done | bytes 262176 | tf_op jit(solution)/shard_map/ppermute | solution.py:228
  82.7 6.0 %collective-permute-start.19 = (f32[32,512]{1,0:T(8,128)S(1)}, f32[32,512]{1,0:T(8,128)S(1)}, u32[]{:S(2)}, u32[]{:S(2)}) collective-permute-start(f32[32,512]{1,0:T(8,128)S(1)} %get-tuple-element.50), channel_id=1, source_target_pairs={{0,384},{32,416},{64,448},{96,480},{128,0},{160,32},{192,64},{224,... | collective-permute-start | bytes 196616 | tf_op jit(solution)/shard_map/ppermute | solution.py:232
  88.7 4.3 %collective-permute-start.13 = (f32[32,512]{1,0:T(8,128)S(1)}, f32[32,512]{1,0:T(8,128)S(1)}, u32[]{:S(2)}, u32[]{:S(2)}) collective-permute-start(f32[32,512]{1,0:T(8,128)S(1)} %get-tuple-element.36), channel_id=1, source_target_pairs={{0,384},{32,416},{64,448},{96,480},{128,0},{160,32},{192,64},{224,... | collective-permute-start | bytes 196616 | tf_op jit(solution)/shard_map/ppermute | solution.py:232
  93.1 5.4 %collective-permute-start.18 = (f32[32,1024]{1,0:T(8,128)S(1)}, f32[32,1024]{1,0:T(8,128)S(1)}, u32[]{:S(2)}, u32[]{:S(2)}) collective-permute-start(f32[32,1024]{1,0:T(8,128)S(1)} %shard_map.38), channel_id=1, source_target_pairs={{0,128},{32,160},{64,192},{96,224},{128,256},{160,288},{192,320},{... | collective-permute-start | bytes 393224 | tf_op jit(solution)/shard_map/ppermute | solution.py:232
  98.9 6.0 %collective-permute-start.20 = (f32[32,512]{1,0:T(8,128)S(1)}, f32[32,512]{1,0:T(8,128)S(1)}, u32[]{:S(2)}, u32[]{:S(2)}) collective-permute-start(f32[32,512]{1,0:T(8,128)S(1)} %shard_map.40), channel_id=1, source_target_pairs={{0,384},{32,416},{64,448},{96,480},{128,0},{160,32},{192,64},{224,... | collective-permute-start | bytes 196616 | tf_op jit(solution)/shard_map/ppermute | solution.py:232
  104.9 3.2 %collective-permute-done.18.from_below = f32[32,1024]{1,0:T(8,128)S(1)} collective-permute-done((f32[32,1024]{1,0:T(8,128)S(1)}, f32[32,1024]{1,0:T(8,128)S(1)}, u32[]{:S(2)}, u32[]{:S(2)}) %collective-permute-start.18) | collective-permute-done | bytes 131104 | tf_op jit(solution)/shard_map/ppermute | solution.py:232
  (36 shorter events, 12.9 us)
Async XLA Ops:
  0.0 1.0 copy-start
  1.0 0.7 copy-start.1
  2.3 6.9 %collective-permute-start.2 = (f32[1024,128]{1,0:T(8,128)S(1)}, f32[1024,128]{1,0:T(8,128)S(1)}, u32[]{:S(2)}, u32[]{:S(2)}) collective-permute-start(f32[1024,128]{1,0:T(8,128)S(1)} %shard_map.28.own), channel_id=1, source_target_pairs={{0,4},{4,0},{8,12},{12,8},{16,20},{20,16},{24,28},{28,24},{1,5},{5... | collective-permute-start | bytes 1572872 | tf_op jit(solution)/shard_map/ppermute | solution.py:210
  4.2 13.9 %collective-permute-start = (f32[1024,128]{1,0:T(8,128)S(1)}, f32[1024,128]{1,0:T(8,128)S(1)}, u32[]{:S(2)}, u32[]{:S(2)}) collective-permute-start(f32[1024,128]{1,0:T(8,128)S(1)} %shard_map.28.own), channel_id=1, source_target_pairs={{1,0},{12,4},{2,1},{13,5},{3,2},{14,6},{0,3},{15,7},{9,8},{20,12},... | collective-permute-start | bytes 1572872 | tf_op jit(solution)/shard_map/ppermute | solution.py:219
  9.2 12.9 %collective-permute-start.3 = (f32[1024,128]{1,0:T(8,128)S(1)}, f32[1024,128]{1,0:T(8,128)S(1)}, u32[]{:S(2)}, u32[]{:S(2)}) collective-permute-start(f32[1024,128]{1,0:T(8,128)S(1)} %collective-permute-done.2.other), channel_id=1, source_target_pairs={{3,0},{28,4},{0,1},{29,5},{1,2},{30,6},{2,3},{31,7},{11,8},{4,12},... | collective-permute-start | bytes 1572872 | tf_op jit(solution)/shard_map/ppermute | solution.py:219
  11.1 16.0 %collective-permute-start.7 = (f32[1024,128]{1,0:T(8,128)S(1)}, f32[1024,128]{1,0:T(8,128)S(1)}, u32[]{:S(2)}, u32[]{:S(2)}) collective-permute-start(f32[1024,128]{1,0:T(8,128)S(1)} %shard_map.28.own), channel_id=1, source_target_pairs={{3,0},{28,4},{0,1},{29,5},{1,2},{30,6},{2,3},{31,7},{11,8},{4,12},... | collective-permute-start | bytes 1572872 | tf_op jit(solution)/shard_map/ppermute | solution.py:219
  13.6 15.5 %collective-permute-start.6 = (f32[1024,128]{1,0:T(8,128)S(1)}, f32[1024,128]{1,0:T(8,128)S(1)}, u32[]{:S(2)}, u32[]{:S(2)}) collective-permute-start(f32[1024,128]{1,0:T(8,128)S(1)} %collective-permute-done.2.other), channel_id=1, source_target_pairs={{1,0},{12,4},{2,1},{13,5},{3,2},{14,6},{0,3},{15,7},{9,8},{20,12},... | collective-permute-start | bytes 1572872 | tf_op jit(solution)/shard_map/ppermute | solution.py:219
  18.2 13.4 %collective-permute-start.1 = (f32[1024,128]{1,0:T(8,128)S(1)}, f32[1024,128]{1,0:T(8,128)S(1)}, u32[]{:S(2)}, u32[]{:S(2)}) collective-permute-start(f32[1024,128]{1,0:T(8,128)S(1)} %collective-permute-done.first.o1), channel_id=1, source_target_pairs={{1,0},{12,4},{2,1},{13,5},{3,2},{14,6},{0,3},{15,7},{9,8},{20,12},... | collective-permute-start | bytes 1572872 | tf_op jit(solution)/shard_map/ppermute | solution.py:219
  22.1 12.3 %collective-permute-start.4 = (f32[1024,128]{1,0:T(8,128)S(1)}, f32[1024,128]{1,0:T(8,128)S(1)}, u32[]{:S(2)}, u32[]{:S(2)}) collective-permute-start(f32[1024,128]{1,0:T(8,128)S(1)} %collective-permute-done.3.second.s3), channel_id=1, source_target_pairs={{3,0},{28,4},{0,1},{29,5},{1,2},{30,6},{2,3},{31,7},{11,8},{4,12},... | collective-permute-start | bytes 1572872 | tf_op jit(solution)/shard_map/ppermute | solution.py:219
  27.1 9.4 %collective-permute-start.8 = (f32[2048,128]{1,0:T(8,128)S(1)}, f32[2048,128]{1,0:T(8,128)S(1)}, u32[]{:S(2)}, u32[]{:S(2)}) collective-permute-start(f32[2048,128]{1,0:T(8,128)S(1)} %shard_map.30), channel_id=1, source_target_pairs={{0,4},{4,0},{8,12},{12,8},{16,20},{20,16},{24,28},{28,24},{1,5},{5... | collective-permute-start | bytes 3145736 | tf_op jit(solution)/shard_map/ppermute | solution.py:210
  29.1 7.4 %collective-permute-start.9 = (f32[2048,128]{1,0:T(8,128)S(1)}, f32[2048,128]{1,0:T(8,128)S(1)}, u32[]{:S(2)}, u32[]{:S(2)}) collective-permute-start(f32[2048,128]{1,0:T(8,128)S(1)} %shard_map.31), channel_id=1, source_target_pairs={{0,4},{4,0},{8,12},{12,8},{16,20},{20,16},{24,28},{28,24},{1,5},{5... | collective-permute-start | bytes 3145736 | tf_op jit(solution)/shard_map/ppermute | solution.py:210
  34.5 5.5 %collective-permute-start.5 = (f32[2048,128]{1,0:T(8,128)S(1)}, f32[2048,128]{1,0:T(8,128)S(1)}, u32[]{:S(2)}, u32[]{:S(2)}) collective-permute-start(f32[2048,128]{1,0:T(8,128)S(1)} %shard_map.29), channel_id=1, source_target_pairs={{0,4},{4,0},{8,12},{12,8},{16,20},{20,16},{24,28},{28,24},{1,5},{5... | collective-permute-start | bytes 3145736 | tf_op jit(solution)/shard_map/ppermute | solution.py:210
  40.8 23.8 %collective-permute-start.10 = (f32[128,512]{1,0:T(8,128)S(1)}, f32[128,512]{1,0:T(8,128)S(1)}, u32[]{:S(2)}, u32[]{:S(2)}) collective-permute-start(f32[128,512]{1,0:T(8,128)S(1)} %get-tuple-element.32), channel_id=1, source_target_pairs={{0,32},{32,64},{64,96},{96,128},{128,160},{160,192},{192,224},{224... | collective-permute-start | bytes 786440 | tf_op jit(solution)/shard_map/ppermute | solution.py:232
  44.5 22.2 %collective-permute-start.11 = (f32[128,512]{1,0:T(8,128)S(1)}, f32[128,512]{1,0:T(8,128)S(1)}, u32[]{:S(2)}, u32[]{:S(2)}) collective-permute-start(f32[128,512]{1,0:T(8,128)S(1)} %get-tuple-element.33), channel_id=1, source_target_pairs={{0,480},{32,0},{64,32},{96,64},{128,96},{160,128},{192,160},{224,1... | collective-permute-start | bytes 786440 | tf_op jit(solution)/shard_map/ppermute | solution.py:232
  54.1 13.9 %collective-permute-start.12 = (f32[128,512]{1,0:T(8,128)S(1)}, f32[128,512]{1,0:T(8,128)S(1)}, u32[]{:S(2)}, u32[]{:S(2)}) collective-permute-start(f32[128,512]{1,0:T(8,128)S(1)} %get-tuple-element.34), channel_id=1, source_target_pairs={{0,64},{4,452},{8,72},{12,460},{16,80},{20,468},{24,88},{28,476},{... | collective-permute-start | bytes 786440 | tf_op jit(solution)/shard_map/ppermute | solution.py:228
  57.5 18.5 %collective-permute-start.14 = (f32[128,512]{1,0:T(8,128)S(1)}, f32[128,512]{1,0:T(8,128)S(1)}, u32[]{:S(2)}, u32[]{:S(2)}) collective-permute-start(f32[128,512]{1,0:T(8,128)S(1)} %get-tuple-element.42), channel_id=1, source_target_pairs={{0,32},{32,64},{64,96},{96,128},{128,160},{160,192},{192,224},{224... | collective-permute-start | bytes 786440 | tf_op jit(solution)/shard_map/ppermute | solution.py:232
  59.4 16.5 %collective-permute-start.15 = (f32[128,512]{1,0:T(8,128)S(1)}, f32[128,512]{1,0:T(8,128)S(1)}, u32[]{:S(2)}, u32[]{:S(2)}) collective-permute-start(f32[128,512]{1,0:T(8,128)S(1)} %get-tuple-element.43), channel_id=1, source_target_pairs={{0,480},{32,0},{64,32},{96,64},{128,96},{160,128},{192,160},{224,1... | collective-permute-start | bytes 786440 | tf_op jit(solution)/shard_map/ppermute | solution.py:232
  64.6 18.1 %collective-permute-start.16 = (f32[128,512]{1,0:T(8,128)S(1)}, f32[128,512]{1,0:T(8,128)S(1)}, u32[]{:S(2)}, u32[]{:S(2)}) collective-permute-start(f32[128,512]{1,0:T(8,128)S(1)} %get-tuple-element.44), channel_id=1, source_target_pairs={{0,64},{4,452},{8,72},{12,460},{16,80},{20,468},{24,88},{28,476},{... | collective-permute-start | bytes 786440 | tf_op jit(solution)/shard_map/ppermute | solution.py:228
  68.0 25.1 %collective-permute-start.17 = (f32[32,512]{1,0:T(8,128)S(1)}, f32[32,512]{1,0:T(8,128)S(1)}, u32[]{:S(2)}, u32[]{:S(2)}) collective-permute-start(f32[32,512]{1,0:T(8,128)S(1)} %get-tuple-element.48), channel_id=1, source_target_pairs={{0,128},{32,160},{64,192},{96,224},{128,256},{160,288},{192,320},{... | collective-permute-start | bytes 196616 | tf_op jit(solution)/shard_map/ppermute | solution.py:232
  82.7 16.1 %collective-permute-start.19 = (f32[32,512]{1,0:T(8,128)S(1)}, f32[32,512]{1,0:T(8,128)S(1)}, u32[]{:S(2)}, u32[]{:S(2)}) collective-permute-start(f32[32,512]{1,0:T(8,128)S(1)} %get-tuple-element.50), channel_id=1, source_target_pairs={{0,384},{32,416},{64,448},{96,480},{128,0},{160,32},{192,64},{224,... | collective-permute-start | bytes 196616 | tf_op jit(solution)/shard_map/ppermute | solution.py:232
  88.7 10.1 %collective-permute-start.13 = (f32[32,512]{1,0:T(8,128)S(1)}, f32[32,512]{1,0:T(8,128)S(1)}, u32[]{:S(2)}, u32[]{:S(2)}) collective-permute-start(f32[32,512]{1,0:T(8,128)S(1)} %get-tuple-element.36), channel_id=1, source_target_pairs={{0,384},{32,416},{64,448},{96,480},{128,0},{160,32},{192,64},{224,... | collective-permute-start | bytes 196616 | tf_op jit(solution)/shard_map/ppermute | solution.py:232
  93.1 15.1 %collective-permute-start.18 = (f32[32,1024]{1,0:T(8,128)S(1)}, f32[32,1024]{1,0:T(8,128)S(1)}, u32[]{:S(2)}, u32[]{:S(2)}) collective-permute-start(f32[32,1024]{1,0:T(8,128)S(1)} %shard_map.38), channel_id=1, source_target_pairs={{0,128},{32,160},{64,192},{96,224},{128,256},{160,288},{192,320},{... | collective-permute-start | bytes 393224 | tf_op jit(solution)/shard_map/ppermute | solution.py:232
  98.9 11.2 %collective-permute-start.20 = (f32[32,512]{1,0:T(8,128)S(1)}, f32[32,512]{1,0:T(8,128)S(1)}, u32[]{:S(2)}, u32[]{:S(2)}) collective-permute-start(f32[32,512]{1,0:T(8,128)S(1)} %shard_map.40), channel_id=1, source_target_pairs={{0,384},{32,416},{64,448},{96,480},{128,0},{160,32},{192,64},{224,... | collective-permute-start | bytes 196616 | tf_op jit(solution)/shard_map/ppermute | solution.py:232

commit v10 on v8

--- a/solution.py
+++ b/solution.py
@@ -20,7 +20,7 @@
 F32, BF16 = jnp.float32, jnp.bfloat16
 
 
-def call(kernel, outs, operands, specs=None, scratch=(), flops=0, nbytes=1 << 20, after=None):
+def call(kernel, outs, operands, specs=None, scratch=(), flops=0, nbytes=1 << 20, after=None, limit=LIMIT):
     if after is not None:
         inner_kernel, count = kernel, len(operands)
         kernel = lambda *refs: inner_kernel(*refs[:count], *refs[count + 1 :])
@@ -33,15 +33,25 @@
         in_specs=specs or [VMEM] * len(operands),
         out_specs=tuple(VMEM for _ in outs),
         scratch_shapes=list(scratch),
-        compiler_params=pltpu.CompilerParams(vmem_limit_bytes=LIMIT),
+        compiler_params=pltpu.CompilerParams(vmem_limit_bytes=limit),
         cost_estimate=pl.CostEstimate(flops=flops, bytes_accessed=nbytes, transcendentals=0),
     )(*operands)
 
 
-def mask_kernel(graph, pattern, masked):
-    for k in range(graph.shape[0] // TILE):
+def mask_kernel(graph, pattern, masked, raw, flags, sems):
+    tiles = graph.shape[0] // TILE
+    flag_copy = pltpu.make_async_copy(pattern, flags, sems.at[tiles])
+    flag_copy.start()
+    copies = []
+    for k in range(tiles):
         rows = pl.ds(k * TILE, TILE)
-        masked[rows, :] = graph[rows, :] * pattern[k].astype(F32)
+        copies.append(pltpu.make_async_copy(graph.at[rows, :], raw.at[rows, :], sems.at[k]))
+        copies[k].start()
+    flag_copy.wait()
+    for k in range(tiles):
+        rows = pl.ds(k * TILE, TILE)
+        copies[k].wait()
+        masked[rows, :] = raw[rows, :] * flags[k].astype(F32)
 
 
 def core():
@@ -101,12 +111,12 @@
     return pair.at[pl.ds(0, inner), :], pair.at[pl.ds(inner, inner), :]
 
 
-def first_product_kernel(own, other, o1, s1, o3, s3, oo, ss, left_high, left_low, right_high, right_low, total):
+def first_product_kernel(own, other, o1, s1, o3, s3, o1_s3, o3_s1, left_high, left_low, right_high, right_low, total):
     left, right = (left_high, left_low), (right_high, right_low)
     take_left(0, own, *left)
     take_right(0, core(), own, *right)
     take_right(0, 1 - core(), other, *right)
-    (o1_swapped, o3_swapped), (s1_swapped, s3_swapped) = halves(oo), halves(ss)
+    (o1_swapped, s3_swapped), (o3_swapped, s1_swapped) = halves(o1_s3), halves(o3_s1)
     place(1, o1, s1, o1_swapped, s1_swapped, left, right)
     place(2, o3, s3, o3_swapped, s3_swapped, left, right)
     for index in range(3):
@@ -246,22 +256,33 @@
 
 def on_device(graph, pattern):
     inner = graph.shape[0]
-    (masked,) = call(mask_kernel, [(inner, TILE)], (graph, pattern.reshape(-1)), [VMEM, SMEM])
+    tiles = inner // TILE
+    (masked,) = call(
+        mask_kernel,
+        [(inner, TILE)],
+        (graph, pattern.reshape(-1)),
+        [pl.BlockSpec(memory_space=pltpu.HBM)] * 2,
+        scratch=[
+            pltpu.VMEM((inner, TILE), F32),
+            pltpu.SMEM((tiles,), jnp.int32),
+            pltpu.SemaphoreType.DMA((tiles + 1,)),
+        ],
+        limit=62 * 1024 * 1024,
+    )
     other = swap(masked)
     o1, o3 = fetch(masked, 1), fetch(masked, 3)
     s3, s1 = fetch(other, 3), fetch(other, 1)
     o2, s2 = fetch(o1, 1), fetch(s3, 3)
 
-    def swap_two(first, second):
-        return swap(call(join_kernel, [(2 * inner, TILE)], (first, second))[0])
+    def swap_two(first, second, after=None):
+        return swap(call(join_kernel, [(2 * inner, TILE)], (first, second), after=after)[0])
 
     known, wide = 3 * TILE, 6 * TILE
     parts = call(
         first_product_kernel,
         [((known, inner), BF16)] * 2 + [((inner, wide), BF16)] * 2 + [(known, wide)],
-        (masked, other, o1, s1, o3, s3, swap_two(o1, o3), swap_two(s1, s3)),
-        flops=6 * known * wide * inner,
-        nbytes=8 << 20,
+        (masked, other, o1, s1, o3, s3, swap_two(o1, s3), swap_two(o3, s1)),
+        nbytes=1 << 10,
     )
     left_high, left_low, right_high, right_low, part = parts
     second = (o2, s2, swap_two(o2, s2))

time: 106 us -> 106 us (level)
  the two profiles are of different devices: /device:TPU:24 before, /device:TPU:16 now
where the time goes in v10:
time: 106 us; the launch traced here: 105 us
  starting transfers between devices  54.4 us (51%)
  waiting for transfers between devices  41.6 us (39%)
  Pallas kernels  8.96 us (8%)
    ppermute x4, waiting for transfers between devices, pass_on(): return lax.ppermute(value, ('layer', 'row'), pairs)  25.3 us
    ppermute x6, starting transfers between devices, fetch(): return lax.ppermute(value, ('row', 'col'), pairs)  20.5 us
    ppermute x4, starting transfers between devices, shift_layers(): lax.ppermute(value, 'layer', [(z, (z + distance) % N_LAYER) for z in rang...  17 us
    ppermute x4, waiting for transfers between devices, shift_layers(): lax.ppermute(value, 'layer', [(z, (z + distance) % N_LAYER) for z in rang...  10.8 us
    ppermute x4, starting transfers between devices, pass_on(): return lax.ppermute(value, ('layer', 'row'), pairs)  9.14 us
    pallas_call x15, Pallas kernels, call(): pl.pallas_call(kernel, out_shape=tuple((jax.ShapeDtypeStruct(s, d) for s,...  8.96 us
    ppermute x4, starting transfers between devices, swap(): return lax.ppermute(value, 'row', [(i, i ^ 1) for i in range(N_ROW)])  7.81 us
    ppermute x6, waiting for transfers between devices, fetch(): return lax.ppermute(value, ('row', 'col'), pairs)  5.47 us
  transfers between devices with their start and end apart: 18, of which 11 were waited for; matrix products, arithmetic and copies ran while one was open for 0% of the time, Pallas kernels for 5%

profile of v10, /device:TPU:16, one launch (start us, length us, event | category | flops | bytes accessed | tf_op | source)
XLA Modules:
  0.0 105.3 jit_solution(7917593990841147071)
XLA Ops:
  0.0 1.9 %shard_map.28.own = f32[1024,128]{1,0:T(8,128)} custom-call(f32[1024,128]{1,0:T(8,128)} %graph.1, s32[8]{0:T(128)} %bitcast.1), custom_call_target="tpu_custom_call" | custom-call | bytes 1048576 | tf_op jit(solution)/shard_map/pallas_call | solution.py:30
  3.9 2.4 %collective-permute-start = (f32[1024,128]{1,0:T(8,128)}, f32[1024,128]{1,0:T(8,128)S(1)}, u32[]{:S(2)}, u32[]{:S(2)}) collective-permute-start(f32[1024,128]{1,0:T(8,128)} %shard_map.28.own), channel_id=1, source_target_pairs={{1,0},{12,4},{2,1},{13,5},{3,2},{14,6},{0,3},{15,7},{9,8},{20,12},... | collective-permute-start | bytes 1572872 | tf_op jit(solution)/shard_map/ppermute | solution.py:241
  6.3 3.5 %collective-permute-start.3 = (f32[1024,128]{1,0:T(8,128)S(1)}, f32[1024,128]{1,0:T(8,128)S(1)}, u32[]{:S(2)}, u32[]{:S(2)}) collective-permute-start(f32[1024,128]{1,0:T(8,128)S(1)} %collective-permute-done.2.other), channel_id=1, source_target_pairs={{3,0},{28,4},{0,1},{29,5},{1,2},{30,6},{2,3},{31,7},{11,8},{4,12},... | collective-permute-start | bytes 1572872 | tf_op jit(solution)/shard_map/ppermute | solution.py:241
  9.8 6.9 %collective-permute-start.7 = (f32[1024,128]{1,0:T(8,128)}, f32[1024,128]{1,0:T(8,128)S(1)}, u32[]{:S(2)}, u32[]{:S(2)}) collective-permute-start(f32[1024,128]{1,0:T(8,128)} %shard_map.28.own), channel_id=1, source_target_pairs={{3,0},{28,4},{0,1},{29,5},{1,2},{30,6},{2,3},{31,7},{11,8},{4,12},... | collective-permute-start | bytes 1572872 | tf_op jit(solution)/shard_map/ppermute | solution.py:241
  16.7 1.9 %collective-permute-start.6 = (f32[1024,128]{1,0:T(8,128)S(1)}, f32[1024,128]{1,0:T(8,128)S(1)}, u32[]{:S(2)}, u32[]{:S(2)}) collective-permute-start(f32[1024,128]{1,0:T(8,128)S(1)} %collective-permute-done.2.other), channel_id=1, source_target_pairs={{1,0},{12,4},{2,1},{13,5},{3,2},{14,6},{0,3},{15,7},{9,8},{20,12},... | collective-permute-start | bytes 1572872 | tf_op jit(solution)/shard_map/ppermute | solution.py:241
  18.6 3.2 %collective-permute-start.1 = (f32[1024,128]{1,0:T(8,128)S(1)}, f32[1024,128]{1,0:T(8,128)S(1)}, u32[]{:S(2)}, u32[]{:S(2)}) collective-permute-start(f32[1024,128]{1,0:T(8,128)S(1)} %collective-permute-done.first.o1), channel_id=1, source_target_pairs={{1,0},{12,4},{2,1},{13,5},{3,2},{14,6},{0,3},{15,7},{9,8},{20,12},... | collective-permute-start | bytes 1572872 | tf_op jit(solution)/shard_map/ppermute | solution.py:241
  21.8 2.7 %collective-permute-start.4 = (f32[1024,128]{1,0:T(8,128)S(1)}, f32[1024,128]{1,0:T(8,128)S(1)}, u32[]{:S(2)}, u32[]{:S(2)}) collective-permute-start(f32[1024,128]{1,0:T(8,128)S(1)} %collective-permute-done.3.second.s3), channel_id=1, source_target_pairs={{3,0},{28,4},{0,1},{29,5},{1,2},{30,6},{2,3},{31,7},{11,8},{4,12},... | collective-permute-start | bytes 1572872 | tf_op jit(solution)/shard_map/ppermute | solution.py:241
  24.6 2.1 %collective-permute-start.8 = (f32[2048,128]{1,0:T(8,128)S(1)}, f32[2048,128]{1,0:T(8,128)S(1)}, u32[]{:S(2)}, u32[]{:S(2)}) collective-permute-start(f32[2048,128]{1,0:T(8,128)S(1)} %shard_map.30), channel_id=1, source_target_pairs={{0,4},{4,0},{8,12},{12,8},{16,20},{20,16},{24,28},{28,24},{1,5},{5... | collective-permute-start | bytes 3145736 | tf_op jit(solution)/shard_map/ppermute | solution.py:232
  27.8 1.9 %collective-permute-start.9 = (f32[2048,128]{1,0:T(8,128)S(1)}, f32[2048,128]{1,0:T(8,128)S(1)}, u32[]{:S(2)}, u32[]{:S(2)}) collective-permute-start(f32[2048,128]{1,0:T(8,128)S(1)} %shard_map.31), channel_id=1, source_target_pairs={{0,4},{4,0},{8,12},{12,8},{16,20},{20,16},{24,28},{28,24},{1,5},{5... | collective-permute-start | bytes 3145736 | tf_op jit(solution)/shard_map/ppermute | solution.py:232
  29.7 3.6 %collective-permute-done.1.first.o2 = f32[1024,128]{1,0:T(8,128)S(1)} collective-permute-done((f32[1024,128]{1,0:T(8,128)S(1)}, f32[1024,128]{1,0:T(8,128)S(1)}, u32[]{:S(2)}, u32[]{:S(2)}) %collective-permute-start.1) | collective-permute-done | bytes 524320 | tf_op jit(solution)/shard_map/ppermute | solution.py:241
  34.2 1.9 %collective-permute-start.5 = (f32[2048,128]{1,0:T(8,128)S(1)}, f32[2048,128]{1,0:T(8,128)S(1)}, u32[]{:S(2)}, u32[]{:S(2)}) collective-permute-start(f32[2048,128]{1,0:T(8,128)S(1)} %shard_map.29), channel_id=1, source_target_pairs={{0,4},{4,0},{8,12},{12,8},{16,20},{20,16},{24,28},{28,24},{1,5},{5... | collective-permute-start | bytes 3145736 | tf_op jit(solution)/shard_map/ppermute | solution.py:232
  36.1 3.4 %shard_map.32 = (bf16[384,1024]{1,0:T(8,128)(2,1)S(1)}, bf16[384,1024]{1,0:T(8,128)(2,1)S(1)}, bf16[1024,768]{1,0:T(8,128)(2,1)S(1)}, bf16[1024,768]{1,0:T(8,128)(2,1)S(1)}, f32[384,768]{1,0:T(8,128)S(1)}) custom-call(f32[1024,128]{1,0:T(8,128)S(1)} %copy-done, f32[1024,128]{1,0:T(8,128)S(1)} %collective-permute-done.2.other, ...), custom_call_target="tpu_custom_call" | custom-call | bytes 1024 | tf_op jit(solution)/shard_map/pallas_call | solution.py:30
  40.5 1.9 %collective-permute-start.10 = (f32[256,512]{1,0:T(8,128)S(1)}, f32[256,512]{1,0:T(8,128)S(1)}, u32[]{:S(2)}, u32[]{:S(2)}) collective-permute-start(f32[256,512]{1,0:T(8,128)S(1)} %get-tuple-element.32), channel_id=1, source_target_pairs={{0,32},{4,484},{8,40},{12,492},{16,48},{20,500},{24,56},{28,508},{... | collective-permute-start | bytes 1572872 | tf_op jit(solution)/shard_map/ppermute | solution.py:250
  44.0 3.4 %collective-permute-start.12 = (f32[256,512]{1,0:T(8,128)S(1)}, f32[256,512]{1,0:T(8,128)S(1)}, u32[]{:S(2)}, u32[]{:S(2)}) collective-permute-start(f32[256,512]{1,0:T(8,128)S(1)} %get-tuple-element.41), channel_id=1, source_target_pairs={{0,32},{4,484},{8,40},{12,492},{16,48},{20,500},{24,56},{28,508},{... | collective-permute-start | bytes 1572872 | tf_op jit(solution)/shard_map/ppermute | solution.py:250
  47.4 9.3 %collective-permute-done.10.came = f32[256,512]{1,0:T(8,128)S(1)} collective-permute-done((f32[256,512]{1,0:T(8,128)S(1)}, f32[256,512]{1,0:T(8,128)S(1)}, u32[]{:S(2)}, u32[]{:S(2)}) %collective-permute-start.10) | collective-permute-done | bytes 524320 | tf_op jit(solution)/shard_map/ppermute | solution.py:250
  56.8 1.9 %collective-permute-start.11 = (f32[128,512]{1,0:T(8,128)S(1)}, f32[128,512]{1,0:T(8,128)S(1)}, u32[]{:S(2)}, u32[]{:S(2)}) collective-permute-start(f32[128,512]{1,0:T(8,128)S(1)} %get-tuple-element.34), channel_id=1, source_target_pairs={{0,64},{4,452},{8,72},{12,460},{16,80},{20,468},{24,88},{28,476},{... | collective-permute-start | bytes 786440 | tf_op jit(solution)/shard_map/ppermute | solution.py:250
  58.7 3.6 %collective-permute-done.12.refs_1_ = f32[256,512]{1,0:T(8,128)S(1)} collective-permute-done((f32[256,512]{1,0:T(8,128)S(1)}, f32[256,512]{1,0:T(8,128)S(1)}, u32[]{:S(2)}, u32[]{:S(2)}) %collective-permute-start.12) | collective-permute-done | bytes 524320 | tf_op jit(solution)/shard_map/ppermute | solution.py:250
  64.3 5.2 %collective-permute-done.11.came = f32[128,512]{1,0:T(8,128)S(1)} collective-permute-done((f32[128,512]{1,0:T(8,128)S(1)}, f32[128,512]{1,0:T(8,128)S(1)}, u32[]{:S(2)}, u32[]{:S(2)}) %collective-permute-start.11) | collective-permute-done | bytes 262176 | tf_op jit(solution)/shard_map/ppermute | solution.py:250
  71.5 7.2 %collective-permute-done.13.refs_1_ = f32[128,512]{1,0:T(8,128)S(1)} collective-permute-done((f32[128,512]{1,0:T(8,128)S(1)}, f32[128,512]{1,0:T(8,128)S(1)}, u32[]{:S(2)}, u32[]{:S(2)}) %collective-permute-start.13) | collective-permute-done | bytes 262176 | tf_op jit(solution)/shard_map/ppermute | solution.py:250
  78.7 5.3 %collective-permute-start.16 = (f32[32,512]{1,0:T(8,128)S(1)}, f32[32,512]{1,0:T(8,128)S(1)}, u32[]{:S(2)}, u32[]{:S(2)}) collective-permute-start(f32[32,512]{1,0:T(8,128)S(1)} %get-tuple-element.50), channel_id=1, source_target_pairs={{0,384},{32,416},{64,448},{96,480},{128,0},{160,32},{192,64},{224,... | collective-permute-start | bytes 196616 | tf_op jit(solution)/shard_map/ppermute | solution.py:254
  84.1 4.4 %collective-permute-start.15 = (f32[32,1024]{1,0:T(8,128)S(1)}, f32[32,1024]{1,0:T(8,128)S(1)}, u32[]{:S(2)}, u32[]{:S(2)}) collective-permute-start(f32[32,1024]{1,0:T(8,128)S(1)} %shard_map.39.refs_3_), channel_id=1, source_target_pairs={{0,128},{32,160},{64,192},{96,224},{128,256},{160,288},{192,320},{... | collective-permute-start | bytes 393224 | tf_op jit(solution)/shard_map/ppermute | solution.py:254
  88.8 5.3 %collective-permute-start.17 = (f32[32,1024]{1,0:T(8,128)S(1)}, f32[32,1024]{1,0:T(8,128)S(1)}, u32[]{:S(2)}, u32[]{:S(2)}) collective-permute-start(f32[32,1024]{1,0:T(8,128)S(1)} %shard_map.41), channel_id=1, source_target_pairs={{0,384},{32,416},{64,448},{96,480},{128,0},{160,32},{192,64},{224,... | collective-permute-start | bytes 393224 | tf_op jit(solution)/shard_map/ppermute | solution.py:254
  94.1 6.0 %collective-permute-done.15.from_below = f32[32,1024]{1,0:T(8,128)S(1)} collective-permute-done((f32[32,1024]{1,0:T(8,128)S(1)}, f32[32,1024]{1,0:T(8,128)S(1)}, u32[]{:S(2)}, u32[]{:S(2)}) %collective-permute-start.15) | collective-permute-done | bytes 131104 | tf_op jit(solution)/shard_map/ppermute | solution.py:254
  100.1 4.5 %collective-permute-done.17.from_above = f32[32,1024]{1,0:T(8,128)S(1)} collective-permute-done((f32[32,1024]{1,0:T(8,128)S(1)}, f32[32,1024]{1,0:T(8,128)S(1)}, u32[]{:S(2)}, u32[]{:S(2)}) %collective-permute-start.17) | collective-permute-done | bytes 131104 | tf_op jit(solution)/shard_map/ppermute | solution.py:254
  (29 shorter events, 11.5 us)
Async XLA Ops:
  2.0 4.3 %collective-permute-start.2 = (f32[1024,128]{1,0:T(8,128)}, f32[1024,128]{1,0:T(8,128)S(1)}, u32[]{:S(2)}, u32[]{:S(2)}) collective-permute-start(f32[1024,128]{1,0:T(8,128)} %shard_map.28.own), channel_id=1, source_target_pairs={{0,4},{4,0},{8,12},{12,8},{16,20},{20,16},{24,28},{28,24},{1,5},{5... | collective-permute-start | bytes 1572872 | tf_op jit(solution)/shard_map/ppermute | solution.py:232
  3.9 14.7 %collective-permute-start = (f32[1024,128]{1,0:T(8,128)}, f32[1024,128]{1,0:T(8,128)S(1)}, u32[]{:S(2)}, u32[]{:S(2)}) collective-permute-start(f32[1024,128]{1,0:T(8,128)} %shard_map.28.own), channel_id=1, source_target_pairs={{1,0},{12,4},{2,1},{13,5},{3,2},{14,6},{0,3},{15,7},{9,8},{20,12},... | collective-permute-start | bytes 1572872 | tf_op jit(solution)/shard_map/ppermute | solution.py:241
  6.3 15.5 %collective-permute-start.3 = (f32[1024,128]{1,0:T(8,128)S(1)}, f32[1024,128]{1,0:T(8,128)S(1)}, u32[]{:S(2)}, u32[]{:S(2)}) collective-permute-start(f32[1024,128]{1,0:T(8,128)S(1)} %collective-permute-done.2.other), channel_id=1, source_target_pairs={{3,0},{28,4},{0,1},{29,5},{1,2},{30,6},{2,3},{31,7},{11,8},{4,12},... | collective-permute-start | bytes 1572872 | tf_op jit(solution)/shard_map/ppermute | solution.py:241
  9.8 17.0 %collective-permute-start.7 = (f32[1024,128]{1,0:T(8,128)}, f32[1024,128]{1,0:T(8,128)S(1)}, u32[]{:S(2)}, u32[]{:S(2)}) collective-permute-start(f32[1024,128]{1,0:T(8,128)} %shard_map.28.own), channel_id=1, source_target_pairs={{3,0},{28,4},{0,1},{29,5},{1,2},{30,6},{2,3},{31,7},{11,8},{4,12},... | collective-permute-start | bytes 1572872 | tf_op jit(solution)/shard_map/ppermute | solution.py:241
  16.7 11.1 %collective-permute-start.6 = (f32[1024,128]{1,0:T(8,128)S(1)}, f32[1024,128]{1,0:T(8,128)S(1)}, u32[]{:S(2)}, u32[]{:S(2)}) collective-permute-start(f32[1024,128]{1,0:T(8,128)S(1)} %collective-permute-done.2.other), channel_id=1, source_target_pairs={{1,0},{12,4},{2,1},{13,5},{3,2},{14,6},{0,3},{15,7},{9,8},{20,12},... | collective-permute-start | bytes 1572872 | tf_op jit(solution)/shard_map/ppermute | solution.py:241
  18.6 14.8 %collective-permute-start.1 = (f32[1024,128]{1,0:T(8,128)S(1)}, f32[1024,128]{1,0:T(8,128)S(1)}, u32[]{:S(2)}, u32[]{:S(2)}) collective-permute-start(f32[1024,128]{1,0:T(8,128)S(1)} %collective-permute-done.first.o1), channel_id=1, source_target_pairs={{1,0},{12,4},{2,1},{13,5},{3,2},{14,6},{0,3},{15,7},{9,8},{20,12},... | collective-permute-start | bytes 1572872 | tf_op jit(solution)/shard_map/ppermute | solution.py:241
  21.8 12.3 %collective-permute-start.4 = (f32[1024,128]{1,0:T(8,128)S(1)}, f32[1024,128]{1,0:T(8,128)S(1)}, u32[]{:S(2)}, u32[]{:S(2)}) collective-permute-start(f32[1024,128]{1,0:T(8,128)S(1)} %collective-permute-done.3.second.s3), channel_id=1, source_target_pairs={{3,0},{28,4},{0,1},{29,5},{1,2},{30,6},{2,3},{31,7},{11,8},{4,12},... | collective-permute-start | bytes 1572872 | tf_op jit(solution)/shard_map/ppermute | solution.py:241
  24.6 11.6 %copy-start = (f32[1024,128]{1,0:T(8,128)S(1)}, f32[1024,128]{1,0:T(8,128)}, u32[]{:S(2)}) copy-start(f32[1024,128]{1,0:T(8,128)} %shard_map.28.own) | copy-start | bytes 1572868
  24.6 11.5 %collective-permute-start.8 = (f32[2048,128]{1,0:T(8,128)S(1)}, f32[2048,128]{1,0:T(8,128)S(1)}, u32[]{:S(2)}, u32[]{:S(2)}) collective-permute-start(f32[2048,128]{1,0:T(8,128)S(1)} %shard_map.30), channel_id=1, source_target_pairs={{0,4},{4,0},{8,12},{12,8},{16,20},{20,16},{24,28},{28,24},{1,5},{5... | collective-permute-start | bytes 3145736 | tf_op jit(solution)/shard_map/ppermute | solution.py:232
  27.8 8.3 %collective-permute-start.9 = (f32[2048,128]{1,0:T(8,128)S(1)}, f32[2048,128]{1,0:T(8,128)S(1)}, u32[]{:S(2)}, u32[]{:S(2)}) collective-permute-start(f32[2048,128]{1,0:T(8,128)S(1)} %shard_map.31), channel_id=1, source_target_pairs={{0,4},{4,0},{8,12},{12,8},{16,20},{20,16},{24,28},{28,24},{1,5},{5... | collective-permute-start | bytes 3145736 | tf_op jit(solution)/shard_map/ppermute | solution.py:232
  34.2 5.4 %collective-permute-start.5 = (f32[2048,128]{1,0:T(8,128)S(1)}, f32[2048,128]{1,0:T(8,128)S(1)}, u32[]{:S(2)}, u32[]{:S(2)}) collective-permute-start(f32[2048,128]{1,0:T(8,128)S(1)} %shard_map.29), channel_id=1, source_target_pairs={{0,4},{4,0},{8,12},{12,8},{16,20},{20,16},{24,28},{28,24},{1,5},{5... | collective-permute-start | bytes 3145736 | tf_op jit(solution)/shard_map/ppermute | solution.py:232
  40.5 16.2 %collective-permute-start.10 = (f32[256,512]{1,0:T(8,128)S(1)}, f32[256,512]{1,0:T(8,128)S(1)}, u32[]{:S(2)}, u32[]{:S(2)}) collective-permute-start(f32[256,512]{1,0:T(8,128)S(1)} %get-tuple-element.32), channel_id=1, source_target_pairs={{0,32},{4,484},{8,40},{12,492},{16,48},{20,500},{24,56},{28,508},{... | collective-permute-start | bytes 1572872 | tf_op jit(solution)/shard_map/ppermute | solution.py:250
  44.0 18.3 %collective-permute-start.12 = (f32[256,512]{1,0:T(8,128)S(1)}, f32[256,512]{1,0:T(8,128)S(1)}, u32[]{:S(2)}, u32[]{:S(2)}) collective-permute-start(f32[256,512]{1,0:T(8,128)S(1)} %get-tuple-element.41), channel_id=1, source_target_pairs={{0,32},{4,484},{8,40},{12,492},{16,48},{20,500},{24,56},{28,508},{... | collective-permute-start | bytes 1572872 | tf_op jit(solution)/shard_map/ppermute | solution.py:250
  56.8 12.8 %collective-permute-start.11 = (f32[128,512]{1,0:T(8,128)S(1)}, f32[128,512]{1,0:T(8,128)S(1)}, u32[]{:S(2)}, u32[]{:S(2)}) collective-permute-start(f32[128,512]{1,0:T(8,128)S(1)} %get-tuple-element.34), channel_id=1, source_target_pairs={{0,64},{4,452},{8,72},{12,460},{16,80},{20,468},{24,88},{28,476},{... | collective-permute-start | bytes 786440 | tf_op jit(solution)/shard_map/ppermute | solution.py:250
  62.4 16.3 %collective-permute-start.13 = (f32[128,512]{1,0:T(8,128)S(1)}, f32[128,512]{1,0:T(8,128)S(1)}, u32[]{:S(2)}, u32[]{:S(2)}) collective-permute-start(f32[128,512]{1,0:T(8,128)S(1)} %get-tuple-element.43), channel_id=1, source_target_pairs={{0,64},{4,452},{8,72},{12,460},{16,80},{20,468},{24,88},{28,476},{... | collective-permute-start | bytes 786440 | tf_op jit(solution)/shard_map/ppermute | solution.py:250
  69.6 14.4 %collective-permute-start.14 = (f32[32,512]{1,0:T(8,128)S(1)}, f32[32,512]{1,0:T(8,128)S(1)}, u32[]{:S(2)}, u32[]{:S(2)}) collective-permute-start(f32[32,512]{1,0:T(8,128)S(1)} %get-tuple-element.47), channel_id=1, source_target_pairs={{0,128},{32,160},{64,192},{96,224},{128,256},{160,288},{192,320},{... | collective-permute-start | bytes 196616 | tf_op jit(solution)/shard_map/ppermute | solution.py:254
  78.7 10.1 %collective-permute-start.16 = (f32[32,512]{1,0:T(8,128)S(1)}, f32[32,512]{1,0:T(8,128)S(1)}, u32[]{:S(2)}, u32[]{:S(2)}) collective-permute-start(f32[32,512]{1,0:T(8,128)S(1)} %get-tuple-element.50), channel_id=1, source_target_pairs={{0,384},{32,416},{64,448},{96,480},{128,0},{160,32},{192,64},{224,... | collective-permute-start | bytes 196616 | tf_op jit(solution)/shard_map/ppermute | solution.py:254
  84.1 16.1 %collective-permute-start.15 = (f32[32,1024]{1,0:T(8,128)S(1)}, f32[32,1024]{1,0:T(8,128)S(1)}, u32[]{:S(2)}, u32[]{:S(2)}) collective-permute-start(f32[32,1024]{1,0:T(8,128)S(1)} %shard_map.39.refs_3_), channel_id=1, source_target_pairs={{0,128},{32,160},{64,192},{96,224},{128,256},{160,288},{192,320},{... | collective-permute-start | bytes 393224 | tf_op jit(solution)/shard_map/ppermute | solution.py:254
  88.8 15.9 %collective-permute-start.17 = (f32[32,1024]{1,0:T(8,128)S(1)}, f32[32,1024]{1,0:T(8,128)S(1)}, u32[]{:S(2)}, u32[]{:S(2)}) collective-permute-start(f32[32,1024]{1,0:T(8,128)S(1)} %shard_map.41), channel_id=1, source_target_pairs={{0,384},{32,416},{64,448},{96,480},{128,0},{160,32},{192,64},{224,... | collective-permute-start | bytes 393224 | tf_op jit(solution)/shard_map/ppermute | solution.py:254

commit v11 on v10

--- a/solution.py
+++ b/solution.py
@@ -92,36 +92,49 @@
     right_low[:, columns] = low
 
 
-def place(index, first, second, first_swapped, second_swapped, left, right):
-    @pl.when(core() == 0)
-    def _():
-        take_left(index, first, *left)
-        take_right(index, 0, second_swapped, *right)
-        take_right(index, 1, first_swapped, *right)
-
-    @pl.when(core() == 1)
-    def _():
-        take_left(index, second_swapped, *left)
-        take_right(index, 0, second, *right)
-        take_right(index, 1, first, *right)
-
-
 def halves(pair):
     inner = pair.shape[0] // 2
     return pair.at[pl.ds(0, inner), :], pair.at[pl.ds(inner, inner), :]
 
 
-def first_product_kernel(own, other, o1, s1, o3, s3, o1_s3, o3_s1, left_high, left_low, right_high, right_low, total):
+def early_product_kernel(own, other, o1, s1, o3, s3, left_high, left_low, right_high, right_low, total):
     left, right = (left_high, left_low), (right_high, right_low)
     take_left(0, own, *left)
     take_right(0, core(), own, *right)
     take_right(0, 1 - core(), other, *right)
-    (o1_swapped, s3_swapped), (o3_swapped, s1_swapped) = halves(o1_s3), halves(o3_s1)
-    place(1, o1, s1, o1_swapped, s1_swapped, left, right)
-    place(2, o3, s3, o3_swapped, s3_swapped, left, right)
-    for index in range(3):
-        columns = pl.ds(index * 2 * TILE, 2 * TILE)
+
+    @pl.when(core() == 0)
+    def _():
+        take_left(1, o1, *left)
+        take_left(2, o3, *left)
+        columns = pl.ds(0, 2 * TILE)
         total[:, columns] = product(left_high[...], left_low[...], right_high[:, columns], right_low[:, columns])
+
+    @pl.when(core() == 1)
+    def _():
+        for index, o, s in ((1, o1, s1), (2, o3, s3)):
+            take_right(index, 0, s, *right)
+            take_right(index, 1, o, *right)
+        rows = pl.ds(0, TILE)
+        total[rows, :] = product(left_high[rows, :], left_low[rows, :], right_high[...], right_low[...])
+
+
+def first_product_kernel(o1_s3, o3_s1, early_left, early_left_low, early_right, early_right_low, *refs):
+    left_high, left_low, right_high, right_low, beside, below = refs
+    (o1, s3), (o3, s1) = halves(o1_s3), halves(o3_s1)
+
+    @pl.when(core() == 0)
+    def _():
+        for index, o, s in ((0, o1, s1), (1, o3, s3)):
+            take_right(index, 0, s, right_high, right_low)
+            take_right(index, 1, o, right_high, right_low)
+        beside[...] = product(early_left[...], early_left_low[...], right_high[...], right_low[...])
+
+    @pl.when(core() == 1)
+    def _():
+        take_left(0, s1, left_high, left_low)
+        take_left(1, s3, left_high, left_low)
+        below[...] = product(left_high[...], left_low[...], early_right[...], early_right_low[...])
 
 
 def turn():
@@ -146,43 +159,64 @@
         send[rows, :] = total[rows_of(lax.rem(z + turn() + 2 * j + N_LAYER, N_LAYER)), :]
 
 
-def second_product_kernel(o2, s2, both, right_high, right_low, part, send, keep, last_high, last_low, total):
-    swapped = both.at[pl.ds(s2.shape[0], s2.shape[0]), :]
+def second_product_kernel(o2, s2, both, early_right, early_right_low, early, right_high, right_low, beside, below, *refs):
+    send, keep, last_high, last_low, total = refs
+    known, wide = early.shape[0], 2 * TILE
+    first, next_ = pl.ds(0, wide), pl.ds(wide, wide)
+
+    def last_rows(columns, high, low):
+        total[known:, columns] = product(last_high[...], last_low[...], high, low)
 
     @pl.when(core() == 0)
     def _():
         take_left(0, o2, last_high, last_low)
+        total[:known, first] = early[:, first]
+        total[:known, next_] = beside[:, first]
+        last_rows(first, early_right[:, first], early_right_low[:, first])
+        last_rows(next_, right_high[:, first], right_low[:, first])
 
     @pl.when(core() == 1)
     def _():
-        take_left(0, swapped, last_high, last_low)
-
-    known, columns = part.shape[0], pl.ds(0, total.shape[1])
-    total[:known, :] = part[:, columns]
-    total[known:, :] = product(last_high[...], last_low[...], right_high[:, columns], right_low[:, columns])
+        columns = pl.ds(0, 2 * wide)
+        take_left(0, both.at[pl.ds(s2.shape[0], s2.shape[0]), :], last_high, last_low)
+        total[:TILE, :] = early[:TILE, columns]
+        total[TILE:known, :] = below[:, columns]
+        last_rows(columns, early_right[:, columns], early_right_low[:, columns])
+
     scatter(total, send, keep)
 
 
-def third_product_kernel(o2, s2, both, last_high, last_low, left_high, left_low, right_high, right_low, part, *refs):
-    send, keep, far_high, far_low, total = refs
+def third_product_kernel(o2, s2, both, last_high, last_low, *refs):
+    early_left, early_left_low, early_right, early_right_low, early = refs[:5]
+    left_high, left_low, right_high, right_low, beside, below = refs[5:11]
+    send, keep, far_high, far_low, total = refs[11:]
     o2_swapped, s2_swapped = halves(both)
+    known, wide = early.shape[0], 2 * TILE
+    first, next_, third = (pl.ds(i * wide, wide) for i in range(3))
+
+    def far(rows, high, low):
+        total[rows, next_] = product(high, low, far_high[...], far_low[...])
 
     @pl.when(core() == 0)
     def _():
         take_right(0, 0, s2_swapped, far_high, far_low)
         take_right(0, 1, o2_swapped, far_high, far_low)
+        total[:known, first] = beside[:, next_]
+        total[known:, first] = product(last_high[...], last_low[...], right_high[:, next_], right_low[:, next_])
+        far(pl.ds(0, known), early_left[...], early_left_low[...])
+        far(pl.ds(known, TILE), last_high[...], last_low[...])
 
     @pl.when(core() == 1)
     def _():
         take_right(0, 0, s2, far_high, far_low)
         take_right(0, 1, o2, far_high, far_low)
-
-    known, wide = part.shape[0], 2 * TILE
-    columns = pl.ds(part.shape[1] - wide, wide)
-    total[:known, :wide] = part[:, columns]
-    total[known:, :wide] = product(last_high[...], last_low[...], right_high[:, columns], right_low[:, columns])
-    total[:known, wide:] = product(left_high[...], left_low[...], far_high[...], far_low[...])
-    total[known:, wide:] = product(last_high[...], last_low[...], far_high[...], far_low[...])
+        total[:TILE, first] = early[:TILE, third]
+        total[TILE:known, first] = below[:, third]
+        total[known:, first] = product(last_high[...], last_low[...], early_right[:, third], early_right_low[:, third])
+        far(pl.ds(0, TILE), early_left[:TILE, :], early_left_low[:TILE, :])
+        far(pl.ds(TILE, known - TILE), left_high[...], left_low[...])
+        far(pl.ds(known, TILE), last_high[...], last_low[...])
+
     scatter(total, send, keep)
 
 
@@ -278,20 +312,24 @@
         return swap(call(join_kernel, [(2 * inner, TILE)], (first, second), after=after)[0])
 
     known, wide = 3 * TILE, 6 * TILE
-    parts = call(
+    shapes = [((known, inner), BF16)] * 2 + [((inner, wide), BF16)] * 2 + [(known, wide)]
+    early = call(early_product_kernel, shapes, (masked, other, o1, s1, o3, s3), nbytes=1 << 10)
+    second = (o2, s2, swap_two(o2, s2, after=early[4]))
+    late = call(
         first_product_kernel,
-        [((known, inner), BF16)] * 2 + [((inner, wide), BF16)] * 2 + [(known, wide)],
-        (masked, other, o1, s1, o3, s3, swap_two(o1, s3), swap_two(o3, s1)),
-        nbytes=1 << 10,
-    )
-    left_high, left_low, right_high, right_low, part = parts
-    second = (o2, s2, swap_two(o2, s2))
+        [((known - TILE, inner), BF16)] * 2
+        + [((inner, wide - 2 * TILE), BF16)] * 2
+        + [(known, wide - 2 * TILE), (known - TILE, wide)],
+        (swap_two(o1, s3), swap_two(o3, s1), *early[:4]),
+        flops=4 * known * wide * inner,
+        nbytes=8 << 20,
+    )
     out = (8 * SUB, 4 * TILE)
     total = pltpu.VMEM((4 * TILE, 4 * TILE), F32)
     send_a, keep_a, *last = call(
         second_product_kernel,
         [out, out, ((TILE, inner), BF16), ((TILE, inner), BF16)],
-        (*second, right_high, right_low, part),
+        (*second, *early[2:], *late[2:]),
         scratch=[total],
         flops=6 * TILE * 4 * TILE * inner,
         nbytes=4 << 20,
@@ -299,7 +337,7 @@
     send_b, keep_b = call(
         third_product_kernel,
         [out, out],
-        (*second, *last, left_high, left_low, right_high, right_low, part),
+        (*second, *last, *early, *late),
         scratch=[pltpu.VMEM((inner, 2 * TILE), BF16)] * 2 + [total],
         flops=6 * 5 * TILE * 2 * TILE * inner,
         nbytes=4 << 20,

time: 106 us -> 104 us (0.981)
  the two profiles are of different devices: /device:TPU:16 before, /device:TPU:6 now
where the time goes in v11:
time: 104 us; the launch traced here: 102 us
  starting transfers between devices  59 us (57%)
  waiting for transfers between devices  34.8 us (33%)
  Pallas kernels  8.17 us (8%)
    ppermute x4, waiting for transfers between devices, pass_on(): return lax.ppermute(value, ('layer', 'row'), pairs)  25.4 us
    ppermute x6, starting transfers between devices, fetch(): return lax.ppermute(value, ('row', 'col'), pairs)  19.7 us
    ppermute x4, starting transfers between devices, shift_layers(): lax.ppermute(value, 'layer', [(z, (z + distance) % N_LAYER) for z in rang...  17.1 us
    ppermute x4, starting transfers between devices, pass_on(): return lax.ppermute(value, ('layer', 'row'), pairs)  11.5 us
    ppermute x4, starting transfers between devices, swap(): return lax.ppermute(value, 'row', [(i, i ^ 1) for i in range(N_ROW)])  10.6 us
    pallas_call x16, Pallas kernels, call(): pl.pallas_call(kernel, out_shape=tuple((jax.ShapeDtypeStruct(s, d) for s,...  8.17 us
    ppermute x4, waiting for transfers between devices, shift_layers(): lax.ppermute(value, 'layer', [(z, (z + distance) % N_LAYER) for z in rang...  6.25 us
    ppermute x6, waiting for transfers between devices, fetch(): return lax.ppermute(value, ('row', 'col'), pairs)  2.08 us
  transfers between devices with their start and end apart: 18, of which 8 were waited for; matrix products, arithmetic and copies ran while one was open for 0% of the time, Pallas kernels for 5%

profile of v11, /device:TPU:6, one launch (start us, length us, event | category | flops | bytes accessed | tf_op | source)
XLA Modules:
  0.0 102.3 jit_solution(7052980036604724477)
XLA Ops:
  0.0 1.9 %shard_map.28.own = f32[1024,128]{1,0:T(8,128)} custom-call(f32[1024,128]{1,0:T(8,128)} %graph.1, s32[8]{0:T(128)} %bitcast.1), custom_call_target="tpu_custom_call" | custom-call | bytes 1048576 | tf_op jit(solution)/shard_map/pallas_call | solution.py:30
  3.9 4.9 %collective-permute-start = (f32[1024,128]{1,0:T(8,128)}, f32[1024,128]{1,0:T(8,128)S(1)}, u32[]{:S(2)}, u32[]{:S(2)}) collective-permute-start(f32[1024,128]{1,0:T(8,128)} %shard_map.28.own), channel_id=1, source_target_pairs={{1,0},{12,4},{2,1},{13,5},{3,2},{14,6},{0,3},{15,7},{9,8},{20,12},... | collective-permute-start | bytes 1572872 | tf_op jit(solution)/shard_map/ppermute | solution.py:275
  8.8 1.9 %collective-permute-start.3 = (f32[1024,128]{1,0:T(8,128)S(1)}, f32[1024,128]{1,0:T(8,128)S(1)}, u32[]{:S(2)}, u32[]{:S(2)}) collective-permute-start(f32[1024,128]{1,0:T(8,128)S(1)} %collective-permute-done.2.other), channel_id=1, source_target_pairs={{3,0},{28,4},{0,1},{29,5},{1,2},{30,6},{2,3},{31,7},{11,8},{4,12},... | collective-permute-start | bytes 1572872 | tf_op jit(solution)/shard_map/ppermute | solution.py:275
  10.7 2.5 %collective-permute-start.6 = (f32[1024,128]{1,0:T(8,128)}, f32[1024,128]{1,0:T(8,128)S(1)}, u32[]{:S(2)}, u32[]{:S(2)}) collective-permute-start(f32[1024,128]{1,0:T(8,128)} %shard_map.28.own), channel_id=1, source_target_pairs={{3,0},{28,4},{0,1},{29,5},{1,2},{30,6},{2,3},{31,7},{11,8},{4,12},... | collective-permute-start | bytes 1572872 | tf_op jit(solution)/shard_map/ppermute | solution.py:275
  13.2 4.6 %collective-permute-start.5 = (f32[1024,128]{1,0:T(8,128)S(1)}, f32[1024,128]{1,0:T(8,128)S(1)}, u32[]{:S(2)}, u32[]{:S(2)}) collective-permute-start(f32[1024,128]{1,0:T(8,128)S(1)} %collective-permute-done.2.other), channel_id=1, source_target_pairs={{1,0},{12,4},{2,1},{13,5},{3,2},{14,6},{0,3},{15,7},{9,8},{20,12},... | collective-permute-start | bytes 1572872 | tf_op jit(solution)/shard_map/ppermute | solution.py:275
  17.8 3.9 %collective-permute-start.1 = (f32[1024,128]{1,0:T(8,128)S(1)}, f32[1024,128]{1,0:T(8,128)S(1)}, u32[]{:S(2)}, u32[]{:S(2)}) collective-permute-start(f32[1024,128]{1,0:T(8,128)S(1)} %collective-permute-done.o1.first), channel_id=1, source_target_pairs={{1,0},{12,4},{2,1},{13,5},{3,2},{14,6},{0,3},{15,7},{9,8},{20,12},... | collective-permute-start | bytes 1572872 | tf_op jit(solution)/shard_map/ppermute | solution.py:275
  21.8 1.9 %collective-permute-start.4 = (f32[1024,128]{1,0:T(8,128)S(1)}, f32[1024,128]{1,0:T(8,128)S(1)}, u32[]{:S(2)}, u32[]{:S(2)}) collective-permute-start(f32[1024,128]{1,0:T(8,128)S(1)} %collective-permute-done.3.s3.second), channel_id=1, source_target_pairs={{3,0},{28,4},{0,1},{29,5},{1,2},{30,6},{2,3},{31,7},{11,8},{4,12},... | collective-permute-start | bytes 1572872 | tf_op jit(solution)/shard_map/ppermute | solution.py:275
  23.8 4.0 %collective-permute-start.8 = (f32[2048,128]{1,0:T(8,128)S(1)}, f32[2048,128]{1,0:T(8,128)S(1)}, u32[]{:S(2)}, u32[]{:S(2)}) collective-permute-start(f32[2048,128]{1,0:T(8,128)S(1)} %shard_map.31), channel_id=1, source_target_pairs={{0,4},{4,0},{8,12},{12,8},{16,20},{20,16},{24,28},{28,24},{1,5},{5... | collective-permute-start | bytes 3145736 | tf_op jit(solution)/shard_map/ppermute | solution.py:266
  27.9 2.7 %collective-permute-start.9 = (f32[2048,128]{1,0:T(8,128)S(1)}, f32[2048,128]{1,0:T(8,128)S(1)}, u32[]{:S(2)}, u32[]{:S(2)}) collective-permute-start(f32[2048,128]{1,0:T(8,128)S(1)} %shard_map.32), channel_id=1, source_target_pairs={{0,4},{4,0},{8,12},{12,8},{16,20},{20,16},{24,28},{28,24},{1,5},{5... | collective-permute-start | bytes 3145736 | tf_op jit(solution)/shard_map/ppermute | solution.py:266
  32.0 2.1 %collective-permute-done.4.refs_1_.s2 = f32[1024,128]{1,0:T(8,128)S(1)} collective-permute-done((f32[1024,128]{1,0:T(8,128)S(1)}, f32[1024,128]{1,0:T(8,128)S(1)}, u32[]{:S(2)}, u32[]{:S(2)}) %collective-permute-start.4) | collective-permute-done | bytes 524320 | tf_op jit(solution)/shard_map/ppermute | solution.py:275
  34.1 2.0 %collective-permute-start.7 = (f32[2048,128]{1,0:T(8,128)S(1)}, f32[2048,128]{1,0:T(8,128)S(1)}, u32[]{:S(2)}, u32[]{:S(2)}) collective-permute-start(f32[2048,128]{1,0:T(8,128)S(1)} %shard_map.30), channel_id=1, source_target_pairs={{0,4},{4,0},{8,12},{12,8},{16,20},{20,16},{24,28},{28,24},{1,5},{5... | collective-permute-start | bytes 3145736 | tf_op jit(solution)/shard_map/ppermute | solution.py:266
  39.5 3.8 %collective-permute-start.10 = (f32[256,512]{1,0:T(8,128)S(1)}, f32[256,512]{1,0:T(8,128)S(1)}, u32[]{:S(2)}, u32[]{:S(2)}) collective-permute-start(f32[256,512]{1,0:T(8,128)S(1)} %get-tuple-element.44), channel_id=1, source_target_pairs={{0,32},{4,484},{8,40},{12,492},{16,48},{20,500},{24,56},{28,508},{... | collective-permute-start | bytes 1572872 | tf_op jit(solution)/shard_map/ppermute | solution.py:284
  44.8 3.8 %collective-permute-start.12 = (f32[256,512]{1,0:T(8,128)S(1)}, f32[256,512]{1,0:T(8,128)S(1)}, u32[]{:S(2)}, u32[]{:S(2)}) collective-permute-start(f32[256,512]{1,0:T(8,128)S(1)} %get-tuple-element.53), channel_id=1, source_target_pairs={{0,32},{4,484},{8,40},{12,492},{16,48},{20,500},{24,56},{28,508},{... | collective-permute-start | bytes 1572872 | tf_op jit(solution)/shard_map/ppermute | solution.py:284
  48.6 9.4 %collective-permute-done.10.came = f32[256,512]{1,0:T(8,128)S(1)} collective-permute-done((f32[256,512]{1,0:T(8,128)S(1)}, f32[256,512]{1,0:T(8,128)S(1)}, u32[]{:S(2)}, u32[]{:S(2)}) %collective-permute-start.10) | collective-permute-done | bytes 524320 | tf_op jit(solution)/shard_map/ppermute | solution.py:284
  58.1 1.9 %collective-permute-start.11 = (f32[128,512]{1,0:T(8,128)S(1)}, f32[128,512]{1,0:T(8,128)S(1)}, u32[]{:S(2)}, u32[]{:S(2)}) collective-permute-start(f32[128,512]{1,0:T(8,128)S(1)} %get-tuple-element.46), channel_id=1, source_target_pairs={{0,64},{4,452},{8,72},{12,460},{16,80},{20,468},{24,88},{28,476},{... | collective-permute-start | bytes 786440 | tf_op jit(solution)/shard_map/ppermute | solution.py:284
  60.0 3.6 %collective-permute-done.12.refs_1_ = f32[256,512]{1,0:T(8,128)S(1)} collective-permute-done((f32[256,512]{1,0:T(8,128)S(1)}, f32[256,512]{1,0:T(8,128)S(1)}, u32[]{:S(2)}, u32[]{:S(2)}) %collective-permute-start.12) | collective-permute-done | bytes 524320 | tf_op jit(solution)/shard_map/ppermute | solution.py:284
  63.7 1.9 %collective-permute-start.13 = (f32[128,512]{1,0:T(8,128)S(1)}, f32[128,512]{1,0:T(8,128)S(1)}, u32[]{:S(2)}, u32[]{:S(2)}) collective-permute-start(f32[128,512]{1,0:T(8,128)S(1)} %get-tuple-element.55), channel_id=1, source_target_pairs={{0,64},{4,452},{8,72},{12,460},{16,80},{20,468},{24,88},{28,476},{... | collective-permute-start | bytes 786440 | tf_op jit(solution)/shard_map/ppermute | solution.py:284
  65.7 5.2 %collective-permute-done.11.came = f32[128,512]{1,0:T(8,128)S(1)} collective-permute-done((f32[128,512]{1,0:T(8,128)S(1)}, f32[128,512]{1,0:T(8,128)S(1)}, u32[]{:S(2)}, u32[]{:S(2)}) %collective-permute-start.11) | collective-permute-done | bytes 262176 | tf_op jit(solution)/shard_map/ppermute | solution.py:284
  70.9 1.9 %collective-permute-start.14 = (f32[32,512]{1,0:T(8,128)S(1)}, f32[32,512]{1,0:T(8,128)S(1)}, u32[]{:S(2)}, u32[]{:S(2)}) collective-permute-start(f32[32,512]{1,0:T(8,128)S(1)} %get-tuple-element.59), channel_id=1, source_target_pairs={{0,128},{32,160},{64,192},{96,224},{128,256},{160,288},{192,320},{... | collective-permute-start | bytes 196616 | tf_op jit(solution)/shard_map/ppermute | solution.py:288
  72.9 7.2 %collective-permute-done.13.refs_1_ = f32[128,512]{1,0:T(8,128)S(1)} collective-permute-done((f32[128,512]{1,0:T(8,128)S(1)}, f32[128,512]{1,0:T(8,128)S(1)}, u32[]{:S(2)}, u32[]{:S(2)}) %collective-permute-start.13) | collective-permute-done | bytes 262176 | tf_op jit(solution)/shard_map/ppermute | solution.py:284
  80.0 4.6 %collective-permute-start.16 = (f32[32,512]{1,0:T(8,128)S(1)}, f32[32,512]{1,0:T(8,128)S(1)}, u32[]{:S(2)}, u32[]{:S(2)}) collective-permute-start(f32[32,512]{1,0:T(8,128)S(1)} %get-tuple-element.62), channel_id=1, source_target_pairs={{0,384},{32,416},{64,448},{96,480},{128,0},{160,32},{192,64},{224,... | collective-permute-start | bytes 196616 | tf_op jit(solution)/shard_map/ppermute | solution.py:288
  84.7 5.1 %collective-permute-start.15 = (f32[32,1024]{1,0:T(8,128)S(1)}, f32[32,1024]{1,0:T(8,128)S(1)}, u32[]{:S(2)}, u32[]{:S(2)}) collective-permute-start(f32[32,1024]{1,0:T(8,128)S(1)} %shard_map.40.refs_3_), channel_id=1, source_target_pairs={{0,128},{32,160},{64,192},{96,224},{128,256},{160,288},{192,320},{... | collective-permute-start | bytes 393224 | tf_op jit(solution)/shard_map/ppermute | solution.py:288
  90.1 5.5 %collective-permute-start.17 = (f32[32,1024]{1,0:T(8,128)S(1)}, f32[32,1024]{1,0:T(8,128)S(1)}, u32[]{:S(2)}, u32[]{:S(2)}) collective-permute-start(f32[32,1024]{1,0:T(8,128)S(1)} %shard_map.42), channel_id=1, source_target_pairs={{0,384},{32,416},{64,448},{96,480},{128,0},{160,32},{192,64},{224,... | collective-permute-start | bytes 393224 | tf_op jit(solution)/shard_map/ppermute | solution.py:288
  95.6 6.0 %collective-permute-done.15.from_below = f32[32,1024]{1,0:T(8,128)S(1)} collective-permute-done((f32[32,1024]{1,0:T(8,128)S(1)}, f32[32,1024]{1,0:T(8,128)S(1)}, u32[]{:S(2)}, u32[]{:S(2)}) %collective-permute-start.15) | collective-permute-done | bytes 131104 | tf_op jit(solution)/shard_map/ppermute | solution.py:288
  (30 shorter events, 9.4 us)
Async XLA Ops:
  2.0 6.9 %collective-permute-start.2 = (f32[1024,128]{1,0:T(8,128)}, f32[1024,128]{1,0:T(8,128)S(1)}, u32[]{:S(2)}, u32[]{:S(2)}) collective-permute-start(f32[1024,128]{1,0:T(8,128)} %shard_map.28.own), channel_id=1, source_target_pairs={{0,4},{4,0},{8,12},{12,8},{16,20},{20,16},{24,28},{28,24},{1,5},{5... | collective-permute-start | bytes 1572872 | tf_op jit(solution)/shard_map/ppermute | solution.py:266
  3.9 13.9 %collective-permute-start = (f32[1024,128]{1,0:T(8,128)}, f32[1024,128]{1,0:T(8,128)S(1)}, u32[]{:S(2)}, u32[]{:S(2)}) collective-permute-start(f32[1024,128]{1,0:T(8,128)} %shard_map.28.own), channel_id=1, source_target_pairs={{1,0},{12,4},{2,1},{13,5},{3,2},{14,6},{0,3},{15,7},{9,8},{20,12},... | collective-permute-start | bytes 1572872 | tf_op jit(solution)/shard_map/ppermute | solution.py:275
  8.8 12.9 %collective-permute-start.3 = (f32[1024,128]{1,0:T(8,128)S(1)}, f32[1024,128]{1,0:T(8,128)S(1)}, u32[]{:S(2)}, u32[]{:S(2)}) collective-permute-start(f32[1024,128]{1,0:T(8,128)S(1)} %collective-permute-done.2.other), channel_id=1, source_target_pairs={{3,0},{28,4},{0,1},{29,5},{1,2},{30,6},{2,3},{31,7},{11,8},{4,12},... | collective-permute-start | bytes 1572872 | tf_op jit(solution)/shard_map/ppermute | solution.py:275
  10.7 17.0 %collective-permute-start.6 = (f32[1024,128]{1,0:T(8,128)}, f32[1024,128]{1,0:T(8,128)S(1)}, u32[]{:S(2)}, u32[]{:S(2)}) collective-permute-start(f32[1024,128]{1,0:T(8,128)} %shard_map.28.own), channel_id=1, source_target_pairs={{3,0},{28,4},{0,1},{29,5},{1,2},{30,6},{2,3},{31,7},{11,8},{4,12},... | collective-permute-start | bytes 1572872 | tf_op jit(solution)/shard_map/ppermute | solution.py:275
  13.2 14.5 %collective-permute-start.5 = (f32[1024,128]{1,0:T(8,128)S(1)}, f32[1024,128]{1,0:T(8,128)S(1)}, u32[]{:S(2)}, u32[]{:S(2)}) collective-permute-start(f32[1024,128]{1,0:T(8,128)S(1)} %collective-permute-done.2.other), channel_id=1, source_target_pairs={{1,0},{12,4},{2,1},{13,5},{3,2},{14,6},{0,3},{15,7},{9,8},{20,12},... | collective-permute-start | bytes 1572872 | tf_op jit(solution)/shard_map/ppermute | solution.py:275
  17.8 14.1 %collective-permute-start.1 = (f32[1024,128]{1,0:T(8,128)S(1)}, f32[1024,128]{1,0:T(8,128)S(1)}, u32[]{:S(2)}, u32[]{:S(2)}) collective-permute-start(f32[1024,128]{1,0:T(8,128)S(1)} %collective-permute-done.o1.first), channel_id=1, source_target_pairs={{1,0},{12,4},{2,1},{13,5},{3,2},{14,6},{0,3},{15,7},{9,8},{20,12},... | collective-permute-start | bytes 1572872 | tf_op jit(solution)/shard_map/ppermute | solution.py:275
  21.8 12.3 %collective-permute-start.4 = (f32[1024,128]{1,0:T(8,128)S(1)}, f32[1024,128]{1,0:T(8,128)S(1)}, u32[]{:S(2)}, u32[]{:S(2)}) collective-permute-start(f32[1024,128]{1,0:T(8,128)S(1)} %collective-permute-done.3.s3.second), channel_id=1, source_target_pairs={{3,0},{28,4},{0,1},{29,5},{1,2},{30,6},{2,3},{31,7},{11,8},{4,12},... | collective-permute-start | bytes 1572872 | tf_op jit(solution)/shard_map/ppermute | solution.py:275
  23.8 6.8 %copy-start = (f32[1024,128]{1,0:T(8,128)S(1)}, f32[1024,128]{1,0:T(8,128)}, u32[]{:S(2)}) copy-start(f32[1024,128]{1,0:T(8,128)} %shard_map.28.own) | copy-start | bytes 1572868
  23.8 12.4 %collective-permute-start.8 = (f32[2048,128]{1,0:T(8,128)S(1)}, f32[2048,128]{1,0:T(8,128)S(1)}, u32[]{:S(2)}, u32[]{:S(2)}) collective-permute-start(f32[2048,128]{1,0:T(8,128)S(1)} %shard_map.31), channel_id=1, source_target_pairs={{0,4},{4,0},{8,12},{12,8},{16,20},{20,16},{24,28},{28,24},{1,5},{5... | collective-permute-start | bytes 3145736 | tf_op jit(solution)/shard_map/ppermute | solution.py:266
  27.9 8.3 %collective-permute-start.9 = (f32[2048,128]{1,0:T(8,128)S(1)}, f32[2048,128]{1,0:T(8,128)S(1)}, u32[]{:S(2)}, u32[]{:S(2)}) collective-permute-start(f32[2048,128]{1,0:T(8,128)S(1)} %shard_map.32), channel_id=1, source_target_pairs={{0,4},{4,0},{8,12},{12,8},{16,20},{20,16},{24,28},{28,24},{1,5},{5... | collective-permute-start | bytes 3145736 | tf_op jit(solution)/shard_map/ppermute | solution.py:266
  34.1 4.6 %collective-permute-start.7 = (f32[2048,128]{1,0:T(8,128)S(1)}, f32[2048,128]{1,0:T(8,128)S(1)}, u32[]{:S(2)}, u32[]{:S(2)}) collective-permute-start(f32[2048,128]{1,0:T(8,128)S(1)} %shard_map.30), channel_id=1, source_target_pairs={{0,4},{4,0},{8,12},{12,8},{16,20},{20,16},{24,28},{28,24},{1,5},{5... | collective-permute-start | bytes 3145736 | tf_op jit(solution)/shard_map/ppermute | solution.py:266
  39.5 18.6 %collective-permute-start.10 = (f32[256,512]{1,0:T(8,128)S(1)}, f32[256,512]{1,0:T(8,128)S(1)}, u32[]{:S(2)}, u32[]{:S(2)}) collective-permute-start(f32[256,512]{1,0:T(8,128)S(1)} %get-tuple-element.44), channel_id=1, source_target_pairs={{0,32},{4,484},{8,40},{12,492},{16,48},{20,500},{24,56},{28,508},{... | collective-permute-start | bytes 1572872 | tf_op jit(solution)/shard_map/ppermute | solution.py:284
  44.8 18.9 %collective-permute-start.12 = (f32[256,512]{1,0:T(8,128)S(1)}, f32[256,512]{1,0:T(8,128)S(1)}, u32[]{:S(2)}, u32[]{:S(2)}) collective-permute-start(f32[256,512]{1,0:T(8,128)S(1)} %get-tuple-element.53), channel_id=1, source_target_pairs={{0,32},{4,484},{8,40},{12,492},{16,48},{20,500},{24,56},{28,508},{... | collective-permute-start | bytes 1572872 | tf_op jit(solution)/shard_map/ppermute | solution.py:284
  58.1 12.8 %collective-permute-start.11 = (f32[128,512]{1,0:T(8,128)S(1)}, f32[128,512]{1,0:T(8,128)S(1)}, u32[]{:S(2)}, u32[]{:S(2)}) collective-permute-start(f32[128,512]{1,0:T(8,128)S(1)} %get-tuple-element.46), channel_id=1, source_target_pairs={{0,64},{4,452},{8,72},{12,460},{16,80},{20,468},{24,88},{28,476},{... | collective-permute-start | bytes 786440 | tf_op jit(solution)/shard_map/ppermute | solution.py:284
  63.7 16.3 %collective-permute-start.13 = (f32[128,512]{1,0:T(8,128)S(1)}, f32[128,512]{1,0:T(8,128)S(1)}, u32[]{:S(2)}, u32[]{:S(2)}) collective-permute-start(f32[128,512]{1,0:T(8,128)S(1)} %get-tuple-element.55), channel_id=1, source_target_pairs={{0,64},{4,452},{8,72},{12,460},{16,80},{20,468},{24,88},{28,476},{... | collective-permute-start | bytes 786440 | tf_op jit(solution)/shard_map/ppermute | solution.py:284
  70.9 13.8 %collective-permute-start.14 = (f32[32,512]{1,0:T(8,128)S(1)}, f32[32,512]{1,0:T(8,128)S(1)}, u32[]{:S(2)}, u32[]{:S(2)}) collective-permute-start(f32[32,512]{1,0:T(8,128)S(1)} %get-tuple-element.59), channel_id=1, source_target_pairs={{0,128},{32,160},{64,192},{96,224},{128,256},{160,288},{192,320},{... | collective-permute-start | bytes 196616 | tf_op jit(solution)/shard_map/ppermute | solution.py:288
  80.0 10.1 %collective-permute-start.16 = (f32[32,512]{1,0:T(8,128)S(1)}, f32[32,512]{1,0:T(8,128)S(1)}, u32[]{:S(2)}, u32[]{:S(2)}) collective-permute-start(f32[32,512]{1,0:T(8,128)S(1)} %get-tuple-element.62), channel_id=1, source_target_pairs={{0,384},{32,416},{64,448},{96,480},{128,0},{160,32},{192,64},{224,... | collective-permute-start | bytes 196616 | tf_op jit(solution)/shard_map/ppermute | solution.py:288
  84.7 16.9 %collective-permute-start.15 = (f32[32,1024]{1,0:T(8,128)S(1)}, f32[32,1024]{1,0:T(8,128)S(1)}, u32[]{:S(2)}, u32[]{:S(2)}) collective-permute-start(f32[32,1024]{1,0:T(8,128)S(1)} %shard_map.40.refs_3_), channel_id=1, source_target_pairs={{0,128},{32,160},{64,192},{96,224},{128,256},{160,288},{192,320},{... | collective-permute-start | bytes 393224 | tf_op jit(solution)/shard_map/ppermute | solution.py:288
  90.1 11.5 %collective-permute-start.17 = (f32[32,1024]{1,0:T(8,128)S(1)}, f32[32,1024]{1,0:T(8,128)S(1)}, u32[]{:S(2)}, u32[]{:S(2)}) collective-permute-start(f32[32,1024]{1,0:T(8,128)S(1)} %shard_map.42), channel_id=1, source_target_pairs={{0,384},{32,416},{64,448},{96,480},{128,0},{160,32},{192,64},{224,... | collective-permute-start | bytes 393224 | tf_op jit(solution)/shard_map/ppermute | solution.py:288

commit v12 on v11

--- a/solution.py
+++ b/solution.py
@@ -275,6 +275,15 @@
     return lax.ppermute(value, ("row", "col"), pairs)
 
 
+def fetch_across(value, t):
+    pairs = []
+    for x in range(N_X):
+        for y in range(N_COL):
+            pairs.append(((2 * x + 1) * N_COL + (y + t) % N_COL, (2 * x) * N_COL + y))
+            pairs.append(((2 * ((x + t) % N_X)) * N_COL + y, (2 * x + 1) * N_COL + y))
+    return lax.ppermute(value, ("row", "col"), pairs)
+
+
 def pass_on(value, distance):
     pairs = []
     for z in range(N_LAYER):
@@ -305,7 +314,7 @@
     )
     other = swap(masked)
     o1, o3 = fetch(masked, 1), fetch(masked, 3)
-    s3, s1 = fetch(other, 3), fetch(other, 1)
+    s3, s1 = fetch_across(masked, 3), fetch_across(masked, 1)
     o2, s2 = fetch(o1, 1), fetch(s3, 3)
 
     def swap_two(first, second, after=None):

time: 104 us -> 105 us (level)
  the two profiles are of different devices: /device:TPU:6 before, /device:TPU:16 now
where the time goes in v12:
time: 105 us; the launch traced here: 104 us
  starting transfers between devices  57.2 us (54%)
  waiting for transfers between devices  38.4 us (37%)
  Pallas kernels  8.15 us (8%)
    ppermute x4, waiting for transfers between devices, pass_on(): return lax.ppermute(value, ('layer', 'row'), pairs)  25.4 us
    ppermute x4, starting transfers between devices, shift_layers(): lax.ppermute(value, 'layer', [(z, (z + distance) % N_LAYER) for z in rang...  17 us
    ppermute x4, starting transfers between devices, fetch(): return lax.ppermute(value, ('row', 'col'), pairs)  12.6 us
    ppermute x4, starting transfers between devices, pass_on(): return lax.ppermute(value, ('layer', 'row'), pairs)  10.5 us
    ppermute x4, waiting for transfers between devices, shift_layers(): lax.ppermute(value, 'layer', [(z, (z + distance) % N_LAYER) for z in rang...  9.95 us
    ppermute x4, starting transfers between devices, swap(): return lax.ppermute(value, 'row', [(i, i ^ 1) for i in range(N_ROW)])  9.23 us
    pallas_call x16, Pallas kernels, call(): pl.pallas_call(kernel, out_shape=tuple((jax.ShapeDtypeStruct(s, d) for s,...  8.15 us
    ppermute x2, starting transfers between devices, fetch_across(): return lax.ppermute(value, ('row', 'col'), pairs)  7.87 us
  transfers between devices with their start and end apart: 18, of which 9 were waited for; matrix products, arithmetic and copies ran while one was open for 0% of the time, Pallas kernels for 5%

profile of v12, /device:TPU:16, one launch (start us, length us, event | category | flops | bytes accessed | tf_op | source)
XLA Modules:
  0.0 104.1 jit_solution(13626516257179496969)
XLA Ops:
  0.0 1.9 %shard_map.28.own = f32[1024,128]{1,0:T(8,128)} custom-call(f32[1024,128]{1,0:T(8,128)} %graph.1, s32[8]{0:T(128)} %bitcast.1), custom_call_target="tpu_custom_call" | custom-call | bytes 1048576 | tf_op jit(solution)/shard_map/pallas_call | solution.py:30
  2.0 2.4 %collective-permute-start = (f32[1024,128]{1,0:T(8,128)}, f32[1024,128]{1,0:T(8,128)S(1)}, u32[]{:S(2)}, u32[]{:S(2)}) collective-permute-start(f32[1024,128]{1,0:T(8,128)} %shard_map.28.own), channel_id=1, source_target_pairs={{1,0},{12,4},{2,1},{13,5},{3,2},{14,6},{0,3},{15,7},{9,8},{20,12},... | collective-permute-start | bytes 1572872 | tf_op jit(solution)/shard_map/ppermute | solution.py:275
  4.3 2.6 %collective-permute-start.2 = (f32[1024,128]{1,0:T(8,128)}, f32[1024,128]{1,0:T(8,128)S(1)}, u32[]{:S(2)}, u32[]{:S(2)}) collective-permute-start(f32[1024,128]{1,0:T(8,128)} %shard_map.28.own), channel_id=1, source_target_pairs={{7,0},{24,4},{4,1},{25,5},{5,2},{26,6},{6,3},{27,7},{15,8},{0,12},... | collective-permute-start | bytes 1572872 | tf_op jit(solution)/shard_map/ppermute | solution.py:284
  7.0 5.2 %collective-permute-start.5 = (f32[1024,128]{1,0:T(8,128)}, f32[1024,128]{1,0:T(8,128)S(1)}, u32[]{:S(2)}, u32[]{:S(2)}) collective-permute-start(f32[1024,128]{1,0:T(8,128)} %shard_map.28.own), channel_id=1, source_target_pairs={{5,0},{8,4},{6,1},{9,5},{7,2},{10,6},{4,3},{11,7},{13,8},{16,12},{... | collective-permute-start | bytes 1572872 | tf_op jit(solution)/shard_map/ppermute | solution.py:284
  12.2 4.4 %collective-permute-start.6 = (f32[1024,128]{1,0:T(8,128)}, f32[1024,128]{1,0:T(8,128)S(1)}, u32[]{:S(2)}, u32[]{:S(2)}) collective-permute-start(f32[1024,128]{1,0:T(8,128)} %shard_map.28.own), channel_id=1, source_target_pairs={{3,0},{28,4},{0,1},{29,5},{1,2},{30,6},{2,3},{31,7},{11,8},{4,12},... | collective-permute-start | bytes 1572872 | tf_op jit(solution)/shard_map/ppermute | solution.py:275
  18.6 2.7 %collective-permute-start.1 = (f32[1024,128]{1,0:T(8,128)S(1)}, f32[1024,128]{1,0:T(8,128)S(1)}, u32[]{:S(2)}, u32[]{:S(2)}) collective-permute-start(f32[1024,128]{1,0:T(8,128)S(1)} %collective-permute-done.o1.first), channel_id=1, source_target_pairs={{1,0},{12,4},{2,1},{13,5},{3,2},{14,6},{0,3},{15,7},{9,8},{20,12},... | collective-permute-start | bytes 1572872 | tf_op jit(solution)/shard_map/ppermute | solution.py:275
  21.3 3.1 %collective-permute-start.3 = (f32[1024,128]{1,0:T(8,128)S(1)}, f32[1024,128]{1,0:T(8,128)S(1)}, u32[]{:S(2)}, u32[]{:S(2)}) collective-permute-start(f32[1024,128]{1,0:T(8,128)S(1)} %collective-permute-done.2.s3.second), channel_id=1, source_target_pairs={{3,0},{28,4},{0,1},{29,5},{1,2},{30,6},{2,3},{31,7},{11,8},{4,12},... | collective-permute-start | bytes 1572872 | tf_op jit(solution)/shard_map/ppermute | solution.py:275
  24.5 2.1 %collective-permute-start.8 = (f32[2048,128]{1,0:T(8,128)S(1)}, f32[2048,128]{1,0:T(8,128)S(1)}, u32[]{:S(2)}, u32[]{:S(2)}) collective-permute-start(f32[2048,128]{1,0:T(8,128)S(1)} %shard_map.31), channel_id=1, source_target_pairs={{0,4},{4,0},{8,12},{12,8},{16,20},{20,16},{24,28},{28,24},{1,5},{5... | collective-permute-start | bytes 3145736 | tf_op jit(solution)/shard_map/ppermute | solution.py:266
  26.7 2.4 %collective-permute-start.9 = (f32[2048,128]{1,0:T(8,128)S(1)}, f32[2048,128]{1,0:T(8,128)S(1)}, u32[]{:S(2)}, u32[]{:S(2)}) collective-permute-start(f32[2048,128]{1,0:T(8,128)S(1)} %shard_map.32), channel_id=1, source_target_pairs={{0,4},{4,0},{8,12},{12,8},{16,20},{20,16},{24,28},{28,24},{1,5},{5... | collective-permute-start | bytes 3145736 | tf_op jit(solution)/shard_map/ppermute | solution.py:266
  30.5 2.3 %collective-permute-done.3.refs_1_.s2 = f32[1024,128]{1,0:T(8,128)S(1)} collective-permute-done((f32[1024,128]{1,0:T(8,128)S(1)}, f32[1024,128]{1,0:T(8,128)S(1)}, u32[]{:S(2)}, u32[]{:S(2)}) %collective-permute-start.3) | collective-permute-done | bytes 524320 | tf_op jit(solution)/shard_map/ppermute | solution.py:275
  32.8 2.8 %collective-permute-start.7 = (f32[2048,128]{1,0:T(8,128)S(1)}, f32[2048,128]{1,0:T(8,128)S(1)}, u32[]{:S(2)}, u32[]{:S(2)}) collective-permute-start(f32[2048,128]{1,0:T(8,128)S(1)} %shard_map.30), channel_id=1, source_target_pairs={{0,4},{4,0},{8,12},{12,8},{16,20},{20,16},{24,28},{28,24},{1,5},{5... | collective-permute-start | bytes 3145736 | tf_op jit(solution)/shard_map/ppermute | solution.py:266
  38.8 2.8 %collective-permute-start.10 = (f32[256,512]{1,0:T(8,128)S(1)}, f32[256,512]{1,0:T(8,128)S(1)}, u32[]{:S(2)}, u32[]{:S(2)}) collective-permute-start(f32[256,512]{1,0:T(8,128)S(1)} %get-tuple-element.44), channel_id=1, source_target_pairs={{0,32},{4,484},{8,40},{12,492},{16,48},{20,500},{24,56},{28,508},{... | collective-permute-start | bytes 1572872 | tf_op jit(solution)/shard_map/ppermute | solution.py:293
  43.0 3.8 %collective-permute-start.12 = (f32[256,512]{1,0:T(8,128)S(1)}, f32[256,512]{1,0:T(8,128)S(1)}, u32[]{:S(2)}, u32[]{:S(2)}) collective-permute-start(f32[256,512]{1,0:T(8,128)S(1)} %get-tuple-element.53), channel_id=1, source_target_pairs={{0,32},{4,484},{8,40},{12,492},{16,48},{20,500},{24,56},{28,508},{... | collective-permute-start | bytes 1572872 | tf_op jit(solution)/shard_map/ppermute | solution.py:293
  46.9 9.4 %collective-permute-done.10.came = f32[256,512]{1,0:T(8,128)S(1)} collective-permute-done((f32[256,512]{1,0:T(8,128)S(1)}, f32[256,512]{1,0:T(8,128)S(1)}, u32[]{:S(2)}, u32[]{:S(2)}) %collective-permute-start.10) | collective-permute-done | bytes 524320 | tf_op jit(solution)/shard_map/ppermute | solution.py:293
  56.3 1.9 %collective-permute-start.11 = (f32[128,512]{1,0:T(8,128)S(1)}, f32[128,512]{1,0:T(8,128)S(1)}, u32[]{:S(2)}, u32[]{:S(2)}) collective-permute-start(f32[128,512]{1,0:T(8,128)S(1)} %get-tuple-element.46), channel_id=1, source_target_pairs={{0,64},{4,452},{8,72},{12,460},{16,80},{20,468},{24,88},{28,476},{... | collective-permute-start | bytes 786440 | tf_op jit(solution)/shard_map/ppermute | solution.py:293
  58.3 3.6 %collective-permute-done.12.refs_1_ = f32[256,512]{1,0:T(8,128)S(1)} collective-permute-done((f32[256,512]{1,0:T(8,128)S(1)}, f32[256,512]{1,0:T(8,128)S(1)}, u32[]{:S(2)}, u32[]{:S(2)}) %collective-permute-start.12) | collective-permute-done | bytes 524320 | tf_op jit(solution)/shard_map/ppermute | solution.py:293
  62.0 1.9 %collective-permute-start.13 = (f32[128,512]{1,0:T(8,128)S(1)}, f32[128,512]{1,0:T(8,128)S(1)}, u32[]{:S(2)}, u32[]{:S(2)}) collective-permute-start(f32[128,512]{1,0:T(8,128)S(1)} %get-tuple-element.55), channel_id=1, source_target_pairs={{0,64},{4,452},{8,72},{12,460},{16,80},{20,468},{24,88},{28,476},{... | collective-permute-start | bytes 786440 | tf_op jit(solution)/shard_map/ppermute | solution.py:293
  63.9 5.2 %collective-permute-done.11.came = f32[128,512]{1,0:T(8,128)S(1)} collective-permute-done((f32[128,512]{1,0:T(8,128)S(1)}, f32[128,512]{1,0:T(8,128)S(1)}, u32[]{:S(2)}, u32[]{:S(2)}) %collective-permute-start.11) | collective-permute-done | bytes 262176 | tf_op jit(solution)/shard_map/ppermute | solution.py:293
  71.1 7.2 %collective-permute-done.13.refs_1_ = f32[128,512]{1,0:T(8,128)S(1)} collective-permute-done((f32[128,512]{1,0:T(8,128)S(1)}, f32[128,512]{1,0:T(8,128)S(1)}, u32[]{:S(2)}, u32[]{:S(2)}) %collective-permute-start.13) | collective-permute-done | bytes 262176 | tf_op jit(solution)/shard_map/ppermute | solution.py:293
  78.3 4.1 %collective-permute-start.16 = (f32[32,512]{1,0:T(8,128)S(1)}, f32[32,512]{1,0:T(8,128)S(1)}, u32[]{:S(2)}, u32[]{:S(2)}) collective-permute-start(f32[32,512]{1,0:T(8,128)S(1)} %get-tuple-element.62), channel_id=1, source_target_pairs={{0,384},{32,416},{64,448},{96,480},{128,0},{160,32},{192,64},{224,... | collective-permute-start | bytes 196616 | tf_op jit(solution)/shard_map/ppermute | solution.py:297
  82.5 5.6 %collective-permute-start.15 = (f32[32,1024]{1,0:T(8,128)S(1)}, f32[32,1024]{1,0:T(8,128)S(1)}, u32[]{:S(2)}, u32[]{:S(2)}) collective-permute-start(f32[32,1024]{1,0:T(8,128)S(1)} %shard_map.40.refs_3_), channel_id=1, source_target_pairs={{0,128},{32,160},{64,192},{96,224},{128,256},{160,288},{192,320},{... | collective-permute-start | bytes 393224 | tf_op jit(solution)/shard_map/ppermute | solution.py:297
  88.4 5.4 %collective-permute-start.17 = (f32[32,1024]{1,0:T(8,128)S(1)}, f32[32,1024]{1,0:T(8,128)S(1)}, u32[]{:S(2)}, u32[]{:S(2)}) collective-permute-start(f32[32,1024]{1,0:T(8,128)S(1)} %shard_map.42), channel_id=1, source_target_pairs={{0,384},{32,416},{64,448},{96,480},{128,0},{160,32},{192,64},{224,... | collective-permute-start | bytes 393224 | tf_op jit(solution)/shard_map/ppermute | solution.py:297
  93.7 6.3 %collective-permute-done.15.from_below = f32[32,1024]{1,0:T(8,128)S(1)} collective-permute-done((f32[32,1024]{1,0:T(8,128)S(1)}, f32[32,1024]{1,0:T(8,128)S(1)}, u32[]{:S(2)}, u32[]{:S(2)}) %collective-permute-start.15) | collective-permute-done | bytes 131104 | tf_op jit(solution)/shard_map/ppermute | solution.py:297
  100.0 3.4 %collective-permute-done.17.from_above = f32[32,1024]{1,0:T(8,128)S(1)} collective-permute-done((f32[32,1024]{1,0:T(8,128)S(1)}, f32[32,1024]{1,0:T(8,128)S(1)}, u32[]{:S(2)}, u32[]{:S(2)}) %collective-permute-start.17) | collective-permute-done | bytes 131104 | tf_op jit(solution)/shard_map/ppermute | solution.py:297
  (30 shorter events, 11.1 us)
Async XLA Ops:
  2.0 16.6 %collective-permute-start = (f32[1024,128]{1,0:T(8,128)}, f32[1024,128]{1,0:T(8,128)S(1)}, u32[]{:S(2)}, u32[]{:S(2)}) collective-permute-start(f32[1024,128]{1,0:T(8,128)} %shard_map.28.own), channel_id=1, source_target_pairs={{1,0},{12,4},{2,1},{13,5},{3,2},{14,6},{0,3},{15,7},{9,8},{20,12},... | collective-permute-start | bytes 1572872 | tf_op jit(solution)/shard_map/ppermute | solution.py:275
  4.3 17.0 %collective-permute-start.2 = (f32[1024,128]{1,0:T(8,128)}, f32[1024,128]{1,0:T(8,128)S(1)}, u32[]{:S(2)}, u32[]{:S(2)}) collective-permute-start(f32[1024,128]{1,0:T(8,128)} %shard_map.28.own), channel_id=1, source_target_pairs={{7,0},{24,4},{4,1},{25,5},{5,2},{26,6},{6,3},{27,7},{15,8},{0,12},... | collective-permute-start | bytes 1572872 | tf_op jit(solution)/shard_map/ppermute | solution.py:284
  7.0 17.5 %collective-permute-start.5 = (f32[1024,128]{1,0:T(8,128)}, f32[1024,128]{1,0:T(8,128)S(1)}, u32[]{:S(2)}, u32[]{:S(2)}) collective-permute-start(f32[1024,128]{1,0:T(8,128)} %shard_map.28.own), channel_id=1, source_target_pairs={{5,0},{8,4},{6,1},{9,5},{7,2},{10,6},{4,3},{11,7},{13,8},{16,12},{... | collective-permute-start | bytes 1572872 | tf_op jit(solution)/shard_map/ppermute | solution.py:284
  12.2 14.4 %collective-permute-start.6 = (f32[1024,128]{1,0:T(8,128)}, f32[1024,128]{1,0:T(8,128)S(1)}, u32[]{:S(2)}, u32[]{:S(2)}) collective-permute-start(f32[1024,128]{1,0:T(8,128)} %shard_map.28.own), channel_id=1, source_target_pairs={{3,0},{28,4},{0,1},{29,5},{1,2},{30,6},{2,3},{31,7},{11,8},{4,12},... | collective-permute-start | bytes 1572872 | tf_op jit(solution)/shard_map/ppermute | solution.py:275
  16.6 12.5 %collective-permute-start.4 = (f32[1024,128]{1,0:T(8,128)}, f32[1024,128]{1,0:T(8,128)S(1)}, u32[]{:S(2)}, u32[]{:S(2)}) collective-permute-start(f32[1024,128]{1,0:T(8,128)} %shard_map.28.own), channel_id=1, source_target_pairs={{0,4},{4,0},{8,12},{12,8},{16,20},{20,16},{24,28},{28,24},{1,5},{5... | collective-permute-start | bytes 1572872 | tf_op jit(solution)/shard_map/ppermute | solution.py:266
  18.6 11.9 %collective-permute-start.1 = (f32[1024,128]{1,0:T(8,128)S(1)}, f32[1024,128]{1,0:T(8,128)S(1)}, u32[]{:S(2)}, u32[]{:S(2)}) collective-permute-start(f32[1024,128]{1,0:T(8,128)S(1)} %collective-permute-done.o1.first), channel_id=1, source_target_pairs={{1,0},{12,4},{2,1},{13,5},{3,2},{14,6},{0,3},{15,7},{9,8},{20,12},... | collective-permute-start | bytes 1572872 | tf_op jit(solution)/shard_map/ppermute | solution.py:275
  21.3 11.4 %collective-permute-start.3 = (f32[1024,128]{1,0:T(8,128)S(1)}, f32[1024,128]{1,0:T(8,128)S(1)}, u32[]{:S(2)}, u32[]{:S(2)}) collective-permute-start(f32[1024,128]{1,0:T(8,128)S(1)} %collective-permute-done.2.s3.second), channel_id=1, source_target_pairs={{3,0},{28,4},{0,1},{29,5},{1,2},{30,6},{2,3},{31,7},{11,8},{4,12},... | collective-permute-start | bytes 1572872 | tf_op jit(solution)/shard_map/ppermute | solution.py:275
  24.5 4.6 %copy-start = (f32[1024,128]{1,0:T(8,128)S(1)}, f32[1024,128]{1,0:T(8,128)}, u32[]{:S(2)}) copy-start(f32[1024,128]{1,0:T(8,128)} %shard_map.28.own) | copy-start | bytes 1572868
  24.5 11.2 %collective-permute-start.8 = (f32[2048,128]{1,0:T(8,128)S(1)}, f32[2048,128]{1,0:T(8,128)S(1)}, u32[]{:S(2)}, u32[]{:S(2)}) collective-permute-start(f32[2048,128]{1,0:T(8,128)S(1)} %shard_map.31), channel_id=1, source_target_pairs={{0,4},{4,0},{8,12},{12,8},{16,20},{20,16},{24,28},{28,24},{1,5},{5... | collective-permute-start | bytes 3145736 | tf_op jit(solution)/shard_map/ppermute | solution.py:266
  26.7 9.0 %collective-permute-start.9 = (f32[2048,128]{1,0:T(8,128)S(1)}, f32[2048,128]{1,0:T(8,128)S(1)}, u32[]{:S(2)}, u32[]{:S(2)}) collective-permute-start(f32[2048,128]{1,0:T(8,128)S(1)} %shard_map.32), channel_id=1, source_target_pairs={{0,4},{4,0},{8,12},{12,8},{16,20},{20,16},{24,28},{28,24},{1,5},{5... | collective-permute-start | bytes 3145736 | tf_op jit(solution)/shard_map/ppermute | solution.py:266
  32.8 5.1 %collective-permute-start.7 = (f32[2048,128]{1,0:T(8,128)S(1)}, f32[2048,128]{1,0:T(8,128)S(1)}, u32[]{:S(2)}, u32[]{:S(2)}) collective-permute-start(f32[2048,128]{1,0:T(8,128)S(1)} %shard_map.30), channel_id=1, source_target_pairs={{0,4},{4,0},{8,12},{12,8},{16,20},{20,16},{24,28},{28,24},{1,5},{5... | collective-permute-start | bytes 3145736 | tf_op jit(solution)/shard_map/ppermute | solution.py:266
  38.8 17.5 %collective-permute-start.10 = (f32[256,512]{1,0:T(8,128)S(1)}, f32[256,512]{1,0:T(8,128)S(1)}, u32[]{:S(2)}, u32[]{:S(2)}) collective-permute-start(f32[256,512]{1,0:T(8,128)S(1)} %get-tuple-element.44), channel_id=1, source_target_pairs={{0,32},{4,484},{8,40},{12,492},{16,48},{20,500},{24,56},{28,508},{... | collective-permute-start | bytes 1572872 | tf_op jit(solution)/shard_map/ppermute | solution.py:293
  43.0 18.9 %collective-permute-start.12 = (f32[256,512]{1,0:T(8,128)S(1)}, f32[256,512]{1,0:T(8,128)S(1)}, u32[]{:S(2)}, u32[]{:S(2)}) collective-permute-start(f32[256,512]{1,0:T(8,128)S(1)} %get-tuple-element.53), channel_id=1, source_target_pairs={{0,32},{4,484},{8,40},{12,492},{16,48},{20,500},{24,56},{28,508},{... | collective-permute-start | bytes 1572872 | tf_op jit(solution)/shard_map/ppermute | solution.py:293
  56.3 12.8 %collective-permute-start.11 = (f32[128,512]{1,0:T(8,128)S(1)}, f32[128,512]{1,0:T(8,128)S(1)}, u32[]{:S(2)}, u32[]{:S(2)}) collective-permute-start(f32[128,512]{1,0:T(8,128)S(1)} %get-tuple-element.46), channel_id=1, source_target_pairs={{0,64},{4,452},{8,72},{12,460},{16,80},{20,468},{24,88},{28,476},{... | collective-permute-start | bytes 786440 | tf_op jit(solution)/shard_map/ppermute | solution.py:293
  62.0 16.3 %collective-permute-start.13 = (f32[128,512]{1,0:T(8,128)S(1)}, f32[128,512]{1,0:T(8,128)S(1)}, u32[]{:S(2)}, u32[]{:S(2)}) collective-permute-start(f32[128,512]{1,0:T(8,128)S(1)} %get-tuple-element.55), channel_id=1, source_target_pairs={{0,64},{4,452},{8,72},{12,460},{16,80},{20,468},{24,88},{28,476},{... | collective-permute-start | bytes 786440 | tf_op jit(solution)/shard_map/ppermute | solution.py:293
  69.2 13.3 %collective-permute-start.14 = (f32[32,512]{1,0:T(8,128)S(1)}, f32[32,512]{1,0:T(8,128)S(1)}, u32[]{:S(2)}, u32[]{:S(2)}) collective-permute-start(f32[32,512]{1,0:T(8,128)S(1)} %get-tuple-element.59), channel_id=1, source_target_pairs={{0,128},{32,160},{64,192},{96,224},{128,256},{160,288},{192,320},{... | collective-permute-start | bytes 196616 | tf_op jit(solution)/shard_map/ppermute | solution.py:297
  78.3 10.1 %collective-permute-start.16 = (f32[32,512]{1,0:T(8,128)S(1)}, f32[32,512]{1,0:T(8,128)S(1)}, u32[]{:S(2)}, u32[]{:S(2)}) collective-permute-start(f32[32,512]{1,0:T(8,128)S(1)} %get-tuple-element.62), channel_id=1, source_target_pairs={{0,384},{32,416},{64,448},{96,480},{128,0},{160,32},{192,64},{224,... | collective-permute-start | bytes 196616 | tf_op jit(solution)/shard_map/ppermute | solution.py:297
  82.5 17.6 %collective-permute-start.15 = (f32[32,1024]{1,0:T(8,128)S(1)}, f32[32,1024]{1,0:T(8,128)S(1)}, u32[]{:S(2)}, u32[]{:S(2)}) collective-permute-start(f32[32,1024]{1,0:T(8,128)S(1)} %shard_map.40.refs_3_), channel_id=1, source_target_pairs={{0,128},{32,160},{64,192},{96,224},{128,256},{160,288},{192,320},{... | collective-permute-start | bytes 393224 | tf_op jit(solution)/shard_map/ppermute | solution.py:297
  88.4 15.1 %collective-permute-start.17 = (f32[32,1024]{1,0:T(8,128)S(1)}, f32[32,1024]{1,0:T(8,128)S(1)}, u32[]{:S(2)}, u32[]{:S(2)}) collective-permute-start(f32[32,1024]{1,0:T(8,128)S(1)} %shard_map.42), channel_id=1, source_target_pairs={{0,384},{32,416},{64,448},{96,480},{128,0},{160,32},{192,64},{224,... | collective-permute-start | bytes 393224 | tf_op jit(solution)/shard_map/ppermute | solution.py:297

commit v13 on v11

--- a/solution.py
+++ b/solution.py
@@ -145,22 +145,16 @@
     return pl.ds(pl.multiple_of(index * SUB, SUB), SUB)
 
 
-def scatter(total, send, keep):
-    z, y = lax.axis_index("layer"), lax.axis_index("col")
-
-    def rows_of(layer):
-        t = lax.rem(layer // 4 - y + N_COL, N_COL)
-        index = jnp.where(t < 2, t, 5 - t)
-        return strip(index * 4 + lax.rem(layer, 4))
-
-    for j in range(N_LAYER // 2):
-        rows = pl.ds(j * SUB, SUB)
-        keep[rows, :] = total[rows_of(lax.rem(z + 2 * j, N_LAYER)), :]
-        send[rows, :] = total[rows_of(lax.rem(z + turn() + 2 * j + N_LAYER, N_LAYER)), :]
+def scatter(total, outs):
+    z = lax.axis_index("layer")
+    for shift, out in zip((0, 1, -1, 2), outs):
+        s = lax.rem(z + turn() * shift + 4, 4)
+        for index in range(4):
+            out[pl.ds(index * SUB, SUB), :] = total[strip(index * 4 + s), :]
 
 
 def second_product_kernel(o2, s2, both, early_right, early_right_low, early, right_high, right_low, beside, below, *refs):
-    send, keep, last_high, last_low, total = refs
+    outs, (last_high, last_low, total) = refs[:4], refs[4:]
     known, wide = early.shape[0], 2 * TILE
     first, next_ = pl.ds(0, wide), pl.ds(wide, wide)
 
@@ -183,13 +177,13 @@
         total[TILE:known, :] = below[:, columns]
         last_rows(columns, early_right[:, columns], early_right_low[:, columns])
 
-    scatter(total, send, keep)
+    scatter(total, outs)
 
 
 def third_product_kernel(o2, s2, both, last_high, last_low, *refs):
     early_left, early_left_low, early_right, early_right_low, early = refs[:5]
     left_high, left_low, right_high, right_low, beside, below = refs[5:11]
-    send, keep, far_high, far_low, total = refs[11:]
+    outs, (far_high, far_low, total) = refs[11:15], refs[15:]
     o2_swapped, s2_swapped = halves(both)
     known, wide = early.shape[0], 2 * TILE
     first, next_, third = (pl.ds(i * wide, wide) for i in range(3))
@@ -217,23 +211,19 @@
         far(pl.ds(TILE, known - TILE), left_high[...], left_low[...])
         far(pl.ds(known, TILE), last_high[...], last_low[...])
 
-    scatter(total, send, keep)
-
-
-def stage_kernel(held, came, send, keep):
-    count = held.shape[0] // SUB
-    for i in range(count // 2):
-        rows = pl.ds(i * SUB, SUB)
-        near = pl.ds(2 * i * SUB, SUB)
-        far = strip(lax.rem(turn() + 2 * i + count, count))
-        keep[rows, :] = held[near, :] + came[near, :]
-        send[rows, :] = held[far, :] + came[far, :]
-
-
-def group_kernel(held, came, own, up, far, down):
+    scatter(total, outs)
+
+
+def add_kernel(held, came, out):
+    out[...] = held[...] + came[...]
+
+
+def group_kernel(mine, below, above, own, up, far, down):
+    group, y = lax.axis_index("layer") // 4, lax.axis_index("col")
     for i, out in enumerate((own, up, far, down)):
-        rows = pl.ds(i * SUB, SUB)
-        out[...] = held[rows, :] + came[rows, :]
+        t = lax.rem(group + turn() * i - y + 8, 4)
+        rows = strip(jnp.where(t < 2, t, 5 - t))
+        out[...] = mine[rows, :] + (below[rows, :] + above[rows, :])
 
 
 def up_kernel(first, second, came, out):
@@ -282,10 +272,6 @@
             to = (z + (distance if row % 2 == 0 else -distance)) % N_LAYER
             pairs.append((z * N_ROW + row, to * N_ROW + row))
     return lax.ppermute(value, ("layer", "row"), pairs)
-
-
-def shift_layers(value, distance):
-    return lax.ppermute(value, "layer", [(z, (z + distance) % N_LAYER) for z in range(N_LAYER)])
 
 
 def on_device(graph, pattern):
@@ -324,40 +310,36 @@
         flops=4 * known * wide * inner,
         nbytes=8 << 20,
     )
-    out = (8 * SUB, 4 * TILE)
+    cut = (4 * SUB, 4 * TILE)
     total = pltpu.VMEM((4 * TILE, 4 * TILE), F32)
-    send_a, keep_a, *last = call(
+    mine_a, up_a, down_a, two_a, *last = call(
         second_product_kernel,
-        [out, out, ((TILE, inner), BF16), ((TILE, inner), BF16)],
+        [cut] * 4 + [((TILE, inner), BF16)] * 2,
         (*second, *early[2:], *late[2:]),
         scratch=[total],
         flops=6 * TILE * 4 * TILE * inner,
         nbytes=4 << 20,
     )
-    send_b, keep_b = call(
+    mine_b, up_b, down_b, two_b = call(
         third_product_kernel,
-        [out, out],
+        [cut] * 4,
         (*second, *last, *early, *late),
         scratch=[pltpu.VMEM((inner, 2 * TILE), BF16)] * 2 + [total],
         flops=6 * 5 * TILE * 2 * TILE * inner,
         nbytes=4 << 20,
     )
-    sends, keeps = [send_a, send_b], [keep_a, keep_b]
-    arrived = [pass_on(sends[half], 1) for half in range(2)]
-    done = None
-    for half in range(2):
-        sends[half], keeps[half] = call(
-            stage_kernel, [(4 * SUB, 4 * TILE)] * 2, (keeps[half], arrived[half]), after=done
-        )
-        done = keeps[half]
-        arrived[half] = pass_on(sends[half], 2)
-    first = call(group_kernel, [(SUB, 4 * TILE)] * 4, (keeps[0], arrived[0]))
-    second = call(group_kernel, [(SUB, 4 * TILE)] * 4, (keeps[1], arrived[1]), after=first[0])
+    (up_a,) = call(add_kernel, [cut], (up_a, pass_on(two_a, 1)))
+    (down_b,) = call(add_kernel, [cut], (down_b, pass_on(two_b, -1)), after=up_a)
+    piece = [(SUB, 4 * TILE)] * 4
+    first = call(group_kernel, piece, (mine_a, pass_on(up_a, 1), pass_on(down_a, -1)))
+    second = call(
+        group_kernel, piece, (mine_b, pass_on(up_b, 1), pass_on(down_b, -1)), after=first[0]
+    )
     chunk = [(SUB, 8 * TILE)]
-    (up,) = call(up_kernel, chunk, (first[1], second[1], shift_layers(first[2], 4)))
-    (down,) = call(down_kernel, chunk, (first[3], second[3], shift_layers(second[2], -4)), after=up)
-    (held,) = call(below_kernel, chunk, (first[0], second[0], shift_layers(up, 4)))
-    return call(last_kernel, chunk, (held, shift_layers(down, -4)))[0]
+    (up,) = call(up_kernel, chunk, (first[1], second[1], pass_on(first[2], 4)))
+    (down,) = call(down_kernel, chunk, (first[3], second[3], pass_on(second[2], -4)), after=up)
+    (held,) = call(below_kernel, chunk, (first[0], second[0], pass_on(up, 4)))
+    return call(last_kernel, chunk, (held, pass_on(down, -4)))[0]
 
 
 def solution(mesh):

time: 104 us -> 103 us (level)
  waiting for transfers between devices: 34.8 us -> 14.7 us
  starting transfers between devices: 59 us -> 78 us
    ppermute x4 -> x10, starting transfers between devices: 11.5 us -> 47.7 us  [pass_on(): return lax.ppermute(value, ('layer', 'row'), pairs)]
    ppermute x4 -> x0, starting transfers between devices: 17.1 us -> none  [shift_layers(): lax.ppermute(value, 'layer', [(z, (z + distance) % N_LAYER) for z in rang...]
    ppermute x4 -> x10, waiting for transfers between devices: 25.4 us -> 11.6 us  [pass_on(): return lax.ppermute(value, ('layer', 'row'), pairs)]
    ppermute x4 -> x0, waiting for transfers between devices: 6.25 us -> none  [shift_layers(): lax.ppermute(value, 'layer', [(z, (z + distance) % N_LAYER) for z in rang...]
  transfers between devices with their start and end apart: 18 -> 20, of which waited for: 8 -> 7; matrix products, arithmetic and copies ran while one was open for 0% -> 0% of each run, Pallas kernels for 5% -> 5%
where the time goes in v13:
time: 103 us; the launch traced here: 101 us
  starting transfers between devices  78 us (76%)
  waiting for transfers between devices  14.7 us (14%)
  Pallas kernels  7.94 us (8%)
    ppermute x10, starting transfers between devices, pass_on(): return lax.ppermute(value, ('layer', 'row'), pairs)  47.7 us
    ppermute x6, starting transfers between devices, fetch(): return lax.ppermute(value, ('row', 'col'), pairs)  19.7 us
    ppermute x10, waiting for transfers between devices, pass_on(): return lax.ppermute(value, ('layer', 'row'), pairs)  11.6 us
    ppermute x4, starting transfers between devices, swap(): return lax.ppermute(value, 'row', [(i, i ^ 1) for i in range(N_ROW)])  10.6 us
    pallas_call x16, Pallas kernels, call(): pl.pallas_call(kernel, out_shape=tuple((jax.ShapeDtypeStruct(s, d) for s,...  7.94 us
    ppermute x6, waiting for transfers between devices, fetch(): return lax.ppermute(value, ('row', 'col'), pairs)  2.08 us
  transfers between devices with their start and end apart: 20, of which 7 were waited for; matrix products, arithmetic and copies ran while one was open for 0% of the time, Pallas kernels for 5%

profile of v13, /device:TPU:6, one launch (start us, length us, event | category | flops | bytes accessed | tf_op | source)
XLA Modules:
  0.0 101.0 jit_solution(15136255030923884874)
XLA Ops:
  0.0 1.9 %shard_map.28.own = f32[1024,128]{1,0:T(8,128)} custom-call(f32[1024,128]{1,0:T(8,128)} %graph.1, s32[8]{0:T(128)} %bitcast.1), custom_call_target="tpu_custom_call" | custom-call | bytes 1048576 | tf_op jit(solution)/shard_map/pallas_call | solution.py:30
  2.0 1.9 %collective-permute-start.2 = (f32[1024,128]{1,0:T(8,128)}, f32[1024,128]{1,0:T(8,128)S(1)}, u32[]{:S(2)}, u32[]{:S(2)}) collective-permute-start(f32[1024,128]{1,0:T(8,128)} %shard_map.28.own), channel_id=1, source_target_pairs={{0,4},{4,0},{8,12},{12,8},{16,20},{20,16},{24,28},{28,24},{1,5},{5... | collective-permute-start | bytes 1572872 | tf_op jit(solution)/shard_map/ppermute | solution.py:256
  3.9 4.9 %collective-permute-start = (f32[1024,128]{1,0:T(8,128)}, f32[1024,128]{1,0:T(8,128)S(1)}, u32[]{:S(2)}, u32[]{:S(2)}) collective-permute-start(f32[1024,128]{1,0:T(8,128)} %shard_map.28.own), channel_id=1, source_target_pairs={{1,0},{12,4},{2,1},{13,5},{3,2},{14,6},{0,3},{15,7},{9,8},{20,12},... | collective-permute-start | bytes 1572872 | tf_op jit(solution)/shard_map/ppermute | solution.py:265
  8.8 1.9 %collective-permute-start.3 = (f32[1024,128]{1,0:T(8,128)S(1)}, f32[1024,128]{1,0:T(8,128)S(1)}, u32[]{:S(2)}, u32[]{:S(2)}) collective-permute-start(f32[1024,128]{1,0:T(8,128)S(1)} %collective-permute-done.2.other), channel_id=1, source_target_pairs={{3,0},{28,4},{0,1},{29,5},{1,2},{30,6},{2,3},{31,7},{11,8},{4,12},... | collective-permute-start | bytes 1572872 | tf_op jit(solution)/shard_map/ppermute | solution.py:265
  10.7 2.5 %collective-permute-start.6 = (f32[1024,128]{1,0:T(8,128)}, f32[1024,128]{1,0:T(8,128)S(1)}, u32[]{:S(2)}, u32[]{:S(2)}) collective-permute-start(f32[1024,128]{1,0:T(8,128)} %shard_map.28.own), channel_id=1, source_target_pairs={{3,0},{28,4},{0,1},{29,5},{1,2},{30,6},{2,3},{31,7},{11,8},{4,12},... | collective-permute-start | bytes 1572872 | tf_op jit(solution)/shard_map/ppermute | solution.py:265
  13.2 4.6 %collective-permute-start.5 = (f32[1024,128]{1,0:T(8,128)S(1)}, f32[1024,128]{1,0:T(8,128)S(1)}, u32[]{:S(2)}, u32[]{:S(2)}) collective-permute-start(f32[1024,128]{1,0:T(8,128)S(1)} %collective-permute-done.2.other), channel_id=1, source_target_pairs={{1,0},{12,4},{2,1},{13,5},{3,2},{14,6},{0,3},{15,7},{9,8},{20,12},... | collective-permute-start | bytes 1572872 | tf_op jit(solution)/shard_map/ppermute | solution.py:265
  17.8 3.9 %collective-permute-start.1 = (f32[1024,128]{1,0:T(8,128)S(1)}, f32[1024,128]{1,0:T(8,128)S(1)}, u32[]{:S(2)}, u32[]{:S(2)}) collective-permute-start(f32[1024,128]{1,0:T(8,128)S(1)} %collective-permute-done.o1.first), channel_id=1, source_target_pairs={{1,0},{12,4},{2,1},{13,5},{3,2},{14,6},{0,3},{15,7},{9,8},{20,12},... | collective-permute-start | bytes 1572872 | tf_op jit(solution)/shard_map/ppermute | solution.py:265
  21.8 1.9 %collective-permute-start.4 = (f32[1024,128]{1,0:T(8,128)S(1)}, f32[1024,128]{1,0:T(8,128)S(1)}, u32[]{:S(2)}, u32[]{:S(2)}) collective-permute-start(f32[1024,128]{1,0:T(8,128)S(1)} %collective-permute-done.3.s3.second), channel_id=1, source_target_pairs={{3,0},{28,4},{0,1},{29,5},{1,2},{30,6},{2,3},{31,7},{11,8},{4,12},... | collective-permute-start | bytes 1572872 | tf_op jit(solution)/shard_map/ppermute | solution.py:265
  23.8 4.0 %collective-permute-start.8 = (f32[2048,128]{1,0:T(8,128)S(1)}, f32[2048,128]{1,0:T(8,128)S(1)}, u32[]{:S(2)}, u32[]{:S(2)}) collective-permute-start(f32[2048,128]{1,0:T(8,128)S(1)} %shard_map.31), channel_id=1, source_target_pairs={{0,4},{4,0},{8,12},{12,8},{16,20},{20,16},{24,28},{28,24},{1,5},{5... | collective-permute-start | bytes 3145736 | tf_op jit(solution)/shard_map/ppermute | solution.py:256
  27.9 2.7 %collective-permute-start.9 = (f32[2048,128]{1,0:T(8,128)S(1)}, f32[2048,128]{1,0:T(8,128)S(1)}, u32[]{:S(2)}, u32[]{:S(2)}) collective-permute-start(f32[2048,128]{1,0:T(8,128)S(1)} %shard_map.32), channel_id=1, source_target_pairs={{0,4},{4,0},{8,12},{12,8},{16,20},{20,16},{24,28},{28,24},{1,5},{5... | collective-permute-start | bytes 3145736 | tf_op jit(solution)/shard_map/ppermute | solution.py:256
  32.0 2.1 %collective-permute-done.4.refs_1_.s2 = f32[1024,128]{1,0:T(8,128)S(1)} collective-permute-done((f32[1024,128]{1,0:T(8,128)S(1)}, f32[1024,128]{1,0:T(8,128)S(1)}, u32[]{:S(2)}, u32[]{:S(2)}) %collective-permute-start.4) | collective-permute-done | bytes 524320 | tf_op jit(solution)/shard_map/ppermute | solution.py:265
  34.1 2.0 %collective-permute-start.7 = (f32[2048,128]{1,0:T(8,128)S(1)}, f32[2048,128]{1,0:T(8,128)S(1)}, u32[]{:S(2)}, u32[]{:S(2)}) collective-permute-start(f32[2048,128]{1,0:T(8,128)S(1)} %shard_map.30), channel_id=1, source_target_pairs={{0,4},{4,0},{8,12},{12,8},{16,20},{20,16},{24,28},{28,24},{1,5},{5... | collective-permute-start | bytes 3145736 | tf_op jit(solution)/shard_map/ppermute | solution.py:256
  39.4 3.8 %collective-permute-start.10 = (f32[128,512]{1,0:T(8,128)S(1)}, f32[128,512]{1,0:T(8,128)S(1)}, u32[]{:S(2)}, u32[]{:S(2)}) collective-permute-start(f32[128,512]{1,0:T(8,128)S(1)} %get-tuple-element.45), channel_id=1, source_target_pairs={{0,32},{4,484},{8,40},{12,492},{16,48},{20,500},{24,56},{28,508},{... | collective-permute-start | bytes 786440 | tf_op jit(solution)/shard_map/ppermute | solution.py:274
  44.6 9.5 %collective-permute-start.14 = (f32[128,512]{1,0:T(8,128)S(1)}, f32[128,512]{1,0:T(8,128)S(1)}, u32[]{:S(2)}, u32[]{:S(2)}) collective-permute-start(f32[128,512]{1,0:T(8,128)S(1)} %get-tuple-element.55), channel_id=1, source_target_pairs={{0,480},{4,36},{8,488},{12,44},{16,496},{20,52},{24,504},{28,60},{... | collective-permute-start | bytes 786440 | tf_op jit(solution)/shard_map/ppermute | solution.py:274
  54.1 3.9 %collective-permute-start.12 = (f32[128,512]{1,0:T(8,128)S(1)}, f32[128,512]{1,0:T(8,128)S(1)}, u32[]{:S(2)}, u32[]{:S(2)}) collective-permute-start(f32[128,512]{1,0:T(8,128)S(1)} %get-tuple-element.46), channel_id=1, source_target_pairs={{0,480},{4,36},{8,488},{12,44},{16,496},{20,52},{24,504},{28,60},{... | collective-permute-start | bytes 786440 | tf_op jit(solution)/shard_map/ppermute | solution.py:274
  58.1 1.9 %collective-permute-start.11 = (f32[128,512]{1,0:T(8,128)S(1)}, f32[128,512]{1,0:T(8,128)S(1)}, u32[]{:S(2)}, u32[]{:S(2)}) collective-permute-start(f32[128,512]{1,0:T(8,128)S(1)} %shard_map.35.refs_2_), channel_id=1, source_target_pairs={{0,32},{4,484},{8,40},{12,492},{16,48},{20,500},{24,56},{28,508},{... | collective-permute-start | bytes 786440 | tf_op jit(solution)/shard_map/ppermute | solution.py:274
  60.0 1.9 %collective-permute-start.13 = (f32[128,512]{1,0:T(8,128)S(1)}, f32[128,512]{1,0:T(8,128)S(1)}, u32[]{:S(2)}, u32[]{:S(2)}) collective-permute-start(f32[128,512]{1,0:T(8,128)S(1)} %get-tuple-element.53), channel_id=1, source_target_pairs={{0,32},{4,484},{8,40},{12,492},{16,48},{20,500},{24,56},{28,508},{... | collective-permute-start | bytes 786440 | tf_op jit(solution)/shard_map/ppermute | solution.py:274
  62.0 5.1 %collective-permute-start.15 = (f32[128,512]{1,0:T(8,128)S(1)}, f32[128,512]{1,0:T(8,128)S(1)}, u32[]{:S(2)}, u32[]{:S(2)}) collective-permute-start(f32[128,512]{1,0:T(8,128)S(1)} %shard_map.38), channel_id=1, source_target_pairs={{0,480},{4,36},{8,488},{12,44},{16,496},{20,52},{24,504},{28,60},{... | collective-permute-start | bytes 786440 | tf_op jit(solution)/shard_map/ppermute | solution.py:274
  67.6 2.4 %collective-permute-start.16 = (f32[32,512]{1,0:T(8,128)S(1)}, f32[32,512]{1,0:T(8,128)S(1)}, u32[]{:S(2)}, u32[]{:S(2)}) collective-permute-start(f32[32,512]{1,0:T(8,128)S(1)} %get-tuple-element.59), channel_id=1, source_target_pairs={{0,128},{4,388},{8,136},{12,396},{16,144},{20,404},{24,152},{28,41... | collective-permute-start | bytes 196616 | tf_op jit(solution)/shard_map/ppermute | solution.py:274
  71.1 8.4 %collective-permute-start.18 = (f32[32,512]{1,0:T(8,128)S(1)}, f32[32,512]{1,0:T(8,128)S(1)}, u32[]{:S(2)}, u32[]{:S(2)}) collective-permute-start(f32[32,512]{1,0:T(8,128)S(1)} %get-tuple-element.62), channel_id=1, source_target_pairs={{0,384},{4,132},{8,392},{12,140},{16,400},{20,148},{24,408},{28,15... | collective-permute-start | bytes 196616 | tf_op jit(solution)/shard_map/ppermute | solution.py:274
  79.9 1.9 %collective-permute-start.17 = (f32[32,1024]{1,0:T(8,128)S(1)}, f32[32,1024]{1,0:T(8,128)S(1)}, u32[]{:S(2)}, u32[]{:S(2)}) collective-permute-start(f32[32,1024]{1,0:T(8,128)S(1)} %shard_map.40.refs_3_), channel_id=1, source_target_pairs={{0,128},{4,388},{8,136},{12,396},{16,144},{20,404},{24,152},{28,41... | collective-permute-start | bytes 393224 | tf_op jit(solution)/shard_map/ppermute | solution.py:274
  81.8 4.2 %collective-permute-done.18.refs_2_ = f32[32,512]{1,0:T(8,128)S(1)} collective-permute-done((f32[32,512]{1,0:T(8,128)S(1)}, f32[32,512]{1,0:T(8,128)S(1)}, u32[]{:S(2)}, u32[]{:S(2)}) %collective-permute-start.18) | collective-permute-done | bytes 65568 | tf_op jit(solution)/shard_map/ppermute | solution.py:274
  86.1 8.7 %collective-permute-start.19 = (f32[32,1024]{1,0:T(8,128)S(1)}, f32[32,1024]{1,0:T(8,128)S(1)}, u32[]{:S(2)}, u32[]{:S(2)}) collective-permute-start(f32[32,1024]{1,0:T(8,128)S(1)} %shard_map.42), channel_id=1, source_target_pairs={{0,384},{4,132},{8,392},{12,140},{16,400},{20,148},{24,408},{28,15... | collective-permute-start | bytes 393224 | tf_op jit(solution)/shard_map/ppermute | solution.py:274
  94.8 5.6 %collective-permute-done.17.from_below = f32[32,1024]{1,0:T(8,128)S(1)} collective-permute-done((f32[32,1024]{1,0:T(8,128)S(1)}, f32[32,1024]{1,0:T(8,128)S(1)}, u32[]{:S(2)}, u32[]{:S(2)}) %collective-permute-start.17) | collective-permute-done | bytes 131104 | tf_op jit(solution)/shard_map/ppermute | solution.py:274
  (34 shorter events, 8.8 us)
Async XLA Ops:
  2.0 6.9 %collective-permute-start.2 = (f32[1024,128]{1,0:T(8,128)}, f32[1024,128]{1,0:T(8,128)S(1)}, u32[]{:S(2)}, u32[]{:S(2)}) collective-permute-start(f32[1024,128]{1,0:T(8,128)} %shard_map.28.own), channel_id=1, source_target_pairs={{0,4},{4,0},{8,12},{12,8},{16,20},{20,16},{24,28},{28,24},{1,5},{5... | collective-permute-start | bytes 1572872 | tf_op jit(solution)/shard_map/ppermute | solution.py:256
  3.9 13.9 %collective-permute-start = (f32[1024,128]{1,0:T(8,128)}, f32[1024,128]{1,0:T(8,128)S(1)}, u32[]{:S(2)}, u32[]{:S(2)}) collective-permute-start(f32[1024,128]{1,0:T(8,128)} %shard_map.28.own), channel_id=1, source_target_pairs={{1,0},{12,4},{2,1},{13,5},{3,2},{14,6},{0,3},{15,7},{9,8},{20,12},... | collective-permute-start | bytes 1572872 | tf_op jit(solution)/shard_map/ppermute | solution.py:265
  8.8 12.9 %collective-permute-start.3 = (f32[1024,128]{1,0:T(8,128)S(1)}, f32[1024,128]{1,0:T(8,128)S(1)}, u32[]{:S(2)}, u32[]{:S(2)}) collective-permute-start(f32[1024,128]{1,0:T(8,128)S(1)} %collective-permute-done.2.other), channel_id=1, source_target_pairs={{3,0},{28,4},{0,1},{29,5},{1,2},{30,6},{2,3},{31,7},{11,8},{4,12},... | collective-permute-start | bytes 1572872 | tf_op jit(solution)/shard_map/ppermute | solution.py:265
  10.7 17.0 %collective-permute-start.6 = (f32[1024,128]{1,0:T(8,128)}, f32[1024,128]{1,0:T(8,128)S(1)}, u32[]{:S(2)}, u32[]{:S(2)}) collective-permute-start(f32[1024,128]{1,0:T(8,128)} %shard_map.28.own), channel_id=1, source_target_pairs={{3,0},{28,4},{0,1},{29,5},{1,2},{30,6},{2,3},{31,7},{11,8},{4,12},... | collective-permute-start | bytes 1572872 | tf_op jit(solution)/shard_map/ppermute | solution.py:265
  13.2 14.5 %collective-permute-start.5 = (f32[1024,128]{1,0:T(8,128)S(1)}, f32[1024,128]{1,0:T(8,128)S(1)}, u32[]{:S(2)}, u32[]{:S(2)}) collective-permute-start(f32[1024,128]{1,0:T(8,128)S(1)} %collective-permute-done.2.other), channel_id=1, source_target_pairs={{1,0},{12,4},{2,1},{13,5},{3,2},{14,6},{0,3},{15,7},{9,8},{20,12},... | collective-permute-start | bytes 1572872 | tf_op jit(solution)/shard_map/ppermute | solution.py:265
  17.8 14.1 %collective-permute-start.1 = (f32[1024,128]{1,0:T(8,128)S(1)}, f32[1024,128]{1,0:T(8,128)S(1)}, u32[]{:S(2)}, u32[]{:S(2)}) collective-permute-start(f32[1024,128]{1,0:T(8,128)S(1)} %collective-permute-done.o1.first), channel_id=1, source_target_pairs={{1,0},{12,4},{2,1},{13,5},{3,2},{14,6},{0,3},{15,7},{9,8},{20,12},... | collective-permute-start | bytes 1572872 | tf_op jit(solution)/shard_map/ppermute | solution.py:265
  21.8 12.3 %collective-permute-start.4 = (f32[1024,128]{1,0:T(8,128)S(1)}, f32[1024,128]{1,0:T(8,128)S(1)}, u32[]{:S(2)}, u32[]{:S(2)}) collective-permute-start(f32[1024,128]{1,0:T(8,128)S(1)} %collective-permute-done.3.s3.second), channel_id=1, source_target_pairs={{3,0},{28,4},{0,1},{29,5},{1,2},{30,6},{2,3},{31,7},{11,8},{4,12},... | collective-permute-start | bytes 1572872 | tf_op jit(solution)/shard_map/ppermute | solution.py:265
  23.8 6.8 %copy-start = (f32[1024,128]{1,0:T(8,128)S(1)}, f32[1024,128]{1,0:T(8,128)}, u32[]{:S(2)}) copy-start(f32[1024,128]{1,0:T(8,128)} %shard_map.28.own) | copy-start | bytes 1572868
  23.8 12.4 %collective-permute-start.8 = (f32[2048,128]{1,0:T(8,128)S(1)}, f32[2048,128]{1,0:T(8,128)S(1)}, u32[]{:S(2)}, u32[]{:S(2)}) collective-permute-start(f32[2048,128]{1,0:T(8,128)S(1)} %shard_map.31), channel_id=1, source_target_pairs={{0,4},{4,0},{8,12},{12,8},{16,20},{20,16},{24,28},{28,24},{1,5},{5... | collective-permute-start | bytes 3145736 | tf_op jit(solution)/shard_map/ppermute | solution.py:256
  27.9 8.3 %collective-permute-start.9 = (f32[2048,128]{1,0:T(8,128)S(1)}, f32[2048,128]{1,0:T(8,128)S(1)}, u32[]{:S(2)}, u32[]{:S(2)}) collective-permute-start(f32[2048,128]{1,0:T(8,128)S(1)} %shard_map.32), channel_id=1, source_target_pairs={{0,4},{4,0},{8,12},{12,8},{16,20},{20,16},{24,28},{28,24},{1,5},{5... | collective-permute-start | bytes 3145736 | tf_op jit(solution)/shard_map/ppermute | solution.py:256
  34.1 4.6 %collective-permute-start.7 = (f32[2048,128]{1,0:T(8,128)S(1)}, f32[2048,128]{1,0:T(8,128)S(1)}, u32[]{:S(2)}, u32[]{:S(2)}) collective-permute-start(f32[2048,128]{1,0:T(8,128)S(1)} %shard_map.30), channel_id=1, source_target_pairs={{0,4},{4,0},{8,12},{12,8},{16,20},{20,16},{24,28},{28,24},{1,5},{5... | collective-permute-start | bytes 3145736 | tf_op jit(solution)/shard_map/ppermute | solution.py:256
  39.4 18.6 %collective-permute-start.10 = (f32[128,512]{1,0:T(8,128)S(1)}, f32[128,512]{1,0:T(8,128)S(1)}, u32[]{:S(2)}, u32[]{:S(2)}) collective-permute-start(f32[128,512]{1,0:T(8,128)S(1)} %get-tuple-element.45), channel_id=1, source_target_pairs={{0,32},{4,484},{8,40},{12,492},{16,48},{20,500},{24,56},{28,508},{... | collective-permute-start | bytes 786440 | tf_op jit(solution)/shard_map/ppermute | solution.py:274
  44.6 17.3 %collective-permute-start.14 = (f32[128,512]{1,0:T(8,128)S(1)}, f32[128,512]{1,0:T(8,128)S(1)}, u32[]{:S(2)}, u32[]{:S(2)}) collective-permute-start(f32[128,512]{1,0:T(8,128)S(1)} %get-tuple-element.55), channel_id=1, source_target_pairs={{0,480},{4,36},{8,488},{12,44},{16,496},{20,52},{24,504},{28,60},{... | collective-permute-start | bytes 786440 | tf_op jit(solution)/shard_map/ppermute | solution.py:274
  54.1 13.0 %collective-permute-start.12 = (f32[128,512]{1,0:T(8,128)S(1)}, f32[128,512]{1,0:T(8,128)S(1)}, u32[]{:S(2)}, u32[]{:S(2)}) collective-permute-start(f32[128,512]{1,0:T(8,128)S(1)} %get-tuple-element.46), channel_id=1, source_target_pairs={{0,480},{4,36},{8,488},{12,44},{16,496},{20,52},{24,504},{28,60},{... | collective-permute-start | bytes 786440 | tf_op jit(solution)/shard_map/ppermute | solution.py:274
  58.1 9.5 %collective-permute-start.11 = (f32[128,512]{1,0:T(8,128)S(1)}, f32[128,512]{1,0:T(8,128)S(1)}, u32[]{:S(2)}, u32[]{:S(2)}) collective-permute-start(f32[128,512]{1,0:T(8,128)S(1)} %shard_map.35.refs_2_), channel_id=1, source_target_pairs={{0,32},{4,484},{8,40},{12,492},{16,48},{20,500},{24,56},{28,508},{... | collective-permute-start | bytes 786440 | tf_op jit(solution)/shard_map/ppermute | solution.py:274
  60.0 11.0 %collective-permute-start.13 = (f32[128,512]{1,0:T(8,128)S(1)}, f32[128,512]{1,0:T(8,128)S(1)}, u32[]{:S(2)}, u32[]{:S(2)}) collective-permute-start(f32[128,512]{1,0:T(8,128)S(1)} %get-tuple-element.53), channel_id=1, source_target_pairs={{0,32},{4,484},{8,40},{12,492},{16,48},{20,500},{24,56},{28,508},{... | collective-permute-start | bytes 786440 | tf_op jit(solution)/shard_map/ppermute | solution.py:274
  62.0 9.0 %collective-permute-start.15 = (f32[128,512]{1,0:T(8,128)S(1)}, f32[128,512]{1,0:T(8,128)S(1)}, u32[]{:S(2)}, u32[]{:S(2)}) collective-permute-start(f32[128,512]{1,0:T(8,128)S(1)} %shard_map.38), channel_id=1, source_target_pairs={{0,480},{4,36},{8,488},{12,44},{16,496},{20,52},{24,504},{28,60},{... | collective-permute-start | bytes 786440 | tf_op jit(solution)/shard_map/ppermute | solution.py:274
  67.6 12.3 %collective-permute-start.16 = (f32[32,512]{1,0:T(8,128)S(1)}, f32[32,512]{1,0:T(8,128)S(1)}, u32[]{:S(2)}, u32[]{:S(2)}) collective-permute-start(f32[32,512]{1,0:T(8,128)S(1)} %get-tuple-element.59), channel_id=1, source_target_pairs={{0,128},{4,388},{8,136},{12,396},{16,144},{20,404},{24,152},{28,41... | collective-permute-start | bytes 196616 | tf_op jit(solution)/shard_map/ppermute | solution.py:274
  71.1 15.0 %collective-permute-start.18 = (f32[32,512]{1,0:T(8,128)S(1)}, f32[32,512]{1,0:T(8,128)S(1)}, u32[]{:S(2)}, u32[]{:S(2)}) collective-permute-start(f32[32,512]{1,0:T(8,128)S(1)} %get-tuple-element.62), channel_id=1, source_target_pairs={{0,384},{4,132},{8,392},{12,140},{16,400},{20,148},{24,408},{28,15... | collective-permute-start | bytes 196616 | tf_op jit(solution)/shard_map/ppermute | solution.py:274
  79.9 20.4 %collective-permute-start.17 = (f32[32,1024]{1,0:T(8,128)S(1)}, f32[32,1024]{1,0:T(8,128)S(1)}, u32[]{:S(2)}, u32[]{:S(2)}) collective-permute-start(f32[32,1024]{1,0:T(8,128)S(1)} %shard_map.40.refs_3_), channel_id=1, source_target_pairs={{0,128},{4,388},{8,136},{12,396},{16,144},{20,404},{24,152},{28,41... | collective-permute-start | bytes 393224 | tf_op jit(solution)/shard_map/ppermute | solution.py:274
  86.1 14.3 %collective-permute-start.19 = (f32[32,1024]{1,0:T(8,128)S(1)}, f32[32,1024]{1,0:T(8,128)S(1)}, u32[]{:S(2)}, u32[]{:S(2)}) collective-permute-start(f32[32,1024]{1,0:T(8,128)S(1)} %shard_map.42), channel_id=1, source_target_pairs={{0,384},{4,132},{8,392},{12,140},{16,400},{20,148},{24,408},{28,15... | collective-permute-start | bytes 393224 | tf_op jit(solution)/shard_map/ppermute | solution.py:274

commit v14 on v13

--- a/solution.py
+++ b/solution.py
@@ -20,7 +20,7 @@
 F32, BF16 = jnp.float32, jnp.bfloat16
 
 
-def call(kernel, outs, operands, specs=None, scratch=(), flops=0, nbytes=1 << 20, after=None, limit=LIMIT):
+def call(kernel, outs, operands, specs=None, scratch=(), flops=0, nbytes=1 << 20, after=None, limit=LIMIT, out_spec=VMEM):
     if after is not None:
         inner_kernel, count = kernel, len(operands)
         kernel = lambda *refs: inner_kernel(*refs[:count], *refs[count + 1 :])
@@ -31,27 +31,31 @@
         kernel,
         out_shape=tuple(jax.ShapeDtypeStruct(s, d) for s, d in outs),
         in_specs=specs or [VMEM] * len(operands),
-        out_specs=tuple(VMEM for _ in outs),
+        out_specs=tuple(out_spec for _ in outs),
         scratch_shapes=list(scratch),
         compiler_params=pltpu.CompilerParams(vmem_limit_bytes=limit),
         cost_estimate=pl.CostEstimate(flops=flops, bytes_accessed=nbytes, transcendentals=0),
     )(*operands)
 
 
-def mask_kernel(graph, pattern, masked, raw, flags, sems):
+def mask_kernel(graph, pattern, masked, raw, flags, sems, out_sems):
     tiles = graph.shape[0] // TILE
     flag_copy = pltpu.make_async_copy(pattern, flags, sems.at[tiles])
     flag_copy.start()
-    copies = []
+    copies, outs = [], []
     for k in range(tiles):
         rows = pl.ds(k * TILE, TILE)
         copies.append(pltpu.make_async_copy(graph.at[rows, :], raw.at[rows, :], sems.at[k]))
+        outs.append(pltpu.make_async_copy(raw.at[rows, :], masked.at[rows, :], out_sems.at[k]))
         copies[k].start()
     flag_copy.wait()
     for k in range(tiles):
         rows = pl.ds(k * TILE, TILE)
         copies[k].wait()
-        masked[rows, :] = raw[rows, :] * flags[k].astype(F32)
+        raw[rows, :] = raw[rows, :] * flags[k].astype(F32)
+        outs[k].start()
+    for out in outs:
+        out.wait()
 
 
 def core():
@@ -59,9 +63,9 @@
 
 
 def join_kernel(first, second, pair):
-    inner = first.shape[0]
-    pair[:inner, :] = first[...]
-    pair[inner:, :] = second[...]
+    rows = first.shape[0]
+    pair[:rows, :] = first[...]
+    pair[rows:, :] = second[...]
 
 
 def split(value):
@@ -218,8 +222,9 @@
     out[...] = held[...] + came[...]
 
 
-def group_kernel(mine, below, above, own, up, far, down):
+def group_kernel(half, mine, below, both_above, own, up, far, down):
     group, y = lax.axis_index("layer") // 4, lax.axis_index("col")
+    above = both_above.at[pl.ds(half * mine.shape[0], mine.shape[0]), :]
     for i, out in enumerate((own, up, far, down)):
         t = lax.rem(group + turn() * i - y + 8, 4)
         rows = strip(jnp.where(t < 2, t, 5 - t))
@@ -286,8 +291,10 @@
             pltpu.VMEM((inner, TILE), F32),
             pltpu.SMEM((tiles,), jnp.int32),
             pltpu.SemaphoreType.DMA((tiles + 1,)),
+            pltpu.SemaphoreType.DMA((tiles,)),
         ],
         limit=62 * 1024 * 1024,
+        out_spec=pl.BlockSpec(memory_space=pltpu.HBM),
     )
     other = swap(masked)
     o1, o3 = fetch(masked, 1), fetch(masked, 3)
@@ -328,13 +335,13 @@
         flops=6 * 5 * TILE * 2 * TILE * inner,
         nbytes=4 << 20,
     )
+    (downs,) = call(join_kernel, [(8 * SUB, 4 * TILE)], (down_a, down_b))
+    above = pass_on(downs, -1)
     (up_a,) = call(add_kernel, [cut], (up_a, pass_on(two_a, 1)))
-    (down_b,) = call(add_kernel, [cut], (down_b, pass_on(two_b, -1)), after=up_a)
+    (up_b,) = call(add_kernel, [cut], (up_b, pass_on(two_b, 1)), after=up_a)
     piece = [(SUB, 4 * TILE)] * 4
-    first = call(group_kernel, piece, (mine_a, pass_on(up_a, 1), pass_on(down_a, -1)))
-    second = call(
-        group_kernel, piece, (mine_b, pass_on(up_b, 1), pass_on(down_b, -1)), after=first[0]
-    )
+    first = call(functools.partial(group_kernel, 0), piece, (mine_a, pass_on(up_a, 1), above))
+    second = call(functools.partial(group_kernel, 1), piece, (mine_b, pass_on(up_b, 1), above), after=first[0])
     chunk = [(SUB, 8 * TILE)]
     (up,) = call(up_kernel, chunk, (first[1], second[1], pass_on(first[2], 4)))
     (down,) = call(down_kernel, chunk, (first[3], second[3], pass_on(second[2], -4)), after=up)

time: 103 us -> 102 us (level)
  starting transfers between devices: 78 us -> 68.4 us
  waiting for transfers between devices: 14.7 us -> 24.1 us
    ppermute x10 -> x9, starting transfers between devices: 47.7 us -> 38 us  [pass_on(): return lax.ppermute(value, ('layer', 'row'), pairs)]
    ppermute x10 -> x9, waiting for transfers between devices: 11.6 us -> 21 us  [pass_on(): return lax.ppermute(value, ('layer', 'row'), pairs)]
    pallas_call x16 -> x17, Pallas kernels: 7.94 us -> 7.87 us  [call(): pl.pallas_call(kernel, out_shape=tuple((jax.ShapeDtypeStruct(s, d) for s,...]
  transfers between devices with their start and end apart: 20 -> 19, of which waited for: 7 -> 7; matrix products, arithmetic and copies ran while one was open for 0% -> 0% of each run, Pallas kernels for 5% -> 5%
where the time goes in v14:
time: 102 us; the launch traced here: 101 us
  starting transfers between devices  68.4 us (67%)
  waiting for transfers between devices  24.1 us (24%)
  Pallas kernels  7.87 us (8%)
    ppermute x9, starting transfers between devices, pass_on(): return lax.ppermute(value, ('layer', 'row'), pairs)  38 us
    ppermute x9, waiting for transfers between devices, pass_on(): return lax.ppermute(value, ('layer', 'row'), pairs)  21 us
    ppermute x6, starting transfers between devices, fetch(): return lax.ppermute(value, ('row', 'col'), pairs)  19.7 us
    ppermute x4, starting transfers between devices, swap(): return lax.ppermute(value, 'row', [(i, i ^ 1) for i in range(N_ROW)])  10.6 us
    pallas_call x17, Pallas kernels, call(): pl.pallas_call(kernel, out_shape=tuple((jax.ShapeDtypeStruct(s, d) for s,...  7.87 us
    ppermute x6, waiting for transfers between devices, fetch(): return lax.ppermute(value, ('row', 'col'), pairs)  2.08 us
  transfers between devices with their start and end apart: 19, of which 7 were waited for; matrix products, arithmetic and copies ran while one was open for 0% of the time, Pallas kernels for 5%

profile of v14, /device:TPU:6, one launch (start us, length us, event | category | flops | bytes accessed | tf_op | source)
XLA Modules:
  0.0 100.7 jit_solution(17540517641551068143)
XLA Ops:
  1.8 1.9 %collective-permute-start.2 = (f32[1024,128]{1,0:T(8,128)}, f32[1024,128]{1,0:T(8,128)S(1)}, u32[]{:S(2)}, u32[]{:S(2)}) collective-permute-start(f32[1024,128]{1,0:T(8,128)} %shard_map.28.own), channel_id=1, source_target_pairs={{0,4},{4,0},{8,12},{12,8},{16,20},{20,16},{24,28},{28,24},{1,5},{5... | collective-permute-start | bytes 1572872 | tf_op jit(solution)/shard_map/ppermute | solution.py:261
  3.8 4.9 %collective-permute-start = (f32[1024,128]{1,0:T(8,128)}, f32[1024,128]{1,0:T(8,128)S(1)}, u32[]{:S(2)}, u32[]{:S(2)}) collective-permute-start(f32[1024,128]{1,0:T(8,128)} %shard_map.28.own), channel_id=1, source_target_pairs={{1,0},{12,4},{2,1},{13,5},{3,2},{14,6},{0,3},{15,7},{9,8},{20,12},... | collective-permute-start | bytes 1572872 | tf_op jit(solution)/shard_map/ppermute | solution.py:270
  8.7 1.9 %collective-permute-start.3 = (f32[1024,128]{1,0:T(8,128)S(1)}, f32[1024,128]{1,0:T(8,128)S(1)}, u32[]{:S(2)}, u32[]{:S(2)}) collective-permute-start(f32[1024,128]{1,0:T(8,128)S(1)} %collective-permute-done.2.other), channel_id=1, source_target_pairs={{3,0},{28,4},{0,1},{29,5},{1,2},{30,6},{2,3},{31,7},{11,8},{4,12},... | collective-permute-start | bytes 1572872 | tf_op jit(solution)/shard_map/ppermute | solution.py:270
  10.6 2.5 %collective-permute-start.6 = (f32[1024,128]{1,0:T(8,128)}, f32[1024,128]{1,0:T(8,128)S(1)}, u32[]{:S(2)}, u32[]{:S(2)}) collective-permute-start(f32[1024,128]{1,0:T(8,128)} %shard_map.28.own), channel_id=1, source_target_pairs={{3,0},{28,4},{0,1},{29,5},{1,2},{30,6},{2,3},{31,7},{11,8},{4,12},... | collective-permute-start | bytes 1572872 | tf_op jit(solution)/shard_map/ppermute | solution.py:270
  13.1 4.6 %collective-permute-start.5 = (f32[1024,128]{1,0:T(8,128)S(1)}, f32[1024,128]{1,0:T(8,128)S(1)}, u32[]{:S(2)}, u32[]{:S(2)}) collective-permute-start(f32[1024,128]{1,0:T(8,128)S(1)} %collective-permute-done.2.other), channel_id=1, source_target_pairs={{1,0},{12,4},{2,1},{13,5},{3,2},{14,6},{0,3},{15,7},{9,8},{20,12},... | collective-permute-start | bytes 1572872 | tf_op jit(solution)/shard_map/ppermute | solution.py:270
  17.7 3.9 %collective-permute-start.1 = (f32[1024,128]{1,0:T(8,128)S(1)}, f32[1024,128]{1,0:T(8,128)S(1)}, u32[]{:S(2)}, u32[]{:S(2)}) collective-permute-start(f32[1024,128]{1,0:T(8,128)S(1)} %collective-permute-done.o1.first), channel_id=1, source_target_pairs={{1,0},{12,4},{2,1},{13,5},{3,2},{14,6},{0,3},{15,7},{9,8},{20,12},... | collective-permute-start | bytes 1572872 | tf_op jit(solution)/shard_map/ppermute | solution.py:270
  21.7 1.9 %collective-permute-start.4 = (f32[1024,128]{1,0:T(8,128)S(1)}, f32[1024,128]{1,0:T(8,128)S(1)}, u32[]{:S(2)}, u32[]{:S(2)}) collective-permute-start(f32[1024,128]{1,0:T(8,128)S(1)} %collective-permute-done.3.s3.second), channel_id=1, source_target_pairs={{3,0},{28,4},{0,1},{29,5},{1,2},{30,6},{2,3},{31,7},{11,8},{4,12},... | collective-permute-start | bytes 1572872 | tf_op jit(solution)/shard_map/ppermute | solution.py:270
  23.7 4.0 %collective-permute-start.8 = (f32[2048,128]{1,0:T(8,128)S(1)}, f32[2048,128]{1,0:T(8,128)S(1)}, u32[]{:S(2)}, u32[]{:S(2)}) collective-permute-start(f32[2048,128]{1,0:T(8,128)S(1)} %shard_map.31), channel_id=1, source_target_pairs={{0,4},{4,0},{8,12},{12,8},{16,20},{20,16},{24,28},{28,24},{1,5},{5... | collective-permute-start | bytes 3145736 | tf_op jit(solution)/shard_map/ppermute | solution.py:261
  27.8 2.7 %collective-permute-start.9 = (f32[2048,128]{1,0:T(8,128)S(1)}, f32[2048,128]{1,0:T(8,128)S(1)}, u32[]{:S(2)}, u32[]{:S(2)}) collective-permute-start(f32[2048,128]{1,0:T(8,128)S(1)} %shard_map.32), channel_id=1, source_target_pairs={{0,4},{4,0},{8,12},{12,8},{16,20},{20,16},{24,28},{28,24},{1,5},{5... | collective-permute-start | bytes 3145736 | tf_op jit(solution)/shard_map/ppermute | solution.py:261
  31.9 2.1 %collective-permute-done.4.refs_1_.s2 = f32[1024,128]{1,0:T(8,128)S(1)} collective-permute-done((f32[1024,128]{1,0:T(8,128)S(1)}, f32[1024,128]{1,0:T(8,128)S(1)}, u32[]{:S(2)}, u32[]{:S(2)}) %collective-permute-start.4) | collective-permute-done | bytes 524320 | tf_op jit(solution)/shard_map/ppermute | solution.py:270
  34.0 2.0 %collective-permute-start.7 = (f32[2048,128]{1,0:T(8,128)S(1)}, f32[2048,128]{1,0:T(8,128)S(1)}, u32[]{:S(2)}, u32[]{:S(2)}) collective-permute-start(f32[2048,128]{1,0:T(8,128)S(1)} %shard_map.30), channel_id=1, source_target_pairs={{0,4},{4,0},{8,12},{12,8},{16,20},{20,16},{24,28},{28,24},{1,5},{5... | collective-permute-start | bytes 3145736 | tf_op jit(solution)/shard_map/ppermute | solution.py:261
  39.3 3.8 %collective-permute-start.10 = (f32[128,512]{1,0:T(8,128)S(1)}, f32[128,512]{1,0:T(8,128)S(1)}, u32[]{:S(2)}, u32[]{:S(2)}) collective-permute-start(f32[128,512]{1,0:T(8,128)S(1)} %get-tuple-element.45), channel_id=1, source_target_pairs={{0,32},{4,484},{8,40},{12,492},{16,48},{20,500},{24,56},{28,508},{... | collective-permute-start | bytes 786440 | tf_op jit(solution)/shard_map/ppermute | solution.py:279
  44.5 9.5 %collective-permute-start.12 = (f32[256,512]{1,0:T(8,128)S(1)}, f32[256,512]{1,0:T(8,128)S(1)}, u32[]{:S(2)}, u32[]{:S(2)}) collective-permute-start(f32[256,512]{1,0:T(8,128)S(1)} %shard_map.37), channel_id=1, source_target_pairs={{0,480},{4,36},{8,488},{12,44},{16,496},{20,52},{24,504},{28,60},{... | collective-permute-start | bytes 1572872 | tf_op jit(solution)/shard_map/ppermute | solution.py:279
  54.0 1.9 %collective-permute-start.13 = (f32[128,512]{1,0:T(8,128)S(1)}, f32[128,512]{1,0:T(8,128)S(1)}, u32[]{:S(2)}, u32[]{:S(2)}) collective-permute-start(f32[128,512]{1,0:T(8,128)S(1)} %get-tuple-element.55), channel_id=1, source_target_pairs={{0,32},{4,484},{8,40},{12,492},{16,48},{20,500},{24,56},{28,508},{... | collective-permute-start | bytes 786440 | tf_op jit(solution)/shard_map/ppermute | solution.py:279
  56.0 1.9 %collective-permute-start.11 = (f32[128,512]{1,0:T(8,128)S(1)}, f32[128,512]{1,0:T(8,128)S(1)}, u32[]{:S(2)}, u32[]{:S(2)}) collective-permute-start(f32[128,512]{1,0:T(8,128)S(1)} %shard_map.35.refs_2_), channel_id=1, source_target_pairs={{0,32},{4,484},{8,40},{12,492},{16,48},{20,500},{24,56},{28,508},{... | collective-permute-start | bytes 786440 | tf_op jit(solution)/shard_map/ppermute | solution.py:279
  58.0 8.2 %collective-permute-done.13.refs_1_ = f32[128,512]{1,0:T(8,128)S(1)} collective-permute-done((f32[128,512]{1,0:T(8,128)S(1)}, f32[128,512]{1,0:T(8,128)S(1)}, u32[]{:S(2)}, u32[]{:S(2)}) %collective-permute-start.13) | collective-permute-done | bytes 262176 | tf_op jit(solution)/shard_map/ppermute | solution.py:279
  66.2 1.9 %collective-permute-start.14 = (f32[128,512]{1,0:T(8,128)S(1)}, f32[128,512]{1,0:T(8,128)S(1)}, u32[]{:S(2)}, u32[]{:S(2)}) collective-permute-start(f32[128,512]{1,0:T(8,128)S(1)} %shard_map.39), channel_id=1, source_target_pairs={{0,32},{4,484},{8,40},{12,492},{16,48},{20,500},{24,56},{28,508},{... | collective-permute-start | bytes 786440 | tf_op jit(solution)/shard_map/ppermute | solution.py:279
  69.0 1.9 %collective-permute-start.15 = (f32[32,512]{1,0:T(8,128)S(1)}, f32[32,512]{1,0:T(8,128)S(1)}, u32[]{:S(2)}, u32[]{:S(2)}) collective-permute-start(f32[32,512]{1,0:T(8,128)S(1)} %get-tuple-element.59), channel_id=1, source_target_pairs={{0,128},{4,388},{8,136},{12,396},{16,144},{20,404},{24,152},{28,41... | collective-permute-start | bytes 196616 | tf_op jit(solution)/shard_map/ppermute | solution.py:279
  70.9 6.1 %collective-permute-done.14.refs_1_ = f32[128,512]{1,0:T(8,128)S(1)} collective-permute-done((f32[128,512]{1,0:T(8,128)S(1)}, f32[128,512]{1,0:T(8,128)S(1)}, u32[]{:S(2)}, u32[]{:S(2)}) %collective-permute-start.14) | collective-permute-done | bytes 262176 | tf_op jit(solution)/shard_map/ppermute | solution.py:279
  77.1 5.5 %collective-permute-start.17 = (f32[32,512]{1,0:T(8,128)S(1)}, f32[32,512]{1,0:T(8,128)S(1)}, u32[]{:S(2)}, u32[]{:S(2)}) collective-permute-start(f32[32,512]{1,0:T(8,128)S(1)} %get-tuple-element.62), channel_id=1, source_target_pairs={{0,384},{4,132},{8,392},{12,140},{16,400},{20,148},{24,408},{28,15... | collective-permute-start | bytes 196616 | tf_op jit(solution)/shard_map/ppermute | solution.py:279
  82.6 4.3 %collective-permute-start.16 = (f32[32,1024]{1,0:T(8,128)S(1)}, f32[32,1024]{1,0:T(8,128)S(1)}, u32[]{:S(2)}, u32[]{:S(2)}) collective-permute-start(f32[32,1024]{1,0:T(8,128)S(1)} %shard_map.41.refs_3_), channel_id=1, source_target_pairs={{0,128},{4,388},{8,136},{12,396},{16,144},{20,404},{24,152},{28,41... | collective-permute-start | bytes 393224 | tf_op jit(solution)/shard_map/ppermute | solution.py:279
  86.9 2.3 %collective-permute-done.17.refs_2_ = f32[32,512]{1,0:T(8,128)S(1)} collective-permute-done((f32[32,512]{1,0:T(8,128)S(1)}, f32[32,512]{1,0:T(8,128)S(1)}, u32[]{:S(2)}, u32[]{:S(2)}) %collective-permute-start.17) | collective-permute-done | bytes 65568 | tf_op jit(solution)/shard_map/ppermute | solution.py:279
  89.2 7.2 %collective-permute-start.18 = (f32[32,1024]{1,0:T(8,128)S(1)}, f32[32,1024]{1,0:T(8,128)S(1)}, u32[]{:S(2)}, u32[]{:S(2)}) collective-permute-start(f32[32,1024]{1,0:T(8,128)S(1)} %shard_map.43), channel_id=1, source_target_pairs={{0,384},{4,132},{8,392},{12,140},{16,400},{20,148},{24,408},{28,15... | collective-permute-start | bytes 393224 | tf_op jit(solution)/shard_map/ppermute | solution.py:279
  96.4 3.6 %collective-permute-done.16.from_below = f32[32,1024]{1,0:T(8,128)S(1)} collective-permute-done((f32[32,1024]{1,0:T(8,128)S(1)}, f32[32,1024]{1,0:T(8,128)S(1)}, u32[]{:S(2)}, u32[]{:S(2)}) %collective-permute-start.16) | collective-permute-done | bytes 131104 | tf_op jit(solution)/shard_map/ppermute | solution.py:279
  (33 shorter events, 9.8 us)
Async XLA Ops:
  1.8 6.9 %collective-permute-start.2 = (f32[1024,128]{1,0:T(8,128)}, f32[1024,128]{1,0:T(8,128)S(1)}, u32[]{:S(2)}, u32[]{:S(2)}) collective-permute-start(f32[1024,128]{1,0:T(8,128)} %shard_map.28.own), channel_id=1, source_target_pairs={{0,4},{4,0},{8,12},{12,8},{16,20},{20,16},{24,28},{28,24},{1,5},{5... | collective-permute-start | bytes 1572872 | tf_op jit(solution)/shard_map/ppermute | solution.py:261
  3.8 13.9 %collective-permute-start = (f32[1024,128]{1,0:T(8,128)}, f32[1024,128]{1,0:T(8,128)S(1)}, u32[]{:S(2)}, u32[]{:S(2)}) collective-permute-start(f32[1024,128]{1,0:T(8,128)} %shard_map.28.own), channel_id=1, source_target_pairs={{1,0},{12,4},{2,1},{13,5},{3,2},{14,6},{0,3},{15,7},{9,8},{20,12},... | collective-permute-start | bytes 1572872 | tf_op jit(solution)/shard_map/ppermute | solution.py:270
  8.7 12.9 %collective-permute-start.3 = (f32[1024,128]{1,0:T(8,128)S(1)}, f32[1024,128]{1,0:T(8,128)S(1)}, u32[]{:S(2)}, u32[]{:S(2)}) collective-permute-start(f32[1024,128]{1,0:T(8,128)S(1)} %collective-permute-done.2.other), channel_id=1, source_target_pairs={{3,0},{28,4},{0,1},{29,5},{1,2},{30,6},{2,3},{31,7},{11,8},{4,12},... | collective-permute-start | bytes 1572872 | tf_op jit(solution)/shard_map/ppermute | solution.py:270
  10.6 17.0 %collective-permute-start.6 = (f32[1024,128]{1,0:T(8,128)}, f32[1024,128]{1,0:T(8,128)S(1)}, u32[]{:S(2)}, u32[]{:S(2)}) collective-permute-start(f32[1024,128]{1,0:T(8,128)} %shard_map.28.own), channel_id=1, source_target_pairs={{3,0},{28,4},{0,1},{29,5},{1,2},{30,6},{2,3},{31,7},{11,8},{4,12},... | collective-permute-start | bytes 1572872 | tf_op jit(solution)/shard_map/ppermute | solution.py:270
  13.1 14.5 %collective-permute-start.5 = (f32[1024,128]{1,0:T(8,128)S(1)}, f32[1024,128]{1,0:T(8,128)S(1)}, u32[]{:S(2)}, u32[]{:S(2)}) collective-permute-start(f32[1024,128]{1,0:T(8,128)S(1)} %collective-permute-done.2.other), channel_id=1, source_target_pairs={{1,0},{12,4},{2,1},{13,5},{3,2},{14,6},{0,3},{15,7},{9,8},{20,12},... | collective-permute-start | bytes 1572872 | tf_op jit(solution)/shard_map/ppermute | solution.py:270
  17.7 14.1 %collective-permute-start.1 = (f32[1024,128]{1,0:T(8,128)S(1)}, f32[1024,128]{1,0:T(8,128)S(1)}, u32[]{:S(2)}, u32[]{:S(2)}) collective-permute-start(f32[1024,128]{1,0:T(8,128)S(1)} %collective-permute-done.o1.first), channel_id=1, source_target_pairs={{1,0},{12,4},{2,1},{13,5},{3,2},{14,6},{0,3},{15,7},{9,8},{20,12},... | collective-permute-start | bytes 1572872 | tf_op jit(solution)/shard_map/ppermute | solution.py:270
  21.7 12.3 %collective-permute-start.4 = (f32[1024,128]{1,0:T(8,128)S(1)}, f32[1024,128]{1,0:T(8,128)S(1)}, u32[]{:S(2)}, u32[]{:S(2)}) collective-permute-start(f32[1024,128]{1,0:T(8,128)S(1)} %collective-permute-done.3.s3.second), channel_id=1, source_target_pairs={{3,0},{28,4},{0,1},{29,5},{1,2},{30,6},{2,3},{31,7},{11,8},{4,12},... | collective-permute-start | bytes 1572872 | tf_op jit(solution)/shard_map/ppermute | solution.py:270
  23.7 6.8 %copy-start = (f32[1024,128]{1,0:T(8,128)S(1)}, f32[1024,128]{1,0:T(8,128)}, u32[]{:S(2)}) copy-start(f32[1024,128]{1,0:T(8,128)} %shard_map.28.own) | copy-start | bytes 1572868
  23.7 12.4 %collective-permute-start.8 = (f32[2048,128]{1,0:T(8,128)S(1)}, f32[2048,128]{1,0:T(8,128)S(1)}, u32[]{:S(2)}, u32[]{:S(2)}) collective-permute-start(f32[2048,128]{1,0:T(8,128)S(1)} %shard_map.31), channel_id=1, source_target_pairs={{0,4},{4,0},{8,12},{12,8},{16,20},{20,16},{24,28},{28,24},{1,5},{5... | collective-permute-start | bytes 3145736 | tf_op jit(solution)/shard_map/ppermute | solution.py:261
  27.8 8.3 %collective-permute-start.9 = (f32[2048,128]{1,0:T(8,128)S(1)}, f32[2048,128]{1,0:T(8,128)S(1)}, u32[]{:S(2)}, u32[]{:S(2)}) collective-permute-start(f32[2048,128]{1,0:T(8,128)S(1)} %shard_map.32), channel_id=1, source_target_pairs={{0,4},{4,0},{8,12},{12,8},{16,20},{20,16},{24,28},{28,24},{1,5},{5... | collective-permute-start | bytes 3145736 | tf_op jit(solution)/shard_map/ppermute | solution.py:261
  34.0 4.6 %collective-permute-start.7 = (f32[2048,128]{1,0:T(8,128)S(1)}, f32[2048,128]{1,0:T(8,128)S(1)}, u32[]{:S(2)}, u32[]{:S(2)}) collective-permute-start(f32[2048,128]{1,0:T(8,128)S(1)} %shard_map.30), channel_id=1, source_target_pairs={{0,4},{4,0},{8,12},{12,8},{16,20},{20,16},{24,28},{28,24},{1,5},{5... | collective-permute-start | bytes 3145736 | tf_op jit(solution)/shard_map/ppermute | solution.py:261
  39.3 16.7 %collective-permute-start.10 = (f32[128,512]{1,0:T(8,128)S(1)}, f32[128,512]{1,0:T(8,128)S(1)}, u32[]{:S(2)}, u32[]{:S(2)}) collective-permute-start(f32[128,512]{1,0:T(8,128)S(1)} %get-tuple-element.45), channel_id=1, source_target_pairs={{0,32},{4,484},{8,40},{12,492},{16,48},{20,500},{24,56},{28,508},{... | collective-permute-start | bytes 786440 | tf_op jit(solution)/shard_map/ppermute | solution.py:279
  44.5 24.4 %collective-permute-start.12 = (f32[256,512]{1,0:T(8,128)S(1)}, f32[256,512]{1,0:T(8,128)S(1)}, u32[]{:S(2)}, u32[]{:S(2)}) collective-permute-start(f32[256,512]{1,0:T(8,128)S(1)} %shard_map.37), channel_id=1, source_target_pairs={{0,480},{4,36},{8,488},{12,44},{16,496},{20,52},{24,504},{28,60},{... | collective-permute-start | bytes 1572872 | tf_op jit(solution)/shard_map/ppermute | solution.py:279
  54.0 12.1 %collective-permute-start.13 = (f32[128,512]{1,0:T(8,128)S(1)}, f32[128,512]{1,0:T(8,128)S(1)}, u32[]{:S(2)}, u32[]{:S(2)}) collective-permute-start(f32[128,512]{1,0:T(8,128)S(1)} %get-tuple-element.55), channel_id=1, source_target_pairs={{0,32},{4,484},{8,40},{12,492},{16,48},{20,500},{24,56},{28,508},{... | collective-permute-start | bytes 786440 | tf_op jit(solution)/shard_map/ppermute | solution.py:279
  56.0 12.9 %collective-permute-start.11 = (f32[128,512]{1,0:T(8,128)S(1)}, f32[128,512]{1,0:T(8,128)S(1)}, u32[]{:S(2)}, u32[]{:S(2)}) collective-permute-start(f32[128,512]{1,0:T(8,128)S(1)} %shard_map.35.refs_2_), channel_id=1, source_target_pairs={{0,32},{4,484},{8,40},{12,492},{16,48},{20,500},{24,56},{28,508},{... | collective-permute-start | bytes 786440 | tf_op jit(solution)/shard_map/ppermute | solution.py:279
  66.2 10.9 %collective-permute-start.14 = (f32[128,512]{1,0:T(8,128)S(1)}, f32[128,512]{1,0:T(8,128)S(1)}, u32[]{:S(2)}, u32[]{:S(2)}) collective-permute-start(f32[128,512]{1,0:T(8,128)S(1)} %shard_map.39), channel_id=1, source_target_pairs={{0,32},{4,484},{8,40},{12,492},{16,48},{20,500},{24,56},{28,508},{... | collective-permute-start | bytes 786440 | tf_op jit(solution)/shard_map/ppermute | solution.py:279
  69.0 13.6 %collective-permute-start.15 = (f32[32,512]{1,0:T(8,128)S(1)}, f32[32,512]{1,0:T(8,128)S(1)}, u32[]{:S(2)}, u32[]{:S(2)}) collective-permute-start(f32[32,512]{1,0:T(8,128)S(1)} %get-tuple-element.59), channel_id=1, source_target_pairs={{0,128},{4,388},{8,136},{12,396},{16,144},{20,404},{24,152},{28,41... | collective-permute-start | bytes 196616 | tf_op jit(solution)/shard_map/ppermute | solution.py:279
  77.1 12.1 %collective-permute-start.17 = (f32[32,512]{1,0:T(8,128)S(1)}, f32[32,512]{1,0:T(8,128)S(1)}, u32[]{:S(2)}, u32[]{:S(2)}) collective-permute-start(f32[32,512]{1,0:T(8,128)S(1)} %get-tuple-element.62), channel_id=1, source_target_pairs={{0,384},{4,132},{8,392},{12,140},{16,400},{20,148},{24,408},{28,15... | collective-permute-start | bytes 196616 | tf_op jit(solution)/shard_map/ppermute | solution.py:279
  82.6 17.4 %collective-permute-start.16 = (f32[32,1024]{1,0:T(8,128)S(1)}, f32[32,1024]{1,0:T(8,128)S(1)}, u32[]{:S(2)}, u32[]{:S(2)}) collective-permute-start(f32[32,1024]{1,0:T(8,128)S(1)} %shard_map.41.refs_3_), channel_id=1, source_target_pairs={{0,128},{4,388},{8,136},{12,396},{16,144},{20,404},{24,152},{28,41... | collective-permute-start | bytes 393224 | tf_op jit(solution)/shard_map/ppermute | solution.py:279
  89.2 10.8 %collective-permute-start.18 = (f32[32,1024]{1,0:T(8,128)S(1)}, f32[32,1024]{1,0:T(8,128)S(1)}, u32[]{:S(2)}, u32[]{:S(2)}) collective-permute-start(f32[32,1024]{1,0:T(8,128)S(1)} %shard_map.43), channel_id=1, source_target_pairs={{0,384},{4,132},{8,392},{12,140},{16,400},{20,148},{24,408},{28,15... | collective-permute-start | bytes 393224 | tf_op jit(solution)/shard_map/ppermute | solution.py:279

commit v15 on v14

--- a/solution.py
+++ b/solution.py
@@ -231,16 +231,16 @@
         out[...] = mine[rows, :] + (below[rows, :] + above[rows, :])
 
 
-def up_kernel(first, second, came, out):
+def up_kernel(first, first_came, second, second_came, out):
     half = first.shape[1]
-    out[:, :half] = first[...] + came[...]
-    out[:, half:] = second[...]
-
-
-def down_kernel(first, second, came, out):
+    out[:, :half] = first[...] + first_came[...]
+    out[:, half:] = second[...] + second_came[...]
+
+
+def beside_kernel(first, second, out):
     half = first.shape[1]
     out[:, :half] = first[...]
-    out[:, half:] = second[...] + came[...]
+    out[:, half:] = second[...]
 
 
 def below_kernel(first, second, from_below, out):
@@ -343,10 +343,10 @@
     first = call(functools.partial(group_kernel, 0), piece, (mine_a, pass_on(up_a, 1), above))
     second = call(functools.partial(group_kernel, 1), piece, (mine_b, pass_on(up_b, 1), above), after=first[0])
     chunk = [(SUB, 8 * TILE)]
-    (up,) = call(up_kernel, chunk, (first[1], second[1], pass_on(first[2], 4)))
-    (down,) = call(down_kernel, chunk, (first[3], second[3], pass_on(second[2], -4)), after=up)
-    (held,) = call(below_kernel, chunk, (first[0], second[0], pass_on(up, 4)))
-    return call(last_kernel, chunk, (held, pass_on(down, -4)))[0]
+    (down,) = call(beside_kernel, chunk, (first[3], second[3]))
+    (held,) = call(below_kernel, chunk, (first[0], second[0], pass_on(down, -4)))
+    (up,) = call(up_kernel, chunk, (first[1], pass_on(first[2], 4), second[1], pass_on(second[2], 4)))
+    return call(last_kernel, chunk, (held, pass_on(up, 4)))[0]
 
 
 def solution(mesh):

time: 102 us -> 102 us (level)
  waiting for transfers between devices: 24.1 us -> 29.9 us
  starting transfers between devices: 68.4 us -> 63.2 us
    ppermute x9, waiting for transfers between devices: 21 us -> 26.8 us  [pass_on(): return lax.ppermute(value, ('layer', 'row'), pairs)]
    ppermute x9, starting transfers between devices: 38 us -> 32.9 us  [pass_on(): return lax.ppermute(value, ('layer', 'row'), pairs)]
  transfers between devices with their start and end apart: 19 -> 19, of which waited for: 7 -> 8; matrix products, arithmetic and copies ran while one was open for 0% -> 0% of each run, Pallas kernels for 5% -> 5%
where the time goes in v15:
time: 102 us; the launch traced here: 101 us
  starting transfers between devices  63.2 us (62%)
  waiting for transfers between devices  29.9 us (29%)
  Pallas kernels  7.86 us (8%)
    ppermute x9, starting transfers between devices, pass_on(): return lax.ppermute(value, ('layer', 'row'), pairs)  32.9 us
    ppermute x9, waiting for transfers between devices, pass_on(): return lax.ppermute(value, ('layer', 'row'), pairs)  26.8 us
    ppermute x6, starting transfers between devices, fetch(): return lax.ppermute(value, ('row', 'col'), pairs)  19.7 us
    ppermute x4, starting transfers between devices, swap(): return lax.ppermute(value, 'row', [(i, i ^ 1) for i in range(N_ROW)])  10.6 us
    pallas_call x17, Pallas kernels, call(): pl.pallas_call(kernel, out_shape=tuple((jax.ShapeDtypeStruct(s, d) for s,...  7.86 us
    ppermute x6, waiting for transfers between devices, fetch(): return lax.ppermute(value, ('row', 'col'), pairs)  2.08 us
  transfers between devices with their start and end apart: 19, of which 8 were waited for; matrix products, arithmetic and copies ran while one was open for 0% of the time, Pallas kernels for 5%

profile of v15, /device:TPU:6, one launch (start us, length us, event | category | flops | bytes accessed | tf_op | source)
XLA Modules:
  0.0 101.3 jit_solution(7094760358497618319)
XLA Ops:
  3.8 4.9 %collective-permute-start = (f32[1024,128]{1,0:T(8,128)}, f32[1024,128]{1,0:T(8,128)S(1)}, u32[]{:S(2)}, u32[]{:S(2)}) collective-permute-start(f32[1024,128]{1,0:T(8,128)} %shard_map.28.own), channel_id=1, source_target_pairs={{1,0},{12,4},{2,1},{13,5},{3,2},{14,6},{0,3},{15,7},{9,8},{20,12},... | collective-permute-start | bytes 1572872 | tf_op jit(solution)/shard_map/ppermute | solution.py:270
  8.7 1.9 %collective-permute-start.3 = (f32[1024,128]{1,0:T(8,128)S(1)}, f32[1024,128]{1,0:T(8,128)S(1)}, u32[]{:S(2)}, u32[]{:S(2)}) collective-permute-start(f32[1024,128]{1,0:T(8,128)S(1)} %collective-permute-done.2.other), channel_id=1, source_target_pairs={{3,0},{28,4},{0,1},{29,5},{1,2},{30,6},{2,3},{31,7},{11,8},{4,12},... | collective-permute-start | bytes 1572872 | tf_op jit(solution)/shard_map/ppermute | solution.py:270
  10.6 2.5 %collective-permute-start.6 = (f32[1024,128]{1,0:T(8,128)}, f32[1024,128]{1,0:T(8,128)S(1)}, u32[]{:S(2)}, u32[]{:S(2)}) collective-permute-start(f32[1024,128]{1,0:T(8,128)} %shard_map.28.own), channel_id=1, source_target_pairs={{3,0},{28,4},{0,1},{29,5},{1,2},{30,6},{2,3},{31,7},{11,8},{4,12},... | collective-permute-start | bytes 1572872 | tf_op jit(solution)/shard_map/ppermute | solution.py:270
  13.1 4.6 %collective-permute-start.5 = (f32[1024,128]{1,0:T(8,128)S(1)}, f32[1024,128]{1,0:T(8,128)S(1)}, u32[]{:S(2)}, u32[]{:S(2)}) collective-permute-start(f32[1024,128]{1,0:T(8,128)S(1)} %collective-permute-done.2.other), channel_id=1, source_target_pairs={{1,0},{12,4},{2,1},{13,5},{3,2},{14,6},{0,3},{15,7},{9,8},{20,12},... | collective-permute-start | bytes 1572872 | tf_op jit(solution)/shard_map/ppermute | solution.py:270
  17.7 3.9 %collective-permute-start.1 = (f32[1024,128]{1,0:T(8,128)S(1)}, f32[1024,128]{1,0:T(8,128)S(1)}, u32[]{:S(2)}, u32[]{:S(2)}) collective-permute-start(f32[1024,128]{1,0:T(8,128)S(1)} %collective-permute-done.o1.first), channel_id=1, source_target_pairs={{1,0},{12,4},{2,1},{13,5},{3,2},{14,6},{0,3},{15,7},{9,8},{20,12},... | collective-permute-start | bytes 1572872 | tf_op jit(solution)/shard_map/ppermute | solution.py:270
  21.7 1.9 %collective-permute-start.4 = (f32[1024,128]{1,0:T(8,128)S(1)}, f32[1024,128]{1,0:T(8,128)S(1)}, u32[]{:S(2)}, u32[]{:S(2)}) collective-permute-start(f32[1024,128]{1,0:T(8,128)S(1)} %collective-permute-done.3.s3.second), channel_id=1, source_target_pairs={{3,0},{28,4},{0,1},{29,5},{1,2},{30,6},{2,3},{31,7},{11,8},{4,12},... | collective-permute-start | bytes 1572872 | tf_op jit(solution)/shard_map/ppermute | solution.py:270
  23.7 4.0 %collective-permute-start.8 = (f32[2048,128]{1,0:T(8,128)S(1)}, f32[2048,128]{1,0:T(8,128)S(1)}, u32[]{:S(2)}, u32[]{:S(2)}) collective-permute-start(f32[2048,128]{1,0:T(8,128)S(1)} %shard_map.31), channel_id=1, source_target_pairs={{0,4},{4,0},{8,12},{12,8},{16,20},{20,16},{24,28},{28,24},{1,5},{5... | collective-permute-start | bytes 3145736 | tf_op jit(solution)/shard_map/ppermute | solution.py:261
  27.8 2.7 %collective-permute-start.9 = (f32[2048,128]{1,0:T(8,128)S(1)}, f32[2048,128]{1,0:T(8,128)S(1)}, u32[]{:S(2)}, u32[]{:S(2)}) collective-permute-start(f32[2048,128]{1,0:T(8,128)S(1)} %shard_map.32), channel_id=1, source_target_pairs={{0,4},{4,0},{8,12},{12,8},{16,20},{20,16},{24,28},{28,24},{1,5},{5... | collective-permute-start | bytes 3145736 | tf_op jit(solution)/shard_map/ppermute | solution.py:261
  31.9 2.1 %collective-permute-done.4.refs_1_.s2 = f32[1024,128]{1,0:T(8,128)S(1)} collective-permute-done((f32[1024,128]{1,0:T(8,128)S(1)}, f32[1024,128]{1,0:T(8,128)S(1)}, u32[]{:S(2)}, u32[]{:S(2)}) %collective-permute-start.4) | collective-permute-done | bytes 524320 | tf_op jit(solution)/shard_map/ppermute | solution.py:270
  34.0 2.0 %collective-permute-start.7 = (f32[2048,128]{1,0:T(8,128)S(1)}, f32[2048,128]{1,0:T(8,128)S(1)}, u32[]{:S(2)}, u32[]{:S(2)}) collective-permute-start(f32[2048,128]{1,0:T(8,128)S(1)} %shard_map.30), channel_id=1, source_target_pairs={{0,4},{4,0},{8,12},{12,8},{16,20},{20,16},{24,28},{28,24},{1,5},{5... | collective-permute-start | bytes 3145736 | tf_op jit(solution)/shard_map/ppermute | solution.py:261
  39.3 3.8 %collective-permute-start.10 = (f32[128,512]{1,0:T(8,128)S(1)}, f32[128,512]{1,0:T(8,128)S(1)}, u32[]{:S(2)}, u32[]{:S(2)}) collective-permute-start(f32[128,512]{1,0:T(8,128)S(1)} %get-tuple-element.45), channel_id=1, source_target_pairs={{0,32},{4,484},{8,40},{12,492},{16,48},{20,500},{24,56},{28,508},{... | collective-permute-start | bytes 786440 | tf_op jit(solution)/shard_map/ppermute | solution.py:279
  44.5 9.5 %collective-permute-start.12 = (f32[256,512]{1,0:T(8,128)S(1)}, f32[256,512]{1,0:T(8,128)S(1)}, u32[]{:S(2)}, u32[]{:S(2)}) collective-permute-start(f32[256,512]{1,0:T(8,128)S(1)} %shard_map.37), channel_id=1, source_target_pairs={{0,480},{4,36},{8,488},{12,44},{16,496},{20,52},{24,504},{28,60},{... | collective-permute-start | bytes 1572872 | tf_op jit(solution)/shard_map/ppermute | solution.py:279
  54.0 1.9 %collective-permute-start.13 = (f32[128,512]{1,0:T(8,128)S(1)}, f32[128,512]{1,0:T(8,128)S(1)}, u32[]{:S(2)}, u32[]{:S(2)}) collective-permute-start(f32[128,512]{1,0:T(8,128)S(1)} %get-tuple-element.55), channel_id=1, source_target_pairs={{0,32},{4,484},{8,40},{12,492},{16,48},{20,500},{24,56},{28,508},{... | collective-permute-start | bytes 786440 | tf_op jit(solution)/shard_map/ppermute | solution.py:279
  56.0 1.9 %collective-permute-start.11 = (f32[128,512]{1,0:T(8,128)S(1)}, f32[128,512]{1,0:T(8,128)S(1)}, u32[]{:S(2)}, u32[]{:S(2)}) collective-permute-start(f32[128,512]{1,0:T(8,128)S(1)} %shard_map.35.refs_2_), channel_id=1, source_target_pairs={{0,32},{4,484},{8,40},{12,492},{16,48},{20,500},{24,56},{28,508},{... | collective-permute-start | bytes 786440 | tf_op jit(solution)/shard_map/ppermute | solution.py:279
  58.0 8.2 %collective-permute-done.13.refs_1_ = f32[128,512]{1,0:T(8,128)S(1)} collective-permute-done((f32[128,512]{1,0:T(8,128)S(1)}, f32[128,512]{1,0:T(8,128)S(1)}, u32[]{:S(2)}, u32[]{:S(2)}) %collective-permute-start.13) | collective-permute-done | bytes 262176 | tf_op jit(solution)/shard_map/ppermute | solution.py:279
  66.2 1.9 %collective-permute-start.14 = (f32[128,512]{1,0:T(8,128)S(1)}, f32[128,512]{1,0:T(8,128)S(1)}, u32[]{:S(2)}, u32[]{:S(2)}) collective-permute-start(f32[128,512]{1,0:T(8,128)S(1)} %shard_map.39), channel_id=1, source_target_pairs={{0,32},{4,484},{8,40},{12,492},{16,48},{20,500},{24,56},{28,508},{... | collective-permute-start | bytes 786440 | tf_op jit(solution)/shard_map/ppermute | solution.py:279
  69.0 1.9 %collective-permute-start.16 = (f32[32,512]{1,0:T(8,128)S(1)}, f32[32,512]{1,0:T(8,128)S(1)}, u32[]{:S(2)}, u32[]{:S(2)}) collective-permute-start(f32[32,512]{1,0:T(8,128)S(1)} %get-tuple-element.60), channel_id=1, source_target_pairs={{0,128},{4,388},{8,136},{12,396},{16,144},{20,404},{24,152},{28,41... | collective-permute-start | bytes 196616 | tf_op jit(solution)/shard_map/ppermute | solution.py:279
  70.9 6.1 %collective-permute-done.14.refs_1_ = f32[128,512]{1,0:T(8,128)S(1)} collective-permute-done((f32[128,512]{1,0:T(8,128)S(1)}, f32[128,512]{1,0:T(8,128)S(1)}, u32[]{:S(2)}, u32[]{:S(2)}) %collective-permute-start.14) | collective-permute-done | bytes 262176 | tf_op jit(solution)/shard_map/ppermute | solution.py:279
  77.1 1.9 %collective-permute-start.17 = (f32[32,512]{1,0:T(8,128)S(1)}, f32[32,512]{1,0:T(8,128)S(1)}, u32[]{:S(2)}, u32[]{:S(2)}) collective-permute-start(f32[32,512]{1,0:T(8,128)S(1)} %get-tuple-element.62), channel_id=1, source_target_pairs={{0,128},{4,388},{8,136},{12,396},{16,144},{20,404},{24,152},{28,41... | collective-permute-start | bytes 196616 | tf_op jit(solution)/shard_map/ppermute | solution.py:279
  79.0 7.8 %collective-permute-start.15 = (f32[32,1024]{1,0:T(8,128)S(1)}, f32[32,1024]{1,0:T(8,128)S(1)}, u32[]{:S(2)}, u32[]{:S(2)}) collective-permute-start(f32[32,1024]{1,0:T(8,128)S(1)} %shard_map.41), channel_id=1, source_target_pairs={{0,384},{4,132},{8,392},{12,140},{16,400},{20,148},{24,408},{28,15... | collective-permute-start | bytes 393224 | tf_op jit(solution)/shard_map/ppermute | solution.py:279
  86.9 2.4 %collective-permute-done.17.second_came = f32[32,512]{1,0:T(8,128)S(1)} collective-permute-done((f32[32,512]{1,0:T(8,128)S(1)}, f32[32,512]{1,0:T(8,128)S(1)}, u32[]{:S(2)}, u32[]{:S(2)}) %collective-permute-start.17) | collective-permute-done | bytes 65568 | tf_op jit(solution)/shard_map/ppermute | solution.py:279
  89.3 2.1 %collective-permute-start.18 = (f32[32,1024]{1,0:T(8,128)S(1)}, f32[32,1024]{1,0:T(8,128)S(1)}, u32[]{:S(2)}, u32[]{:S(2)}) collective-permute-start(f32[32,1024]{1,0:T(8,128)S(1)} %shard_map.43), channel_id=1, source_target_pairs={{0,128},{4,388},{8,136},{12,396},{16,144},{20,404},{24,152},{28,41... | collective-permute-start | bytes 393224 | tf_op jit(solution)/shard_map/ppermute | solution.py:279
  91.4 2.4 %collective-permute-done.15.from_below = f32[32,1024]{1,0:T(8,128)S(1)} collective-permute-done((f32[32,1024]{1,0:T(8,128)S(1)}, f32[32,1024]{1,0:T(8,128)S(1)}, u32[]{:S(2)}, u32[]{:S(2)}) %collective-permute-start.15) | collective-permute-done | bytes 131104 | tf_op jit(solution)/shard_map/ppermute | solution.py:279
  93.7 6.9 %collective-permute-done.18.from_above = f32[32,1024]{1,0:T(8,128)S(1)} collective-permute-done((f32[32,1024]{1,0:T(8,128)S(1)}, f32[32,1024]{1,0:T(8,128)S(1)}, u32[]{:S(2)}, u32[]{:S(2)}) %collective-permute-start.18) | collective-permute-done | bytes 131104 | tf_op jit(solution)/shard_map/ppermute | solution.py:279
  (33 shorter events, 11.7 us)
Async XLA Ops:
  1.8 6.9 %collective-permute-start.2 = (f32[1024,128]{1,0:T(8,128)}, f32[1024,128]{1,0:T(8,128)S(1)}, u32[]{:S(2)}, u32[]{:S(2)}) collective-permute-start(f32[1024,128]{1,0:T(8,128)} %shard_map.28.own), channel_id=1, source_target_pairs={{0,4},{4,0},{8,12},{12,8},{16,20},{20,16},{24,28},{28,24},{1,5},{5... | collective-permute-start | bytes 1572872 | tf_op jit(solution)/shard_map/ppermute | solution.py:261
  3.8 13.9 %collective-permute-start = (f32[1024,128]{1,0:T(8,128)}, f32[1024,128]{1,0:T(8,128)S(1)}, u32[]{:S(2)}, u32[]{:S(2)}) collective-permute-start(f32[1024,128]{1,0:T(8,128)} %shard_map.28.own), channel_id=1, source_target_pairs={{1,0},{12,4},{2,1},{13,5},{3,2},{14,6},{0,3},{15,7},{9,8},{20,12},... | collective-permute-start | bytes 1572872 | tf_op jit(solution)/shard_map/ppermute | solution.py:270
  8.7 12.9 %collective-permute-start.3 = (f32[1024,128]{1,0:T(8,128)S(1)}, f32[1024,128]{1,0:T(8,128)S(1)}, u32[]{:S(2)}, u32[]{:S(2)}) collective-permute-start(f32[1024,128]{1,0:T(8,128)S(1)} %collective-permute-done.2.other), channel_id=1, source_target_pairs={{3,0},{28,4},{0,1},{29,5},{1,2},{30,6},{2,3},{31,7},{11,8},{4,12},... | collective-permute-start | bytes 1572872 | tf_op jit(solution)/shard_map/ppermute | solution.py:270
  10.6 17.0 %collective-permute-start.6 = (f32[1024,128]{1,0:T(8,128)}, f32[1024,128]{1,0:T(8,128)S(1)}, u32[]{:S(2)}, u32[]{:S(2)}) collective-permute-start(f32[1024,128]{1,0:T(8,128)} %shard_map.28.own), channel_id=1, source_target_pairs={{3,0},{28,4},{0,1},{29,5},{1,2},{30,6},{2,3},{31,7},{11,8},{4,12},... | collective-permute-start | bytes 1572872 | tf_op jit(solution)/shard_map/ppermute | solution.py:270
  13.1 14.5 %collective-permute-start.5 = (f32[1024,128]{1,0:T(8,128)S(1)}, f32[1024,128]{1,0:T(8,128)S(1)}, u32[]{:S(2)}, u32[]{:S(2)}) collective-permute-start(f32[1024,128]{1,0:T(8,128)S(1)} %collective-permute-done.2.other), channel_id=1, source_target_pairs={{1,0},{12,4},{2,1},{13,5},{3,2},{14,6},{0,3},{15,7},{9,8},{20,12},... | collective-permute-start | bytes 1572872 | tf_op jit(solution)/shard_map/ppermute | solution.py:270
  17.7 14.1 %collective-permute-start.1 = (f32[1024,128]{1,0:T(8,128)S(1)}, f32[1024,128]{1,0:T(8,128)S(1)}, u32[]{:S(2)}, u32[]{:S(2)}) collective-permute-start(f32[1024,128]{1,0:T(8,128)S(1)} %collective-permute-done.o1.first), channel_id=1, source_target_pairs={{1,0},{12,4},{2,1},{13,5},{3,2},{14,6},{0,3},{15,7},{9,8},{20,12},... | collective-permute-start | bytes 1572872 | tf_op jit(solution)/shard_map/ppermute | solution.py:270
  21.7 12.3 %collective-permute-start.4 = (f32[1024,128]{1,0:T(8,128)S(1)}, f32[1024,128]{1,0:T(8,128)S(1)}, u32[]{:S(2)}, u32[]{:S(2)}) collective-permute-start(f32[1024,128]{1,0:T(8,128)S(1)} %collective-permute-done.3.s3.second), channel_id=1, source_target_pairs={{3,0},{28,4},{0,1},{29,5},{1,2},{30,6},{2,3},{31,7},{11,8},{4,12},... | collective-permute-start | bytes 1572872 | tf_op jit(solution)/shard_map/ppermute | solution.py:270
  23.7 6.8 %copy-start = (f32[1024,128]{1,0:T(8,128)S(1)}, f32[1024,128]{1,0:T(8,128)}, u32[]{:S(2)}) copy-start(f32[1024,128]{1,0:T(8,128)} %shard_map.28.own) | copy-start | bytes 1572868
  23.7 12.4 %collective-permute-start.8 = (f32[2048,128]{1,0:T(8,128)S(1)}, f32[2048,128]{1,0:T(8,128)S(1)}, u32[]{:S(2)}, u32[]{:S(2)}) collective-permute-start(f32[2048,128]{1,0:T(8,128)S(1)} %shard_map.31), channel_id=1, source_target_pairs={{0,4},{4,0},{8,12},{12,8},{16,20},{20,16},{24,28},{28,24},{1,5},{5... | collective-permute-start | bytes 3145736 | tf_op jit(solution)/shard_map/ppermute | solution.py:261
  27.8 8.3 %collective-permute-start.9 = (f32[2048,128]{1,0:T(8,128)S(1)}, f32[2048,128]{1,0:T(8,128)S(1)}, u32[]{:S(2)}, u32[]{:S(2)}) collective-permute-start(f32[2048,128]{1,0:T(8,128)S(1)} %shard_map.32), channel_id=1, source_target_pairs={{0,4},{4,0},{8,12},{12,8},{16,20},{20,16},{24,28},{28,24},{1,5},{5... | collective-permute-start | bytes 3145736 | tf_op jit(solution)/shard_map/ppermute | solution.py:261
  34.0 4.6 %collective-permute-start.7 = (f32[2048,128]{1,0:T(8,128)S(1)}, f32[2048,128]{1,0:T(8,128)S(1)}, u32[]{:S(2)}, u32[]{:S(2)}) collective-permute-start(f32[2048,128]{1,0:T(8,128)S(1)} %shard_map.30), channel_id=1, source_target_pairs={{0,4},{4,0},{8,12},{12,8},{16,20},{20,16},{24,28},{28,24},{1,5},{5... | collective-permute-start | bytes 3145736 | tf_op jit(solution)/shard_map/ppermute | solution.py:261
  39.3 16.7 %collective-permute-start.10 = (f32[128,512]{1,0:T(8,128)S(1)}, f32[128,512]{1,0:T(8,128)S(1)}, u32[]{:S(2)}, u32[]{:S(2)}) collective-permute-start(f32[128,512]{1,0:T(8,128)S(1)} %get-tuple-element.45), channel_id=1, source_target_pairs={{0,32},{4,484},{8,40},{12,492},{16,48},{20,500},{24,56},{28,508},{... | collective-permute-start | bytes 786440 | tf_op jit(solution)/shard_map/ppermute | solution.py:279
  44.5 24.4 %collective-permute-start.12 = (f32[256,512]{1,0:T(8,128)S(1)}, f32[256,512]{1,0:T(8,128)S(1)}, u32[]{:S(2)}, u32[]{:S(2)}) collective-permute-start(f32[256,512]{1,0:T(8,128)S(1)} %shard_map.37), channel_id=1, source_target_pairs={{0,480},{4,36},{8,488},{12,44},{16,496},{20,52},{24,504},{28,60},{... | collective-permute-start | bytes 1572872 | tf_op jit(solution)/shard_map/ppermute | solution.py:279
  54.0 12.1 %collective-permute-start.13 = (f32[128,512]{1,0:T(8,128)S(1)}, f32[128,512]{1,0:T(8,128)S(1)}, u32[]{:S(2)}, u32[]{:S(2)}) collective-permute-start(f32[128,512]{1,0:T(8,128)S(1)} %get-tuple-element.55), channel_id=1, source_target_pairs={{0,32},{4,484},{8,40},{12,492},{16,48},{20,500},{24,56},{28,508},{... | collective-permute-start | bytes 786440 | tf_op jit(solution)/shard_map/ppermute | solution.py:279
  56.0 12.9 %collective-permute-start.11 = (f32[128,512]{1,0:T(8,128)S(1)}, f32[128,512]{1,0:T(8,128)S(1)}, u32[]{:S(2)}, u32[]{:S(2)}) collective-permute-start(f32[128,512]{1,0:T(8,128)S(1)} %shard_map.35.refs_2_), channel_id=1, source_target_pairs={{0,32},{4,484},{8,40},{12,492},{16,48},{20,500},{24,56},{28,508},{... | collective-permute-start | bytes 786440 | tf_op jit(solution)/shard_map/ppermute | solution.py:279
  66.2 10.9 %collective-permute-start.14 = (f32[128,512]{1,0:T(8,128)S(1)}, f32[128,512]{1,0:T(8,128)S(1)}, u32[]{:S(2)}, u32[]{:S(2)}) collective-permute-start(f32[128,512]{1,0:T(8,128)S(1)} %shard_map.39), channel_id=1, source_target_pairs={{0,32},{4,484},{8,40},{12,492},{16,48},{20,500},{24,56},{28,508},{... | collective-permute-start | bytes 786440 | tf_op jit(solution)/shard_map/ppermute | solution.py:279
  69.0 17.9 %collective-permute-start.16 = (f32[32,512]{1,0:T(8,128)S(1)}, f32[32,512]{1,0:T(8,128)S(1)}, u32[]{:S(2)}, u32[]{:S(2)}) collective-permute-start(f32[32,512]{1,0:T(8,128)S(1)} %get-tuple-element.60), channel_id=1, source_target_pairs={{0,128},{4,388},{8,136},{12,396},{16,144},{20,404},{24,152},{28,41... | collective-permute-start | bytes 196616 | tf_op jit(solution)/shard_map/ppermute | solution.py:279
  77.1 12.2 %collective-permute-start.17 = (f32[32,512]{1,0:T(8,128)S(1)}, f32[32,512]{1,0:T(8,128)S(1)}, u32[]{:S(2)}, u32[]{:S(2)}) collective-permute-start(f32[32,512]{1,0:T(8,128)S(1)} %get-tuple-element.62), channel_id=1, source_target_pairs={{0,128},{4,388},{8,136},{12,396},{16,144},{20,404},{24,152},{28,41... | collective-permute-start | bytes 196616 | tf_op jit(solution)/shard_map/ppermute | solution.py:279
  79.0 14.7 %collective-permute-start.15 = (f32[32,1024]{1,0:T(8,128)S(1)}, f32[32,1024]{1,0:T(8,128)S(1)}, u32[]{:S(2)}, u32[]{:S(2)}) collective-permute-start(f32[32,1024]{1,0:T(8,128)S(1)} %shard_map.41), channel_id=1, source_target_pairs={{0,384},{4,132},{8,392},{12,140},{16,400},{20,148},{24,408},{28,15... | collective-permute-start | bytes 393224 | tf_op jit(solution)/shard_map/ppermute | solution.py:279
  89.3 11.4 %collective-permute-start.18 = (f32[32,1024]{1,0:T(8,128)S(1)}, f32[32,1024]{1,0:T(8,128)S(1)}, u32[]{:S(2)}, u32[]{:S(2)}) collective-permute-start(f32[32,1024]{1,0:T(8,128)S(1)} %shard_map.43), channel_id=1, source_target_pairs={{0,128},{4,388},{8,136},{12,396},{16,144},{20,404},{24,152},{28,41... | collective-permute-start | bytes 393224 | tf_op jit(solution)/shard_map/ppermute | solution.py:279

commit v16 on v15

--- a/solution.py
+++ b/solution.py
@@ -222,9 +222,8 @@
     out[...] = held[...] + came[...]
 
 
-def group_kernel(half, mine, below, both_above, own, up, far, down):
+def group_kernel(mine, below, above, own, up, far, down):
     group, y = lax.axis_index("layer") // 4, lax.axis_index("col")
-    above = both_above.at[pl.ds(half * mine.shape[0], mine.shape[0]), :]
     for i, out in enumerate((own, up, far, down)):
         t = lax.rem(group + turn() * i - y + 8, 4)
         rows = strip(jnp.where(t < 2, t, 5 - t))
@@ -335,13 +334,11 @@
         flops=6 * 5 * TILE * 2 * TILE * inner,
         nbytes=4 << 20,
     )
-    (downs,) = call(join_kernel, [(8 * SUB, 4 * TILE)], (down_a, down_b))
-    above = pass_on(downs, -1)
     (up_a,) = call(add_kernel, [cut], (up_a, pass_on(two_a, 1)))
     (up_b,) = call(add_kernel, [cut], (up_b, pass_on(two_b, 1)), after=up_a)
     piece = [(SUB, 4 * TILE)] * 4
-    first = call(functools.partial(group_kernel, 0), piece, (mine_a, pass_on(up_a, 1), above))
-    second = call(functools.partial(group_kernel, 1), piece, (mine_b, pass_on(up_b, 1), above), after=first[0])
+    first = call(group_kernel, piece, (mine_a, pass_on(up_a, 1), pass_on(down_a, -1)))
+    second = call(group_kernel, piece, (mine_b, pass_on(up_b, 1), pass_on(down_b, -1)), after=first[0])
     chunk = [(SUB, 8 * TILE)]
     (down,) = call(beside_kernel, chunk, (first[3], second[3]))
     (held,) = call(below_kernel, chunk, (first[0], second[0], pass_on(down, -4)))

time: 102 us -> 101 us (level)
  waiting for transfers between devices: 29.9 us -> 13.1 us
  starting transfers between devices: 63.2 us -> 79.4 us
    ppermute x9 -> x10, waiting for transfers between devices: 26.8 us -> 10 us  [pass_on(): return lax.ppermute(value, ('layer', 'row'), pairs)]
    ppermute x9 -> x10, starting transfers between devices: 32.9 us -> 49 us  [pass_on(): return lax.ppermute(value, ('layer', 'row'), pairs)]
    pallas_call x17 -> x16, Pallas kernels: 7.86 us -> 7.82 us  [call(): pl.pallas_call(kernel, out_shape=tuple((jax.ShapeDtypeStruct(s, d) for s,...]
  transfers between devices with their start and end apart: 19 -> 20, of which waited for: 8 -> 7; matrix products, arithmetic and copies ran while one was open for 0% -> 0% of each run, Pallas kernels for 5% -> 5%
where the time goes in v16:
time: 101 us
  starting transfers between devices  79.4 us (79%)
  waiting for transfers between devices  13.1 us (13%)
  Pallas kernels  7.82 us (8%)
    ppermute x10, starting transfers between devices, pass_on(): return lax.ppermute(value, ('layer', 'row'), pairs)  49 us
    ppermute x6, starting transfers between devices, fetch(): return lax.ppermute(value, ('row', 'col'), pairs)  19.7 us
    ppermute x4, starting transfers between devices, swap(): return lax.ppermute(value, 'row', [(i, i ^ 1) for i in range(N_ROW)])  10.6 us
    ppermute x10, waiting for transfers between devices, pass_on(): return lax.ppermute(value, ('layer', 'row'), pairs)  10 us
    pallas_call x16, Pallas kernels, call(): pl.pallas_call(kernel, out_shape=tuple((jax.ShapeDtypeStruct(s, d) for s,...  7.82 us
    ppermute x6, waiting for transfers between devices, fetch(): return lax.ppermute(value, ('row', 'col'), pairs)  2.08 us
  transfers between devices with their start and end apart: 20, of which 7 were waited for; matrix products, arithmetic and copies ran while one was open for 0% of the time, Pallas kernels for 5%

profile of v16, /device:TPU:6, one launch (start us, length us, event | category | flops | bytes accessed | tf_op | source)
XLA Modules:
  0.0 100.7 jit_solution(707459700685289959)
XLA Ops:
  0.0 1.8 %shard_map.28.own = f32[1024,128]{1,0:T(8,128)} custom-call(f32[1024,128]{1,0:T(8,128)} %graph.1, s32[8]{0:T(128)} %bitcast.1), custom_call_target="tpu_custom_call" | custom-call | bytes 1048576 | tf_op jit(solution)/shard_map/pallas_call | solution.py:30
  1.8 1.9 %collective-permute-start.2 = (f32[1024,128]{1,0:T(8,128)}, f32[1024,128]{1,0:T(8,128)S(1)}, u32[]{:S(2)}, u32[]{:S(2)}) collective-permute-start(f32[1024,128]{1,0:T(8,128)} %shard_map.28.own), channel_id=1, source_target_pairs={{0,4},{4,0},{8,12},{12,8},{16,20},{20,16},{24,28},{28,24},{1,5},{5... | collective-permute-start | bytes 1572872 | tf_op jit(solution)/shard_map/ppermute | solution.py:260
  3.8 4.9 %collective-permute-start = (f32[1024,128]{1,0:T(8,128)}, f32[1024,128]{1,0:T(8,128)S(1)}, u32[]{:S(2)}, u32[]{:S(2)}) collective-permute-start(f32[1024,128]{1,0:T(8,128)} %shard_map.28.own), channel_id=1, source_target_pairs={{1,0},{12,4},{2,1},{13,5},{3,2},{14,6},{0,3},{15,7},{9,8},{20,12},... | collective-permute-start | bytes 1572872 | tf_op jit(solution)/shard_map/ppermute | solution.py:269
  8.7 1.9 %collective-permute-start.3 = (f32[1024,128]{1,0:T(8,128)S(1)}, f32[1024,128]{1,0:T(8,128)S(1)}, u32[]{:S(2)}, u32[]{:S(2)}) collective-permute-start(f32[1024,128]{1,0:T(8,128)S(1)} %collective-permute-done.2.other), channel_id=1, source_target_pairs={{3,0},{28,4},{0,1},{29,5},{1,2},{30,6},{2,3},{31,7},{11,8},{4,12},... | collective-permute-start | bytes 1572872 | tf_op jit(solution)/shard_map/ppermute | solution.py:269
  10.6 2.5 %collective-permute-start.6 = (f32[1024,128]{1,0:T(8,128)}, f32[1024,128]{1,0:T(8,128)S(1)}, u32[]{:S(2)}, u32[]{:S(2)}) collective-permute-start(f32[1024,128]{1,0:T(8,128)} %shard_map.28.own), channel_id=1, source_target_pairs={{3,0},{28,4},{0,1},{29,5},{1,2},{30,6},{2,3},{31,7},{11,8},{4,12},... | collective-permute-start | bytes 1572872 | tf_op jit(solution)/shard_map/ppermute | solution.py:269
  13.1 4.6 %collective-permute-start.5 = (f32[1024,128]{1,0:T(8,128)S(1)}, f32[1024,128]{1,0:T(8,128)S(1)}, u32[]{:S(2)}, u32[]{:S(2)}) collective-permute-start(f32[1024,128]{1,0:T(8,128)S(1)} %collective-permute-done.2.other), channel_id=1, source_target_pairs={{1,0},{12,4},{2,1},{13,5},{3,2},{14,6},{0,3},{15,7},{9,8},{20,12},... | collective-permute-start | bytes 1572872 | tf_op jit(solution)/shard_map/ppermute | solution.py:269
  17.7 3.9 %collective-permute-start.1 = (f32[1024,128]{1,0:T(8,128)S(1)}, f32[1024,128]{1,0:T(8,128)S(1)}, u32[]{:S(2)}, u32[]{:S(2)}) collective-permute-start(f32[1024,128]{1,0:T(8,128)S(1)} %collective-permute-done.o1.first), channel_id=1, source_target_pairs={{1,0},{12,4},{2,1},{13,5},{3,2},{14,6},{0,3},{15,7},{9,8},{20,12},... | collective-permute-start | bytes 1572872 | tf_op jit(solution)/shard_map/ppermute | solution.py:269
  21.7 1.9 %collective-permute-start.4 = (f32[1024,128]{1,0:T(8,128)S(1)}, f32[1024,128]{1,0:T(8,128)S(1)}, u32[]{:S(2)}, u32[]{:S(2)}) collective-permute-start(f32[1024,128]{1,0:T(8,128)S(1)} %collective-permute-done.3.s3.second), channel_id=1, source_target_pairs={{3,0},{28,4},{0,1},{29,5},{1,2},{30,6},{2,3},{31,7},{11,8},{4,12},... | collective-permute-start | bytes 1572872 | tf_op jit(solution)/shard_map/ppermute | solution.py:269
  23.7 4.0 %collective-permute-start.8 = (f32[2048,128]{1,0:T(8,128)S(1)}, f32[2048,128]{1,0:T(8,128)S(1)}, u32[]{:S(2)}, u32[]{:S(2)}) collective-permute-start(f32[2048,128]{1,0:T(8,128)S(1)} %shard_map.31), channel_id=1, source_target_pairs={{0,4},{4,0},{8,12},{12,8},{16,20},{20,16},{24,28},{28,24},{1,5},{5... | collective-permute-start | bytes 3145736 | tf_op jit(solution)/shard_map/ppermute | solution.py:260
  27.8 2.7 %collective-permute-start.9 = (f32[2048,128]{1,0:T(8,128)S(1)}, f32[2048,128]{1,0:T(8,128)S(1)}, u32[]{:S(2)}, u32[]{:S(2)}) collective-permute-start(f32[2048,128]{1,0:T(8,128)S(1)} %shard_map.32), channel_id=1, source_target_pairs={{0,4},{4,0},{8,12},{12,8},{16,20},{20,16},{24,28},{28,24},{1,5},{5... | collective-permute-start | bytes 3145736 | tf_op jit(solution)/shard_map/ppermute | solution.py:260
  31.9 2.1 %collective-permute-done.4.refs_1_.s2 = f32[1024,128]{1,0:T(8,128)S(1)} collective-permute-done((f32[1024,128]{1,0:T(8,128)S(1)}, f32[1024,128]{1,0:T(8,128)S(1)}, u32[]{:S(2)}, u32[]{:S(2)}) %collective-permute-start.4) | collective-permute-done | bytes 524320 | tf_op jit(solution)/shard_map/ppermute | solution.py:269
  34.0 2.0 %collective-permute-start.7 = (f32[2048,128]{1,0:T(8,128)S(1)}, f32[2048,128]{1,0:T(8,128)S(1)}, u32[]{:S(2)}, u32[]{:S(2)}) collective-permute-start(f32[2048,128]{1,0:T(8,128)S(1)} %shard_map.30), channel_id=1, source_target_pairs={{0,4},{4,0},{8,12},{12,8},{16,20},{20,16},{24,28},{28,24},{1,5},{5... | collective-permute-start | bytes 3145736 | tf_op jit(solution)/shard_map/ppermute | solution.py:260
  39.3 3.8 %collective-permute-start.10 = (f32[128,512]{1,0:T(8,128)S(1)}, f32[128,512]{1,0:T(8,128)S(1)}, u32[]{:S(2)}, u32[]{:S(2)}) collective-permute-start(f32[128,512]{1,0:T(8,128)S(1)} %get-tuple-element.45), channel_id=1, source_target_pairs={{0,32},{4,484},{8,40},{12,492},{16,48},{20,500},{24,56},{28,508},{... | collective-permute-start | bytes 786440 | tf_op jit(solution)/shard_map/ppermute | solution.py:278
  44.5 3.8 %collective-permute-start.13 = (f32[128,512]{1,0:T(8,128)S(1)}, f32[128,512]{1,0:T(8,128)S(1)}, u32[]{:S(2)}, u32[]{:S(2)}) collective-permute-start(f32[128,512]{1,0:T(8,128)S(1)} %get-tuple-element.54), channel_id=1, source_target_pairs={{0,32},{4,484},{8,40},{12,492},{16,48},{20,500},{24,56},{28,508},{... | collective-permute-start | bytes 786440 | tf_op jit(solution)/shard_map/ppermute | solution.py:278
  48.3 7.6 %collective-permute-start.12 = (f32[128,512]{1,0:T(8,128)S(1)}, f32[128,512]{1,0:T(8,128)S(1)}, u32[]{:S(2)}, u32[]{:S(2)}) collective-permute-start(f32[128,512]{1,0:T(8,128)S(1)} %get-tuple-element.46), channel_id=1, source_target_pairs={{0,480},{4,36},{8,488},{12,44},{16,496},{20,52},{24,504},{28,60},{... | collective-permute-start | bytes 786440 | tf_op jit(solution)/shard_map/ppermute | solution.py:278
  56.0 1.9 %collective-permute-start.11 = (f32[128,512]{1,0:T(8,128)S(1)}, f32[128,512]{1,0:T(8,128)S(1)}, u32[]{:S(2)}, u32[]{:S(2)}) collective-permute-start(f32[128,512]{1,0:T(8,128)S(1)} %shard_map.35.refs_2_), channel_id=1, source_target_pairs={{0,32},{4,484},{8,40},{12,492},{16,48},{20,500},{24,56},{28,508},{... | collective-permute-start | bytes 786440 | tf_op jit(solution)/shard_map/ppermute | solution.py:278
  57.9 5.1 %collective-permute-start.15 = (f32[128,512]{1,0:T(8,128)S(1)}, f32[128,512]{1,0:T(8,128)S(1)}, u32[]{:S(2)}, u32[]{:S(2)}) collective-permute-start(f32[128,512]{1,0:T(8,128)S(1)} %get-tuple-element.55), channel_id=1, source_target_pairs={{0,480},{4,36},{8,488},{12,44},{16,496},{20,52},{24,504},{28,60},{... | collective-permute-start | bytes 786440 | tf_op jit(solution)/shard_map/ppermute | solution.py:278
  63.1 1.9 %collective-permute-start.14 = (f32[128,512]{1,0:T(8,128)S(1)}, f32[128,512]{1,0:T(8,128)S(1)}, u32[]{:S(2)}, u32[]{:S(2)}) collective-permute-start(f32[128,512]{1,0:T(8,128)S(1)} %shard_map.38), channel_id=1, source_target_pairs={{0,32},{4,484},{8,40},{12,492},{16,48},{20,500},{24,56},{28,508},{... | collective-permute-start | bytes 786440 | tf_op jit(solution)/shard_map/ppermute | solution.py:278
  66.0 5.7 %collective-permute-start.17 = (f32[32,512]{1,0:T(8,128)S(1)}, f32[32,512]{1,0:T(8,128)S(1)}, u32[]{:S(2)}, u32[]{:S(2)}) collective-permute-start(f32[32,512]{1,0:T(8,128)S(1)} %get-tuple-element.60), channel_id=1, source_target_pairs={{0,128},{4,388},{8,136},{12,396},{16,144},{20,404},{24,152},{28,41... | collective-permute-start | bytes 196616 | tf_op jit(solution)/shard_map/ppermute | solution.py:278
  72.6 8.3 %collective-permute-start.18 = (f32[32,512]{1,0:T(8,128)S(1)}, f32[32,512]{1,0:T(8,128)S(1)}, u32[]{:S(2)}, u32[]{:S(2)}) collective-permute-start(f32[32,512]{1,0:T(8,128)S(1)} %get-tuple-element.62), channel_id=1, source_target_pairs={{0,128},{4,388},{8,136},{12,396},{16,144},{20,404},{24,152},{28,41... | collective-permute-start | bytes 196616 | tf_op jit(solution)/shard_map/ppermute | solution.py:278
  80.9 1.9 %collective-permute-start.16 = (f32[32,1024]{1,0:T(8,128)S(1)}, f32[32,1024]{1,0:T(8,128)S(1)}, u32[]{:S(2)}, u32[]{:S(2)}) collective-permute-start(f32[32,1024]{1,0:T(8,128)S(1)} %shard_map.40), channel_id=1, source_target_pairs={{0,384},{4,132},{8,392},{12,140},{16,400},{20,148},{24,408},{28,15... | collective-permute-start | bytes 393224 | tf_op jit(solution)/shard_map/ppermute | solution.py:278
  82.9 4.8 %collective-permute-done.18.second_came = f32[32,512]{1,0:T(8,128)S(1)} collective-permute-done((f32[32,512]{1,0:T(8,128)S(1)}, f32[32,512]{1,0:T(8,128)S(1)}, u32[]{:S(2)}, u32[]{:S(2)}) %collective-permute-start.18) | collective-permute-done | bytes 65568 | tf_op jit(solution)/shard_map/ppermute | solution.py:278
  87.6 8.8 %collective-permute-start.19 = (f32[32,1024]{1,0:T(8,128)S(1)}, f32[32,1024]{1,0:T(8,128)S(1)}, u32[]{:S(2)}, u32[]{:S(2)}) collective-permute-start(f32[32,1024]{1,0:T(8,128)S(1)} %shard_map.42), channel_id=1, source_target_pairs={{0,128},{4,388},{8,136},{12,396},{16,144},{20,404},{24,152},{28,41... | collective-permute-start | bytes 393224 | tf_op jit(solution)/shard_map/ppermute | solution.py:278
  97.7 2.3 %collective-permute-done.19.from_above = f32[32,1024]{1,0:T(8,128)S(1)} collective-permute-done((f32[32,1024]{1,0:T(8,128)S(1)}, f32[32,1024]{1,0:T(8,128)S(1)}, u32[]{:S(2)}, u32[]{:S(2)}) %collective-permute-start.19) | collective-permute-done | bytes 131104 | tf_op jit(solution)/shard_map/ppermute | solution.py:278
  (34 shorter events, 10.0 us)
Async XLA Ops:
  1.8 6.9 %collective-permute-start.2 = (f32[1024,128]{1,0:T(8,128)}, f32[1024,128]{1,0:T(8,128)S(1)}, u32[]{:S(2)}, u32[]{:S(2)}) collective-permute-start(f32[1024,128]{1,0:T(8,128)} %shard_map.28.own), channel_id=1, source_target_pairs={{0,4},{4,0},{8,12},{12,8},{16,20},{20,16},{24,28},{28,24},{1,5},{5... | collective-permute-start | bytes 1572872 | tf_op jit(solution)/shard_map/ppermute | solution.py:260
  3.8 13.9 %collective-permute-start = (f32[1024,128]{1,0:T(8,128)}, f32[1024,128]{1,0:T(8,128)S(1)}, u32[]{:S(2)}, u32[]{:S(2)}) collective-permute-start(f32[1024,128]{1,0:T(8,128)} %shard_map.28.own), channel_id=1, source_target_pairs={{1,0},{12,4},{2,1},{13,5},{3,2},{14,6},{0,3},{15,7},{9,8},{20,12},... | collective-permute-start | bytes 1572872 | tf_op jit(solution)/shard_map/ppermute | solution.py:269
  8.7 12.9 %collective-permute-start.3 = (f32[1024,128]{1,0:T(8,128)S(1)}, f32[1024,128]{1,0:T(8,128)S(1)}, u32[]{:S(2)}, u32[]{:S(2)}) collective-permute-start(f32[1024,128]{1,0:T(8,128)S(1)} %collective-permute-done.2.other), channel_id=1, source_target_pairs={{3,0},{28,4},{0,1},{29,5},{1,2},{30,6},{2,3},{31,7},{11,8},{4,12},... | collective-permute-start | bytes 1572872 | tf_op jit(solution)/shard_map/ppermute | solution.py:269
  10.6 17.0 %collective-permute-start.6 = (f32[1024,128]{1,0:T(8,128)}, f32[1024,128]{1,0:T(8,128)S(1)}, u32[]{:S(2)}, u32[]{:S(2)}) collective-permute-start(f32[1024,128]{1,0:T(8,128)} %shard_map.28.own), channel_id=1, source_target_pairs={{3,0},{28,4},{0,1},{29,5},{1,2},{30,6},{2,3},{31,7},{11,8},{4,12},... | collective-permute-start | bytes 1572872 | tf_op jit(solution)/shard_map/ppermute | solution.py:269
  13.1 14.5 %collective-permute-start.5 = (f32[1024,128]{1,0:T(8,128)S(1)}, f32[1024,128]{1,0:T(8,128)S(1)}, u32[]{:S(2)}, u32[]{:S(2)}) collective-permute-start(f32[1024,128]{1,0:T(8,128)S(1)} %collective-permute-done.2.other), channel_id=1, source_target_pairs={{1,0},{12,4},{2,1},{13,5},{3,2},{14,6},{0,3},{15,7},{9,8},{20,12},... | collective-permute-start | bytes 1572872 | tf_op jit(solution)/shard_map/ppermute | solution.py:269
  17.7 14.1 %collective-permute-start.1 = (f32[1024,128]{1,0:T(8,128)S(1)}, f32[1024,128]{1,0:T(8,128)S(1)}, u32[]{:S(2)}, u32[]{:S(2)}) collective-permute-start(f32[1024,128]{1,0:T(8,128)S(1)} %collective-permute-done.o1.first), channel_id=1, source_target_pairs={{1,0},{12,4},{2,1},{13,5},{3,2},{14,6},{0,3},{15,7},{9,8},{20,12},... | collective-permute-start | bytes 1572872 | tf_op jit(solution)/shard_map/ppermute | solution.py:269
  21.7 12.3 %collective-permute-start.4 = (f32[1024,128]{1,0:T(8,128)S(1)}, f32[1024,128]{1,0:T(8,128)S(1)}, u32[]{:S(2)}, u32[]{:S(2)}) collective-permute-start(f32[1024,128]{1,0:T(8,128)S(1)} %collective-permute-done.3.s3.second), channel_id=1, source_target_pairs={{3,0},{28,4},{0,1},{29,5},{1,2},{30,6},{2,3},{31,7},{11,8},{4,12},... | collective-permute-start | bytes 1572872 | tf_op jit(solution)/shard_map/ppermute | solution.py:269
  23.7 6.8 %copy-start = (f32[1024,128]{1,0:T(8,128)S(1)}, f32[1024,128]{1,0:T(8,128)}, u32[]{:S(2)}) copy-start(f32[1024,128]{1,0:T(8,128)} %shard_map.28.own) | copy-start | bytes 1572868
  23.7 12.4 %collective-permute-start.8 = (f32[2048,128]{1,0:T(8,128)S(1)}, f32[2048,128]{1,0:T(8,128)S(1)}, u32[]{:S(2)}, u32[]{:S(2)}) collective-permute-start(f32[2048,128]{1,0:T(8,128)S(1)} %shard_map.31), channel_id=1, source_target_pairs={{0,4},{4,0},{8,12},{12,8},{16,20},{20,16},{24,28},{28,24},{1,5},{5... | collective-permute-start | bytes 3145736 | tf_op jit(solution)/shard_map/ppermute | solution.py:260
  27.8 8.3 %collective-permute-start.9 = (f32[2048,128]{1,0:T(8,128)S(1)}, f32[2048,128]{1,0:T(8,128)S(1)}, u32[]{:S(2)}, u32[]{:S(2)}) collective-permute-start(f32[2048,128]{1,0:T(8,128)S(1)} %shard_map.32), channel_id=1, source_target_pairs={{0,4},{4,0},{8,12},{12,8},{16,20},{20,16},{24,28},{28,24},{1,5},{5... | collective-permute-start | bytes 3145736 | tf_op jit(solution)/shard_map/ppermute | solution.py:260
  34.0 4.6 %collective-permute-start.7 = (f32[2048,128]{1,0:T(8,128)S(1)}, f32[2048,128]{1,0:T(8,128)S(1)}, u32[]{:S(2)}, u32[]{:S(2)}) collective-permute-start(f32[2048,128]{1,0:T(8,128)S(1)} %shard_map.30), channel_id=1, source_target_pairs={{0,4},{4,0},{8,12},{12,8},{16,20},{20,16},{24,28},{28,24},{1,5},{5... | collective-permute-start | bytes 3145736 | tf_op jit(solution)/shard_map/ppermute | solution.py:260
  39.3 16.6 %collective-permute-start.10 = (f32[128,512]{1,0:T(8,128)S(1)}, f32[128,512]{1,0:T(8,128)S(1)}, u32[]{:S(2)}, u32[]{:S(2)}) collective-permute-start(f32[128,512]{1,0:T(8,128)S(1)} %get-tuple-element.45), channel_id=1, source_target_pairs={{0,32},{4,484},{8,40},{12,492},{16,48},{20,500},{24,56},{28,508},{... | collective-permute-start | bytes 786440 | tf_op jit(solution)/shard_map/ppermute | solution.py:278
  44.5 18.6 %collective-permute-start.13 = (f32[128,512]{1,0:T(8,128)S(1)}, f32[128,512]{1,0:T(8,128)S(1)}, u32[]{:S(2)}, u32[]{:S(2)}) collective-permute-start(f32[128,512]{1,0:T(8,128)S(1)} %get-tuple-element.54), channel_id=1, source_target_pairs={{0,32},{4,484},{8,40},{12,492},{16,48},{20,500},{24,56},{28,508},{... | collective-permute-start | bytes 786440 | tf_op jit(solution)/shard_map/ppermute | solution.py:278
  48.3 16.7 %collective-permute-start.12 = (f32[128,512]{1,0:T(8,128)S(1)}, f32[128,512]{1,0:T(8,128)S(1)}, u32[]{:S(2)}, u32[]{:S(2)}) collective-permute-start(f32[128,512]{1,0:T(8,128)S(1)} %get-tuple-element.46), channel_id=1, source_target_pairs={{0,480},{4,36},{8,488},{12,44},{16,496},{20,52},{24,504},{28,60},{... | collective-permute-start | bytes 786440 | tf_op jit(solution)/shard_map/ppermute | solution.py:278
  56.0 9.9 %collective-permute-start.11 = (f32[128,512]{1,0:T(8,128)S(1)}, f32[128,512]{1,0:T(8,128)S(1)}, u32[]{:S(2)}, u32[]{:S(2)}) collective-permute-start(f32[128,512]{1,0:T(8,128)S(1)} %shard_map.35.refs_2_), channel_id=1, source_target_pairs={{0,32},{4,484},{8,40},{12,492},{16,48},{20,500},{24,56},{28,508},{... | collective-permute-start | bytes 786440 | tf_op jit(solution)/shard_map/ppermute | solution.py:278
  57.9 13.8 %collective-permute-start.15 = (f32[128,512]{1,0:T(8,128)S(1)}, f32[128,512]{1,0:T(8,128)S(1)}, u32[]{:S(2)}, u32[]{:S(2)}) collective-permute-start(f32[128,512]{1,0:T(8,128)S(1)} %get-tuple-element.55), channel_id=1, source_target_pairs={{0,480},{4,36},{8,488},{12,44},{16,496},{20,52},{24,504},{28,60},{... | collective-permute-start | bytes 786440 | tf_op jit(solution)/shard_map/ppermute | solution.py:278
  63.1 9.5 %collective-permute-start.14 = (f32[128,512]{1,0:T(8,128)S(1)}, f32[128,512]{1,0:T(8,128)S(1)}, u32[]{:S(2)}, u32[]{:S(2)}) collective-permute-start(f32[128,512]{1,0:T(8,128)S(1)} %shard_map.38), channel_id=1, source_target_pairs={{0,32},{4,484},{8,40},{12,492},{16,48},{20,500},{24,56},{28,508},{... | collective-permute-start | bytes 786440 | tf_op jit(solution)/shard_map/ppermute | solution.py:278
  66.0 16.9 %collective-permute-start.17 = (f32[32,512]{1,0:T(8,128)S(1)}, f32[32,512]{1,0:T(8,128)S(1)}, u32[]{:S(2)}, u32[]{:S(2)}) collective-permute-start(f32[32,512]{1,0:T(8,128)S(1)} %get-tuple-element.60), channel_id=1, source_target_pairs={{0,128},{4,388},{8,136},{12,396},{16,144},{20,404},{24,152},{28,41... | collective-permute-start | bytes 196616 | tf_op jit(solution)/shard_map/ppermute | solution.py:278
  72.6 15.0 %collective-permute-start.18 = (f32[32,512]{1,0:T(8,128)S(1)}, f32[32,512]{1,0:T(8,128)S(1)}, u32[]{:S(2)}, u32[]{:S(2)}) collective-permute-start(f32[32,512]{1,0:T(8,128)S(1)} %get-tuple-element.62), channel_id=1, source_target_pairs={{0,128},{4,388},{8,136},{12,396},{16,144},{20,404},{24,152},{28,41... | collective-permute-start | bytes 196616 | tf_op jit(solution)/shard_map/ppermute | solution.py:278
  80.9 16.8 %collective-permute-start.16 = (f32[32,1024]{1,0:T(8,128)S(1)}, f32[32,1024]{1,0:T(8,128)S(1)}, u32[]{:S(2)}, u32[]{:S(2)}) collective-permute-start(f32[32,1024]{1,0:T(8,128)S(1)} %shard_map.40), channel_id=1, source_target_pairs={{0,384},{4,132},{8,392},{12,140},{16,400},{20,148},{24,408},{28,15... | collective-permute-start | bytes 393224 | tf_op jit(solution)/shard_map/ppermute | solution.py:278
  87.6 12.3 %collective-permute-start.19 = (f32[32,1024]{1,0:T(8,128)S(1)}, f32[32,1024]{1,0:T(8,128)S(1)}, u32[]{:S(2)}, u32[]{:S(2)}) collective-permute-start(f32[32,1024]{1,0:T(8,128)S(1)} %shard_map.42), channel_id=1, source_target_pairs={{0,128},{4,388},{8,136},{12,396},{16,144},{20,404},{24,152},{28,41... | collective-permute-start | bytes 393224 | tf_op jit(solution)/shard_map/ppermute | solution.py:278
